TPU v7x, 32 devices: a whole 2x2x4 slice. The times are simulated.
32 devices in a mesh: groups: 2 (over y), rows: 4 (over z), cols: 2 (over x), pair: 2 (over core).
Axes of the slice: x: 2, y: 2, z: 4, core: 2. Of those that a mesh axis runs over, the one named last changes fastest.
Arguments:
- frames: bfloat16 [2, 240, 60, 256], P('pair', ('groups', 'rows'), 'cols'), parts along dimension 1, may hold values from -28 to 28
- conv_first: bfloat16 [9, 256, 256], replicated, may hold values from -0.125 to 0.125
- conv_second: bfloat16 [9, 256, 256], replicated, may hold values from -0.125 to 0.125
- candidates: int32 [8, 2, 9], P(('groups', 'rows'), 'cols'), parts along dimension 0, may hold values from -1 to 8, as said below
- counts: int32 [8, 2], P(('groups', 'rows'), 'cols'), parts along dimension 0, may hold values from 1 to 6, as said below
- cotangent: float32 [2, 240, 60], P(None, ('groups', 'rows', 'pair'), 'cols'), parts along dimension 1, may hold values from -1536 to 1536
Outputs:
- flow: float32 [2, 240, 60], P(None, ('groups', 'rows', 'pair'), 'cols'), parts along dimension 1
- grad_first: float32 [240, 60, 256], P(('groups', 'rows', 'pair'), 'cols'), parts along dimension 0
- grad_second: float32 [240, 60, 256], P(('groups', 'rows', 'pair'), 'cols'), parts along dimension 0
There are 2 independent parts, one for each index of `groups`. A program takes and returns all parts, laid end to end along the dimension named above; an argument that names none is the same for every part. Nothing has to cross between parts.
Inputs may be any that keep to these rules, and one draw needn't show every extreme that they name: `candidates`: for each query tile the first counts entries are different codes of tiles of its 3 x 3 neighbourhood that lie inside the grid, the first of them 4 (the tile itself); the remaining entries are -1. `counts`: some tile lists every tile of its neighbourhood inside the grid, 6.
All inputs are finite; a program needn't handle non-finite values.
Results may differ from a plain program's by a relative error of at most 0.0095.
The roundings to bfloat16 on the way count: a program that leaves them out, or rounds other values in their place, can miss the bound.
Values may be sent and summed in bfloat16 or wider, within the bound.
No kernel may reach another device: no remote copies, remote signals or barrier semaphores. Data moves between devices by JAX's collectives and lax.ppermute only.
A program may use at most 64 MiB of HBM per device.

v0:
```python
import jax
import jax.numpy as jnp
from jax import lax
from jax.sharding import PartitionSpec as P

TILE = 30
HALF = 15


def padded(cells, sides, width):
    for axis, dim in sides:
        count = lax.axis_size(axis)
        ends = count - 1
        head = lax.slice_in_dim(cells, 0, width, axis=dim)
        tail = lax.slice_in_dim(cells, cells.shape[dim] - width, cells.shape[dim], axis=dim)
        cells = jnp.concatenate(
            [
                lax.ppermute(tail, axis, [(i, (i + 1) % count) for i in range(ends)]),
                cells,
                lax.ppermute(head, axis, [((i + 1) % count, i) for i in range(ends)]),
            ],
            axis=dim,
        )
    return cells


def from_partner(value, axis, bit):
    mask = 2**bit
    pairs = [(source, source ^ mask) for source in range(lax.axis_size(axis))]
    return lax.ppermute(value, axis, pairs)


def shifted(value, axis, steps):
    count = lax.axis_size(axis)
    leading, last = (max(0, -steps), min(count, count - steps))
    return lax.ppermute(value, axis, [(source, source + steps) for source in range(leading, last)])


def conv_valid(field_ext, weights, out_rows, out_cols):
    channels = field_ext.shape[2]
    accumulated = jnp.zeros((out_rows * out_cols, weights.shape[2]), jnp.float32)
    for tap_index in range(9):
        row_start = tap_index // 3
        col_start = tap_index % 3
        window = field_ext[row_start : row_start + out_rows, col_start : col_start + out_cols]
        accumulated = accumulated + jnp.dot(
            window.reshape(out_rows * out_cols, channels),
            weights[tap_index],
            preferred_element_type=jnp.float32,
        )
    return accumulated.reshape(out_rows, out_cols, weights.shape[2])


def softmax_stats(query, fetch, code_list, count, key_row, key_col):
    scale = query.shape[1] ** (-0.5)
    cells = query.shape[0]

    def softmax_step(slot_index, state):
        best, norm_sum, sum_row, sum_col = state
        tile_code = code_list[slot_index]
        targets = fetch(tile_code)
        pos_row = (tile_code // 3 - 1).astype(jnp.float32) + key_row
        pos_col = (tile_code % 3 - 1).astype(jnp.float32) + key_col
        scores = (
            lax.dot_general(
                query, targets, (((1,), (1,)), ((), ())), preferred_element_type=jnp.float32
            )
            * scale
        )
        new_best = jnp.maximum(best, jnp.max(scores, axis=1))
        factor = jnp.exp(best - new_best)
        expo = jnp.exp(scores - new_best[:, None])
        norm_sum = norm_sum * factor + jnp.sum(expo, axis=1)
        sum_row = sum_row * factor + jnp.sum(expo * pos_row[None, :], axis=1)
        sum_col = sum_col * factor + jnp.sum(expo * pos_col[None, :], axis=1)
        return (new_best, norm_sum, sum_row, sum_col)

    start = (
        jnp.full((cells,), -jnp.inf, jnp.float32),
        jnp.zeros((cells,), jnp.float32),
        jnp.zeros((cells,), jnp.float32),
        jnp.zeros((cells,), jnp.float32),
    )
    return lax.fori_loop(0, count, softmax_step, start)


def gradient_pass(
    query,
    fetch,
    code_list,
    count,
    key_row,
    key_col,
    query_row,
    query_col,
    cot_row,
    cot_col,
    stats,
    accumulator,
    deposit,
):
    scale = query.shape[1] ** (-0.5)
    best, norm_sum, sum_row, sum_col = stats
    flow_row = sum_row / norm_sum - query_row
    flow_col = sum_col / norm_sum - query_col
    mean_pull = cot_row * flow_row + cot_col * flow_col

    def gradient_step(slot_index, state):
        grad_query, acc_state = state
        tile_code = code_list[slot_index]
        targets = fetch(tile_code)
        pos_row = (tile_code // 3 - 1).astype(jnp.float32) + key_row
        pos_col = (tile_code % 3 - 1).astype(jnp.float32) + key_col
        scores = (
            lax.dot_general(
                query, targets, (((1,), (1,)), ((), ())), preferred_element_type=jnp.float32
            )
            * scale
        )
        probs = jnp.exp(scores - best[:, None]) / norm_sum[:, None]
        pull = cot_row[:, None] * (pos_row[None, :] - query_row[:, None]) + cot_col[:, None] * (
            pos_col[None, :] - query_col[:, None]
        )
        dscore = (probs * (pull - mean_pull[:, None]) * scale).astype(jnp.bfloat16)
        grad_query = grad_query + jnp.dot(dscore, targets, preferred_element_type=jnp.float32)
        contrib = lax.dot_general(
            dscore, query, (((0,), (0,)), ((), ())), preferred_element_type=jnp.float32
        )
        return (grad_query, deposit(acc_state, tile_code, contrib))

    start = (jnp.zeros(query.shape, jnp.float32), accumulator)
    return (flow_row, flow_col, lax.fori_loop(0, count, gradient_step, start))


def make_access(second_ext, tile_slot, channels):
    anchor = jnp.zeros((), jnp.int32)

    def corner(tile_code):
        return (TILE * (tile_code // 3), TILE * (tile_slot + tile_code % 3), anchor)

    def fetch(tile_code):
        return lax.dynamic_slice(second_ext, corner(tile_code), (TILE, TILE, channels)).reshape(
            TILE * TILE, channels
        )

    def deposit(acc_in, tile_code, contrib):
        where_at = corner(tile_code)
        current = lax.dynamic_slice(acc_in, where_at, (TILE, TILE, channels))
        return lax.dynamic_update_slice(
            acc_in, current + contrib.reshape(TILE, TILE, channels), where_at
        )

    return (fetch, deposit)


def shards(frames, conv_first, conv_second, candidates, counts, cotangent):
    frame = frames[0]
    band_width = frame.shape[1]
    channels = frame.shape[2]
    col_index = lax.axis_index("cols")
    core_index = lax.axis_index("pair")
    frame_ext = padded(frame, (("rows", 0), ("cols", 1)), 1)
    hidden = jax.nn.relu(conv_valid(frame_ext, conv_first, TILE, band_width)).astype(jnp.bfloat16)
    hidden_ext = padded(hidden, (("rows", 0), ("cols", 1)), 1)
    features = (
        frame.astype(jnp.float32) + conv_valid(hidden_ext, conv_second, TILE, band_width)
    ).astype(jnp.bfloat16)
    partner = from_partner(features, "pair", 0)
    first = jnp.where(core_index == 0, features, partner)
    second = jnp.where(core_index == 0, partner, features)
    second_ext = padded(second, (("rows", 0), ("cols", 1)), TILE)
    query_band = lax.dynamic_slice_in_dim(first, core_index * HALF, HALF, 0)
    key_cell = jnp.arange(TILE * TILE, dtype=jnp.int32)
    key_row = (key_cell // TILE).astype(jnp.float32) / TILE
    key_col = (key_cell % TILE).astype(jnp.float32) / TILE
    query_cell = jnp.arange(HALF * TILE, dtype=jnp.int32)
    query_row = (core_index * HALF + query_cell // TILE).astype(jnp.float32) / TILE
    query_col = (query_cell % TILE).astype(jnp.float32) / TILE
    terms = jnp.zeros(second_ext.shape, jnp.float32)
    fetch, deposit = make_access(second_ext, 0, channels)
    query = query_band.reshape(HALF * TILE, channels)
    pulls = cotangent.reshape(2, HALF * TILE)
    code_list = candidates[0, 0]
    count = counts[0, 0]
    stats = softmax_stats(query, fetch, code_list, count, key_row, key_col)
    flow_row, flow_col, (grad_query, terms) = gradient_pass(
        query,
        fetch,
        code_list,
        count,
        key_row,
        key_col,
        query_row,
        query_col,
        pulls[0],
        pulls[1],
        stats,
        terms,
        deposit,
    )
    flow_parts = jnp.stack([flow_row, flow_col]).reshape(2, HALF, TILE)
    grad_parts = grad_query.reshape(HALF, TILE, channels)
    col_count = lax.axis_size("cols")
    own_terms = terms[TILE : 2 * TILE, TILE : TILE + band_width]
    for row_step in (-1, 0, 1):
        for col_step in (-1, 0, 1):
            if row_step == 0 and col_step == 0:
                continue
            band_terms = terms[TILE * (1 + row_step) : TILE * (2 + row_step)]
            if col_step == -1:
                piece = band_terms[:, 0:TILE]
            elif col_step == 0:
                piece = band_terms[:, TILE : TILE + band_width]
            else:
                piece = band_terms[:, TILE + band_width :]
            valid_dest = (col_index + col_step >= 0) & (col_index + col_step < col_count)
            piece = jnp.where(valid_dest, piece, 0.0)
            arrived = shifted(piece, ("rows", "cols"), row_step * col_count + col_step)
            if col_step == -1:
                own_terms = own_terms.at[:, band_width - TILE :].add(arrived)
            elif col_step == 0:
                own_terms = own_terms + arrived
            else:
                own_terms = own_terms.at[:, 0:TILE].add(arrived)
    grad_second = lax.psum_scatter(own_terms, "pair", scatter_dimension=0, tiled=True)
    return (flow_parts, grad_parts, grad_second)


def solution(mesh):
    in_specs = (
        P("pair", ("groups", "rows"), "cols", None),
        P(),
        P(),
        P(("groups", "rows"), "cols", None),
        P(("groups", "rows"), "cols"),
        P(None, ("groups", "rows", "pair"), "cols"),
    )
    out_specs = (
        P(None, ("groups", "rows", "pair"), "cols"),
        P(("groups", "rows", "pair"), "cols", None),
        P(("groups", "rows", "pair"), "cols", None),
    )
    return jax.shard_map(shards, mesh=mesh, in_specs=in_specs, out_specs=out_specs, check_vma=False)
```

profile of v0, /device:TPU:12, one launch (start us, length us, event | category | flops | bytes accessed | tf_op | source)
XLA Modules:
  0.0 429.7 jit_solution(7559912732203871769)
XLA Ops:
  10.4 3.5 collective-permute-start
  17.0 3.4 collective-permute-start.2
  41.3 3.5 collective-permute-start.4
  47.3 3.3 collective-permute-done.5
  84.7 2.4 collective-permute-start.10
  87.1 3.5 collective-permute-start.9
  90.5 9.3 %collective-permute-done.10 = bf16[30,30,256]{2,1,0:T(8,128)(2,1)S(1)} collective-permute-done((bf16[30,30,256]{2,1,0:T(8,128)(2,1)S(1)}, bf16[30,30,256]{2,1,0:T(8,128)(2,1)S(1)}, u32[]{:S(2)}, u32[]{:S(2)}) %collective-permute-start.10) | collective-permute-done | bytes 460832 | tf_op jit(solution)/shard_map/ppermute | solution.py:20
  104.5 6.8 %collective-permute-start.11 = (bf16[90,30,256]{2,1,0:T(8,128)(2,1)}, bf16[90,30,256]{2,1,0:T(8,128)(2,1)}, u32[]{:S(2)}, u32[]{:S(2)}) collective-permute-start(bf16[90,30,256]{2,1,0:T(8,128)(2,1)} %pad_maximum_fusion.1), channel_id=1, source_target_pairs={{0,2},{1,3},{4,6},{5,7},{8,10},{9,11},{12,14},{13,15},{16,18},{17,... | collective-permute-start | bytes 4147208 | tf_op jit(solution)/shard_map/ppermute | solution.py:18
  111.9 26.7 %collective-permute-done.12 = bf16[90,30,256]{2,1,0:T(8,128)(2,1)} collective-permute-done((bf16[90,30,256]{2,1,0:T(8,128)(2,1)}, bf16[90,30,256]{2,1,0:T(8,128)(2,1)}, u32[]{:S(2)}, u32[]{:S(2)}) %collective-permute-start.12) | collective-permute-done | bytes 1382432 | tf_op jit(solution)/shard_map/ppermute | solution.py:20
  140.9 4.7 %pad_maximum_fusion = bf16[90,90,256]{2,1,0:T(8,128)(2,1)} fusion(bf16[90,30,256]{2,1,0:T(8,128)(2,1)} %collective-permute-done.12, bf16[30,30,256]{2,1,0:T(8,128)(2,1)S(1)} %collective-permute-done.10, bf16[30,30,256]{2,1,0:T(8,128)(2,1)S(1)} %broadcast_select_fusion, bf16[30,30,256]{2,1,0:T(8,128)(2,1)S(1)} %collective-permute-done.9, ...), kind=kLoop, calls=%fused_computation.72 | loop fusion | flops 20736000 | bytes 8294400 | tf_op jit(solution)/shard_map/concatenate | solution.py:16
  145.7 12.8 %while.48 = (s32[]{:T(128)}, f32[450]{0:T(512)S(1)}, f32[450]{0:T(512)S(1)}, f32[450]{0:T(512)S(1)}, f32[450]{0:T(512)S(1)}, /*index=5*/s32[]{:T(128)}, s32[9]{0...) while((s32[]{:T(128)}, f32[450]{0:T(512)S(1)}, ...), condition=%wide.region_5.6_spmd.clone, body=%wide.region_0.5_spmd.clone.sunk | while | flops 211023008 | bytes 5827082 | solution.py:84
  158.5 4.5 %broadcast_in_dim.30 = f32[90,90,256]{2,1,0:T(8,128)} broadcast(f32[]{:T(128)} %constant.396.clone.1), dimensions={} | broadcast | bytes 8294404 | tf_op jit(solution)/shard_map/broadcast_in_dim | solution.py:179
  163.1 28.9 %while.49 = (s32[]{:T(128)}, f32[450,256]{1,0:T(8,128)S(1)}, f32[90,90,256]{2,1,0:T(8,128)}, s32[]{:T(128)}, s32[9]{0:T(128)S(1)}, /*index=5*/bf16[90,90,256]{2,...) while((s32[]{:T(128)}, f32[450,256]{1,0:T(8,128)S(1)}, ...), condition=%wide.region_7.8_spmd.clone, body=%wide.region_6.7_spmd.clone.sunk | while | flops 627309376 | bytes 13981130 | solution.py:132
  171.3 6.0 %dynamic_update_slice.9 = f32[90,90,256]{2,1,0:T(8,128)} dynamic-update-slice(f32[90,90,256]{2,1,0:T(8,128)} %get-tuple-element.965, f32[30,30,256]{2,1,0:T(8,128)S(1)} %dynamic-slice_add_fusion.2, s32[]{:T(128)S(6)} %select_n.332, s32[]{:T(128)S(6)} %select_n.334, s32[]{:T(128)} %constant.394.clone.1..sunk.1) | dynamic-update-slice | bytes 1843204 | tf_op jit(solution)/shard_map/while/body/dynamic_update_slice | solution.py:149
  185.5 5.8 %dynamic_update_slice.9 = f32[90,90,256]{2,1,0:T(8,128)} dynamic-update-slice(f32[90,90,256]{2,1,0:T(8,128)} %get-tuple-element.965, f32[30,30,256]{2,1,0:T(8,128)S(1)} %dynamic-slice_add_fusion.2, s32[]{:T(128)S(6)} %select_n.332, s32[]{:T(128)S(6)} %select_n.334, s32[]{:T(128)} %constant.394.clone.1..sunk.1) | dynamic-update-slice | bytes 1843204 | tf_op jit(solution)/shard_map/while/body/dynamic_update_slice | solution.py:149
  191.9 4.8 %slice_select_fusion.7 = (f32[30,30,256]{2,1,0:T(8,128)S(1)}, f32[30,30,256]{2,1,0:T(8,128)S(1)}, f32[30,30,256]{2,1,0:T(8,128)S(1)}, f32[30,30,256]{2,1,0:T(8,1...) fusion(f32[90,90,256]{2,1,0:T(8,128)} %get-tuple-element.560, ...), kind=kLoop, calls=%fused_computation.100 | loop fusion | flops 1843200 | bytes 14745603 | tf_op jit(solution)/shard_map/jit(_where)/select_n | solution.py:217
  196.8 86.4 %collective-permute-start.20 = (f32[30,30,256]{2,1,0:T(8,128)S(1)}, f32[30,30,256]{2,1,0:T(8,128)S(1)}, u32[]{:S(2)}, u32[]{:S(2)}) collective-permute-start(f32[30,30,256]{2,1,0:T(8,128)S(1)} %get-tuple-element.689), channel_id=1, source_target_pairs={{0,6},{2,8},{4,10},{6,12},{8,14},{1,7},{3,9},{5,11},{7,13},{9,15},... | collective-permute-start | bytes 2764808 | tf_op jit(solution)/shard_map/ppermute | solution.py:36
  288.9 4.8 %collective-permute-start.16 = (f32[30,30,256]{2,1,0:T(8,128)S(1)}, f32[30,30,256]{2,1,0:T(8,128)S(1)}, u32[]{:S(2)}, u32[]{:S(2)}) collective-permute-start(f32[30,30,256]{2,1,0:T(8,128)S(1)} %get-tuple-element.686), channel_id=1, source_target_pairs={{2,0},{4,2},{6,4},{8,6},{10,8},{12,10},{14,12},{3,1},{5,3},{7,5},{... | collective-permute-start | bytes 2764808 | tf_op jit(solution)/shard_map/ppermute | solution.py:36
  293.7 21.4 %collective-permute-done.20 = f32[30,30,256]{2,1,0:T(8,128)S(1)} collective-permute-done((f32[30,30,256]{2,1,0:T(8,128)S(1)}, f32[30,30,256]{2,1,0:T(8,128)S(1)}, u32[]{:S(2)}, u32[]{:S(2)}) %collective-permute-start.20) | collective-permute-done | bytes 921632 | tf_op jit(solution)/shard_map/ppermute | solution.py:36
  317.0 15.9 %collective-permute-done.19 = f32[30,30,256]{2,1,0:T(8,128)S(1)} collective-permute-done((f32[30,30,256]{2,1,0:T(8,128)S(1)}, f32[30,30,256]{2,1,0:T(8,128)S(1)}, u32[]{:S(2)}, u32[]{:S(2)}) %collective-permute-start.19) | collective-permute-done | bytes 921632 | tf_op jit(solution)/shard_map/ppermute | solution.py:36
  334.9 30.3 %collective-permute-done.18 = f32[30,30,256]{2,1,0:T(8,128)S(1)} collective-permute-done((f32[30,30,256]{2,1,0:T(8,128)S(1)}, f32[30,30,256]{2,1,0:T(8,128)S(1)}, u32[]{:S(2)}, u32[]{:S(2)}) %collective-permute-start.18) | collective-permute-done | bytes 921632 | tf_op jit(solution)/shard_map/ppermute | solution.py:36
  366.5 40.8 %collective-permute-done.17 = f32[30,30,256]{2,1,0:T(8,128)S(1)} collective-permute-done((f32[30,30,256]{2,1,0:T(8,128)S(1)}, f32[30,30,256]{2,1,0:T(8,128)S(1)}, u32[]{:S(2)}, u32[]{:S(2)}) %collective-permute-start.17) | collective-permute-done | bytes 921632 | tf_op jit(solution)/shard_map/ppermute | solution.py:36
  407.3 3.3 add_add_fusion
  412.2 10.6 %reduce-scatter.2.cloned.1.call-done = f32[15,30,256]{2,1,0:T(8,128)} async-done(((f32[30,30,256]{2,1,0:T(8,128)}), f32[15,30,256]{2,1,0:T(8,128)}) %reduce-scatter.2.cloned.1.call-update) | async-done | bytes 460816 | tf_op jit(solution)/shard_map/reduce_scatter | solution.py:225
  (162 shorter events, 100.9 us)
Async XLA Ops:
  7.2 415.6 %reduce-scatter.2.cloned.1.call-start = ((), (), s32[]{:S(2)}) async-start(), calls=%async_computation.1 | async-start | bytes 1474560 | tf_op jit(solution)/shard_map/reduce_scatter | solution.py:225
  8.0 7.8 %collective-permute-start.1 = (bf16[1,30,256]{2,1,0:T(8,128)(2,1)S(1)}, bf16[1,30,256]{2,1,0:T(8,128)(2,1)S(1)}, u32[]{:S(2)}, u32[]{:S(2)}) collective-permute-start(bf16[1,30,256]{2,1,0:T(8,128)(2,1)S(1)} %get-tuple-element.717), channel_id=1, source_target_pairs={{4,0},{8,4},{12,8},{5,1},{9,5},{13,9},{6,2},{10,6},{14,10},{7,3},{... | collective-permute-start | bytes 46088 | tf_op jit(solution)/shard_map/ppermute | solution.py:20
  10.4 5.6 %collective-permute-start = (bf16[1,30,256]{2,1,0:T(8,128)(2,1)S(1)}, bf16[1,30,256]{2,1,0:T(8,128)(2,1)S(1)}, u32[]{:S(2)}, u32[]{:S(2)}) collective-permute-start(bf16[1,30,256]{2,1,0:T(8,128)(2,1)S(1)} %get-tuple-element.716), channel_id=1, source_target_pairs={{0,4},{4,8},{8,12},{1,5},{5,9},{9,13},{2,6},{6,10},{10,14},{3,7},{... | collective-permute-start | bytes 46088 | tf_op jit(solution)/shard_map/ppermute | solution.py:18
  17.0 7.0 %collective-permute-start.2 = (bf16[32,1,256]{2,1,0:T(2,128)(2,1)S(1)}, bf16[32,1,256]{2,1,0:T(2,128)(2,1)S(1)}, u32[]{:S(2)}, u32[]{:S(2)}) collective-permute-start(bf16[32,1,256]{2,1,0:T(2,128)(2,1)S(1)} %get-tuple-element.709), channel_id=1, source_target_pairs={{0,2},{1,3},{4,6},{5,7},{8,10},{9,11},{12,14},{13,15},{16,18},{17,... | collective-permute-start | bytes 49160 | tf_op jit(solution)/shard_map/ppermute | solution.py:18
  20.4 5.8 %collective-permute-start.3 = (bf16[32,1,256]{2,1,0:T(2,128)(2,1)S(1)}, bf16[32,1,256]{2,1,0:T(2,128)(2,1)S(1)}, u32[]{:S(2)}, u32[]{:S(2)}) collective-permute-start(bf16[32,1,256]{2,1,0:T(2,128)(2,1)S(1)} %get-tuple-element.710), channel_id=1, source_target_pairs={{2,0},{3,1},{6,4},{7,5},{10,8},{11,9},{14,12},{15,13},{18,16},{19,... | collective-permute-start | bytes 49160 | tf_op jit(solution)/shard_map/ppermute | solution.py:20
  41.3 6.0 %collective-permute-start.4 = (bf16[1,30,256]{2,1,0:T(8,128)(2,1)S(1)}, bf16[1,30,256]{2,1,0:T(8,128)(2,1)S(1)}, u32[]{:S(2)}, u32[]{:S(2)}) collective-permute-start(bf16[1,30,256]{2,1,0:T(8,128)(2,1)S(1)} %get-tuple-element.719), channel_id=1, source_target_pairs={{0,4},{4,8},{8,12},{1,5},{5,9},{9,13},{2,6},{6,10},{10,14},{3,7},{... | collective-permute-start | bytes 46088 | tf_op jit(solution)/shard_map/ppermute | solution.py:18
  44.9 5.6 %collective-permute-start.5 = (bf16[1,30,256]{2,1,0:T(8,128)(2,1)S(1)}, bf16[1,30,256]{2,1,0:T(8,128)(2,1)S(1)}, u32[]{:S(2)}, u32[]{:S(2)}) collective-permute-start(bf16[1,30,256]{2,1,0:T(8,128)(2,1)S(1)} %get-tuple-element.718), channel_id=1, source_target_pairs={{4,0},{8,4},{12,8},{5,1},{9,5},{13,9},{6,2},{10,6},{14,10},{7,3},{... | collective-permute-start | bytes 46088 | tf_op jit(solution)/shard_map/ppermute | solution.py:20
  50.8 7.3 %collective-permute-start.6 = (bf16[32,1,256]{2,1,0:T(2,128)(2,1)S(1)}, bf16[32,1,256]{2,1,0:T(2,128)(2,1)S(1)}, u32[]{:S(2)}, u32[]{:S(2)}) collective-permute-start(bf16[32,1,256]{2,1,0:T(2,128)(2,1)S(1)} %get-tuple-element.699), channel_id=1, source_target_pairs={{0,2},{1,3},{4,6},{5,7},{8,10},{9,11},{12,14},{13,15},{16,18},{17,... | collective-permute-start | bytes 49160 | tf_op jit(solution)/shard_map/ppermute | solution.py:18
  53.1 5.8 %collective-permute-start.7 = (bf16[32,1,256]{2,1,0:T(2,128)(2,1)S(1)}, bf16[32,1,256]{2,1,0:T(2,128)(2,1)S(1)}, u32[]{:S(2)}, u32[]{:S(2)}) collective-permute-start(bf16[32,1,256]{2,1,0:T(2,128)(2,1)S(1)} %get-tuple-element.700), channel_id=1, source_target_pairs={{2,0},{3,1},{6,4},{7,5},{10,8},{11,9},{14,12},{15,13},{18,16},{19,... | collective-permute-start | bytes 49160 | tf_op jit(solution)/shard_map/ppermute | solution.py:20
  82.7 1.9 collective-permute-start.8
  82.8 28.6 %copy-start.11 = (f32[2,15,30]{2,0,1:T(2,128)S(1)}, f32[2,15,30]{2,0,1:T(2,128)}, u32[]{:S(2)}) copy-start(f32[2,15,30]{2,0,1:T(2,128)} %param.39) | copy-start | bytes 10804
  84.7 15.2 %collective-permute-start.10 = (bf16[30,30,256]{2,1,0:T(8,128)(2,1)S(1)}, bf16[30,30,256]{2,1,0:T(8,128)(2,1)S(1)}, u32[]{:S(2)}, u32[]{:S(2)}) collective-permute-start(bf16[30,30,256]{2,1,0:T(8,128)(2,1)S(1)} %broadcast_select_fusion), channel_id=1, source_target_pairs={{4,0},{8,4},{12,8},{5,1},{9,5},{13,9},{6,2},{10,6},{14,10},{7,3},{... | collective-permute-start | bytes 1382408 | tf_op jit(solution)/shard_map/ppermute | solution.py:20
  87.1 14.9 %collective-permute-start.9 = (bf16[30,30,256]{2,1,0:T(8,128)(2,1)S(1)}, bf16[30,30,256]{2,1,0:T(8,128)(2,1)S(1)}, u32[]{:S(2)}, u32[]{:S(2)}) collective-permute-start(bf16[30,30,256]{2,1,0:T(8,128)(2,1)S(1)} %broadcast_select_fusion), channel_id=1, source_target_pairs={{0,4},{4,8},{8,12},{1,5},{5,9},{9,13},{2,6},{6,10},{10,14},{3,7},{... | collective-permute-start | bytes 1382408 | tf_op jit(solution)/shard_map/ppermute | solution.py:18
  103.2 35.4 %collective-permute-start.12 = (bf16[90,30,256]{2,1,0:T(8,128)(2,1)}, bf16[90,30,256]{2,1,0:T(8,128)(2,1)}, u32[]{:S(2)}, u32[]{:S(2)}) collective-permute-start(bf16[90,30,256]{2,1,0:T(8,128)(2,1)} %pad_maximum_fusion.1), channel_id=1, source_target_pairs={{2,0},{3,1},{6,4},{7,5},{10,8},{11,9},{14,12},{15,13},{18,16},{19,... | collective-permute-start | bytes 4147208 | tf_op jit(solution)/shard_map/ppermute | solution.py:20
  104.5 36.4 %collective-permute-start.11 = (bf16[90,30,256]{2,1,0:T(8,128)(2,1)}, bf16[90,30,256]{2,1,0:T(8,128)(2,1)}, u32[]{:S(2)}, u32[]{:S(2)}) collective-permute-start(bf16[90,30,256]{2,1,0:T(8,128)(2,1)} %pad_maximum_fusion.1), channel_id=1, source_target_pairs={{0,2},{1,3},{4,6},{5,7},{8,10},{9,11},{12,14},{13,15},{16,18},{17,... | collective-permute-start | bytes 4147208 | tf_op jit(solution)/shard_map/ppermute | solution.py:18
  111.9 33.8 %copy-start.12 = (s32[1,1,9]{2,1,0:T(1,128)S(1)}, s32[1,1,9]{2,1,0:T(1,128)}, u32[]{:S(2)}) copy-start(s32[1,1,9]{2,1,0:T(1,128)} %param.37) | copy-start | bytes 112
  196.8 118.4 %collective-permute-start.20 = (f32[30,30,256]{2,1,0:T(8,128)S(1)}, f32[30,30,256]{2,1,0:T(8,128)S(1)}, u32[]{:S(2)}, u32[]{:S(2)}) collective-permute-start(f32[30,30,256]{2,1,0:T(8,128)S(1)} %get-tuple-element.689), channel_id=1, source_target_pairs={{0,6},{2,8},{4,10},{6,12},{8,14},{1,7},{3,9},{5,11},{7,13},{9,15},... | collective-permute-start | bytes 2764808 | tf_op jit(solution)/shard_map/ppermute | solution.py:36
  283.1 49.8 %collective-permute-start.19 = (f32[30,30,256]{2,1,0:T(8,128)S(1)}, f32[30,30,256]{2,1,0:T(8,128)S(1)}, u32[]{:S(2)}, u32[]{:S(2)}) collective-permute-start(f32[30,30,256]{2,1,0:T(8,128)S(1)} %get-tuple-element.683), channel_id=1, source_target_pairs={{0,4},{2,6},{4,8},{6,10},{8,12},{10,14},{1,5},{3,7},{5,9},{7,11},{... | collective-permute-start | bytes 2764808 | tf_op jit(solution)/shard_map/ppermute | solution.py:36
  285.1 80.1 %collective-permute-start.18 = (f32[30,30,256]{2,1,0:T(8,128)S(1)}, f32[30,30,256]{2,1,0:T(8,128)S(1)}, u32[]{:S(2)}, u32[]{:S(2)}) collective-permute-start(f32[30,30,256]{2,1,0:T(8,128)S(1)} %get-tuple-element.684), channel_id=1, source_target_pairs={{0,2},{2,4},{4,6},{6,8},{8,10},{10,12},{12,14},{1,3},{3,5},{5,7},{... | collective-permute-start | bytes 2764808 | tf_op jit(solution)/shard_map/ppermute | solution.py:36
  287.0 120.3 %collective-permute-start.17 = (f32[30,30,256]{2,1,0:T(8,128)S(1)}, f32[30,30,256]{2,1,0:T(8,128)S(1)}, u32[]{:S(2)}, u32[]{:S(2)}) collective-permute-start(f32[30,30,256]{2,1,0:T(8,128)S(1)} %get-tuple-element.685), channel_id=1, source_target_pairs={{0,2},{2,4},{4,6},{6,8},{8,10},{10,12},{12,14},{1,3},{3,5},{5,7},{... | collective-permute-start | bytes 2764808 | tf_op jit(solution)/shard_map/ppermute | solution.py:36
  288.9 118.3 %collective-permute-start.16 = (f32[30,30,256]{2,1,0:T(8,128)S(1)}, f32[30,30,256]{2,1,0:T(8,128)S(1)}, u32[]{:S(2)}, u32[]{:S(2)}) collective-permute-start(f32[30,30,256]{2,1,0:T(8,128)S(1)} %get-tuple-element.686), channel_id=1, source_target_pairs={{2,0},{4,2},{6,4},{8,6},{10,8},{12,10},{14,12},{3,1},{5,3},{7,5},{... | collective-permute-start | bytes 2764808 | tf_op jit(solution)/shard_map/ppermute | solution.py:36
  315.1 92.1 %collective-permute-start.15 = (f32[30,30,256]{2,1,0:T(8,128)S(1)}, f32[30,30,256]{2,1,0:T(8,128)S(1)}, u32[]{:S(2)}, u32[]{:S(2)}) collective-permute-start(f32[30,30,256]{2,1,0:T(8,128)S(1)} %get-tuple-element.687), channel_id=1, source_target_pairs={{2,0},{4,2},{6,4},{8,6},{10,8},{12,10},{14,12},{3,1},{5,3},{7,5},{... | collective-permute-start | bytes 2764808 | tf_op jit(solution)/shard_map/ppermute | solution.py:36
  332.9 74.3 %collective-permute-start.14 = (f32[30,30,256]{2,1,0:T(8,128)S(1)}, f32[30,30,256]{2,1,0:T(8,128)S(1)}, u32[]{:S(2)}, u32[]{:S(2)}) collective-permute-start(f32[30,30,256]{2,1,0:T(8,128)S(1)} %get-tuple-element.688), channel_id=1, source_target_pairs={{4,0},{6,2},{8,4},{10,6},{12,8},{14,10},{5,1},{7,3},{9,5},{11,7},{... | collective-permute-start | bytes 2764808 | tf_op jit(solution)/shard_map/ppermute | solution.py:36
  365.2 42.1 %collective-permute-start.13 = (f32[30,30,256]{2,1,0:T(8,128)S(1)}, f32[30,30,256]{2,1,0:T(8,128)S(1)}, u32[]{:S(2)}, u32[]{:S(2)}) collective-permute-start(f32[30,30,256]{2,1,0:T(8,128)S(1)} %get-tuple-element.682), channel_id=1, source_target_pairs={{6,0},{8,2},{10,4},{12,6},{14,8},{7,1},{9,3},{11,5},{13,7},{15,9},... | collective-permute-start | bytes 2764808 | tf_op jit(solution)/shard_map/ppermute | solution.py:36
  (11 other events, 35.4 us)
Sparse Core Ops, SparseCore 0:
  410.7 12.0 reduce-scatter.1
where the time goes:
time: 433 us; the launch traced here: 430 us
  waiting for transfers between devices  168 us (39%)
  starting transfers between devices  136 us (31%)
  local copies, waits for them, and re-layouts  51.1 us (12%)
  matrix products  25.2 us (6%)
  other arithmetic  22.4 us (5%)
  between operations  14.7 us (3%)
  loops' own time  12.5 us (3%)
    ppermute x8, waiting for transfers between devices, shifted(): lax.ppermute(value, axis, [(source, source + steps) for source in range(l...  108 us
    ppermute x8, starting transfers between devices, shifted(): lax.ppermute(value, axis, [(source, source + steps) for source in range(l...  102 us
    ppermute x6, waiting for transfers between devices, padded(): lax.ppermute(head, axis, [((i + 1) % count, i) for i in range(ends)])  42.3 us
    ppermute x6, starting transfers between devices, padded(): lax.ppermute(tail, axis, [(i, (i + 1) % count) for i in range(ends)])  23 us
    dot_general x18, matrix products, conv_valid(): jnp.dot(window.reshape(out_rows * out_cols, channels), weights[tap_index]...  20.6 us
    reshape x16, local copies, waits for them, and re-layouts, conv_valid(): window.reshape(out_rows * out_cols, channels)  17.7 us
    dynamic_update_slice x2, local copies, waits for them, and re-layouts, deposit(): lax.dynamic_update_slice(acc_in, current + contrib.reshape(TILE, TILE, ch...  11.8 us
    ppermute x6, starting transfers between devices, padded(): lax.ppermute(head, axis, [((i + 1) % count, i) for i in range(ends)])  10.9 us
  transfers between devices with their start and end apart: 22, of which 14 were waited for; matrix products, arithmetic and copies ran while one was open for 2% of the time, Pallas kernels for 0%

commit v1 on v0

v1 whole, which is shorter than its diff:
```python
import functools
import math

import jax
import jax.numpy as jnp
from jax import lax
from jax.experimental import pallas as pl
from jax.experimental.pallas import tpu as pltpu
from jax.sharding import PartitionSpec as P

TILE = 30
HALF = 15
PADW = 32
HC = HALF * PADW
BODY = HALF + 2
EXT = HALF + 4
HID = HALF + 2
AXES = ("rows", "cols", "pair")
VMEM = pl.BlockSpec(memory_space=pltpu.VMEM)
SMEM = pl.BlockSpec(memory_space=pltpu.SMEM)
ANY = pl.BlockSpec(memory_space=pl.ANY)


def send(value, step):
    n_r, n_c = lax.axis_size("rows"), lax.axis_size("cols")
    pairs = []
    for r in range(n_r):
        for k in range(n_c):
            for c in range(2):
                r2, k2, c2 = step(r, k, c)
                if 0 <= r2 < n_r and 0 <= k2 < n_c:
                    pairs.append(((r * n_c + k) * 2 + c, (r2 * n_c + k2) * 2 + c2))
    return lax.ppermute(value, AXES, pairs)


def partner(value):
    return send(value, lambda r, k, c: (r, k, 1 - c))


def updown(value):
    return send(value, lambda r, k, c: (r + 1 - 2 * c, k, c))


def sideways(value):
    if lax.axis_size("cols") == 2:
        return [send(value, lambda r, k, c: (r, 1 - k, c))]
    return [
        send(value, lambda r, k, c: (r, k + 1, c)),
        send(value, lambda r, k, c: (r, k - 1, c)),
    ]


def gather_tiles(half):
    level = [jnp.stack([half, partner(half)])]
    for side in sideways(half):
        level.append(jnp.stack([side, partner(side)]))
    got = [updown(t) for t in level]
    other = [partner(t) for t in got]
    return level, got, other


def encode_kernel(frame, n_r, n_c, sc, mine, got, xl, xr, z, w1, w2, out, ext, xcat, hid, hcat):
    core, row, col = sc[0], sc[1], sc[2]
    first_row = 2 * (1 - core)
    use_own = core == frame
    own_rows = mine[pl.ds((BODY - 4) * core, BODY)]
    body = jnp.where(use_own, own_rows, got[...]).astype(jnp.float32)
    slot = jnp.where(use_own, 0, 1)
    left = jnp.where(col > 0, xl[slot].astype(jnp.float32), 0.0)
    right = jnp.where(col < n_c - 1, xr[slot].astype(jnp.float32), 0.0)
    ext[pl.ds(first_row, BODY), 2 : 2 + TILE] = body
    ext[pl.ds(first_row, BODY), 0:2] = left
    ext[pl.ds(first_row, BODY), 2 + TILE : 4 + TILE] = right
    ext[pl.ds(BODY * core, 2), 0 : 4 + TILE] = z[1 - slot].astype(jnp.float32)
    ch = body.shape[-1]
    for b in range(3):
        xcat[:, b * ch : (b + 1) * ch] = (
            ext[:, b : b + PADW].astype(jnp.bfloat16).reshape(EXT * PADW, ch)
        )
    acc = jnp.zeros((HID * PADW, ch), jnp.float32)
    for a in range(3):
        acc += jnp.dot(
            xcat[a * PADW : (a + HID) * PADW], w1[a], preferred_element_type=jnp.float32
        )
    hr = lax.broadcasted_iota(jnp.int32, (HID, PADW, ch), 0) + (row * TILE + core * HALF - 1)
    hc = lax.broadcasted_iota(jnp.int32, (HID, PADW, ch), 1) + (col * TILE - 1)
    inside = (hr >= 0) & (hr < n_r * TILE) & (hc >= 0) & (hc < n_c * TILE)
    hidden = jnp.where(inside, jnp.maximum(acc, 0.0).reshape(HID, PADW, ch), 0.0)
    hid[0 : HID * PADW] = hidden.reshape(HID * PADW, ch)
    hid[HID * PADW :] = jnp.zeros((8, ch), jnp.float32)
    for b in range(3):
        hcat[:, b * ch : (b + 1) * ch] = hid[b : b + HID * PADW].astype(jnp.bfloat16)
    acc2 = ext[2 : 2 + HALF, 2 : 2 + PADW].reshape(HC, ch)
    for a in range(3):
        acc2 += jnp.dot(hcat[a * PADW : a * PADW + HC], w2[a], preferred_element_type=jnp.float32)
    oc = lax.broadcasted_iota(jnp.int32, (HALF, PADW, ch), 1)
    out[...] = (
        jnp.where(oc < TILE, acc2.reshape(HALF, PADW, ch), 0.0)
        .astype(jnp.bfloat16)
        .reshape(HC, ch)
    )


def encode(frame, n_r, n_c, sc, mine, got, xl, xr, z, w1, w2):
    ch = mine.shape[-1]
    return pl.pallas_call(
        functools.partial(encode_kernel, frame, n_r, n_c),
        out_shape=jax.ShapeDtypeStruct((HC, ch), jnp.bfloat16),
        in_specs=[SMEM] + [VMEM] * 7,
        out_specs=VMEM,
        scratch_shapes=[
            pltpu.VMEM((EXT, 40, ch), jnp.float32),
            pltpu.VMEM((EXT * PADW, 3 * ch), jnp.bfloat16),
            pltpu.VMEM((HID * PADW + 8, ch), jnp.float32),
            pltpu.VMEM((HID * PADW, 3 * ch), jnp.bfloat16),
        ],
        compiler_params=pltpu.CompilerParams(vmem_limit_bytes=40 * 2**20),
        cost_estimate=pl.CostEstimate(
            flops=2 * HC * 9 * ch * ch * 2, bytes_accessed=4 * 10**6, transcendentals=0
        ),
        name=f"encode_frame{frame}",
    )(sc, mine, got, xl, xr, z, w1, w2)


def load_all(level, got, other, buf, sems, core):
    n_cs = len(level)
    copies = []
    for j in range(n_cs):
        up, down = j, 2 * n_cs + j
        copies.append(pltpu.make_async_copy(level[j], buf.at[n_cs + j], sems.at[n_cs + j]))
        copies.append(
            pltpu.make_async_copy(got[j], buf.at[jnp.where(core == 0, up, down)], sems.at[up])
        )
        copies.append(
            pltpu.make_async_copy(other[j], buf.at[jnp.where(core == 0, down, up)], sems.at[down])
        )
    for copy in copies:
        copy.start()
    for copy in copies:
        copy.wait()


def slot_steps(slot, n_cs, n_c, col):
    dr = slot // n_cs - 1
    j = slot % n_cs
    if n_c == 2:
        dc = jnp.where(j == 0, 0, 1 - 2 * col)
    else:
        dc = jnp.where(j == 0, 0, 2 * j - 3)
    return dr, dc


def query_kernel(n_c, n_cs, c2, sc, cand, count, q, ctg, *refs):
    level, got, other = refs[:n_cs], refs[n_cs : 2 * n_cs], refs[2 * n_cs : 3 * n_cs]
    flow, stats, dq, buf, sems, s_scr, m_run, n_run, r_run, c_run, d_scr, acc, q4 = refs[3 * n_cs :]
    core, col = sc[0], sc[2]
    slots = 3 * n_cs
    load_all(level, got, other, buf, sems, core)
    m_run[...] = jnp.full(m_run.shape, -jnp.inf, jnp.float32)
    for ref in (n_run, r_run, c_run):
        ref[...] = jnp.zeros(ref.shape, jnp.float32)
    acc[...] = jnp.zeros(acc.shape, jnp.float32)
    rb = 16
    lane = lax.broadcasted_iota(jnp.int32, (rb, 128), 1)
    lane_ok = lane % PADW < TILE
    lane_last = lane_ok & (lane < HC - 384)
    in_row = lane < HC - 384

    def listed(slot):
        dr, dc = slot_steps(slot, n_cs, n_c, col)
        code = 3 * (dr + 1) + dc + 1
        hit = jnp.int32(0)
        for s in range(9):
            hit = jnp.where((cand[s] == code) & (s < count[0]), 1, hit)
        return dr, dc, hit

    def half_of(dr, i):
        return jnp.where(dr == 0, core ^ i, jnp.where(dr < 0, i, 1 - i))

    def stats_step(slot, carry):
        dr, dc, hit = listed(slot)

        @pl.when(hit == 1)
        def _():
            for i in range(2):
                s_scr[slot, :, i * 512 : i * 512 + HC] = lax.dot_general(
                    q[...], buf[slot, i], (((1,), (1,)), ((), ())), preferred_element_type=jnp.float32
                )
            base = [
                (30 * dr + 15 * half_of(dr, i)).astype(jnp.float32) for i in range(2)
            ]
            col_base = (30 * dc).astype(jnp.float32)
            for g in range(HC // rb):
                rows = slice(g * rb, (g + 1) * rb)
                s = [s_scr[slot, rows, v * 128 : v * 128 + 128] for v in range(8)]
                top = jnp.maximum(
                    jnp.maximum(jnp.maximum(s[0], s[1]), s[2]),
                    jnp.maximum(jnp.maximum(s[4], s[5]), s[6]),
                )
                top = jnp.maximum(
                    jnp.where(lane_ok, top, -jnp.inf),
                    jnp.where(lane_last, jnp.maximum(s[3], s[7]), -jnp.inf),
                )
                best = jnp.max(top, axis=1, keepdims=True) * c2
                old = m_run[rows]
                new = jnp.maximum(old, best)
                m_run[rows] = new
                factor = jnp.exp2(old - new)
                e = [jnp.exp2(x * c2 - new) for x in s]
                total, weighted = [], []
                for i in range(2):
                    e0, e1, e2, e3 = e[4 * i : 4 * i + 4]
                    a3 = jnp.where(in_row, e3, 0.0)
                    a2 = a3 + e2
                    a1 = a2 + e1
                    total.append(a1 + e0)
                    weighted.append(4.0 * (a1 + a2 + a3))
                both = total[0] + total[1]
                n_run[rows] = n_run[rows] * factor + both
                r_run[rows] = r_run[rows] * factor + (
                    weighted[0] + weighted[1] + base[0] * total[0] + base[1] * total[1]
                )
                c_run[rows] = c_run[rows] * factor + col_base * both

        return carry

    lax.fori_loop(0, slots, stats_step, 0)

    wide = lax.broadcasted_iota(jnp.int32, (HC, 128), 1)
    ok = wide % PADW < TILE
    norm = n_run[...]
    n_sum = jnp.sum(jnp.where(ok, norm, 0.0), axis=1, keepdims=True)
    r_sum = jnp.sum(
        jnp.where(ok, r_run[...] + (wide // PADW).astype(jnp.float32) * norm, 0.0),
        axis=1,
        keepdims=True,
    )
    c_sum = jnp.sum(
        jnp.where(ok, c_run[...] + (wide % PADW).astype(jnp.float32) * norm, 0.0),
        axis=1,
        keepdims=True,
    )
    cell = lax.broadcasted_iota(jnp.int32, (HC, 128), 0)
    q_row = (cell // PADW + HALF * core).astype(jnp.float32)
    q_col = (cell % PADW).astype(jnp.float32)
    mean_r = r_sum / n_sum
    mean_c = c_sum / n_sum
    pulls = jnp.transpose(
        jnp.concatenate([ctg[...], jnp.zeros((120, HC), jnp.float32)], axis=0)
    )
    scale = 1.0 / (TILE * math.sqrt(q.shape[1]))
    cr = pulls[:, 0:1] * scale
    cc = pulls[:, 1:2] * scale
    shift = cr * mean_r + cc * mean_c
    level2 = jnp.where(q_col < TILE, m_run[...] + jnp.log2(n_sum), 1e30)
    q4[0] = level2
    q4[1] = jnp.broadcast_to(cr, (HC, 128))
    q4[2] = jnp.broadcast_to(cc, (HC, 128))
    q4[3] = jnp.broadcast_to(shift, (HC, 128))
    flags = jnp.zeros((HC, 128), jnp.float32)
    for slot in range(slots):
        dr, dc, hit = listed(slot)
        code = 3 * (dr + 1) + dc + 1
        flags = jnp.where((cell == code) & (hit == 1), 1.0, flags)
    packed = flags
    for k, value in enumerate(
        (level2, cr, cc, shift, flags, (mean_r - q_row) / TILE, (mean_c - q_col) / TILE)
    ):
        packed = jnp.where(wide == k, value, packed)
    turned = jnp.transpose(packed)
    stats[...] = turned[0:8]
    flow[...] = turned[5:7]

    def grad_step(slot, carry):
        dr, dc, hit = listed(slot)

        @pl.when(hit == 1)
        def _():
            lane_row = (lane // PADW).astype(jnp.float32)
            lane_col = (lane % PADW + 30 * dc).astype(jnp.float32)
            for i in range(2):
                base = lane_row + (30 * dr + 15 * half_of(dr, i)).astype(jnp.float32)
                for g in range(HC // rb):
                    rows = slice(g * rb, (g + 1) * rb)
                    lev, gr, gc, sh = (q4[k, rows] for k in range(4))
                    pull = gr * base + (gc * lane_col - sh)
                    for v in range(4):
                        s = s_scr[slot, rows, i * 512 + v * 128 : i * 512 + v * 128 + 128]
                        p = jnp.exp2(s * c2 - lev)
                        d = jnp.where(lane_last if v == 3 else lane_ok, p * pull, 0.0)
                        d_scr[rows, v * 128 : v * 128 + 128] = d.astype(jnp.bfloat16)
                        if v < 3:
                            pull = pull + 4.0 * gr
                acc[...] += jnp.dot(
                    d_scr[:, 0:HC], buf[slot, i], preferred_element_type=jnp.float32
                )

        return carry

    lax.fori_loop(0, slots, grad_step, 0)
    dq[...] = acc[...].reshape(HALF, PADW, acc.shape[1])[:, :TILE]


def query_side(n_c, sc, cand, count, q, ctg, level, got, other):
    n_cs = len(level)
    ch = q.shape[1]
    slots = 3 * n_cs
    c2 = math.log2(math.e) / math.sqrt(ch)
    pairs = slots * 2 * HC * HC
    return pl.pallas_call(
        functools.partial(query_kernel, n_c, n_cs, c2),
        out_shape=(
            jax.ShapeDtypeStruct((2, HC), jnp.float32),
            jax.ShapeDtypeStruct((8, HC), jnp.float32),
            jax.ShapeDtypeStruct((HALF, TILE, ch), jnp.float32),
        ),
        in_specs=[SMEM, SMEM, SMEM, VMEM, VMEM] + [ANY] * slots,
        out_specs=(VMEM, VMEM, VMEM),
        scratch_shapes=[
            pltpu.VMEM((slots, 2, HC, ch), jnp.bfloat16),
            pltpu.SemaphoreType.DMA((slots,)),
            pltpu.VMEM((slots, HC, 1024), jnp.float32),
            pltpu.VMEM((HC, 128), jnp.float32),
            pltpu.VMEM((HC, 128), jnp.float32),
            pltpu.VMEM((HC, 128), jnp.float32),
            pltpu.VMEM((HC, 128), jnp.float32),
            pltpu.VMEM((HC, 512), jnp.bfloat16),
            pltpu.VMEM((HC, ch), jnp.float32),
            pltpu.VMEM((4, HC, 128), jnp.float32),
        ],
        compiler_params=pltpu.CompilerParams(vmem_limit_bytes=48 * 2**20),
        cost_estimate=pl.CostEstimate(
            flops=4 * pairs * ch, bytes_accessed=6 * 10**6, transcendentals=2 * pairs
        ),
        name="query_side",
    )(sc, cand, count, q, ctg, *level, *got, *other)


def target_kernel(n_c, n_cs, c2, sc, tgt, *refs):
    slots = 3 * n_cs
    feats = refs[:slots]
    stats = refs[slots : 2 * slots]
    out, buf, sems, st, st_sems, s_scr, d_scr, v_scr, acc = refs[2 * slots :]
    core, col = sc[0], sc[2]
    load_all(feats[:n_cs], feats[n_cs : 2 * n_cs], feats[2 * n_cs :], buf, sems, core)
    load_all(stats[:n_cs], stats[n_cs : 2 * n_cs], stats[2 * n_cs :], st, st_sems, core)
    acc[...] = jnp.zeros(acc.shape, jnp.float32)

    def step(slot, carry):
        dr, dc = slot_steps(slot, n_cs, n_c, col)
        code = 8 - (3 * (dr + 1) + dc + 1)
        where_at = lax.broadcasted_iota(jnp.int32, (8, HC), 1)
        which = lax.broadcasted_iota(jnp.int32, (8, HC), 0)
        flag = jnp.sum(jnp.where((where_at == code) & (which == 4), st[slot, 0], 0.0))

        @pl.when(flag > 0.5)
        def _():
            col_t = (
                lax.broadcasted_iota(jnp.int32, (PADW, HC), 0) - 30 * dc
            ).astype(jnp.float32)
            for i in range(2):
                s_scr[...] = lax.dot_general(
                    tgt[...], buf[slot, i], (((1,), (1,)), ((), ())), preferred_element_type=jnp.float32
                )
                lev, gr, gc, sh = (st[slot, i, k : k + 1, :] for k in range(4))
                v_scr[...] = gc * col_t - sh
                for g in range(HALF):
                    rows = slice(g * PADW, (g + 1) * PADW)
                    row_t = (g + HALF * core - 30 * dr).astype(jnp.float32)
                    p = jnp.exp2(s_scr[rows] * c2 - lev)
                    d = p * (v_scr[...] + gr * row_t)
                    d_scr[rows] = d.astype(jnp.bfloat16)
                acc[...] += jnp.dot(d_scr[...], buf[slot, i], preferred_element_type=jnp.float32)

        return carry

    lax.fori_loop(0, slots, step, 0)
    out[...] = acc[...].reshape(HALF, PADW, acc.shape[1])[:, :TILE]


def target_side(n_c, sc, tgt, feats, stats):
    level, got, other = feats
    n_cs = len(level)
    ch = tgt.shape[1]
    slots = 3 * n_cs
    c2 = math.log2(math.e) / math.sqrt(ch)
    pairs = slots * 2 * HC * HC
    return pl.pallas_call(
        functools.partial(target_kernel, n_c, n_cs, c2),
        out_shape=jax.ShapeDtypeStruct((HALF, TILE, ch), jnp.float32),
        in_specs=[SMEM, VMEM] + [ANY] * (2 * slots),
        out_specs=VMEM,
        scratch_shapes=[
            pltpu.VMEM((slots, 2, HC, ch), jnp.bfloat16),
            pltpu.SemaphoreType.DMA((slots,)),
            pltpu.VMEM((slots, 2, 8, HC), jnp.float32),
            pltpu.SemaphoreType.DMA((slots,)),
            pltpu.VMEM((HC, HC), jnp.float32),
            pltpu.VMEM((HC, HC), jnp.bfloat16),
            pltpu.VMEM((PADW, HC), jnp.float32),
            pltpu.VMEM((HC, ch), jnp.float32),
        ],
        compiler_params=pltpu.CompilerParams(vmem_limit_bytes=48 * 2**20),
        cost_estimate=pl.CostEstimate(
            flops=4 * pairs * ch, bytes_accessed=6 * 10**6, transcendentals=pairs
        ),
        name="target_side",
    )(sc, tgt, *level, *got, *other, *stats[0], *stats[1], *stats[2])


def shards(frames, conv_first, conv_second, candidates, counts, cotangent):
    mine = frames[0]
    ch = mine.shape[2]
    n_r, n_c = lax.axis_size("rows"), lax.axis_size("cols")
    core, row, col = (lax.axis_index(a) for a in ("pair", "rows", "cols"))
    sc = jnp.stack([core, row, col]).astype(jnp.int32)
    w1 = conv_first.reshape(3, 3 * ch, ch)
    w2 = conv_second.reshape(3, 3 * ch, ch)
    got = partner(lax.dynamic_slice_in_dim(mine, (BODY - 4) * (1 - core), BODY, 0))
    own = lax.dynamic_slice_in_dim(mine, (BODY - 4) * core, BODY, 0)
    bodies = (own, got)
    if n_c == 2:
        edge = jnp.stack([jnp.where(col == 0, b[:, TILE - 2 :], b[:, :2]) for b in bodies])
        xl = xr = send(edge, lambda r, k, c: (r, 1 - k, c))
    else:
        xl = send(jnp.stack([b[:, TILE - 2 :] for b in bodies]), lambda r, k, c: (r, k + 1, c))
        xr = send(jnp.stack([b[:, :2] for b in bodies]), lambda r, k, c: (r, k - 1, c))
    lines = []
    for i, b in enumerate(bodies):
        at = HALF * core
        left = jnp.where(col > 0, lax.dynamic_slice_in_dim(xl[i], at, 2, 0), 0)
        right = jnp.where(col < n_c - 1, lax.dynamic_slice_in_dim(xr[i], at, 2, 0), 0)
        lines.append(
            jnp.concatenate([left, lax.dynamic_slice_in_dim(b, at, 2, 0), right], axis=1)
        )
    z = send(jnp.stack(lines), lambda r, k, c: (r - 1 + 2 * c, k, 1 - c))
    second = encode(1, n_r, n_c, sc, mine, got, xl, xr, z, w1, w2)
    first = encode(0, n_r, n_c, sc, mine, got, xl, xr, z, w1, w2)
    ctg = jnp.pad(cotangent, ((0, 6), (0, 0), (0, PADW - TILE))).reshape(8, HC)
    targets = gather_tiles(second)
    queries = gather_tiles(first)
    flow, stats, grad_first = query_side(
        n_c, sc, candidates.reshape(9), counts.reshape(1), first, ctg, *targets
    )
    grad_second = target_side(n_c, sc, second, queries, gather_tiles(stats))
    return flow.reshape(2, HALF, PADW)[:, :, :TILE], grad_first, grad_second


def solution(mesh):
    in_specs = (
        P("pair", ("groups", "rows"), "cols", None),
        P(),
        P(),
        P(("groups", "rows"), "cols", None),
        P(("groups", "rows"), "cols"),
        P(None, ("groups", "rows", "pair"), "cols"),
    )
    out_specs = (
        P(None, ("groups", "rows", "pair"), "cols"),
        P(("groups", "rows", "pair"), "cols", None),
        P(("groups", "rows", "pair"), "cols", None),
    )
    return jax.shard_map(shards, mesh=mesh, in_specs=in_specs, out_specs=out_specs, check_vma=False)
```

time: 433 us -> 96.3 us (0.22)
  waiting for transfers between devices: 168 us -> 35 us
  starting transfers between devices: 136 us -> 24.4 us
  local copies, waits for them, and re-layouts: 51.1 us -> 4.08 us
  Pallas kernels: 0 us -> 30.4 us
  matrix products: 25.2 us -> 0 us
  other arithmetic: 22.4 us -> 0.47 us
  between operations: 14.7 us -> 1.59 us
  loops' own time: 12.5 us -> 0 us
    ppermute x21 -> x24, waiting for transfers between devices: 157 us -> 35 us  [send(): return lax.ppermute(value, AXES, pairs)]
    ppermute x21 -> x24, starting transfers between devices: 136 us -> 24.4 us  [send(): return lax.ppermute(value, AXES, pairs)]
    pallas_call x0 -> x4, Pallas kernels: none -> 30.4 us  [the longest x1 15.1 us: query_side(): pl.pallas_call(functools.partial(query_kernel, n_c, n_cs, c2), out_shape=...]
    dot_general x26 -> x0, matrix products: 25.2 us -> none  [the longest x18 20.6 us: conv_valid(): jnp.dot(window.reshape(out_rows * out_cols, channels), weights[tap_index]...]
    reshape x25 -> x2, local copies, waits for them, and re-layouts: 20.6 us -> 0.16 us  [the longest x1 0.09 us: shards(): ctg = jnp.pad(cotangent, ((0, 6), (0, 0), (0, PADW - TILE))).reshape(8, HC)]
    another operation x2 -> x0, loops' own time: 12.5 us -> none  [the longest x1 6.4 us: softmax_stats(): return lax.fori_loop(0, count, softmax_step, start)]
    dynamic_update_slice x2 -> x0, local copies, waits for them, and re-layouts: 11.8 us -> none  [deposit(): lax.dynamic_update_slice(acc_in, current + contrib.reshape(TILE, TILE, ch...]
    reduce_scatter x1 -> x0, waiting for transfers between devices: 10.6 us -> none  [shards(): lax.psum_scatter(own_terms, 'pair', scatter_dimension=0, tiled=True)]
  transfers between devices with their start and end apart: 22 -> 24, of which waited for: 14 -> 12; matrix products, arithmetic and copies ran while one was open for 2% -> 2% of each run, Pallas kernels for 0% -> 19%
where the time goes in v1:
time: 96.3 us; the launch traced here: 95.9 us
  waiting for transfers between devices  35 us (36%)
  Pallas kernels  30.4 us (32%)
  starting transfers between devices  24.4 us (25%)
  local copies, waits for them, and re-layouts  4.08 us (4%)
  between operations  1.59 us (2%)
    ppermute x24, waiting for transfers between devices, send(): return lax.ppermute(value, AXES, pairs)  35 us
    ppermute x24, starting transfers between devices, send(): return lax.ppermute(value, AXES, pairs)  24.4 us
    pallas_call x1, Pallas kernels, query_side(): pl.pallas_call(functools.partial(query_kernel, n_c, n_cs, c2), out_shape=...  15.1 us
    pallas_call x1, Pallas kernels, target_side(): pl.pallas_call(functools.partial(target_kernel, n_c, n_cs, c2), out_shape...  9.02 us
    pallas_call x2, Pallas kernels, encode(): pl.pallas_call(functools.partial(encode_kernel, frame, n_r, n_c), out_sha...  6.27 us
  transfers between devices with their start and end apart: 24, of which 12 were waited for; matrix products, arithmetic and copies ran while one was open for 2% of the time, Pallas kernels for 19%

profile of v1, /device:TPU:12, one launch (start us, length us, event | category | flops | bytes accessed | tf_op | source)
XLA Modules:
  0.0 95.9 jit_solution(6506734628223516871)
XLA Ops:
  0.7 1.2 %dynamic-slice_bitcast_fusion = (bf16[17,30,256]{2,1,0:T(8,128)(2,1)S(1)}, bf16[17,30,256]{2,1,0:T(8,128)(2,1)S(1)}) fusion(bf16[1,30,30,256]{3,2,1,0:T(8,128)(2,1)} %param.6, s32[]{:T(128)S(6)} %select_n.66, s32[]{:T(128)S(6)} %select_n.64), kind=kLoop, calls=%fused_computation.4 | loop fusion | bytes 1044488 | tf_op jit(solution)/shard_map/dynamic_slice | solution.py:420
  3.6 1.6 %collective-permute-start.1 = (bf16[2,17,2,256]{3,2,1,0:T(2,128)(2,1)S(1)}, bf16[2,17,2,256]{3,2,1,0:T(2,128)(2,1)S(1)}, u32[]{:S(2)}, u32[]{:S(2)}) collective-permute-start(bf16[2,17,2,256]{3,2,1,0:T(2,128)(2,1)S(1)} %pad_maximum_fusion.5), channel_id=1, source_target_pairs={{0,2},{1,3},{2,0},{3,1},{4,6},{5,7},{6,4},{7,5},{8,10},{9,11},{10,... | collective-permute-start | bytes 104456 | tf_op jit(solution)/shard_map/ppermute | solution.py:33
  5.1 2.4 %collective-permute-done.1.xl.xr = bf16[2,17,2,256]{3,2,1,0:T(2,128)(2,1)S(1)} collective-permute-done((bf16[2,17,2,256]{3,2,1,0:T(2,128)(2,1)S(1)}, bf16[2,17,2,256]{3,2,1,0:T(2,128)(2,1)S(1)}, u32[]{:S(2)}, u32[]{:S(2)}) %collective-permute-start.1) | collective-permute-done | bytes 34848 | tf_op jit(solution)/shard_map/ppermute | solution.py:33
  7.7 1.9 %collective-permute-start.2 = (bf16[2,2,34,256]{3,2,1,0:T(8,128)(2,1)S(1)}, bf16[2,2,34,256]{3,2,1,0:T(8,128)(2,1)S(1)}, u32[]{:S(2)}, u32[]{:S(2)}) collective-permute-start(bf16[2,2,34,256]{3,2,1,0:T(8,128)(2,1)S(1)} %pad_maximum_fusion.4), channel_id=1, source_target_pairs={{1,4},{3,6},{4,1},{5,8},{6,3},{7,10},{8,5},{9,12},{10,7},{11,14},{... | collective-permute-start | bytes 208904 | tf_op jit(solution)/shard_map/ppermute | solution.py:33
  9.7 3.8 %collective-permute-done.2.z = bf16[2,2,34,256]{3,2,1,0:T(8,128)(2,1)S(1)} collective-permute-done((bf16[2,2,34,256]{3,2,1,0:T(8,128)(2,1)S(1)}, bf16[2,2,34,256]{3,2,1,0:T(8,128)(2,1)S(1)}, u32[]{:S(2)}, u32[]{:S(2)}) %collective-permute-start.2) | collective-permute-done | bytes 69664 | tf_op jit(solution)/shard_map/ppermute | solution.py:33
  13.5 1.3 %copy-done.2 = bf16[9,256,256]{2,1,0:T(8,128)(2,1)S(1)} copy-done((bf16[9,256,256]{2,1,0:T(8,128)(2,1)S(1)}, bf16[9,256,256]{2,1,0:T(8,128)(2,1)}, u32[]{:S(2)}) %copy-start.2) | copy-done | bytes 1179672
  14.8 3.1 %encode_frame1.1.tgt = bf16[480,256]{1,0:T(8,128)(2,1)S(1)} custom-call(s32[3]{0:T(128)S(1)} %pad_add_fusion.sc, bf16[30,30,256]{2,1,0:T(8,128)(2,1)S(1)} %bitcast.44, bf16[17,30,256]{2,1,0:T(8,128)(2,1)S(1)} %collective-permute-done.got, bf16[2,17,2,256]{3,2,1,0:T(2,128)(2,1)S(1)} %collective-permute-done.1.xl.xr, ...), custom_call_target="tpu_custom_call" | custom-call | flops 1132462080 | bytes 4000000 | tf_op jit(solution)/shard_map/encode_frame1/pallas_call | solution.py:106
  17.9 1.6 %collective-permute-start.4 = (bf16[480,256]{1,0:T(8,128)(2,1)S(1)}, bf16[480,256]{1,0:T(8,128)(2,1)S(1)}, u32[]{:S(2)}, u32[]{:S(2)}) collective-permute-start(bf16[480,256]{1,0:T(8,128)(2,1)S(1)} %encode_frame1.1.tgt), channel_id=1, source_target_pairs={{0,2},{1,3},{2,0},{3,1},{4,6},{5,7},{6,4},{7,5},{8,10},{9,11},{10,... | collective-permute-start | bytes 737288 | tf_op jit(solution)/shard_map/ppermute | solution.py:33
  19.5 6.5 %collective-permute-done.4 = bf16[480,256]{1,0:T(8,128)(2,1)S(1)} collective-permute-done((bf16[480,256]{1,0:T(8,128)(2,1)S(1)}, bf16[480,256]{1,0:T(8,128)(2,1)S(1)}, u32[]{:S(2)}, u32[]{:S(2)}) %collective-permute-start.4) | collective-permute-done | bytes 245792 | tf_op jit(solution)/shard_map/ppermute | solution.py:33
  25.9 3.1 %encode_frame0.1.q = bf16[480,256]{1,0:T(8,128)(2,1)S(1)} custom-call(s32[3]{0:T(128)S(1)} %pad_add_fusion.sc, bf16[30,30,256]{2,1,0:T(8,128)(2,1)S(1)} %bitcast.45, bf16[17,30,256]{2,1,0:T(8,128)(2,1)S(1)} %collective-permute-done.got, bf16[2,17,2,256]{3,2,1,0:T(2,128)(2,1)S(1)} %collective-permute-done.1.xl.xr, ...), custom_call_target="tpu_custom_call" | custom-call | flops 1132462080 | bytes 4000000 | tf_op jit(solution)/shard_map/encode_frame0/pallas_call | solution.py:106
  29.1 1.6 %collective-permute-start.11 = (bf16[480,256]{1,0:T(8,128)(2,1)S(1)}, bf16[480,256]{1,0:T(8,128)(2,1)S(1)}, u32[]{:S(2)}, u32[]{:S(2)}) collective-permute-start(bf16[480,256]{1,0:T(8,128)(2,1)S(1)} %encode_frame0.1.q), channel_id=1, source_target_pairs={{0,2},{1,3},{2,0},{3,1},{4,6},{5,7},{6,4},{7,5},{8,10},{9,11},{10,... | collective-permute-start | bytes 737288 | tf_op jit(solution)/shard_map/ppermute | solution.py:33
  30.9 3.5 %collective-permute-start.6 = (bf16[2,480,256]{2,1,0:T(8,128)(2,1)S(1)}, bf16[2,480,256]{2,1,0:T(8,128)(2,1)}, u32[]{:S(2)}, u32[]{:S(2)}) collective-permute-start(bf16[2,480,256]{2,1,0:T(8,128)(2,1)S(1)} %pad_maximum_fusion.refs_0_), channel_id=1, source_target_pairs={{0,4},{2,6},{4,8},{5,1},{6,10},{7,3},{8,12},{9,5},{10,14},{11,7},{... | collective-permute-start | bytes 1474568 | tf_op jit(solution)/shard_map/ppermute | solution.py:33
  34.5 1.9 %collective-permute-start.7 = (bf16[2,480,256]{2,1,0:T(8,128)(2,1)S(1)}, bf16[2,480,256]{2,1,0:T(8,128)(2,1)}, u32[]{:S(2)}, u32[]{:S(2)}) collective-permute-start(bf16[2,480,256]{2,1,0:T(8,128)(2,1)S(1)} %pad_maximum_fusion.1.refs_1_), channel_id=1, source_target_pairs={{0,4},{2,6},{4,8},{5,1},{6,10},{7,3},{8,12},{9,5},{10,14},{11,7},{... | collective-permute-start | bytes 1474568 | tf_op jit(solution)/shard_map/ppermute | solution.py:33
  37.6 3.5 %collective-permute-start.13 = (bf16[2,480,256]{2,1,0:T(8,128)(2,1)S(1)}, bf16[2,480,256]{2,1,0:T(8,128)(2,1)S(1)}, u32[]{:S(2)}, u32[]{:S(2)}) collective-permute-start(bf16[2,480,256]{2,1,0:T(8,128)(2,1)S(1)} %pad_maximum_fusion.2.refs_0_), channel_id=1, source_target_pairs={{0,4},{2,6},{4,8},{5,1},{6,10},{7,3},{8,12},{9,5},{10,14},{11,7},{... | collective-permute-start | bytes 1474568 | tf_op jit(solution)/shard_map/ppermute | solution.py:33
  41.1 2.3 %collective-permute-start.14 = (bf16[2,480,256]{2,1,0:T(8,128)(2,1)S(1)}, bf16[2,480,256]{2,1,0:T(8,128)(2,1)S(1)}, u32[]{:S(2)}, u32[]{:S(2)}) collective-permute-start(bf16[2,480,256]{2,1,0:T(8,128)(2,1)S(1)} %pad_maximum_fusion.3.refs_1_), channel_id=1, source_target_pairs={{0,4},{2,6},{4,8},{5,1},{6,10},{7,3},{8,12},{9,5},{10,14},{11,7},{... | collective-permute-start | bytes 1474568 | tf_op jit(solution)/shard_map/ppermute | solution.py:33
  43.5 3.5 %collective-permute-done.7.refs_3_ = bf16[2,480,256]{2,1,0:T(8,128)(2,1)} collective-permute-done((bf16[2,480,256]{2,1,0:T(8,128)(2,1)S(1)}, bf16[2,480,256]{2,1,0:T(8,128)(2,1)}, u32[]{:S(2)}, u32[]{:S(2)}) %collective-permute-start.7) | collective-permute-done | bytes 491552 | tf_op jit(solution)/shard_map/ppermute | solution.py:33
  47.8 4.4 %collective-permute-done.13.refs_2_ = bf16[2,480,256]{2,1,0:T(8,128)(2,1)S(1)} collective-permute-done((bf16[2,480,256]{2,1,0:T(8,128)(2,1)S(1)}, bf16[2,480,256]{2,1,0:T(8,128)(2,1)S(1)}, u32[]{:S(2)}, u32[]{:S(2)}) %collective-permute-start.13) | collective-permute-done | bytes 491552 | tf_op jit(solution)/shard_map/ppermute | solution.py:33
  52.2 5.3 %collective-permute-done.14.refs_3_ = bf16[2,480,256]{2,1,0:T(8,128)(2,1)S(1)} collective-permute-done((bf16[2,480,256]{2,1,0:T(8,128)(2,1)S(1)}, bf16[2,480,256]{2,1,0:T(8,128)(2,1)S(1)}, u32[]{:S(2)}, u32[]{:S(2)}) %collective-permute-start.14) | collective-permute-done | bytes 491552 | tf_op jit(solution)/shard_map/ppermute | solution.py:33
  57.5 15.1 %query_side.1 = (f32[2,480]{1,0:T(2,128)S(1)}, f32[8,480]{1,0:T(8,128)S(1)}, f32[15,30,256]{2,1,0:T(8,128)}) custom-call(s32[3]{0:T(128)S(1)} %pad_add_fusion.sc, s32[9]{0:T(128)S(1)} %bitcast.53, s32[1]{0:T(128)} %bitcast.43.count, bf16[480,256]{1,0:T(8,128)(2,1)S(1)} %encode_frame0.1.q, f32[8,480]{1,0:T(8,128)S(1)} %reshape.45.ctg, ...), custom_call_target="tpu_custom_call" | custom-call | flops 2831155200 | bytes 6000000 | tf_op jit(solution)/shard_map/query_side/pallas_call | solution.py:310
  73.4 3.0 %collective-permute-done.18 = f32[8,480]{1,0:T(8,128)S(1)} collective-permute-done((f32[8,480]{1,0:T(8,128)S(1)}, f32[8,480]{1,0:T(8,128)S(1)}, u32[]{:S(2)}, u32[]{:S(2)}) %collective-permute-start.18) | collective-permute-done | bytes 15392 | tf_op jit(solution)/shard_map/ppermute | solution.py:33
  76.4 3.5 %collective-permute-start.20 = (f32[2,8,480]{2,1,0:T(8,128)S(1)}, f32[2,8,480]{2,1,0:T(8,128)S(1)}, u32[]{:S(2)}, u32[]{:S(2)}) collective-permute-start(f32[2,8,480]{2,1,0:T(8,128)S(1)} %pad_maximum_fusion.6.refs_6_), channel_id=1, source_target_pairs={{0,4},{2,6},{4,8},{5,1},{6,10},{7,3},{8,12},{9,5},{10,14},{11,7},{... | collective-permute-start | bytes 92168 | tf_op jit(solution)/shard_map/ppermute | solution.py:33
  79.9 1.9 %collective-permute-start.21 = (f32[2,8,480]{2,1,0:T(8,128)S(1)}, f32[2,8,480]{2,1,0:T(8,128)S(1)}, u32[]{:S(2)}, u32[]{:S(2)}) collective-permute-start(f32[2,8,480]{2,1,0:T(8,128)S(1)} %pad_maximum_fusion.7.refs_7_), channel_id=1, source_target_pairs={{0,4},{2,6},{4,8},{5,1},{6,10},{7,3},{8,12},{9,5},{10,14},{11,7},{... | collective-permute-start | bytes 92168 | tf_op jit(solution)/shard_map/ppermute | solution.py:33
  82.2 3.5 %collective-permute-done.21.refs_9_ = f32[2,8,480]{2,1,0:T(8,128)S(1)} collective-permute-done((f32[2,8,480]{2,1,0:T(8,128)S(1)}, f32[2,8,480]{2,1,0:T(8,128)S(1)}, u32[]{:S(2)}, u32[]{:S(2)}) %collective-permute-start.21) | collective-permute-done | bytes 30752 | tf_op jit(solution)/shard_map/ppermute | solution.py:33
  86.9 9.0 %target_side.1 = f32[15,30,256]{2,1,0:T(8,128)} custom-call(s32[3]{0:T(128)S(1)} %pad_add_fusion.sc, bf16[480,256]{1,0:T(8,128)(2,1)S(1)} %encode_frame1.1.tgt, bf16[2,480,256]{2,1,0:T(8,128)(2,1)S(1)} %pad_maximum_fusion.2.refs_0_, bf16[2,480,256]{2,1,0:T(8,128)(2,1)S(1)} %pad_maximum_fusion.3.refs_1_, ...), custom_call_target="tpu_custom_call" | custom-call | flops 2831155200 | bytes 6000000 | tf_op jit(solution)/shard_map/target_side/pallas_call | solution.py:388
  (61 shorter events, 6.1 us)
Async XLA Ops:
  1.9 1.6 %collective-permute-start = (bf16[17,30,256]{2,1,0:T(8,128)(2,1)S(1)}, bf16[17,30,256]{2,1,0:T(8,128)(2,1)S(1)}, u32[]{:S(2)}, u32[]{:S(2)}) collective-permute-start(bf16[17,30,256]{2,1,0:T(8,128)(2,1)S(1)} %get-tuple-element.13), channel_id=1, source_target_pairs={{0,1},{1,0},{2,3},{3,2},{4,5},{5,4},{6,7},{7,6},{8,9},{9,8},{10,11... | collective-permute-start | bytes 783368 | tf_op jit(solution)/shard_map/ppermute | solution.py:33
  3.6 4.0 %collective-permute-start.1 = (bf16[2,17,2,256]{3,2,1,0:T(2,128)(2,1)S(1)}, bf16[2,17,2,256]{3,2,1,0:T(2,128)(2,1)S(1)}, u32[]{:S(2)}, u32[]{:S(2)}) collective-permute-start(bf16[2,17,2,256]{3,2,1,0:T(2,128)(2,1)S(1)} %pad_maximum_fusion.5), channel_id=1, source_target_pairs={{0,2},{1,3},{2,0},{3,1},{4,6},{5,7},{6,4},{7,5},{8,10},{9,11},{10,... | collective-permute-start | bytes 104456 | tf_op jit(solution)/shard_map/ppermute | solution.py:33
  7.7 5.8 %collective-permute-start.2 = (bf16[2,2,34,256]{3,2,1,0:T(8,128)(2,1)S(1)}, bf16[2,2,34,256]{3,2,1,0:T(8,128)(2,1)S(1)}, u32[]{:S(2)}, u32[]{:S(2)}) collective-permute-start(bf16[2,2,34,256]{3,2,1,0:T(8,128)(2,1)S(1)} %pad_maximum_fusion.4), channel_id=1, source_target_pairs={{1,4},{3,6},{4,1},{5,8},{6,3},{7,10},{8,5},{9,12},{10,7},{11,14},{... | collective-permute-start | bytes 208904 | tf_op jit(solution)/shard_map/ppermute | solution.py:33
  17.9 8.0 %collective-permute-start.4 = (bf16[480,256]{1,0:T(8,128)(2,1)S(1)}, bf16[480,256]{1,0:T(8,128)(2,1)S(1)}, u32[]{:S(2)}, u32[]{:S(2)}) collective-permute-start(bf16[480,256]{1,0:T(8,128)(2,1)S(1)} %encode_frame1.1.tgt), channel_id=1, source_target_pairs={{0,2},{1,3},{2,0},{3,1},{4,6},{5,7},{6,4},{7,5},{8,10},{9,11},{10,... | collective-permute-start | bytes 737288 | tf_op jit(solution)/shard_map/ppermute | solution.py:33
  19.5 11.4 %collective-permute-start.3 = (bf16[480,256]{1,0:T(8,128)(2,1)S(1)}, bf16[480,256]{1,0:T(8,128)(2,1)S(1)}, u32[]{:S(2)}, u32[]{:S(2)}) collective-permute-start(bf16[480,256]{1,0:T(8,128)(2,1)S(1)} %encode_frame1.1.tgt), channel_id=1, source_target_pairs={{0,1},{1,0},{2,3},{3,2},{4,5},{5,4},{6,7},{7,6},{8,9},{9,8},{10,11... | collective-permute-start | bytes 737288 | tf_op jit(solution)/shard_map/ppermute | solution.py:33
  25.9 8.5 %collective-permute-start.5 = (bf16[480,256]{1,0:T(8,128)(2,1)S(1)}, bf16[480,256]{1,0:T(8,128)(2,1)S(1)}, u32[]{:S(2)}, u32[]{:S(2)}) collective-permute-start(bf16[480,256]{1,0:T(8,128)(2,1)S(1)} %collective-permute-done.4), channel_id=1, source_target_pairs={{0,1},{1,0},{2,3},{3,2},{4,5},{5,4},{6,7},{7,6},{8,9},{9,8},{10,11... | collective-permute-start | bytes 737288 | tf_op jit(solution)/shard_map/ppermute | solution.py:33
  29.1 8.4 %collective-permute-start.11 = (bf16[480,256]{1,0:T(8,128)(2,1)S(1)}, bf16[480,256]{1,0:T(8,128)(2,1)S(1)}, u32[]{:S(2)}, u32[]{:S(2)}) collective-permute-start(bf16[480,256]{1,0:T(8,128)(2,1)S(1)} %encode_frame0.1.q), channel_id=1, source_target_pairs={{0,2},{1,3},{2,0},{3,1},{4,6},{5,7},{6,4},{7,5},{8,10},{9,11},{10,... | collective-permute-start | bytes 737288 | tf_op jit(solution)/shard_map/ppermute | solution.py:33
  30.6 6.9 %collective-permute-start.10 = (bf16[480,256]{1,0:T(8,128)(2,1)S(1)}, bf16[480,256]{1,0:T(8,128)(2,1)S(1)}, u32[]{:S(2)}, u32[]{:S(2)}) collective-permute-start(bf16[480,256]{1,0:T(8,128)(2,1)S(1)} %encode_frame0.1.q), channel_id=1, source_target_pairs={{0,1},{1,0},{2,3},{3,2},{4,5},{5,4},{6,7},{7,6},{8,9},{9,8},{10,11... | collective-permute-start | bytes 737288 | tf_op jit(solution)/shard_map/ppermute | solution.py:33
  30.9 12.5 %collective-permute-start.6 = (bf16[2,480,256]{2,1,0:T(8,128)(2,1)S(1)}, bf16[2,480,256]{2,1,0:T(8,128)(2,1)}, u32[]{:S(2)}, u32[]{:S(2)}) collective-permute-start(bf16[2,480,256]{2,1,0:T(8,128)(2,1)S(1)} %pad_maximum_fusion.refs_0_), channel_id=1, source_target_pairs={{0,4},{2,6},{4,8},{5,1},{6,10},{7,3},{8,12},{9,5},{10,14},{11,7},{... | collective-permute-start | bytes 1474568 | tf_op jit(solution)/shard_map/ppermute | solution.py:33
  34.5 12.5 %collective-permute-start.7 = (bf16[2,480,256]{2,1,0:T(8,128)(2,1)S(1)}, bf16[2,480,256]{2,1,0:T(8,128)(2,1)}, u32[]{:S(2)}, u32[]{:S(2)}) collective-permute-start(bf16[2,480,256]{2,1,0:T(8,128)(2,1)S(1)} %pad_maximum_fusion.1.refs_1_), channel_id=1, source_target_pairs={{0,4},{2,6},{4,8},{5,1},{6,10},{7,3},{8,12},{9,5},{10,14},{11,7},{... | collective-permute-start | bytes 1474568 | tf_op jit(solution)/shard_map/ppermute | solution.py:33
  37.5 3.6 %collective-permute-start.12 = (bf16[480,256]{1,0:T(8,128)(2,1)S(1)}, bf16[480,256]{1,0:T(8,128)(2,1)S(1)}, u32[]{:S(2)}, u32[]{:S(2)}) collective-permute-start(bf16[480,256]{1,0:T(8,128)(2,1)S(1)} %collective-permute-done.11), channel_id=1, source_target_pairs={{0,1},{1,0},{2,3},{3,2},{4,5},{5,4},{6,7},{7,6},{8,9},{9,8},{10,11... | collective-permute-start | bytes 737288 | tf_op jit(solution)/shard_map/ppermute | solution.py:33
  37.6 14.6 %collective-permute-start.13 = (bf16[2,480,256]{2,1,0:T(8,128)(2,1)S(1)}, bf16[2,480,256]{2,1,0:T(8,128)(2,1)S(1)}, u32[]{:S(2)}, u32[]{:S(2)}) collective-permute-start(bf16[2,480,256]{2,1,0:T(8,128)(2,1)S(1)} %pad_maximum_fusion.2.refs_0_), channel_id=1, source_target_pairs={{0,4},{2,6},{4,8},{5,1},{6,10},{7,3},{8,12},{9,5},{10,14},{11,7},{... | collective-permute-start | bytes 1474568 | tf_op jit(solution)/shard_map/ppermute | solution.py:33
  41.1 16.3 %collective-permute-start.14 = (bf16[2,480,256]{2,1,0:T(8,128)(2,1)S(1)}, bf16[2,480,256]{2,1,0:T(8,128)(2,1)S(1)}, u32[]{:S(2)}, u32[]{:S(2)}) collective-permute-start(bf16[2,480,256]{2,1,0:T(8,128)(2,1)S(1)} %pad_maximum_fusion.3.refs_1_), channel_id=1, source_target_pairs={{0,4},{2,6},{4,8},{5,1},{6,10},{7,3},{8,12},{9,5},{10,14},{11,7},{... | collective-permute-start | bytes 1474568 | tf_op jit(solution)/shard_map/ppermute | solution.py:33
  43.4 14.0 %collective-permute-start.8 = (bf16[2,480,256]{2,1,0:T(8,128)(2,1)}, bf16[2,480,256]{2,1,0:T(8,128)(2,1)}, u32[]{:S(2)}, u32[]{:S(2)}) collective-permute-start(bf16[2,480,256]{2,1,0:T(8,128)(2,1)} %collective-permute-done.6.refs_2_), channel_id=1, source_target_pairs={{0,1},{1,0},{2,3},{3,2},{4,5},{5,4},{6,7},{7,6},{8,9},{9,8},{10,11... | collective-permute-start | bytes 1474568 | tf_op jit(solution)/shard_map/ppermute | solution.py:33
  47.0 10.4 %collective-permute-start.9 = (bf16[2,480,256]{2,1,0:T(8,128)(2,1)}, bf16[2,480,256]{2,1,0:T(8,128)(2,1)}, u32[]{:S(2)}, u32[]{:S(2)}) collective-permute-start(bf16[2,480,256]{2,1,0:T(8,128)(2,1)} %collective-permute-done.7.refs_3_), channel_id=1, source_target_pairs={{0,1},{1,0},{2,3},{3,2},{4,5},{5,4},{6,7},{7,6},{8,9},{9,8},{10,11... | collective-permute-start | bytes 1474568 | tf_op jit(solution)/shard_map/ppermute | solution.py:33
  52.2 34.2 %collective-permute-start.15 = (bf16[2,480,256]{2,1,0:T(8,128)(2,1)S(1)}, bf16[2,480,256]{2,1,0:T(8,128)(2,1)}, u32[]{:S(2)}, u32[]{:S(2)}) collective-permute-start(bf16[2,480,256]{2,1,0:T(8,128)(2,1)S(1)} %collective-permute-done.13.refs_2_), channel_id=1, source_target_pairs={{0,1},{1,0},{2,3},{3,2},{4,5},{5,4},{6,7},{7,6},{8,9},{9,8},{10,11... | collective-permute-start | bytes 1474568 | tf_op jit(solution)/shard_map/ppermute | solution.py:33
  57.4 29.0 %collective-permute-start.16 = (bf16[2,480,256]{2,1,0:T(8,128)(2,1)S(1)}, bf16[2,480,256]{2,1,0:T(8,128)(2,1)}, u32[]{:S(2)}, u32[]{:S(2)}) collective-permute-start(bf16[2,480,256]{2,1,0:T(8,128)(2,1)S(1)} %collective-permute-done.14.refs_3_), channel_id=1, source_target_pairs={{0,1},{1,0},{2,3},{3,2},{4,5},{5,4},{6,7},{7,6},{8,9},{9,8},{10,11... | collective-permute-start | bytes 1474568 | tf_op jit(solution)/shard_map/ppermute | solution.py:33
  72.6 3.8 %collective-permute-start.18 = (f32[8,480]{1,0:T(8,128)S(1)}, f32[8,480]{1,0:T(8,128)S(1)}, u32[]{:S(2)}, u32[]{:S(2)}) collective-permute-start(f32[8,480]{1,0:T(8,128)S(1)} %get-tuple-element.8), channel_id=1, source_target_pairs={{0,2},{1,3},{2,0},{3,1},{4,6},{5,7},{6,4},{7,5},{8,10},{9,11},{10,... | collective-permute-start | bytes 46088 | tf_op jit(solution)/shard_map/ppermute | solution.py:33
  73.1 3.2 %collective-permute-start.17 = (f32[8,480]{1,0:T(8,128)S(1)}, f32[8,480]{1,0:T(8,128)S(1)}, u32[]{:S(2)}, u32[]{:S(2)}) collective-permute-start(f32[8,480]{1,0:T(8,128)S(1)} %get-tuple-element.8), channel_id=1, source_target_pairs={{0,1},{1,0},{2,3},{3,2},{4,5},{5,4},{6,7},{7,6},{8,9},{9,8},{10,11... | collective-permute-start | bytes 46088 | tf_op jit(solution)/shard_map/ppermute | solution.py:33
  76.4 3.5 %collective-permute-start.19 = (f32[8,480]{1,0:T(8,128)S(1)}, f32[8,480]{1,0:T(8,128)S(1)}, u32[]{:S(2)}, u32[]{:S(2)}) collective-permute-start(f32[8,480]{1,0:T(8,128)S(1)} %collective-permute-done.18), channel_id=1, source_target_pairs={{0,1},{1,0},{2,3},{3,2},{4,5},{5,4},{6,7},{7,6},{8,9},{9,8},{10,11... | collective-permute-start | bytes 46088 | tf_op jit(solution)/shard_map/ppermute | solution.py:33
  76.4 5.8 %collective-permute-start.20 = (f32[2,8,480]{2,1,0:T(8,128)S(1)}, f32[2,8,480]{2,1,0:T(8,128)S(1)}, u32[]{:S(2)}, u32[]{:S(2)}) collective-permute-start(f32[2,8,480]{2,1,0:T(8,128)S(1)} %pad_maximum_fusion.6.refs_6_), channel_id=1, source_target_pairs={{0,4},{2,6},{4,8},{5,1},{6,10},{7,3},{8,12},{9,5},{10,14},{11,7},{... | collective-permute-start | bytes 92168 | tf_op jit(solution)/shard_map/ppermute | solution.py:33
  79.9 5.8 %collective-permute-start.21 = (f32[2,8,480]{2,1,0:T(8,128)S(1)}, f32[2,8,480]{2,1,0:T(8,128)S(1)}, u32[]{:S(2)}, u32[]{:S(2)}) collective-permute-start(f32[2,8,480]{2,1,0:T(8,128)S(1)} %pad_maximum_fusion.7.refs_7_), channel_id=1, source_target_pairs={{0,4},{2,6},{4,8},{5,1},{6,10},{7,3},{8,12},{9,5},{10,14},{11,7},{... | collective-permute-start | bytes 92168 | tf_op jit(solution)/shard_map/ppermute | solution.py:33
  82.2 4.2 %collective-permute-start.22 = (f32[2,8,480]{2,1,0:T(8,128)S(1)}, f32[2,8,480]{2,1,0:T(8,128)S(1)}, u32[]{:S(2)}, u32[]{:S(2)}) collective-permute-start(f32[2,8,480]{2,1,0:T(8,128)S(1)} %collective-permute-done.20.refs_8_), channel_id=1, source_target_pairs={{0,1},{1,0},{2,3},{3,2},{4,5},{5,4},{6,7},{7,6},{8,9},{9,8},{10,11... | collective-permute-start | bytes 92168 | tf_op jit(solution)/shard_map/ppermute | solution.py:33
  85.7 1.2 %collective-permute-start.23 = (f32[2,8,480]{2,1,0:T(8,128)S(1)}, f32[2,8,480]{2,1,0:T(8,128)S(1)}, u32[]{:S(2)}, u32[]{:S(2)}) collective-permute-start(f32[2,8,480]{2,1,0:T(8,128)S(1)} %collective-permute-done.21.refs_9_), channel_id=1, source_target_pairs={{0,1},{1,0},{2,3},{3,2},{4,5},{5,4},{6,7},{7,6},{8,9},{9,8},{10,11... | collective-permute-start | bytes 92168 | tf_op jit(solution)/shard_map/ppermute | solution.py:33
  (5 other events, 62.5 us)

commit v2 on v1

--- a/solution.py
+++ b/solution.py
@@ -18,6 +18,7 @@
 AXES = ("rows", "cols", "pair")
 VMEM = pl.BlockSpec(memory_space=pltpu.VMEM)
 SMEM = pl.BlockSpec(memory_space=pltpu.SMEM)
+RB = 16
 ANY = pl.BlockSpec(memory_space=pl.ANY)
 
 
@@ -50,13 +51,8 @@
     ]
 
 
-def gather_tiles(half):
-    level = [jnp.stack([half, partner(half)])]
-    for side in sideways(half):
-        level.append(jnp.stack([side, partner(side)]))
-    got = [updown(t) for t in level]
-    other = [partner(t) for t in got]
-    return level, got, other
+def after(value, *others):
+    return lax.optimization_barrier((value, others))[0]
 
 
 def encode_kernel(frame, n_r, n_c, sc, mine, got, xl, xr, z, w1, w2, out, ext, xcat, hid, hcat):
@@ -64,7 +60,8 @@
     first_row = 2 * (1 - core)
     use_own = core == frame
     own_rows = mine[pl.ds((BODY - 4) * core, BODY)]
-    body = jnp.where(use_own, own_rows, got[...]).astype(jnp.float32)
+    got_rows = got[pl.ds((BODY - 4) * core, BODY)]
+    body = jnp.where(use_own, own_rows, got_rows).astype(jnp.float32)
     slot = jnp.where(use_own, 0, 1)
     left = jnp.where(col > 0, xl[slot].astype(jnp.float32), 0.0)
     right = jnp.where(col < n_c - 1, xr[slot].astype(jnp.float32), 0.0)
@@ -124,20 +121,16 @@
 
 def load_all(level, got, other, buf, sems, core):
     n_cs = len(level)
-    copies = []
     for j in range(n_cs):
         up, down = j, 2 * n_cs + j
-        copies.append(pltpu.make_async_copy(level[j], buf.at[n_cs + j], sems.at[n_cs + j]))
-        copies.append(
-            pltpu.make_async_copy(got[j], buf.at[jnp.where(core == 0, up, down)], sems.at[up])
-        )
-        copies.append(
-            pltpu.make_async_copy(other[j], buf.at[jnp.where(core == 0, down, up)], sems.at[down])
-        )
-    for copy in copies:
-        copy.start()
-    for copy in copies:
-        copy.wait()
+        first, last = jnp.where(core == 0, up, down), jnp.where(core == 0, down, up)
+        pltpu.make_async_copy(level[j], buf.at[n_cs + j], sems.at[n_cs + j]).start()
+        pltpu.make_async_copy(got[j], buf.at[first], sems.at[first]).start()
+        pltpu.make_async_copy(other[j], buf.at[last], sems.at[last]).start()
+
+
+def wait_for(tile, buf, sems, slot):
+    pltpu.make_async_copy(tile, buf.at[slot], sems.at[slot]).wait()
 
 
 def slot_steps(slot, n_cs, n_c, col):
@@ -150,93 +143,119 @@
     return dr, dc
 
 
-def query_kernel(n_c, n_cs, c2, sc, cand, count, q, ctg, *refs):
-    level, got, other = refs[:n_cs], refs[n_cs : 2 * n_cs], refs[2 * n_cs : 3 * n_cs]
-    flow, stats, dq, buf, sems, s_scr, m_run, n_run, r_run, c_run, d_scr, acc, q4 = refs[3 * n_cs :]
+def listed(slot, n_cs, n_c, col, cand, count):
+    dr, dc = slot_steps(slot, n_cs, n_c, col)
+    code = 3 * (dr + 1) + dc + 1
+    hit = jnp.int32(0)
+    for s in range(9):
+        hit = jnp.where((cand[s] == code) & (s < count[0]), 1, hit)
+    return dr, dc, code, hit
+
+
+def half_of(dr, i, core):
+    return jnp.where(dr == 0, core ^ i, jnp.where(dr < 0, i, 1 - i))
+
+
+def lanes(rows):
+    lane = lax.broadcasted_iota(jnp.int32, (rows, 128), 1)
+    return lane, lane % PADW < TILE, lane < HC - 384
+
+
+def add_tile(c2, slot, dr, dc, core, q, buf, s_scr, state):
+    for i in range(2):
+        s_scr[:, i * 512 : i * 512 + HC] = lax.dot_general(
+            q[...], buf[slot, i], (((1,), (1,)), ((), ())), preferred_element_type=jnp.float32
+        )
+    base = [(30 * dr + 15 * half_of(dr, i, core)).astype(jnp.float32) for i in range(2)]
+    col_base = (30 * dc).astype(jnp.float32)
+    lane, lane_ok, in_row = lanes(RB)
+    for g in range(HC // RB):
+        rows = slice(g * RB, (g + 1) * RB)
+        s = [s_scr[rows, v * 128 : v * 128 + 128] for v in range(8)]
+        top = jnp.maximum(
+            jnp.maximum(jnp.maximum(s[0], s[1]), s[2]),
+            jnp.maximum(jnp.maximum(s[4], s[5]), s[6]),
+        )
+        top = jnp.maximum(
+            jnp.where(lane_ok, top, -jnp.inf),
+            jnp.where(lane_ok & in_row, jnp.maximum(s[3], s[7]), -jnp.inf),
+        )
+        best = jnp.max(top, axis=1, keepdims=True) * c2
+        old = state[0, rows]
+        new = jnp.maximum(old, best)
+        state[0, rows] = new
+        factor = jnp.exp2(old - new)
+        e = [jnp.exp2(x * c2 - new) for x in s]
+        total, weighted = [], []
+        for i in range(2):
+            e0, e1, e2, e3 = e[4 * i : 4 * i + 4]
+            a3 = jnp.where(in_row, e3, 0.0)
+            a2 = a3 + e2
+            a1 = a2 + e1
+            total.append(a1 + e0)
+            weighted.append(4.0 * (a1 + a2 + a3))
+        both = total[0] + total[1]
+        state[1, rows] = state[1, rows] * factor + both
+        state[2, rows] = state[2, rows] * factor + (
+            weighted[0] + weighted[1] + base[0] * total[0] + base[1] * total[1]
+        )
+        state[3, rows] = state[3, rows] * factor + col_base * both
+
+
+def near_kernel(n_c, n_cs, c2, sc, cand, count, q, *refs):
+    level, (state, buf, sems, s_scr) = refs[:n_cs], refs[n_cs:]
     core, col = sc[0], sc[2]
-    slots = 3 * n_cs
-    load_all(level, got, other, buf, sems, core)
-    m_run[...] = jnp.full(m_run.shape, -jnp.inf, jnp.float32)
-    for ref in (n_run, r_run, c_run):
-        ref[...] = jnp.zeros(ref.shape, jnp.float32)
-    acc[...] = jnp.zeros(acc.shape, jnp.float32)
-    rb = 16
-    lane = lax.broadcasted_iota(jnp.int32, (rb, 128), 1)
-    lane_ok = lane % PADW < TILE
-    lane_last = lane_ok & (lane < HC - 384)
-    in_row = lane < HC - 384
-
-    def listed(slot):
-        dr, dc = slot_steps(slot, n_cs, n_c, col)
-        code = 3 * (dr + 1) + dc + 1
-        hit = jnp.int32(0)
-        for s in range(9):
-            hit = jnp.where((cand[s] == code) & (s < count[0]), 1, hit)
-        return dr, dc, hit
-
-    def half_of(dr, i):
-        return jnp.where(dr == 0, core ^ i, jnp.where(dr < 0, i, 1 - i))
-
-    def stats_step(slot, carry):
-        dr, dc, hit = listed(slot)
+    for j in range(n_cs):
+        pltpu.make_async_copy(level[j], buf.at[j], sems.at[j]).start()
+    state[0] = jnp.full(state.shape[1:], -jnp.inf, jnp.float32)
+    for k in range(1, 4):
+        state[k] = jnp.zeros(state.shape[1:], jnp.float32)
+
+    def step(j, carry):
+        dr, dc, _, hit = listed(n_cs + j, n_cs, n_c, col, cand, count)
+        wait_for(level[0], buf, sems, j)
 
         @pl.when(hit == 1)
         def _():
-            for i in range(2):
-                s_scr[slot, :, i * 512 : i * 512 + HC] = lax.dot_general(
-                    q[...], buf[slot, i], (((1,), (1,)), ((), ())), preferred_element_type=jnp.float32
-                )
-            base = [
-                (30 * dr + 15 * half_of(dr, i)).astype(jnp.float32) for i in range(2)
-            ]
-            col_base = (30 * dc).astype(jnp.float32)
-            for g in range(HC // rb):
-                rows = slice(g * rb, (g + 1) * rb)
-                s = [s_scr[slot, rows, v * 128 : v * 128 + 128] for v in range(8)]
-                top = jnp.maximum(
-                    jnp.maximum(jnp.maximum(s[0], s[1]), s[2]),
-                    jnp.maximum(jnp.maximum(s[4], s[5]), s[6]),
-                )
-                top = jnp.maximum(
-                    jnp.where(lane_ok, top, -jnp.inf),
-                    jnp.where(lane_last, jnp.maximum(s[3], s[7]), -jnp.inf),
-                )
-                best = jnp.max(top, axis=1, keepdims=True) * c2
-                old = m_run[rows]
-                new = jnp.maximum(old, best)
-                m_run[rows] = new
-                factor = jnp.exp2(old - new)
-                e = [jnp.exp2(x * c2 - new) for x in s]
-                total, weighted = [], []
-                for i in range(2):
-                    e0, e1, e2, e3 = e[4 * i : 4 * i + 4]
-                    a3 = jnp.where(in_row, e3, 0.0)
-                    a2 = a3 + e2
-                    a1 = a2 + e1
-                    total.append(a1 + e0)
-                    weighted.append(4.0 * (a1 + a2 + a3))
-                both = total[0] + total[1]
-                n_run[rows] = n_run[rows] * factor + both
-                r_run[rows] = r_run[rows] * factor + (
-                    weighted[0] + weighted[1] + base[0] * total[0] + base[1] * total[1]
-                )
-                c_run[rows] = c_run[rows] * factor + col_base * both
+            add_tile(c2, j, dr, dc, core, q, buf, s_scr, state)
 
         return carry
 
-    lax.fori_loop(0, slots, stats_step, 0)
-
-    wide = lax.broadcasted_iota(jnp.int32, (HC, 128), 1)
-    ok = wide % PADW < TILE
-    norm = n_run[...]
+    lax.fori_loop(0, n_cs, step, 0)
+
+
+def far_kernel(n_c, n_cs, c2, sc, cand, count, q, ctg, begun, *refs):
+    got, other = refs[:n_cs], refs[n_cs : 2 * n_cs]
+    flow, stats, packed_out, buf, sems, s_scr, state = refs[2 * n_cs :]
+    core, col = sc[0], sc[2]
+    for j in range(n_cs):
+        first, last = jnp.where(core == 0, j, n_cs + j), jnp.where(core == 0, n_cs + j, j)
+        pltpu.make_async_copy(got[j], buf.at[first], sems.at[first]).start()
+        pltpu.make_async_copy(other[j], buf.at[last], sems.at[last]).start()
+    state[...] = begun[...]
+
+    def step(j, carry):
+        slot = jnp.where(j < n_cs, j, n_cs + j)
+        dr, dc, _, hit = listed(slot, n_cs, n_c, col, cand, count)
+        wait_for(got[0], buf, sems, j)
+
+        @pl.when(hit == 1)
+        def _():
+            add_tile(c2, j, dr, dc, core, q, buf, s_scr, state)
+
+        return carry
+
+    lax.fori_loop(0, 2 * n_cs, step, 0)
+    wide, ok, _ = lanes(HC)
+    norm = state[1]
     n_sum = jnp.sum(jnp.where(ok, norm, 0.0), axis=1, keepdims=True)
     r_sum = jnp.sum(
-        jnp.where(ok, r_run[...] + (wide // PADW).astype(jnp.float32) * norm, 0.0),
+        jnp.where(ok, state[2] + (wide // PADW).astype(jnp.float32) * norm, 0.0),
         axis=1,
         keepdims=True,
     )
     c_sum = jnp.sum(
-        jnp.where(ok, c_run[...] + (wide % PADW).astype(jnp.float32) * norm, 0.0),
+        jnp.where(ok, state[3] + (wide % PADW).astype(jnp.float32) * norm, 0.0),
         axis=1,
         keepdims=True,
     )
@@ -252,42 +271,52 @@
     cr = pulls[:, 0:1] * scale
     cc = pulls[:, 1:2] * scale
     shift = cr * mean_r + cc * mean_c
-    level2 = jnp.where(q_col < TILE, m_run[...] + jnp.log2(n_sum), 1e30)
-    q4[0] = level2
-    q4[1] = jnp.broadcast_to(cr, (HC, 128))
-    q4[2] = jnp.broadcast_to(cc, (HC, 128))
-    q4[3] = jnp.broadcast_to(shift, (HC, 128))
+    level2 = jnp.where(q_col < TILE, state[0] + jnp.log2(n_sum), 1e30)
     flags = jnp.zeros((HC, 128), jnp.float32)
-    for slot in range(slots):
-        dr, dc, hit = listed(slot)
-        code = 3 * (dr + 1) + dc + 1
+    for slot in range(3 * n_cs):
+        _, _, code, hit = listed(slot, n_cs, n_c, col, cand, count)
         flags = jnp.where((cell == code) & (hit == 1), 1.0, flags)
     packed = flags
     for k, value in enumerate(
         (level2, cr, cc, shift, flags, (mean_r - q_row) / TILE, (mean_c - q_col) / TILE)
     ):
         packed = jnp.where(wide == k, value, packed)
+    packed_out[...] = packed
     turned = jnp.transpose(packed)
     stats[...] = turned[0:8]
     flow[...] = turned[5:7]
 
-    def grad_step(slot, carry):
-        dr, dc, hit = listed(slot)
+
+def grad_kernel(n_c, n_cs, c2, sc, cand, count, q, packed, *refs):
+    level, got, other = refs[:n_cs], refs[n_cs : 2 * n_cs], refs[2 * n_cs : 3 * n_cs]
+    out, buf, sems, s_scr, d_scr, acc, q4 = refs[3 * n_cs :]
+    core, col = sc[0], sc[2]
+    load_all(level, got, other, buf, sems, core)
+    acc[...] = jnp.zeros(acc.shape, jnp.float32)
+    for k in range(4):
+        q4[k] = jnp.broadcast_to(packed[:, k : k + 1], (HC, 128))
+    lane, lane_ok, in_row = lanes(RB)
+
+    def step(slot, carry):
+        dr, dc, _, hit = listed(slot, n_cs, n_c, col, cand, count)
+        wait_for(level[0], buf, sems, slot)
 
         @pl.when(hit == 1)
         def _():
             lane_row = (lane // PADW).astype(jnp.float32)
             lane_col = (lane % PADW + 30 * dc).astype(jnp.float32)
             for i in range(2):
-                base = lane_row + (30 * dr + 15 * half_of(dr, i)).astype(jnp.float32)
-                for g in range(HC // rb):
-                    rows = slice(g * rb, (g + 1) * rb)
+                s_scr[:, 0:HC] = lax.dot_general(
+                    q[...], buf[slot, i], (((1,), (1,)), ((), ())), preferred_element_type=jnp.float32
+                )
+                base = lane_row + (30 * dr + 15 * half_of(dr, i, core)).astype(jnp.float32)
+                for g in range(HC // RB):
+                    rows = slice(g * RB, (g + 1) * RB)
                     lev, gr, gc, sh = (q4[k, rows] for k in range(4))
                     pull = gr * base + (gc * lane_col - sh)
                     for v in range(4):
-                        s = s_scr[slot, rows, i * 512 + v * 128 : i * 512 + v * 128 + 128]
-                        p = jnp.exp2(s * c2 - lev)
-                        d = jnp.where(lane_last if v == 3 else lane_ok, p * pull, 0.0)
+                        p = jnp.exp2(s_scr[rows, v * 128 : v * 128 + 128] * c2 - lev)
+                        d = jnp.where(lane_ok & in_row if v == 3 else lane_ok, p * pull, 0.0)
                         d_scr[rows, v * 128 : v * 128 + 128] = d.astype(jnp.bfloat16)
                         if v < 3:
                             pull = pull + 4.0 * gr
@@ -297,43 +326,80 @@
 
         return carry
 
-    lax.fori_loop(0, slots, grad_step, 0)
-    dq[...] = acc[...].reshape(HALF, PADW, acc.shape[1])[:, :TILE]
-
-
-def query_side(n_c, sc, cand, count, q, ctg, level, got, other):
-    n_cs = len(level)
-    ch = q.shape[1]
-    slots = 3 * n_cs
-    c2 = math.log2(math.e) / math.sqrt(ch)
-    pairs = slots * 2 * HC * HC
+    lax.fori_loop(0, 3 * n_cs, step, 0)
+    out[...] = acc[...].reshape(HALF, PADW, acc.shape[1])[:, :TILE]
+
+
+def query_near(n_c, sc, cand, count, q, level):
+    n_cs, ch = len(level), q.shape[1]
+    pairs = n_cs * 2 * HC * HC
     return pl.pallas_call(
-        functools.partial(query_kernel, n_c, n_cs, c2),
+        functools.partial(near_kernel, n_c, n_cs, math.log2(math.e) / math.sqrt(ch)),
+        out_shape=jax.ShapeDtypeStruct((4, HC, 128), jnp.float32),
+        in_specs=[SMEM, SMEM, SMEM, VMEM] + [ANY] * n_cs,
+        out_specs=VMEM,
+        scratch_shapes=[
+            pltpu.VMEM((n_cs, 2, HC, ch), jnp.bfloat16),
+            pltpu.SemaphoreType.DMA((n_cs,)),
+            pltpu.VMEM((HC, 1024), jnp.float32),
+        ],
+        compiler_params=pltpu.CompilerParams(vmem_limit_bytes=32 * 2**20),
+        cost_estimate=pl.CostEstimate(
+            flops=2 * pairs * ch, bytes_accessed=6 * 10**6, transcendentals=pairs
+        ),
+        name="query_near",
+    )(sc, cand, count, q, *level)
+
+
+def query_far(n_c, sc, cand, count, q, ctg, begun, got, other):
+    n_cs, ch = len(got), q.shape[1]
+    pairs = 2 * n_cs * 2 * HC * HC
+    return pl.pallas_call(
+        functools.partial(far_kernel, n_c, n_cs, math.log2(math.e) / math.sqrt(ch)),
         out_shape=(
             jax.ShapeDtypeStruct((2, HC), jnp.float32),
             jax.ShapeDtypeStruct((8, HC), jnp.float32),
-            jax.ShapeDtypeStruct((HALF, TILE, ch), jnp.float32),
+            jax.ShapeDtypeStruct((HC, 128), jnp.float32),
         ),
+        in_specs=[SMEM, SMEM, SMEM, VMEM, VMEM, VMEM] + [ANY] * (2 * n_cs),
+        out_specs=(VMEM, VMEM, VMEM),
+        scratch_shapes=[
+            pltpu.VMEM((2 * n_cs, 2, HC, ch), jnp.bfloat16),
+            pltpu.SemaphoreType.DMA((2 * n_cs,)),
+            pltpu.VMEM((HC, 1024), jnp.float32),
+            pltpu.VMEM((4, HC, 128), jnp.float32),
+        ],
+        compiler_params=pltpu.CompilerParams(vmem_limit_bytes=32 * 2**20),
+        cost_estimate=pl.CostEstimate(
+            flops=2 * pairs * ch, bytes_accessed=8 * 10**6, transcendentals=pairs
+        ),
+        name="query_far",
+    )(sc, cand, count, q, ctg, begun, *got, *other)
+
+
+def query_grad(n_c, sc, cand, count, q, packed, level, got, other):
+    n_cs, ch = len(level), q.shape[1]
+    slots = 3 * n_cs
+    pairs = slots * 2 * HC * HC
+    return pl.pallas_call(
+        functools.partial(grad_kernel, n_c, n_cs, math.log2(math.e) / math.sqrt(ch)),
+        out_shape=jax.ShapeDtypeStruct((HALF, TILE, ch), jnp.float32),
         in_specs=[SMEM, SMEM, SMEM, VMEM, VMEM] + [ANY] * slots,
-        out_specs=(VMEM, VMEM, VMEM),
+        out_specs=VMEM,
         scratch_shapes=[
             pltpu.VMEM((slots, 2, HC, ch), jnp.bfloat16),
             pltpu.SemaphoreType.DMA((slots,)),
-            pltpu.VMEM((slots, HC, 1024), jnp.float32),
-            pltpu.VMEM((HC, 128), jnp.float32),
-            pltpu.VMEM((HC, 128), jnp.float32),
-            pltpu.VMEM((HC, 128), jnp.float32),
-            pltpu.VMEM((HC, 128), jnp.float32),
+            pltpu.VMEM((HC, 512), jnp.float32),
             pltpu.VMEM((HC, 512), jnp.bfloat16),
             pltpu.VMEM((HC, ch), jnp.float32),
             pltpu.VMEM((4, HC, 128), jnp.float32),
         ],
-        compiler_params=pltpu.CompilerParams(vmem_limit_bytes=48 * 2**20),
+        compiler_params=pltpu.CompilerParams(vmem_limit_bytes=32 * 2**20),
         cost_estimate=pl.CostEstimate(
-            flops=4 * pairs * ch, bytes_accessed=6 * 10**6, transcendentals=2 * pairs
+            flops=4 * pairs * ch, bytes_accessed=8 * 10**6, transcendentals=2 * pairs
         ),
-        name="query_side",
-    )(sc, cand, count, q, ctg, *level, *got, *other)
+        name="query_grad",
+    )(sc, cand, count, q, packed, *level, *got, *other)
 
 
 def target_kernel(n_c, n_cs, c2, sc, tgt, *refs):
@@ -348,6 +414,8 @@
 
     def step(slot, carry):
         dr, dc = slot_steps(slot, n_cs, n_c, col)
+        wait_for(feats[0], buf, sems, slot)
+        wait_for(stats[0], st, st_sems, slot)
         code = 8 - (3 * (dr + 1) + dc + 1)
         where_at = lax.broadcasted_iota(jnp.int32, (8, HC), 1)
         which = lax.broadcasted_iota(jnp.int32, (8, HC), 0)
@@ -416,8 +484,9 @@
     sc = jnp.stack([core, row, col]).astype(jnp.int32)
     w1 = conv_first.reshape(3, 3 * ch, ch)
     w2 = conv_second.reshape(3, 3 * ch, ch)
-    got = partner(lax.dynamic_slice_in_dim(mine, (BODY - 4) * (1 - core), BODY, 0))
+    got_all = partner(mine)
     own = lax.dynamic_slice_in_dim(mine, (BODY - 4) * core, BODY, 0)
+    got = lax.dynamic_slice_in_dim(got_all, (BODY - 4) * core, BODY, 0)
     bodies = (own, got)
     if n_c == 2:
         edge = jnp.stack([jnp.where(col == 0, b[:, TILE - 2 :], b[:, :2]) for b in bodies])
@@ -434,15 +503,35 @@
             jnp.concatenate([left, lax.dynamic_slice_in_dim(b, at, 2, 0), right], axis=1)
         )
     z = send(jnp.stack(lines), lambda r, k, c: (r - 1 + 2 * c, k, 1 - c))
-    second = encode(1, n_r, n_c, sc, mine, got, xl, xr, z, w1, w2)
-    first = encode(0, n_r, n_c, sc, mine, got, xl, xr, z, w1, w2)
+    cand, count = candidates.reshape(9), counts.reshape(1)
     ctg = jnp.pad(cotangent, ((0, 6), (0, 0), (0, PADW - TILE))).reshape(8, HC)
-    targets = gather_tiles(second)
-    queries = gather_tiles(first)
-    flow, stats, grad_first = query_side(
-        n_c, sc, candidates.reshape(9), counts.reshape(1), first, ctg, *targets
-    )
-    grad_second = target_side(n_c, sc, second, queries, gather_tiles(stats))
+    second = encode(1, n_r, n_c, sc, mine, got_all, xl, xr, z, w1, w2)
+    side = sideways(second)
+    own_tile = jnp.stack([second, partner(second)])
+    own_got = updown(own_tile)
+    first = encode(0, n_r, n_c, sc, after(mine, own_tile), got_all, xl, xr, z, w1, w2)
+    side = [after(x, first) for x in side]
+    level = [own_tile] + [jnp.stack([x, partner(x)]) for x in side]
+    got = [own_got] + [updown(t) for t in level[1:]]
+    q_side = sideways(after(first, level))
+    q_own = jnp.stack([first, partner(first)])
+    begun = query_near(n_c, sc, cand, count, after(first, q_own), level)
+    got = list(after(tuple(got), begun))
+    other = [partner(t) for t in got]
+    q_level = [q_own] + [jnp.stack([x, partner(x)]) for x in after(tuple(q_side), got)]
+    q_got = [updown(t) for t in q_level]
+    flow, stats, packed = query_far(n_c, sc, cand, count, first, ctg, begun, got, other)
+    st_level = [jnp.stack([stats, partner(stats)])]
+    st_level += [jnp.stack([x, partner(x)]) for x in sideways(stats)]
+    st_got = [updown(t) for t in st_level]
+    grad_first = query_grad(n_c, sc, cand, count, first, packed, level, got, other)
+    q_got = list(after(tuple(q_got), packed))
+    q_other = [partner(t) for t in q_got]
+    st_got = list(after(tuple(st_got), grad_first))
+    st_other = [partner(t) for t in st_got]
+    grad_second = target_side(
+        n_c, sc, second, (q_level, q_got, q_other), (st_level, st_got, st_other)
+    )
     return flow.reshape(2, HALF, PADW)[:, :, :TILE], grad_first, grad_second
 
 

time: 96.3 us -> 84.9 us (0.88)
  the two profiles are of different devices: /device:TPU:12 before, /device:TPU:9 now
where the time goes in v2:
time: 84.9 us; the launch traced here: 84.2 us
  starting transfers between devices  35 us (41%)
  Pallas kernels  31.5 us (37%)
  waiting for transfers between devices  10.5 us (12%)
  local copies, waits for them, and re-layouts  5.11 us (6%)
  between operations  1.61 us (2%)
    ppermute x24, starting transfers between devices, send(): return lax.ppermute(value, AXES, pairs)  35 us
    ppermute x24, waiting for transfers between devices, send(): return lax.ppermute(value, AXES, pairs)  10.5 us
    pallas_call x1, Pallas kernels, query_grad(): pl.pallas_call(functools.partial(grad_kernel, n_c, n_cs, math.log2(math.e...  8.95 us
    pallas_call x1, Pallas kernels, target_side(): pl.pallas_call(functools.partial(target_kernel, n_c, n_cs, c2), out_shape...  6.82 us
    pallas_call x1, Pallas kernels, query_far(): pl.pallas_call(functools.partial(far_kernel, n_c, n_cs, math.log2(math.e)...  6.31 us
    pallas_call x2, Pallas kernels, encode(): pl.pallas_call(functools.partial(encode_kernel, frame, n_r, n_c), out_sha...  6.28 us
    unnamed x12, local copies, waits for them, and re-layouts  3.17 us
    pallas_call x1, Pallas kernels, query_near(): pl.pallas_call(functools.partial(near_kernel, n_c, n_cs, math.log2(math.e...  3.15 us
  transfers between devices with their start and end apart: 24, of which 7 were waited for; matrix products, arithmetic and copies ran while one was open for 3% of the time, Pallas kernels for 26%

profile of v2, /device:TPU:9, one launch (start us, length us, event | category | flops | bytes accessed | tf_op | source)
XLA Modules:
  0.0 84.2 jit_solution(7520487022999405386)
XLA Ops:
  3.3 1.3 %collective-permute-start.1 = (bf16[2,17,2,256]{3,2,1,0:T(2,128)(2,1)S(1)}, bf16[2,17,2,256]{3,2,1,0:T(2,128)(2,1)S(1)}, u32[]{:S(2)}, u32[]{:S(2)}) collective-permute-start(bf16[2,17,2,256]{3,2,1,0:T(2,128)(2,1)S(1)} %pad_maximum_fusion.5), channel_id=1, source_target_pairs={{0,2},{1,3},{2,0},{3,1},{4,6},{5,7},{6,4},{7,5},{8,10},{9,11},{10,... | collective-permute-start | bytes 104456 | tf_op jit(solution)/shard_map/ppermute | solution.py:34
  4.6 1.6 %collective-permute-done.1.xl.xr = bf16[2,17,2,256]{3,2,1,0:T(2,128)(2,1)S(1)} collective-permute-done((bf16[2,17,2,256]{3,2,1,0:T(2,128)(2,1)S(1)}, bf16[2,17,2,256]{3,2,1,0:T(2,128)(2,1)S(1)}, u32[]{:S(2)}, u32[]{:S(2)}) %collective-permute-start.1) | collective-permute-done | bytes 34848 | tf_op jit(solution)/shard_map/ppermute | solution.py:34
  6.3 4.5 %collective-permute-start.2 = (bf16[2,2,34,256]{3,2,1,0:T(8,128)(2,1)S(1)}, bf16[2,2,34,256]{3,2,1,0:T(8,128)(2,1)S(1)}, u32[]{:S(2)}, u32[]{:S(2)}) collective-permute-start(bf16[2,2,34,256]{3,2,1,0:T(8,128)(2,1)S(1)} %pad_maximum_fusion.4), channel_id=1, source_target_pairs={{1,4},{3,6},{4,1},{5,8},{6,3},{7,10},{8,5},{9,12},{10,7},{11,14},{... | collective-permute-start | bytes 208904 | tf_op jit(solution)/shard_map/ppermute | solution.py:34
  10.9 2.2 %collective-permute-done.2.z = bf16[2,2,34,256]{3,2,1,0:T(8,128)(2,1)S(1)} collective-permute-done((bf16[2,2,34,256]{3,2,1,0:T(8,128)(2,1)S(1)}, bf16[2,2,34,256]{3,2,1,0:T(8,128)(2,1)S(1)}, u32[]{:S(2)}, u32[]{:S(2)}) %collective-permute-start.2) | collective-permute-done | bytes 69664 | tf_op jit(solution)/shard_map/ppermute | solution.py:34
  15.6 3.1 %encode_frame1.1.tgt = bf16[480,256]{1,0:T(8,128)(2,1)S(1)} custom-call(s32[3]{0:T(128)S(1)} %pad_add_fusion.sc, bf16[30,30,256]{2,1,0:T(8,128)(2,1)S(1)} %bitcast.47, bf16[30,30,256]{2,1,0:T(8,128)(2,1)S(1)} %collective-permute-done.got, bf16[2,17,2,256]{3,2,1,0:T(2,128)(2,1)S(1)} %collective-permute-done.1.xl.xr, ...), custom_call_target="tpu_custom_call" | custom-call | flops 1132462080 | bytes 4000000 | tf_op jit(solution)/shard_map/encode_frame1/pallas_call | solution.py:103
  20.5 3.1 %encode_frame0.1.q = bf16[480,256]{1,0:T(8,128)(2,1)S(1)} custom-call(s32[3]{0:T(128)S(1)} %pad_add_fusion.sc, bf16[30,30,256]{2,1,0:T(8,128)(2,1)S(1)} %bitcast.48, bf16[30,30,256]{2,1,0:T(8,128)(2,1)S(1)} %collective-permute-done.got, bf16[2,17,2,256]{3,2,1,0:T(2,128)(2,1)S(1)} %collective-permute-done.1.xl.xr, ...), custom_call_target="tpu_custom_call" | custom-call | flops 1132462080 | bytes 4000000 | tf_op jit(solution)/shard_map/encode_frame0/pallas_call | solution.py:103
  23.7 3.1 %collective-permute-done.5 = bf16[480,256]{1,0:T(8,128)(2,1)S(1)} collective-permute-done((bf16[480,256]{1,0:T(8,128)(2,1)S(1)}, bf16[480,256]{1,0:T(8,128)(2,1)S(1)}, u32[]{:S(2)}, u32[]{:S(2)}) %collective-permute-start.5) | collective-permute-done | bytes 245792 | tf_op jit(solution)/shard_map/ppermute | solution.py:34
  27.6 1.9 %collective-permute-start.7 = (bf16[2,480,256]{2,1,0:T(8,128)(2,1)S(1)}, bf16[2,480,256]{2,1,0:T(8,128)(2,1)}, u32[]{:S(2)}, u32[]{:S(2)}) collective-permute-start(bf16[2,480,256]{2,1,0:T(8,128)(2,1)S(1)} %pad_maximum_fusion.refs_0_), channel_id=1, source_target_pairs={{0,4},{2,6},{4,8},{5,1},{6,10},{7,3},{8,12},{9,5},{10,14},{11,7},{... | collective-permute-start | bytes 1474568 | tf_op jit(solution)/shard_map/ppermute | solution.py:34
  29.6 1.9 %collective-permute-start.8 = (bf16[2,480,256]{2,1,0:T(8,128)(2,1)S(1)}, bf16[2,480,256]{2,1,0:T(8,128)(2,1)}, u32[]{:S(2)}, u32[]{:S(2)}) collective-permute-start(bf16[2,480,256]{2,1,0:T(8,128)(2,1)S(1)} %pad_maximum_fusion.2.refs_1_), channel_id=1, source_target_pairs={{0,4},{2,6},{4,8},{5,1},{6,10},{7,3},{8,12},{9,5},{10,14},{11,7},{... | collective-permute-start | bytes 1474568 | tf_op jit(solution)/shard_map/ppermute | solution.py:34
  31.5 3.2 %collective-permute-start.4 = (bf16[480,256]{1,0:T(8,128)(2,1)S(1)}, bf16[480,256]{1,0:T(8,128)(2,1)S(1)}, u32[]{:S(2)}, u32[]{:S(2)}) collective-permute-start(bf16[480,256]{1,0:T(8,128)(2,1)S(1)} %encode_frame0.1.q), channel_id=1, source_target_pairs={{0,1},{1,0},{2,3},{3,2},{4,5},{5,4},{6,7},{7,6},{8,9},{9,8},{10,11... | collective-permute-start | bytes 737288 | tf_op jit(solution)/shard_map/ppermute | solution.py:34
  36.7 3.1 %query_near.1.begun = f32[4,480,128]{2,1,0:T(8,128)S(1)} custom-call(s32[3]{0:T(128)S(1)} %pad_add_fusion.sc, s32[9]{0:T(128)S(1)} %bitcast.50, s32[1]{0:T(128)} %bitcast.41.count, bf16[480,256]{1,0:T(8,128)(2,1)S(1)} %encode_frame0.1.q, bf16[2,480,256]{2,1,0:T(8,128)(2,1)S(1)} %pad_maximum_fusion.refs_0_, bf16[2,480,256]{2,1,0:T(8,128)(2,1)S(1)} %pad_maximum_fusion.2.refs_1_), custom_call_target="tpu_custom_call" | custom-call | flops 471859200 | bytes 6000000 | tf_op jit(solution)/shard_map/query_near/pallas_call | solution.py:336
  39.8 3.0 %collective-permute-done.8.refs_1_.refs_3_ = bf16[2,480,256]{2,1,0:T(8,128)(2,1)} collective-permute-done((bf16[2,480,256]{2,1,0:T(8,128)(2,1)S(1)}, bf16[2,480,256]{2,1,0:T(8,128)(2,1)}, u32[]{:S(2)}, u32[]{:S(2)}) %collective-permute-start.8) | collective-permute-done | bytes 491552 | tf_op jit(solution)/shard_map/ppermute | solution.py:34
  43.7 2.2 %collective-permute-start.13 = (bf16[2,480,256]{2,1,0:T(8,128)(2,1)S(1)}, bf16[2,480,256]{2,1,0:T(8,128)(2,1)}, u32[]{:S(2)}, u32[]{:S(2)}) collective-permute-start(bf16[2,480,256]{2,1,0:T(8,128)(2,1)S(1)} %pad_maximum_fusion.1.refs_0_), channel_id=1, source_target_pairs={{0,4},{2,6},{4,8},{5,1},{6,10},{7,3},{8,12},{9,5},{10,14},{11,7},{... | collective-permute-start | bytes 1474568 | tf_op jit(solution)/shard_map/ppermute | solution.py:34
  45.9 1.4 %collective-permute-start.10 = (bf16[2,480,256]{2,1,0:T(8,128)(2,1)}, bf16[2,480,256]{2,1,0:T(8,128)(2,1)}, u32[]{:S(2)}, u32[]{:S(2)}) collective-permute-start(bf16[2,480,256]{2,1,0:T(8,128)(2,1)} %collective-permute-done.8.refs_1_.refs_3_), channel_id=1, source_target_pairs={{0,1},{1,0},{2,3},{3,2},{4,5},{5,4},{6,7},{7,6},{8,9},{9,8},{10,11... | collective-permute-start | bytes 1474568 | tf_op jit(solution)/shard_map/ppermute | solution.py:34
  47.4 2.7 %collective-permute-start.14 = (bf16[2,480,256]{2,1,0:T(8,128)(2,1)S(1)}, bf16[2,480,256]{2,1,0:T(8,128)(2,1)}, u32[]{:S(2)}, u32[]{:S(2)}) collective-permute-start(bf16[2,480,256]{2,1,0:T(8,128)(2,1)S(1)} %pad_maximum_fusion.3.refs_1_), channel_id=1, source_target_pairs={{0,4},{2,6},{4,8},{5,1},{6,10},{7,3},{8,12},{9,5},{10,14},{11,7},{... | collective-permute-start | bytes 1474568 | tf_op jit(solution)/shard_map/ppermute | solution.py:34
  50.3 6.3 %query_far.1 = (f32[2,480]{1,0:T(2,128)S(1)}, f32[8,480]{1,0:T(8,128)S(1)}, f32[480,128]{1,0:T(8,128)S(1)}) custom-call(s32[3]{0:T(128)S(1)} %pad_add_fusion.sc, s32[9]{0:T(128)S(1)} %bitcast.51, s32[1]{0:T(128)} %bitcast.42.count, bf16[480,256]{1,0:T(8,128)(2,1)S(1)} %encode_frame0.1.q, f32[8,480]{1,0:T(8,128)S(1)} %reshape.44.ctg, ...), custom_call_target="tpu_custom_call" | custom-call | flops 943718400 | bytes 8000000 | tf_op jit(solution)/shard_map/query_far/pallas_call | solution.py:357
  56.6 1.3 %collective-permute-start.18 = (f32[8,480]{1,0:T(8,128)S(1)}, f32[8,480]{1,0:T(8,128)S(1)}, u32[]{:S(2)}, u32[]{:S(2)}) collective-permute-start(f32[8,480]{1,0:T(8,128)S(1)} %get-tuple-element.28), channel_id=1, source_target_pairs={{0,2},{1,3},{2,0},{3,1},{4,6},{5,7},{6,4},{7,5},{8,10},{9,11},{10,... | collective-permute-start | bytes 46088 | tf_op jit(solution)/shard_map/ppermute | solution.py:34
  57.9 1.3 %collective-permute-start.17 = (f32[8,480]{1,0:T(8,128)S(1)}, f32[8,480]{1,0:T(8,128)S(1)}, u32[]{:S(2)}, u32[]{:S(2)}) collective-permute-start(f32[8,480]{1,0:T(8,128)S(1)} %get-tuple-element.28), channel_id=1, source_target_pairs={{0,1},{1,0},{2,3},{3,2},{4,5},{5,4},{6,7},{7,6},{8,9},{9,8},{10,11... | collective-permute-start | bytes 46088 | tf_op jit(solution)/shard_map/ppermute | solution.py:34
  59.4 2.0 %collective-permute-start.19 = (f32[8,480]{1,0:T(8,128)S(1)}, f32[8,480]{1,0:T(8,128)S(1)}, u32[]{:S(2)}, u32[]{:S(2)}) collective-permute-start(f32[8,480]{1,0:T(8,128)S(1)} %collective-permute-done.18), channel_id=1, source_target_pairs={{0,1},{1,0},{2,3},{3,2},{4,5},{5,4},{6,7},{7,6},{8,9},{9,8},{10,11... | collective-permute-start | bytes 46088 | tf_op jit(solution)/shard_map/ppermute | solution.py:34
  61.9 1.9 %collective-permute-start.20 = (f32[2,8,480]{2,1,0:T(8,128)S(1)}, f32[2,8,480]{2,1,0:T(8,128)S(1)}, u32[]{:S(2)}, u32[]{:S(2)}) collective-permute-start(f32[2,8,480]{2,1,0:T(8,128)S(1)} %pad_maximum_fusion.6.refs_6_), channel_id=1, source_target_pairs={{0,4},{2,6},{4,8},{5,1},{6,10},{7,3},{8,12},{9,5},{10,14},{11,7},{... | collective-permute-start | bytes 92168 | tf_op jit(solution)/shard_map/ppermute | solution.py:34
  63.9 1.9 %collective-permute-start.21 = (f32[2,8,480]{2,1,0:T(8,128)S(1)}, f32[2,8,480]{2,1,0:T(8,128)S(1)}, u32[]{:S(2)}, u32[]{:S(2)}) collective-permute-start(f32[2,8,480]{2,1,0:T(8,128)S(1)} %pad_maximum_fusion.7.refs_7_), channel_id=1, source_target_pairs={{0,4},{2,6},{4,8},{5,1},{6,10},{7,3},{8,12},{9,5},{10,14},{11,7},{... | collective-permute-start | bytes 92168 | tf_op jit(solution)/shard_map/ppermute | solution.py:34
  65.8 9.0 %query_grad.1 = f32[15,30,256]{2,1,0:T(8,128)} custom-call(s32[3]{0:T(128)S(1)} %pad_add_fusion.sc, s32[9]{0:T(128)S(1)} %bitcast.52, s32[1]{0:T(128)} %bitcast.43.count, bf16[480,256]{1,0:T(8,128)(2,1)S(1)} %encode_frame0.1.q, f32[480,128]{1,0:T(8,128)S(1)} %get-tuple-element.23.packed, bf16[2,480,256]{2,1,0:T(8,128)(2,1)S(1)} %pad_maximum_fusion.refs_0_, ...), custom_call_target="tpu_custom_call" | custom-call | flops 2831155200 | bytes 8000000 | tf_op jit(solution)/shard_map/query_grad/pallas_call | solution.py:384
  74.8 1.4 %collective-permute-start.22 = (f32[2,8,480]{2,1,0:T(8,128)S(1)}, f32[2,8,480]{2,1,0:T(8,128)S(1)}, u32[]{:S(2)}, u32[]{:S(2)}) collective-permute-start(f32[2,8,480]{2,1,0:T(8,128)S(1)} %collective-permute-done.20.refs_8_), channel_id=1, source_target_pairs={{0,1},{1,0},{2,3},{3,2},{4,5},{5,4},{6,7},{7,6},{8,9},{9,8},{10,11... | collective-permute-start | bytes 92168 | tf_op jit(solution)/shard_map/ppermute | solution.py:34
  77.4 6.8 %target_side.1 = f32[15,30,256]{2,1,0:T(8,128)} custom-call(s32[3]{0:T(128)S(1)} %pad_add_fusion.sc, bf16[480,256]{1,0:T(8,128)(2,1)S(1)} %encode_frame1.1.tgt, bf16[2,480,256]{2,1,0:T(8,128)(2,1)S(1)} %pad_maximum_fusion.1.refs_0_, bf16[2,480,256]{2,1,0:T(8,128)(2,1)S(1)} %pad_maximum_fusion.3.refs_1_, ...), custom_call_target="tpu_custom_call" | custom-call | flops 2831155200 | bytes 6000000 | tf_op jit(solution)/shard_map/target_side/pallas_call | solution.py:456
  (63 shorter events, 12.4 us)
Async XLA Ops:
  0.6 2.5 %collective-permute-start = (bf16[30,30,256]{2,1,0:T(8,128)(2,1)}, bf16[30,30,256]{2,1,0:T(8,128)(2,1)S(1)}, u32[]{:S(2)}, u32[]{:S(2)}) collective-permute-start(bf16[30,30,256]{2,1,0:T(8,128)(2,1)} %bitcast.46), channel_id=1, source_target_pairs={{0,1},{1,0},{2,3},{3,2},{4,5},{5,4},{6,7},{7,6},{8,9},{9,8},{10,11... | collective-permute-start | bytes 1382408 | tf_op jit(solution)/shard_map/ppermute | solution.py:34
  3.3 2.9 %collective-permute-start.1 = (bf16[2,17,2,256]{3,2,1,0:T(2,128)(2,1)S(1)}, bf16[2,17,2,256]{3,2,1,0:T(2,128)(2,1)S(1)}, u32[]{:S(2)}, u32[]{:S(2)}) collective-permute-start(bf16[2,17,2,256]{3,2,1,0:T(2,128)(2,1)S(1)} %pad_maximum_fusion.5), channel_id=1, source_target_pairs={{0,2},{1,3},{2,0},{3,1},{4,6},{5,7},{6,4},{7,5},{8,10},{9,11},{10,... | collective-permute-start | bytes 104456 | tf_op jit(solution)/shard_map/ppermute | solution.py:34
  6.3 6.8 %collective-permute-start.2 = (bf16[2,2,34,256]{3,2,1,0:T(8,128)(2,1)S(1)}, bf16[2,2,34,256]{3,2,1,0:T(8,128)(2,1)S(1)}, u32[]{:S(2)}, u32[]{:S(2)}) collective-permute-start(bf16[2,2,34,256]{3,2,1,0:T(8,128)(2,1)S(1)} %pad_maximum_fusion.4), channel_id=1, source_target_pairs={{1,4},{3,6},{4,1},{5,8},{6,3},{7,10},{8,5},{9,12},{10,7},{11,14},{... | collective-permute-start | bytes 208904 | tf_op jit(solution)/shard_map/ppermute | solution.py:34
  18.7 1.7 %collective-permute-start.3 = (bf16[480,256]{1,0:T(8,128)(2,1)S(1)}, bf16[480,256]{1,0:T(8,128)(2,1)S(1)}, u32[]{:S(2)}, u32[]{:S(2)}) collective-permute-start(bf16[480,256]{1,0:T(8,128)(2,1)S(1)} %encode_frame1.1.tgt), channel_id=1, source_target_pairs={{0,1},{1,0},{2,3},{3,2},{4,5},{5,4},{6,7},{7,6},{8,9},{9,8},{10,11... | collective-permute-start | bytes 737288 | tf_op jit(solution)/shard_map/ppermute | solution.py:34
  19.2 7.5 %collective-permute-start.5 = (bf16[480,256]{1,0:T(8,128)(2,1)S(1)}, bf16[480,256]{1,0:T(8,128)(2,1)S(1)}, u32[]{:S(2)}, u32[]{:S(2)}) collective-permute-start(bf16[480,256]{1,0:T(8,128)(2,1)S(1)} %encode_frame1.1.tgt), channel_id=1, source_target_pairs={{0,2},{1,3},{2,0},{3,1},{4,6},{5,7},{6,4},{7,5},{8,10},{9,11},{10,... | collective-permute-start | bytes 737288 | tf_op jit(solution)/shard_map/ppermute | solution.py:34
  26.7 2.8 %collective-permute-start.6 = (bf16[480,256]{1,0:T(8,128)(2,1)S(1)}, bf16[480,256]{1,0:T(8,128)(2,1)S(1)}, u32[]{:S(2)}, u32[]{:S(2)}) collective-permute-start(bf16[480,256]{1,0:T(8,128)(2,1)S(1)} %collective-permute-done.5), channel_id=1, source_target_pairs={{0,1},{1,0},{2,3},{3,2},{4,5},{5,4},{6,7},{7,6},{8,9},{9,8},{10,11... | collective-permute-start | bytes 737288 | tf_op jit(solution)/shard_map/ppermute | solution.py:34
  27.6 12.2 %collective-permute-start.7 = (bf16[2,480,256]{2,1,0:T(8,128)(2,1)S(1)}, bf16[2,480,256]{2,1,0:T(8,128)(2,1)}, u32[]{:S(2)}, u32[]{:S(2)}) collective-permute-start(bf16[2,480,256]{2,1,0:T(8,128)(2,1)S(1)} %pad_maximum_fusion.refs_0_), channel_id=1, source_target_pairs={{0,4},{2,6},{4,8},{5,1},{6,10},{7,3},{8,12},{9,5},{10,14},{11,7},{... | collective-permute-start | bytes 1474568 | tf_op jit(solution)/shard_map/ppermute | solution.py:34
  29.6 13.2 %collective-permute-start.8 = (bf16[2,480,256]{2,1,0:T(8,128)(2,1)S(1)}, bf16[2,480,256]{2,1,0:T(8,128)(2,1)}, u32[]{:S(2)}, u32[]{:S(2)}) collective-permute-start(bf16[2,480,256]{2,1,0:T(8,128)(2,1)S(1)} %pad_maximum_fusion.2.refs_1_), channel_id=1, source_target_pairs={{0,4},{2,6},{4,8},{5,1},{6,10},{7,3},{8,12},{9,5},{10,14},{11,7},{... | collective-permute-start | bytes 1474568 | tf_op jit(solution)/shard_map/ppermute | solution.py:34
  31.5 5.1 %collective-permute-start.4 = (bf16[480,256]{1,0:T(8,128)(2,1)S(1)}, bf16[480,256]{1,0:T(8,128)(2,1)S(1)}, u32[]{:S(2)}, u32[]{:S(2)}) collective-permute-start(bf16[480,256]{1,0:T(8,128)(2,1)S(1)} %encode_frame0.1.q), channel_id=1, source_target_pairs={{0,1},{1,0},{2,3},{3,2},{4,5},{5,4},{6,7},{7,6},{8,9},{9,8},{10,11... | collective-permute-start | bytes 737288 | tf_op jit(solution)/shard_map/ppermute | solution.py:34
  34.7 8.1 %collective-permute-start.11 = (bf16[480,256]{1,0:T(8,128)(2,1)S(1)}, bf16[480,256]{1,0:T(8,128)(2,1)S(1)}, u32[]{:S(2)}, u32[]{:S(2)}) collective-permute-start(bf16[480,256]{1,0:T(8,128)(2,1)S(1)} %encode_frame0.1.q), channel_id=1, source_target_pairs={{0,2},{1,3},{2,0},{3,1},{4,6},{5,7},{6,4},{7,5},{8,10},{9,11},{10,... | collective-permute-start | bytes 737288 | tf_op jit(solution)/shard_map/ppermute | solution.py:34
  42.8 4.5 %collective-permute-start.12 = (bf16[480,256]{1,0:T(8,128)(2,1)S(1)}, bf16[480,256]{1,0:T(8,128)(2,1)S(1)}, u32[]{:S(2)}, u32[]{:S(2)}) collective-permute-start(bf16[480,256]{1,0:T(8,128)(2,1)S(1)} %collective-permute-done.11), channel_id=1, source_target_pairs={{0,1},{1,0},{2,3},{3,2},{4,5},{5,4},{6,7},{7,6},{8,9},{9,8},{10,11... | collective-permute-start | bytes 737288 | tf_op jit(solution)/shard_map/ppermute | solution.py:34
  43.7 17.7 %collective-permute-start.13 = (bf16[2,480,256]{2,1,0:T(8,128)(2,1)S(1)}, bf16[2,480,256]{2,1,0:T(8,128)(2,1)}, u32[]{:S(2)}, u32[]{:S(2)}) collective-permute-start(bf16[2,480,256]{2,1,0:T(8,128)(2,1)S(1)} %pad_maximum_fusion.1.refs_0_), channel_id=1, source_target_pairs={{0,4},{2,6},{4,8},{5,1},{6,10},{7,3},{8,12},{9,5},{10,14},{11,7},{... | collective-permute-start | bytes 1474568 | tf_op jit(solution)/shard_map/ppermute | solution.py:34
  45.9 4.4 %collective-permute-start.10 = (bf16[2,480,256]{2,1,0:T(8,128)(2,1)}, bf16[2,480,256]{2,1,0:T(8,128)(2,1)}, u32[]{:S(2)}, u32[]{:S(2)}) collective-permute-start(bf16[2,480,256]{2,1,0:T(8,128)(2,1)} %collective-permute-done.8.refs_1_.refs_3_), channel_id=1, source_target_pairs={{0,1},{1,0},{2,3},{3,2},{4,5},{5,4},{6,7},{7,6},{8,9},{9,8},{10,11... | collective-permute-start | bytes 1474568 | tf_op jit(solution)/shard_map/ppermute | solution.py:34
  47.3 3.0 %collective-permute-start.9 = (bf16[2,480,256]{2,1,0:T(8,128)(2,1)}, bf16[2,480,256]{2,1,0:T(8,128)(2,1)}, u32[]{:S(2)}, u32[]{:S(2)}) collective-permute-start(bf16[2,480,256]{2,1,0:T(8,128)(2,1)} %collective-permute-done.7.refs_0_.refs_2_), channel_id=1, source_target_pairs={{0,1},{1,0},{2,3},{3,2},{4,5},{5,4},{6,7},{7,6},{8,9},{9,8},{10,11... | collective-permute-start | bytes 1474568 | tf_op jit(solution)/shard_map/ppermute | solution.py:34
  47.4 14.0 %collective-permute-start.14 = (bf16[2,480,256]{2,1,0:T(8,128)(2,1)S(1)}, bf16[2,480,256]{2,1,0:T(8,128)(2,1)}, u32[]{:S(2)}, u32[]{:S(2)}) collective-permute-start(bf16[2,480,256]{2,1,0:T(8,128)(2,1)S(1)} %pad_maximum_fusion.3.refs_1_), channel_id=1, source_target_pairs={{0,4},{2,6},{4,8},{5,1},{6,10},{7,3},{8,12},{9,5},{10,14},{11,7},{... | collective-permute-start | bytes 1474568 | tf_op jit(solution)/shard_map/ppermute | solution.py:34
  56.6 2.8 %collective-permute-start.18 = (f32[8,480]{1,0:T(8,128)S(1)}, f32[8,480]{1,0:T(8,128)S(1)}, u32[]{:S(2)}, u32[]{:S(2)}) collective-permute-start(f32[8,480]{1,0:T(8,128)S(1)} %get-tuple-element.28), channel_id=1, source_target_pairs={{0,2},{1,3},{2,0},{3,1},{4,6},{5,7},{6,4},{7,5},{8,10},{9,11},{10,... | collective-permute-start | bytes 46088 | tf_op jit(solution)/shard_map/ppermute | solution.py:34
  57.9 4.1 %collective-permute-start.17 = (f32[8,480]{1,0:T(8,128)S(1)}, f32[8,480]{1,0:T(8,128)S(1)}, u32[]{:S(2)}, u32[]{:S(2)}) collective-permute-start(f32[8,480]{1,0:T(8,128)S(1)} %get-tuple-element.28), channel_id=1, source_target_pairs={{0,1},{1,0},{2,3},{3,2},{4,5},{5,4},{6,7},{7,6},{8,9},{9,8},{10,11... | collective-permute-start | bytes 46088 | tf_op jit(solution)/shard_map/ppermute | solution.py:34
  59.4 4.5 %collective-permute-start.19 = (f32[8,480]{1,0:T(8,128)S(1)}, f32[8,480]{1,0:T(8,128)S(1)}, u32[]{:S(2)}, u32[]{:S(2)}) collective-permute-start(f32[8,480]{1,0:T(8,128)S(1)} %collective-permute-done.18), channel_id=1, source_target_pairs={{0,1},{1,0},{2,3},{3,2},{4,5},{5,4},{6,7},{7,6},{8,9},{9,8},{10,11... | collective-permute-start | bytes 46088 | tf_op jit(solution)/shard_map/ppermute | solution.py:34
  61.4 16.0 %collective-permute-start.15 = (bf16[2,480,256]{2,1,0:T(8,128)(2,1)}, bf16[2,480,256]{2,1,0:T(8,128)(2,1)S(1)}, u32[]{:S(2)}, u32[]{:S(2)}) collective-permute-start(bf16[2,480,256]{2,1,0:T(8,128)(2,1)} %collective-permute-done.13.refs_2_), channel_id=1, source_target_pairs={{0,1},{1,0},{2,3},{3,2},{4,5},{5,4},{6,7},{7,6},{8,9},{9,8},{10,11... | collective-permute-start | bytes 1474568 | tf_op jit(solution)/shard_map/ppermute | solution.py:34
  61.5 15.9 %collective-permute-start.16 = (bf16[2,480,256]{2,1,0:T(8,128)(2,1)}, bf16[2,480,256]{2,1,0:T(8,128)(2,1)}, u32[]{:S(2)}, u32[]{:S(2)}) collective-permute-start(bf16[2,480,256]{2,1,0:T(8,128)(2,1)} %collective-permute-done.14.refs_3_), channel_id=1, source_target_pairs={{0,1},{1,0},{2,3},{3,2},{4,5},{5,4},{6,7},{7,6},{8,9},{9,8},{10,11... | collective-permute-start | bytes 1474568 | tf_op jit(solution)/shard_map/ppermute | solution.py:34
  61.9 12.8 %collective-permute-start.20 = (f32[2,8,480]{2,1,0:T(8,128)S(1)}, f32[2,8,480]{2,1,0:T(8,128)S(1)}, u32[]{:S(2)}, u32[]{:S(2)}) collective-permute-start(f32[2,8,480]{2,1,0:T(8,128)S(1)} %pad_maximum_fusion.6.refs_6_), channel_id=1, source_target_pairs={{0,4},{2,6},{4,8},{5,1},{6,10},{7,3},{8,12},{9,5},{10,14},{11,7},{... | collective-permute-start | bytes 92168 | tf_op jit(solution)/shard_map/ppermute | solution.py:34
  63.9 10.9 %collective-permute-start.21 = (f32[2,8,480]{2,1,0:T(8,128)S(1)}, f32[2,8,480]{2,1,0:T(8,128)S(1)}, u32[]{:S(2)}, u32[]{:S(2)}) collective-permute-start(f32[2,8,480]{2,1,0:T(8,128)S(1)} %pad_maximum_fusion.7.refs_7_), channel_id=1, source_target_pairs={{0,4},{2,6},{4,8},{5,1},{6,10},{7,3},{8,12},{9,5},{10,14},{11,7},{... | collective-permute-start | bytes 92168 | tf_op jit(solution)/shard_map/ppermute | solution.py:34
  74.8 2.3 %collective-permute-start.22 = (f32[2,8,480]{2,1,0:T(8,128)S(1)}, f32[2,8,480]{2,1,0:T(8,128)S(1)}, u32[]{:S(2)}, u32[]{:S(2)}) collective-permute-start(f32[2,8,480]{2,1,0:T(8,128)S(1)} %collective-permute-done.20.refs_8_), channel_id=1, source_target_pairs={{0,1},{1,0},{2,3},{3,2},{4,5},{5,4},{6,7},{7,6},{8,9},{9,8},{10,11... | collective-permute-start | bytes 92168 | tf_op jit(solution)/shard_map/ppermute | solution.py:34
  76.2 1.2 %collective-permute-start.23 = (f32[2,8,480]{2,1,0:T(8,128)S(1)}, f32[2,8,480]{2,1,0:T(8,128)S(1)}, u32[]{:S(2)}, u32[]{:S(2)}) collective-permute-start(f32[2,8,480]{2,1,0:T(8,128)S(1)} %collective-permute-done.21.refs_9_), channel_id=1, source_target_pairs={{0,1},{1,0},{2,3},{3,2},{4,5},{5,4},{6,7},{7,6},{8,9},{9,8},{10,11... | collective-permute-start | bytes 92168 | tf_op jit(solution)/shard_map/ppermute | solution.py:34
  (5 other events, 41.4 us)

commit v3 on v2

--- a/solution.py
+++ b/solution.py
@@ -19,6 +19,7 @@
 VMEM = pl.BlockSpec(memory_space=pltpu.VMEM)
 SMEM = pl.BlockSpec(memory_space=pltpu.SMEM)
 RB = 16
+COST = pl.CostEstimate(flops=10**6, bytes_accessed=10**4, transcendentals=0)
 ANY = pl.BlockSpec(memory_space=pl.ANY)
 
 
@@ -63,8 +64,9 @@
     got_rows = got[pl.ds((BODY - 4) * core, BODY)]
     body = jnp.where(use_own, own_rows, got_rows).astype(jnp.float32)
     slot = jnp.where(use_own, 0, 1)
-    left = jnp.where(col > 0, xl[slot].astype(jnp.float32), 0.0)
-    right = jnp.where(col < n_c - 1, xr[slot].astype(jnp.float32), 0.0)
+    rows = pl.ds((BODY - 4) * core, BODY)
+    left = jnp.where(col > 0, xl[slot, rows].astype(jnp.float32), 0.0)
+    right = jnp.where(col < n_c - 1, xr[slot, rows].astype(jnp.float32), 0.0)
     ext[pl.ds(first_row, BODY), 2 : 2 + TILE] = body
     ext[pl.ds(first_row, BODY), 0:2] = left
     ext[pl.ds(first_row, BODY), 2 + TILE : 4 + TILE] = right
@@ -98,6 +100,30 @@
     )
 
 
+def fetch_kernel(a, b, a_out, b_out, sems):
+    copies = [
+        pltpu.make_async_copy(a, a_out, sems.at[0]),
+        pltpu.make_async_copy(b, b_out, sems.at[1]),
+    ]
+    for copy in copies:
+        copy.start()
+    for copy in copies:
+        copy.wait()
+
+
+def fetch(a, b):
+    return pl.pallas_call(
+        fetch_kernel,
+        out_shape=[pltpu.VMEM(x.shape, x.dtype) for x in (a, b)],
+        in_specs=[ANY, ANY],
+        out_specs=[VMEM, VMEM],
+        scratch_shapes=[pltpu.SemaphoreType.DMA((2,))],
+        compiler_params=pltpu.CompilerParams(vmem_limit_bytes=2**20),
+        cost_estimate=COST,
+        name="fetch_weights",
+    )(a, b)
+
+
 def encode(frame, n_r, n_c, sc, mine, got, xl, xr, z, w1, w2):
     ch = mine.shape[-1]
     return pl.pallas_call(
@@ -111,20 +137,23 @@
             pltpu.VMEM((HID * PADW + 8, ch), jnp.float32),
             pltpu.VMEM((HID * PADW, 3 * ch), jnp.bfloat16),
         ],
-        compiler_params=pltpu.CompilerParams(vmem_limit_bytes=40 * 2**20),
-        cost_estimate=pl.CostEstimate(
-            flops=2 * HC * 9 * ch * ch * 2, bytes_accessed=4 * 10**6, transcendentals=0
-        ),
+        compiler_params=pltpu.CompilerParams(vmem_limit_bytes=12 * 2**20),
+        cost_estimate=COST,
         name=f"encode_frame{frame}",
     )(sc, mine, got, xl, xr, z, w1, w2)
 
 
-def load_all(level, got, other, buf, sems, core):
-    n_cs = len(level)
+def load_rows(level, got, other, buf, sems, core):
+    first = 2 * core
+    pltpu.make_async_copy(level, buf.at[1], sems.at[1]).start()
+    pltpu.make_async_copy(got, buf.at[first], sems.at[first]).start()
+    pltpu.make_async_copy(other, buf.at[2 - first], sems.at[2 - first]).start()
+
+
+def load_far(got, other, buf, sems, core):
+    n_cs = len(got)
     for j in range(n_cs):
-        up, down = j, 2 * n_cs + j
-        first, last = jnp.where(core == 0, up, down), jnp.where(core == 0, down, up)
-        pltpu.make_async_copy(level[j], buf.at[n_cs + j], sems.at[n_cs + j]).start()
+        first, last = jnp.where(core == 0, j, n_cs + j), jnp.where(core == 0, n_cs + j, j)
         pltpu.make_async_copy(got[j], buf.at[first], sems.at[first]).start()
         pltpu.make_async_copy(other[j], buf.at[last], sems.at[last]).start()
 
@@ -228,10 +257,7 @@
     got, other = refs[:n_cs], refs[n_cs : 2 * n_cs]
     flow, stats, packed_out, buf, sems, s_scr, state = refs[2 * n_cs :]
     core, col = sc[0], sc[2]
-    for j in range(n_cs):
-        first, last = jnp.where(core == 0, j, n_cs + j), jnp.where(core == 0, n_cs + j, j)
-        pltpu.make_async_copy(got[j], buf.at[first], sems.at[first]).start()
-        pltpu.make_async_copy(other[j], buf.at[last], sems.at[last]).start()
+    load_far(got, other, buf, sems, core)
     state[...] = begun[...]
 
     def step(j, carry):
@@ -287,52 +313,79 @@
     flow[...] = turned[5:7]
 
 
-def grad_kernel(n_c, n_cs, c2, sc, cand, count, q, packed, *refs):
-    level, got, other = refs[:n_cs], refs[n_cs : 2 * n_cs], refs[2 * n_cs : 3 * n_cs]
-    out, buf, sems, s_scr, d_scr, acc, q4 = refs[3 * n_cs :]
-    core, col = sc[0], sc[2]
-    load_all(level, got, other, buf, sems, core)
-    acc[...] = jnp.zeros(acc.shape, jnp.float32)
+def spread(packed, q4):
     for k in range(4):
         q4[k] = jnp.broadcast_to(packed[:, k : k + 1], (HC, 128))
+
+
+def grad_tile(c2, slot, dr, dc, core, q, buf, s_scr, d_scr, acc, q4):
     lane, lane_ok, in_row = lanes(RB)
-
-    def step(slot, carry):
-        dr, dc, _, hit = listed(slot, n_cs, n_c, col, cand, count)
-        wait_for(level[0], buf, sems, slot)
+    lane_row = (lane // PADW).astype(jnp.float32)
+    lane_col = (lane % PADW + 30 * dc).astype(jnp.float32)
+    for i in range(2):
+        s_scr[:, 0:HC] = lax.dot_general(
+            q[...], buf[slot, i], (((1,), (1,)), ((), ())), preferred_element_type=jnp.float32
+        )
+        base = lane_row + (30 * dr + 15 * half_of(dr, i, core)).astype(jnp.float32)
+        for g in range(HC // RB):
+            rows = slice(g * RB, (g + 1) * RB)
+            lev, gr, gc, sh = (q4[k, rows] for k in range(4))
+            pull = gr * base + (gc * lane_col - sh)
+            for v in range(4):
+                p = jnp.exp2(s_scr[rows, v * 128 : v * 128 + 128] * c2 - lev)
+                d = jnp.where(lane_ok & in_row if v == 3 else lane_ok, p * pull, 0.0)
+                d_scr[rows, v * 128 : v * 128 + 128] = d.astype(jnp.bfloat16)
+                if v < 3:
+                    pull = pull + 4.0 * gr
+        acc[...] += jnp.dot(d_scr[:, 0:HC], buf[slot, i], preferred_element_type=jnp.float32)
+
+
+def grad_near_kernel(n_c, n_cs, c2, sc, cand, count, q, packed, *refs):
+    level, (acc, buf, sems, s_scr, d_scr, q4) = refs[:n_cs], refs[n_cs:]
+    core, col = sc[0], sc[2]
+    for j in range(n_cs):
+        pltpu.make_async_copy(level[j], buf.at[j], sems.at[j]).start()
+    acc[...] = jnp.zeros(acc.shape, jnp.float32)
+    spread(packed, q4)
+
+    def step(j, carry):
+        dr, dc, _, hit = listed(n_cs + j, n_cs, n_c, col, cand, count)
+        wait_for(level[0], buf, sems, j)
 
         @pl.when(hit == 1)
         def _():
-            lane_row = (lane // PADW).astype(jnp.float32)
-            lane_col = (lane % PADW + 30 * dc).astype(jnp.float32)
-            for i in range(2):
-                s_scr[:, 0:HC] = lax.dot_general(
-                    q[...], buf[slot, i], (((1,), (1,)), ((), ())), preferred_element_type=jnp.float32
-                )
-                base = lane_row + (30 * dr + 15 * half_of(dr, i, core)).astype(jnp.float32)
-                for g in range(HC // RB):
-                    rows = slice(g * RB, (g + 1) * RB)
-                    lev, gr, gc, sh = (q4[k, rows] for k in range(4))
-                    pull = gr * base + (gc * lane_col - sh)
-                    for v in range(4):
-                        p = jnp.exp2(s_scr[rows, v * 128 : v * 128 + 128] * c2 - lev)
-                        d = jnp.where(lane_ok & in_row if v == 3 else lane_ok, p * pull, 0.0)
-                        d_scr[rows, v * 128 : v * 128 + 128] = d.astype(jnp.bfloat16)
-                        if v < 3:
-                            pull = pull + 4.0 * gr
-                acc[...] += jnp.dot(
-                    d_scr[:, 0:HC], buf[slot, i], preferred_element_type=jnp.float32
-                )
+            grad_tile(c2, j, dr, dc, core, q, buf, s_scr, d_scr, acc, q4)
 
         return carry
 
-    lax.fori_loop(0, 3 * n_cs, step, 0)
+    lax.fori_loop(0, n_cs, step, 0)
+
+
+def grad_far_kernel(n_c, n_cs, c2, sc, cand, count, q, packed, begun, *refs):
+    got, other = refs[:n_cs], refs[n_cs : 2 * n_cs]
+    out, buf, sems, s_scr, d_scr, q4, acc = refs[2 * n_cs :]
+    core, col = sc[0], sc[2]
+    load_far(got, other, buf, sems, core)
+    acc[...] = begun[...]
+    spread(packed, q4)
+
+    def step(j, carry):
+        slot = jnp.where(j < n_cs, j, n_cs + j)
+        dr, dc, _, hit = listed(slot, n_cs, n_c, col, cand, count)
+        wait_for(got[0], buf, sems, j)
+
+        @pl.when(hit == 1)
+        def _():
+            grad_tile(c2, j, dr, dc, core, q, buf, s_scr, d_scr, acc, q4)
+
+        return carry
+
+    lax.fori_loop(0, 2 * n_cs, step, 0)
     out[...] = acc[...].reshape(HALF, PADW, acc.shape[1])[:, :TILE]
 
 
 def query_near(n_c, sc, cand, count, q, level):
     n_cs, ch = len(level), q.shape[1]
-    pairs = n_cs * 2 * HC * HC
     return pl.pallas_call(
         functools.partial(near_kernel, n_c, n_cs, math.log2(math.e) / math.sqrt(ch)),
         out_shape=jax.ShapeDtypeStruct((4, HC, 128), jnp.float32),
@@ -343,17 +396,14 @@
             pltpu.SemaphoreType.DMA((n_cs,)),
             pltpu.VMEM((HC, 1024), jnp.float32),
         ],
-        compiler_params=pltpu.CompilerParams(vmem_limit_bytes=32 * 2**20),
-        cost_estimate=pl.CostEstimate(
-            flops=2 * pairs * ch, bytes_accessed=6 * 10**6, transcendentals=pairs
-        ),
+        compiler_params=pltpu.CompilerParams(vmem_limit_bytes=12 * 2**20),
+        cost_estimate=COST,
         name="query_near",
     )(sc, cand, count, q, *level)
 
 
 def query_far(n_c, sc, cand, count, q, ctg, begun, got, other):
     n_cs, ch = len(got), q.shape[1]
-    pairs = 2 * n_cs * 2 * HC * HC
     return pl.pallas_call(
         functools.partial(far_kernel, n_c, n_cs, math.log2(math.e) / math.sqrt(ch)),
         out_shape=(
@@ -369,57 +419,74 @@
             pltpu.VMEM((HC, 1024), jnp.float32),
             pltpu.VMEM((4, HC, 128), jnp.float32),
         ],
-        compiler_params=pltpu.CompilerParams(vmem_limit_bytes=32 * 2**20),
-        cost_estimate=pl.CostEstimate(
-            flops=2 * pairs * ch, bytes_accessed=8 * 10**6, transcendentals=pairs
-        ),
+        compiler_params=pltpu.CompilerParams(vmem_limit_bytes=12 * 2**20),
+        cost_estimate=COST,
         name="query_far",
     )(sc, cand, count, q, ctg, begun, *got, *other)
 
 
-def query_grad(n_c, sc, cand, count, q, packed, level, got, other):
+def grad_near(n_c, sc, cand, count, q, packed, level):
     n_cs, ch = len(level), q.shape[1]
-    slots = 3 * n_cs
-    pairs = slots * 2 * HC * HC
     return pl.pallas_call(
-        functools.partial(grad_kernel, n_c, n_cs, math.log2(math.e) / math.sqrt(ch)),
-        out_shape=jax.ShapeDtypeStruct((HALF, TILE, ch), jnp.float32),
-        in_specs=[SMEM, SMEM, SMEM, VMEM, VMEM] + [ANY] * slots,
+        functools.partial(grad_near_kernel, n_c, n_cs, math.log2(math.e) / math.sqrt(ch)),
+        out_shape=jax.ShapeDtypeStruct((HC, ch), jnp.float32),
+        in_specs=[SMEM, SMEM, SMEM, VMEM, VMEM] + [ANY] * n_cs,
         out_specs=VMEM,
         scratch_shapes=[
-            pltpu.VMEM((slots, 2, HC, ch), jnp.bfloat16),
-            pltpu.SemaphoreType.DMA((slots,)),
+            pltpu.VMEM((n_cs, 2, HC, ch), jnp.bfloat16),
+            pltpu.SemaphoreType.DMA((n_cs,)),
             pltpu.VMEM((HC, 512), jnp.float32),
             pltpu.VMEM((HC, 512), jnp.bfloat16),
-            pltpu.VMEM((HC, ch), jnp.float32),
             pltpu.VMEM((4, HC, 128), jnp.float32),
         ],
-        compiler_params=pltpu.CompilerParams(vmem_limit_bytes=32 * 2**20),
-        cost_estimate=pl.CostEstimate(
-            flops=4 * pairs * ch, bytes_accessed=8 * 10**6, transcendentals=2 * pairs
-        ),
-        name="query_grad",
-    )(sc, cand, count, q, packed, *level, *got, *other)
+        compiler_params=pltpu.CompilerParams(vmem_limit_bytes=12 * 2**20),
+        cost_estimate=COST,
+        name="grad_near",
+    )(sc, cand, count, q, packed, *level)
+
+
+def grad_far(n_c, sc, cand, count, q, packed, begun, got, other):
+    n_cs, ch = len(got), q.shape[1]
+    return pl.pallas_call(
+        functools.partial(grad_far_kernel, n_c, n_cs, math.log2(math.e) / math.sqrt(ch)),
+        out_shape=jax.ShapeDtypeStruct((HALF, TILE, ch), jnp.float32),
+        in_specs=[SMEM, SMEM, SMEM, VMEM, VMEM, VMEM] + [ANY] * (2 * n_cs),
+        out_specs=VMEM,
+        scratch_shapes=[
+            pltpu.VMEM((2 * n_cs, 2, HC, ch), jnp.bfloat16),
+            pltpu.SemaphoreType.DMA((2 * n_cs,)),
+            pltpu.VMEM((HC, 512), jnp.float32),
+            pltpu.VMEM((HC, 512), jnp.bfloat16),
+            pltpu.VMEM((4, HC, 128), jnp.float32),
+            pltpu.VMEM((HC, ch), jnp.float32),
+        ],
+        compiler_params=pltpu.CompilerParams(vmem_limit_bytes=12 * 2**20),
+        cost_estimate=COST,
+        name="grad_far",
+    )(sc, cand, count, q, packed, begun, *got, *other)
 
 
 def target_kernel(n_c, n_cs, c2, sc, tgt, *refs):
-    slots = 3 * n_cs
-    feats = refs[:slots]
-    stats = refs[slots : 2 * slots]
-    out, buf, sems, st, st_sems, s_scr, d_scr, v_scr, acc = refs[2 * slots :]
+    feats, stats = refs[:3], refs[3:6]
+    out, buf, sems, st, st_sems, s_scr, d_scr, v_scr, acc = refs[6:]
     core, col = sc[0], sc[2]
-    load_all(feats[:n_cs], feats[n_cs : 2 * n_cs], feats[2 * n_cs :], buf, sems, core)
-    load_all(stats[:n_cs], stats[n_cs : 2 * n_cs], stats[2 * n_cs :], st, st_sems, core)
+    load_rows(*stats, st, st_sems, core)
+    load_rows(*feats, buf, sems, core)
     acc[...] = jnp.zeros(acc.shape, jnp.float32)
 
     def step(slot, carry):
         dr, dc = slot_steps(slot, n_cs, n_c, col)
-        wait_for(feats[0], buf, sems, slot)
-        wait_for(stats[0], st, st_sems, slot)
+        a, j = slot // n_cs, slot % n_cs
+
+        @pl.when(j == 0)
+        def _():
+            wait_for(feats[0], buf, sems, a)
+            wait_for(stats[0], st, st_sems, a)
+
         code = 8 - (3 * (dr + 1) + dc + 1)
         where_at = lax.broadcasted_iota(jnp.int32, (8, HC), 1)
         which = lax.broadcasted_iota(jnp.int32, (8, HC), 0)
-        flag = jnp.sum(jnp.where((where_at == code) & (which == 4), st[slot, 0], 0.0))
+        flag = jnp.sum(jnp.where((where_at == code) & (which == 4), st[a, j, 0], 0.0))
 
         @pl.when(flag > 0.5)
         def _():
@@ -428,9 +495,9 @@
             ).astype(jnp.float32)
             for i in range(2):
                 s_scr[...] = lax.dot_general(
-                    tgt[...], buf[slot, i], (((1,), (1,)), ((), ())), preferred_element_type=jnp.float32
+                    tgt[...], buf[a, j, i], (((1,), (1,)), ((), ())), preferred_element_type=jnp.float32
                 )
-                lev, gr, gc, sh = (st[slot, i, k : k + 1, :] for k in range(4))
+                lev, gr, gc, sh = (st[a, j, i, k : k + 1, :] for k in range(4))
                 v_scr[...] = gc * col_t - sh
                 for g in range(HALF):
                     rows = slice(g * PADW, (g + 1) * PADW)
@@ -438,42 +505,35 @@
                     p = jnp.exp2(s_scr[rows] * c2 - lev)
                     d = p * (v_scr[...] + gr * row_t)
                     d_scr[rows] = d.astype(jnp.bfloat16)
-                acc[...] += jnp.dot(d_scr[...], buf[slot, i], preferred_element_type=jnp.float32)
+                acc[...] += jnp.dot(d_scr[...], buf[a, j, i], preferred_element_type=jnp.float32)
 
         return carry
 
-    lax.fori_loop(0, slots, step, 0)
+    lax.fori_loop(0, 3 * n_cs, step, 0)
     out[...] = acc[...].reshape(HALF, PADW, acc.shape[1])[:, :TILE]
 
 
 def target_side(n_c, sc, tgt, feats, stats):
-    level, got, other = feats
-    n_cs = len(level)
-    ch = tgt.shape[1]
-    slots = 3 * n_cs
-    c2 = math.log2(math.e) / math.sqrt(ch)
-    pairs = slots * 2 * HC * HC
+    n_cs, ch = feats[0].shape[0], tgt.shape[1]
     return pl.pallas_call(
-        functools.partial(target_kernel, n_c, n_cs, c2),
+        functools.partial(target_kernel, n_c, n_cs, math.log2(math.e) / math.sqrt(ch)),
         out_shape=jax.ShapeDtypeStruct((HALF, TILE, ch), jnp.float32),
-        in_specs=[SMEM, VMEM] + [ANY] * (2 * slots),
+        in_specs=[SMEM, VMEM] + [ANY] * 6,
         out_specs=VMEM,
         scratch_shapes=[
-            pltpu.VMEM((slots, 2, HC, ch), jnp.bfloat16),
-            pltpu.SemaphoreType.DMA((slots,)),
-            pltpu.VMEM((slots, 2, 8, HC), jnp.float32),
-            pltpu.SemaphoreType.DMA((slots,)),
+            pltpu.VMEM((3, n_cs, 2, HC, ch), jnp.bfloat16),
+            pltpu.SemaphoreType.DMA((3,)),
+            pltpu.VMEM((3, n_cs, 2, 8, HC), jnp.float32),
+            pltpu.SemaphoreType.DMA((3,)),
             pltpu.VMEM((HC, HC), jnp.float32),
             pltpu.VMEM((HC, HC), jnp.bfloat16),
             pltpu.VMEM((PADW, HC), jnp.float32),
             pltpu.VMEM((HC, ch), jnp.float32),
         ],
-        compiler_params=pltpu.CompilerParams(vmem_limit_bytes=48 * 2**20),
-        cost_estimate=pl.CostEstimate(
-            flops=4 * pairs * ch, bytes_accessed=6 * 10**6, transcendentals=pairs
-        ),
+        compiler_params=pltpu.CompilerParams(vmem_limit_bytes=12 * 2**20),
+        cost_estimate=COST,
         name="target_side",
-    )(sc, tgt, *level, *got, *other, *stats[0], *stats[1], *stats[2])
+    )(sc, tgt, *feats, *stats)
 
 
 def shards(frames, conv_first, conv_second, candidates, counts, cotangent):
@@ -482,53 +542,52 @@
     n_r, n_c = lax.axis_size("rows"), lax.axis_size("cols")
     core, row, col = (lax.axis_index(a) for a in ("pair", "rows", "cols"))
     sc = jnp.stack([core, row, col]).astype(jnp.int32)
-    w1 = conv_first.reshape(3, 3 * ch, ch)
-    w2 = conv_second.reshape(3, 3 * ch, ch)
-    got_all = partner(mine)
-    own = lax.dynamic_slice_in_dim(mine, (BODY - 4) * core, BODY, 0)
-    got = lax.dynamic_slice_in_dim(got_all, (BODY - 4) * core, BODY, 0)
-    bodies = (own, got)
+    cand, count = candidates.reshape(9), counts.reshape(1)
+    ctg = jnp.pad(cotangent, ((0, 6), (0, 0), (0, PADW - TILE))).reshape(8, HC)
+    other_frame = partner(mine)
+    both = (mine, other_frame)
     if n_c == 2:
-        edge = jnp.stack([jnp.where(col == 0, b[:, TILE - 2 :], b[:, :2]) for b in bodies])
+        edge = jnp.stack([jnp.where(col == 0, f[:, TILE - 2 :], f[:, :2]) for f in both])
         xl = xr = send(edge, lambda r, k, c: (r, 1 - k, c))
     else:
-        xl = send(jnp.stack([b[:, TILE - 2 :] for b in bodies]), lambda r, k, c: (r, k + 1, c))
-        xr = send(jnp.stack([b[:, :2] for b in bodies]), lambda r, k, c: (r, k - 1, c))
+        xl = send(jnp.stack([f[:, TILE - 2 :] for f in both]), lambda r, k, c: (r, k + 1, c))
+        xr = send(jnp.stack([f[:, :2] for f in both]), lambda r, k, c: (r, k - 1, c))
+    w1, w2 = fetch(after(conv_first, both), conv_second)
+    w1, w2 = w1.reshape(3, 3 * ch, ch), w2.reshape(3, 3 * ch, ch)
+    xl_, xr_ = after((xl, xr), w1)
     lines = []
-    for i, b in enumerate(bodies):
-        at = HALF * core
-        left = jnp.where(col > 0, lax.dynamic_slice_in_dim(xl[i], at, 2, 0), 0)
-        right = jnp.where(col < n_c - 1, lax.dynamic_slice_in_dim(xr[i], at, 2, 0), 0)
-        lines.append(
-            jnp.concatenate([left, lax.dynamic_slice_in_dim(b, at, 2, 0), right], axis=1)
-        )
+    for i, f in enumerate(both):
+        ends = [jnp.where(core == 0, x[:2], x[TILE - 2 :]) for x in (xl_[i], f, xr_[i])]
+        ends[0] = jnp.where(col > 0, ends[0], 0)
+        ends[2] = jnp.where(col < n_c - 1, ends[2], 0)
+        lines.append(jnp.concatenate(ends, axis=1))
     z = send(jnp.stack(lines), lambda r, k, c: (r - 1 + 2 * c, k, 1 - c))
-    cand, count = candidates.reshape(9), counts.reshape(1)
-    ctg = jnp.pad(cotangent, ((0, 6), (0, 0), (0, PADW - TILE))).reshape(8, HC)
-    second = encode(1, n_r, n_c, sc, mine, got_all, xl, xr, z, w1, w2)
+    second = encode(1, n_r, n_c, sc, mine, other_frame, xl, xr, z, w1, w2)
     side = sideways(second)
     own_tile = jnp.stack([second, partner(second)])
     own_got = updown(own_tile)
-    first = encode(0, n_r, n_c, sc, after(mine, own_tile), got_all, xl, xr, z, w1, w2)
-    side = [after(x, first) for x in side]
+    first = encode(0, n_r, n_c, sc, after(mine, own_tile), other_frame, xl, xr, z, w1, w2)
+    q_side = sideways(first)
+    side = after(tuple(side), (first, own_got))
     level = [own_tile] + [jnp.stack([x, partner(x)]) for x in side]
     got = [own_got] + [updown(t) for t in level[1:]]
-    q_side = sideways(after(first, level))
-    q_own = jnp.stack([first, partner(first)])
-    begun = query_near(n_c, sc, cand, count, after(first, q_own), level)
+    begun = query_near(n_c, sc, cand, count, first, level)
     got = list(after(tuple(got), begun))
     other = [partner(t) for t in got]
-    q_level = [q_own] + [jnp.stack([x, partner(x)]) for x in after(tuple(q_side), got)]
-    q_got = [updown(t) for t in q_level]
     flow, stats, packed = query_far(n_c, sc, cand, count, first, ctg, begun, got, other)
-    st_level = [jnp.stack([stats, partner(stats)])]
-    st_level += [jnp.stack([x, partner(x)]) for x in sideways(stats)]
-    st_got = [updown(t) for t in st_level]
-    grad_first = query_grad(n_c, sc, cand, count, first, packed, level, got, other)
-    q_got = list(after(tuple(q_got), packed))
-    q_other = [partner(t) for t in q_got]
-    st_got = list(after(tuple(st_got), grad_first))
-    st_other = [partner(t) for t in st_got]
+    q_own = jnp.stack([first, partner(after(first, begun))])
+    q_side = after(tuple(q_side), packed)
+    q_level = jnp.stack([q_own] + [jnp.stack([x, partner(x)]) for x in q_side])
+    q_got = updown(q_level)
+    st_side = sideways(stats)
+    st_own = jnp.stack([stats, partner(stats)])
+    part = grad_near(n_c, sc, cand, count, first, after(packed, (st_own, q_level)), level)
+    st_side = after(tuple(st_side), part)
+    st_level = jnp.stack([st_own] + [jnp.stack([x, partner(x)]) for x in st_side])
+    st_got = updown(st_level)
+    grad_first = grad_far(n_c, sc, cand, count, first, after(packed, st_level), part, got, other)
+    q_got, st_got = after((q_got, st_got), grad_first)
+    q_other, st_other = partner(q_got), partner(st_got)
     grad_second = target_side(
         n_c, sc, second, (q_level, q_got, q_other), (st_level, st_got, st_other)
     )

time: 84.9 us -> 83.7 us (0.986)
  the two profiles are of different devices: /device:TPU:9 before, /device:TPU:12 now
where the time goes in v3:
time: 83.7 us; the launch traced here: 82.2 us
  Pallas kernels  31 us (37%)
  starting transfers between devices  23.4 us (28%)
  waiting for transfers between devices  18.6 us (22%)
  other arithmetic  4.27 us (5%)
  local copies, waits for them, and re-layouts  3.34 us (4%)
  between operations  1.56 us (2%)
    ppermute x20, starting transfers between devices, send(): return lax.ppermute(value, AXES, pairs)  23.4 us
    ppermute x20, waiting for transfers between devices, send(): return lax.ppermute(value, AXES, pairs)  18.6 us
    pallas_call x1, Pallas kernels, target_side(): pl.pallas_call(functools.partial(target_kernel, n_c, n_cs, math.log2(math...  8.17 us
    pallas_call x2, Pallas kernels, encode(): pl.pallas_call(functools.partial(encode_kernel, frame, n_r, n_c), out_sha...  6.26 us
    pallas_call x1, Pallas kernels, grad_far(): pl.pallas_call(functools.partial(grad_far_kernel, n_c, n_cs, math.log2(ma...  4.77 us
    pallas_call x1, Pallas kernels, query_far(): pl.pallas_call(functools.partial(far_kernel, n_c, n_cs, math.log2(math.e)...  4.58 us
    pallas_call x1, Pallas kernels, grad_near(): pl.pallas_call(functools.partial(grad_near_kernel, n_c, n_cs, math.log2(m...  3.54 us
    unnamed x12, local copies, waits for them, and re-layouts  3.17 us
  transfers between devices with their start and end apart: 20, of which 14 were waited for; matrix products, arithmetic and copies ran while one was open for 4% of the time, Pallas kernels for 24%

profile of v3, /device:TPU:12, one launch (start us, length us, event | category | flops | bytes accessed | tf_op | source)
XLA Modules:
  0.0 82.2 jit_solution(989290815896222831)
XLA Ops:
  2.9 1.6 %collective-permute-start.1 = (bf16[2,30,2,256]{3,2,1,0:T(2,128)(2,1)S(1)}, bf16[2,30,2,256]{3,2,1,0:T(2,128)(2,1)S(1)}, u32[]{:S(2)}, u32[]{:S(2)}) collective-permute-start(bf16[2,30,2,256]{3,2,1,0:T(2,128)(2,1)S(1)} %pad_maximum_fusion.5), channel_id=1, source_target_pairs={{0,2},{1,3},{2,0},{3,1},{4,6},{5,7},{6,4},{7,5},{8,10},{9,11},{10,... | collective-permute-start | bytes 184328 | tf_op jit(solution)/shard_map/ppermute | solution.py:35
  4.5 1.3 %copy-done.1 = bf16[9,256,256]{2,1,0:T(8,128)(2,1)S(1)} copy-done((bf16[9,256,256]{2,1,0:T(8,128)(2,1)S(1)}, bf16[9,256,256]{2,1,0:T(8,128)(2,1)}, u32[]{:S(2)}) %copy-start.1) | copy-done | bytes 1179672
  5.8 1.3 %copy-done.2 = bf16[9,256,256]{2,1,0:T(8,128)(2,1)S(1)} copy-done((bf16[9,256,256]{2,1,0:T(8,128)(2,1)S(1)}, bf16[9,256,256]{2,1,0:T(8,128)(2,1)}, u32[]{:S(2)}) %copy-start.2) | copy-done | bytes 1179672
  7.6 1.9 %collective-permute-start.2 = (bf16[2,2,34,256]{3,2,1,0:T(8,128)(2,1)S(1)}, bf16[2,2,34,256]{3,2,1,0:T(8,128)(2,1)S(1)}, u32[]{:S(2)}, u32[]{:S(2)}) collective-permute-start(bf16[2,2,34,256]{3,2,1,0:T(8,128)(2,1)S(1)} %pad_maximum_fusion.3), channel_id=1, source_target_pairs={{1,4},{3,6},{4,1},{5,8},{6,3},{7,10},{8,5},{9,12},{10,7},{11,14},{... | collective-permute-start | bytes 208904 | tf_op jit(solution)/shard_map/ppermute | solution.py:35
  9.7 3.7 %collective-permute-done.2.z = bf16[2,2,34,256]{3,2,1,0:T(8,128)(2,1)S(1)} collective-permute-done((bf16[2,2,34,256]{3,2,1,0:T(8,128)(2,1)S(1)}, bf16[2,2,34,256]{3,2,1,0:T(8,128)(2,1)S(1)}, u32[]{:S(2)}, u32[]{:S(2)}) %collective-permute-start.2) | collective-permute-done | bytes 69664 | tf_op jit(solution)/shard_map/ppermute | solution.py:35
  13.4 3.1 %encode_frame1.1.tgt = bf16[480,256]{1,0:T(8,128)(2,1)S(1)} custom-call(s32[3]{0:T(128)S(1)} %pad_add_fusion.sc, bf16[30,30,256]{2,1,0:T(8,128)(2,1)S(1)} %bitcast.58, bf16[30,30,256]{2,1,0:T(8,128)(2,1)S(1)} %collective-permute-done.got, bf16[2,30,2,256]{3,2,1,0:T(2,128)(2,1)S(1)} %collective-permute-done.1.xl.xr, ...), custom_call_target="tpu_custom_call" | custom-call | flops 1000000 | bytes 10000 | tf_op jit(solution)/shard_map/encode_frame1/pallas_call | solution.py:129
  16.7 1.4 %collective-permute-done.3 = bf16[480,256]{1,0:T(8,128)(2,1)S(1)} collective-permute-done((bf16[480,256]{1,0:T(8,128)(2,1)S(1)}, bf16[480,256]{1,0:T(8,128)(2,1)S(1)}, u32[]{:S(2)}, u32[]{:S(2)}) %collective-permute-start.3) | collective-permute-done | bytes 245792 | tf_op jit(solution)/shard_map/ppermute | solution.py:35
  18.2 3.5 %collective-permute-start.5 = (bf16[2,480,256]{2,1,0:T(8,128)(2,1)S(1)}, bf16[2,480,256]{2,1,0:T(8,128)(2,1)S(1)}, u32[]{:S(2)}, u32[]{:S(2)}) collective-permute-start(bf16[2,480,256]{2,1,0:T(8,128)(2,1)S(1)} %pad_maximum_fusion.1.refs_0_), channel_id=1, source_target_pairs={{0,4},{2,6},{4,8},{5,1},{6,10},{7,3},{8,12},{9,5},{10,14},{11,7},{... | collective-permute-start | bytes 1474568 | tf_op jit(solution)/shard_map/ppermute | solution.py:35
  21.7 1.2 %collective-permute-start.4 = (bf16[480,256]{1,0:T(8,128)(2,1)S(1)}, bf16[480,256]{1,0:T(8,128)(2,1)S(1)}, u32[]{:S(2)}, u32[]{:S(2)}) collective-permute-start(bf16[480,256]{1,0:T(8,128)(2,1)S(1)} %encode_frame1.1.tgt), channel_id=1, source_target_pairs={{0,2},{1,3},{2,0},{3,1},{4,6},{5,7},{6,4},{7,5},{8,10},{9,11},{10,... | collective-permute-start | bytes 737288 | tf_op jit(solution)/shard_map/ppermute | solution.py:35
  22.9 3.1 %encode_frame0.1.q = bf16[480,256]{1,0:T(8,128)(2,1)S(1)} custom-call(s32[3]{0:T(128)S(1)} %pad_add_fusion.sc, bf16[30,30,256]{2,1,0:T(8,128)(2,1)S(1)} %bitcast.59, bf16[30,30,256]{2,1,0:T(8,128)(2,1)S(1)} %collective-permute-done.got, bf16[2,30,2,256]{3,2,1,0:T(2,128)(2,1)S(1)} %collective-permute-done.1.xl.xr, ...), custom_call_target="tpu_custom_call" | custom-call | flops 1000000 | bytes 10000 | tf_op jit(solution)/shard_map/encode_frame0/pallas_call | solution.py:129
  26.0 2.1 %collective-permute-done.4 = bf16[480,256]{1,0:T(8,128)(2,1)S(1)} collective-permute-done((bf16[480,256]{1,0:T(8,128)(2,1)S(1)}, bf16[480,256]{1,0:T(8,128)(2,1)S(1)}, u32[]{:S(2)}, u32[]{:S(2)}) %collective-permute-start.4) | collective-permute-done | bytes 245792 | tf_op jit(solution)/shard_map/ppermute | solution.py:35
  28.9 1.5 %collective-permute-done.6 = bf16[480,256]{1,0:T(8,128)(2,1)S(1)} collective-permute-done((bf16[480,256]{1,0:T(8,128)(2,1)S(1)}, bf16[480,256]{1,0:T(8,128)(2,1)S(1)}, u32[]{:S(2)}, u32[]{:S(2)}) %collective-permute-start.6) | collective-permute-done | bytes 245792 | tf_op jit(solution)/shard_map/ppermute | solution.py:35
  30.5 3.5 %collective-permute-start.7 = (bf16[2,480,256]{2,1,0:T(8,128)(2,1)S(1)}, bf16[2,480,256]{2,1,0:T(8,128)(2,1)S(1)}, u32[]{:S(2)}, u32[]{:S(2)}) collective-permute-start(bf16[2,480,256]{2,1,0:T(8,128)(2,1)S(1)} %pad_maximum_fusion.2.refs_1_), channel_id=1, source_target_pairs={{0,4},{2,6},{4,8},{5,1},{6,10},{7,3},{8,12},{9,5},{10,14},{11,7},{... | collective-permute-start | bytes 1474568 | tf_op jit(solution)/shard_map/ppermute | solution.py:35
  34.6 3.1 %query_near.1.begun = f32[4,480,128]{2,1,0:T(8,128)S(1)} custom-call(s32[3]{0:T(128)S(1)} %pad_add_fusion.sc, s32[9]{0:T(128)S(1)} %bitcast.62, s32[1]{0:T(128)} %bitcast.47.count, bf16[480,256]{1,0:T(8,128)(2,1)S(1)} %encode_frame0.1.q, bf16[2,480,256]{2,1,0:T(8,128)(2,1)S(1)} %pad_maximum_fusion.1.refs_0_, bf16[2,480,256]{2,1,0:T(8,128)(2,1)S(1)} %pad_maximum_fusion.2.refs_1_), custom_call_target="tpu_custom_call" | custom-call | flops 1000000 | bytes 10000 | tf_op jit(solution)/shard_map/query_near/pallas_call | solution.py:389
  37.8 3.4 %collective-permute-done.7.refs_1_ = bf16[2,480,256]{2,1,0:T(8,128)(2,1)S(1)} collective-permute-done((bf16[2,480,256]{2,1,0:T(8,128)(2,1)S(1)}, bf16[2,480,256]{2,1,0:T(8,128)(2,1)S(1)}, u32[]{:S(2)}, u32[]{:S(2)}) %collective-permute-start.7) | collective-permute-done | bytes 491552 | tf_op jit(solution)/shard_map/ppermute | solution.py:35
  43.9 4.6 %query_far.1 = (f32[2,480]{1,0:T(2,128)S(1)}, f32[8,480]{1,0:T(8,128)S(1)}, f32[480,128]{1,0:T(8,128)S(1)}) custom-call(s32[3]{0:T(128)S(1)} %pad_add_fusion.sc, s32[9]{0:T(128)S(1)} %bitcast.63, s32[1]{0:T(128)} %bitcast.48.count, bf16[480,256]{1,0:T(8,128)(2,1)S(1)} %encode_frame0.1.q, f32[8,480]{1,0:T(8,128)S(1)} %reshape.60.ctg, ...), custom_call_target="tpu_custom_call" | custom-call | flops 1000000 | bytes 10000 | tf_op jit(solution)/shard_map/query_far/pallas_call | solution.py:407
  52.5 3.5 %collective-permute-start.16 = (bf16[2,2,480,256]{3,2,1,0:T(8,128)(2,1)S(1)}, bf16[2,2,480,256]{3,2,1,0:T(8,128)(2,1)}, u32[]{:S(2)}, u32[]{:S(2)}) collective-permute-start(bf16[2,2,480,256]{3,2,1,0:T(8,128)(2,1)S(1)} %pad_maximum_fusion.refs_0_), channel_id=1, source_target_pairs={{0,4},{2,6},{4,8},{5,1},{6,10},{7,3},{8,12},{9,5},{10,14},{11,7},{... | collective-permute-start | bytes 2949128 | tf_op jit(solution)/shard_map/ppermute | solution.py:35
  56.0 1.8 %collective-permute-start.11 = (f32[8,480]{1,0:T(8,128)S(1)}, f32[8,480]{1,0:T(8,128)S(1)}, u32[]{:S(2)}, u32[]{:S(2)}) collective-permute-start(f32[8,480]{1,0:T(8,128)S(1)} %get-tuple-element.33), channel_id=1, source_target_pairs={{0,2},{1,3},{2,0},{3,1},{4,6},{5,7},{6,4},{7,5},{8,10},{9,11},{10,... | collective-permute-start | bytes 46088 | tf_op jit(solution)/shard_map/ppermute | solution.py:35
  57.8 3.5 %grad_near.1.begun = f32[480,256]{1,0:T(8,128)S(1)} custom-call(s32[3]{0:T(128)S(1)} %pad_add_fusion.sc, s32[9]{0:T(128)S(1)} %bitcast.64, s32[1]{0:T(128)} %bitcast.49.count, bf16[480,256]{1,0:T(8,128)(2,1)S(1)} %encode_frame0.1.q, f32[480,128]{1,0:T(8,128)S(1)} %get-tuple-element.38.packed, bf16[2,480,256]{2,1,0:T(8,128)(2,1)S(1)} %pad_maximum_fusion.1.refs_0_, ...), custom_call_target="tpu_custom_call" | custom-call | flops 1000000 | bytes 10000 | tf_op jit(solution)/shard_map/grad_near/pallas_call | solution.py:430
  62.7 1.9 %collective-permute-start.17 = (f32[2,2,8,480]{3,2,1,0:T(8,128)S(1)}, f32[2,2,8,480]{3,2,1,0:T(8,128)S(1)}, u32[]{:S(2)}, u32[]{:S(2)}) collective-permute-start(f32[2,2,8,480]{3,2,1,0:T(8,128)S(1)} %pad_maximum_fusion.4.refs_3_), channel_id=1, source_target_pairs={{0,4},{2,6},{4,8},{5,1},{6,10},{7,3},{8,12},{9,5},{10,14},{11,7},{... | collective-permute-start | bytes 184328 | tf_op jit(solution)/shard_map/ppermute | solution.py:35
  64.7 4.8 %grad_far.1 = f32[15,30,256]{2,1,0:T(8,128)} custom-call(s32[3]{0:T(128)S(1)} %pad_add_fusion.sc, s32[9]{0:T(128)S(1)} %bitcast.65, s32[1]{0:T(128)} %bitcast.50.count, bf16[480,256]{1,0:T(8,128)(2,1)S(1)} %encode_frame0.1.q, f32[480,128]{1,0:T(8,128)S(1)} %get-tuple-element.38.packed, f32[480,256]{1,0:T(8,128)S(1)} %grad_near.1.begun, ...), custom_call_target="tpu_custom_call" | custom-call | flops 1000000 | bytes 10000 | tf_op jit(solution)/shard_map/grad_far/pallas_call | solution.py:450
  69.5 2.0 %collective-permute-start.18 = (bf16[2,2,480,256]{3,2,1,0:T(8,128)(2,1)}, bf16[2,2,480,256]{3,2,1,0:T(8,128)(2,1)S(1)}, u32[]{:S(2)}, u32[]{:S(2)}) collective-permute-start(bf16[2,2,480,256]{3,2,1,0:T(8,128)(2,1)} %collective-permute-done.16.refs_1_), channel_id=1, source_target_pairs={{0,1},{1,0},{2,3},{3,2},{4,5},{5,4},{6,7},{7,6},{8,9},{9,8},{10,11... | collective-permute-start | bytes 2949128 | tf_op jit(solution)/shard_map/ppermute | solution.py:35
  72.3 1.4 %collective-permute-done.19.refs_5_ = f32[2,2,8,480]{3,2,1,0:T(8,128)S(1)} collective-permute-done((f32[2,2,8,480]{3,2,1,0:T(8,128)S(1)}, f32[2,2,8,480]{3,2,1,0:T(8,128)S(1)}, u32[]{:S(2)}, u32[]{:S(2)}) %collective-permute-start.19) | collective-permute-done | bytes 61472 | tf_op jit(solution)/shard_map/ppermute | solution.py:35
  74.0 8.2 %target_side.1 = f32[15,30,256]{2,1,0:T(8,128)} custom-call(s32[3]{0:T(128)S(1)} %pad_add_fusion.sc, bf16[480,256]{1,0:T(8,128)(2,1)S(1)} %encode_frame1.1.tgt, bf16[2,2,480,256]{3,2,1,0:T(8,128)(2,1)S(1)} %pad_maximum_fusion.refs_0_, bf16[2,2,480,256]{3,2,1,0:T(8,128)(2,1)} %collective-permute-done.16.refs_1_, ...), custom_call_target="tpu_custom_call" | custom-call | flops 1000000 | bytes 10000 | tf_op jit(solution)/shard_map/target_side/pallas_call | solution.py:518
  (57 shorter events, 13.1 us)
Async XLA Ops:
  0.6 2.1 %collective-permute-start = (bf16[30,30,256]{2,1,0:T(8,128)(2,1)}, bf16[30,30,256]{2,1,0:T(8,128)(2,1)S(1)}, u32[]{:S(2)}, u32[]{:S(2)}) collective-permute-start(bf16[30,30,256]{2,1,0:T(8,128)(2,1)} %bitcast.56), channel_id=1, source_target_pairs={{0,1},{1,0},{2,3},{3,2},{4,5},{5,4},{6,7},{7,6},{8,9},{9,8},{10,11... | collective-permute-start | bytes 1382408 | tf_op jit(solution)/shard_map/ppermute | solution.py:35
  2.9 4.6 %collective-permute-start.1 = (bf16[2,30,2,256]{3,2,1,0:T(2,128)(2,1)S(1)}, bf16[2,30,2,256]{3,2,1,0:T(2,128)(2,1)S(1)}, u32[]{:S(2)}, u32[]{:S(2)}) collective-permute-start(bf16[2,30,2,256]{3,2,1,0:T(2,128)(2,1)S(1)} %pad_maximum_fusion.5), channel_id=1, source_target_pairs={{0,2},{1,3},{2,0},{3,1},{4,6},{5,7},{6,4},{7,5},{8,10},{9,11},{10,... | collective-permute-start | bytes 184328 | tf_op jit(solution)/shard_map/ppermute | solution.py:35
  4.5 1.3 %copy-start.1 = (bf16[9,256,256]{2,1,0:T(8,128)(2,1)S(1)}, bf16[9,256,256]{2,1,0:T(8,128)(2,1)}, u32[]{:S(2)}) copy-start(bf16[9,256,256]{2,1,0:T(8,128)(2,1)} %a) | copy-start | bytes 3538948
  7.0 6.4 %copy-start = (bf16[1,30,30,256]{3,2,1,0:T(8,128)(2,1)S(1)}, bf16[1,30,30,256]{3,2,1,0:T(8,128)(2,1)}, u32[]{:S(2)}) copy-start(bf16[1,30,30,256]{3,2,1,0:T(8,128)(2,1)} %param.6) | copy-start | bytes 1382404
  7.6 5.8 %collective-permute-start.2 = (bf16[2,2,34,256]{3,2,1,0:T(8,128)(2,1)S(1)}, bf16[2,2,34,256]{3,2,1,0:T(8,128)(2,1)S(1)}, u32[]{:S(2)}, u32[]{:S(2)}) collective-permute-start(bf16[2,2,34,256]{3,2,1,0:T(8,128)(2,1)S(1)} %pad_maximum_fusion.3), channel_id=1, source_target_pairs={{1,4},{3,6},{4,1},{5,8},{6,3},{7,10},{8,5},{9,12},{10,7},{11,14},{... | collective-permute-start | bytes 208904 | tf_op jit(solution)/shard_map/ppermute | solution.py:35
  16.5 1.6 %collective-permute-start.3 = (bf16[480,256]{1,0:T(8,128)(2,1)S(1)}, bf16[480,256]{1,0:T(8,128)(2,1)S(1)}, u32[]{:S(2)}, u32[]{:S(2)}) collective-permute-start(bf16[480,256]{1,0:T(8,128)(2,1)S(1)} %encode_frame1.1.tgt), channel_id=1, source_target_pairs={{0,1},{1,0},{2,3},{3,2},{4,5},{5,4},{6,7},{7,6},{8,9},{9,8},{10,11... | collective-permute-start | bytes 737288 | tf_op jit(solution)/shard_map/ppermute | solution.py:35
  18.2 16.5 %copy-start.3 = (s32[1,1,9]{2,1,0:T(1,128)S(1)}, s32[1,1,9]{2,1,0:T(1,128)}, u32[]{:S(2)}) copy-start(s32[1,1,9]{2,1,0:T(1,128)} %param.9) | copy-start | bytes 112
  18.2 10.7 %collective-permute-start.5 = (bf16[2,480,256]{2,1,0:T(8,128)(2,1)S(1)}, bf16[2,480,256]{2,1,0:T(8,128)(2,1)S(1)}, u32[]{:S(2)}, u32[]{:S(2)}) collective-permute-start(bf16[2,480,256]{2,1,0:T(8,128)(2,1)S(1)} %pad_maximum_fusion.1.refs_0_), channel_id=1, source_target_pairs={{0,4},{2,6},{4,8},{5,1},{6,10},{7,3},{8,12},{9,5},{10,14},{11,7},{... | collective-permute-start | bytes 1474568 | tf_op jit(solution)/shard_map/ppermute | solution.py:35
  21.7 6.5 %collective-permute-start.4 = (bf16[480,256]{1,0:T(8,128)(2,1)S(1)}, bf16[480,256]{1,0:T(8,128)(2,1)S(1)}, u32[]{:S(2)}, u32[]{:S(2)}) collective-permute-start(bf16[480,256]{1,0:T(8,128)(2,1)S(1)} %encode_frame1.1.tgt), channel_id=1, source_target_pairs={{0,2},{1,3},{2,0},{3,1},{4,6},{5,7},{6,4},{7,5},{8,10},{9,11},{10,... | collective-permute-start | bytes 737288 | tf_op jit(solution)/shard_map/ppermute | solution.py:35
  28.9 1.5 %collective-permute-start.6 = (bf16[480,256]{1,0:T(8,128)(2,1)S(1)}, bf16[480,256]{1,0:T(8,128)(2,1)S(1)}, u32[]{:S(2)}, u32[]{:S(2)}) collective-permute-start(bf16[480,256]{1,0:T(8,128)(2,1)S(1)} %collective-permute-done.4), channel_id=1, source_target_pairs={{0,1},{1,0},{2,3},{3,2},{4,5},{5,4},{6,7},{7,6},{8,9},{9,8},{10,11... | collective-permute-start | bytes 737288 | tf_op jit(solution)/shard_map/ppermute | solution.py:35
  30.5 12.4 %copy-start.4 = (f32[2,15,30]{2,0,1:T(2,128)S(1)}, f32[2,15,30]{2,0,1:T(2,128)}, u32[]{:S(2)}) copy-start(f32[2,15,30]{2,0,1:T(2,128)} %param.11) | copy-start | bytes 10804
  30.5 10.7 %collective-permute-start.7 = (bf16[2,480,256]{2,1,0:T(8,128)(2,1)S(1)}, bf16[2,480,256]{2,1,0:T(8,128)(2,1)S(1)}, u32[]{:S(2)}, u32[]{:S(2)}) collective-permute-start(bf16[2,480,256]{2,1,0:T(8,128)(2,1)S(1)} %pad_maximum_fusion.2.refs_1_), channel_id=1, source_target_pairs={{0,4},{2,6},{4,8},{5,1},{6,10},{7,3},{8,12},{9,5},{10,14},{11,7},{... | collective-permute-start | bytes 1474568 | tf_op jit(solution)/shard_map/ppermute | solution.py:35
  41.2 2.0 %collective-permute-start.8 = (bf16[2,480,256]{2,1,0:T(8,128)(2,1)S(1)}, bf16[2,480,256]{2,1,0:T(8,128)(2,1)}, u32[]{:S(2)}, u32[]{:S(2)}) collective-permute-start(bf16[2,480,256]{2,1,0:T(8,128)(2,1)S(1)} %collective-permute-done.5.refs_0_), channel_id=1, source_target_pairs={{0,1},{1,0},{2,3},{3,2},{4,5},{5,4},{6,7},{7,6},{8,9},{9,8},{10,11... | collective-permute-start | bytes 1474568 | tf_op jit(solution)/shard_map/ppermute | solution.py:35
  41.2 2.7 %collective-permute-start.9 = (bf16[2,480,256]{2,1,0:T(8,128)(2,1)S(1)}, bf16[2,480,256]{2,1,0:T(8,128)(2,1)}, u32[]{:S(2)}, u32[]{:S(2)}) collective-permute-start(bf16[2,480,256]{2,1,0:T(8,128)(2,1)S(1)} %collective-permute-done.7.refs_1_), channel_id=1, source_target_pairs={{0,1},{1,0},{2,3},{3,2},{4,5},{5,4},{6,7},{7,6},{8,9},{9,8},{10,11... | collective-permute-start | bytes 1474568 | tf_op jit(solution)/shard_map/ppermute | solution.py:35
  41.7 8.0 %collective-permute-start.13 = (bf16[480,256]{1,0:T(8,128)(2,1)S(1)}, bf16[480,256]{1,0:T(8,128)(2,1)}, u32[]{:S(2)}, u32[]{:S(2)}) collective-permute-start(bf16[480,256]{1,0:T(8,128)(2,1)S(1)} %encode_frame0.1.q), channel_id=1, source_target_pairs={{0,2},{1,3},{2,0},{3,1},{4,6},{5,7},{6,4},{7,5},{8,10},{9,11},{10,... | collective-permute-start | bytes 737288 | tf_op jit(solution)/shard_map/ppermute | solution.py:35
  42.9 6.8 %collective-permute-start.12 = (bf16[480,256]{1,0:T(8,128)(2,1)S(1)}, bf16[480,256]{1,0:T(8,128)(2,1)}, u32[]{:S(2)}, u32[]{:S(2)}) collective-permute-start(bf16[480,256]{1,0:T(8,128)(2,1)S(1)} %encode_frame0.1.q), channel_id=1, source_target_pairs={{0,1},{1,0},{2,3},{3,2},{4,5},{5,4},{6,7},{7,6},{8,9},{9,8},{10,11... | collective-permute-start | bytes 737288 | tf_op jit(solution)/shard_map/ppermute | solution.py:35
  49.7 1.7 %collective-permute-start.14 = (bf16[480,256]{1,0:T(8,128)(2,1)}, bf16[480,256]{1,0:T(8,128)(2,1)S(1)}, u32[]{:S(2)}, u32[]{:S(2)}) collective-permute-start(bf16[480,256]{1,0:T(8,128)(2,1)} %collective-permute-done.13), channel_id=1, source_target_pairs={{0,1},{1,0},{2,3},{3,2},{4,5},{5,4},{6,7},{7,6},{8,9},{9,8},{10,11... | collective-permute-start | bytes 737288 | tf_op jit(solution)/shard_map/ppermute | solution.py:35
  52.5 17.0 %collective-permute-start.16 = (bf16[2,2,480,256]{3,2,1,0:T(8,128)(2,1)S(1)}, bf16[2,2,480,256]{3,2,1,0:T(8,128)(2,1)}, u32[]{:S(2)}, u32[]{:S(2)}) collective-permute-start(bf16[2,2,480,256]{3,2,1,0:T(8,128)(2,1)S(1)} %pad_maximum_fusion.refs_0_), channel_id=1, source_target_pairs={{0,4},{2,6},{4,8},{5,1},{6,10},{7,3},{8,12},{9,5},{10,14},{11,7},{... | collective-permute-start | bytes 2949128 | tf_op jit(solution)/shard_map/ppermute | solution.py:35
  56.0 5.3 %collective-permute-start.11 = (f32[8,480]{1,0:T(8,128)S(1)}, f32[8,480]{1,0:T(8,128)S(1)}, u32[]{:S(2)}, u32[]{:S(2)}) collective-permute-start(f32[8,480]{1,0:T(8,128)S(1)} %get-tuple-element.33), channel_id=1, source_target_pairs={{0,2},{1,3},{2,0},{3,1},{4,6},{5,7},{6,4},{7,5},{8,10},{9,11},{10,... | collective-permute-start | bytes 46088 | tf_op jit(solution)/shard_map/ppermute | solution.py:35
  57.7 4.1 %collective-permute-start.10 = (f32[8,480]{1,0:T(8,128)S(1)}, f32[8,480]{1,0:T(8,128)S(1)}, u32[]{:S(2)}, u32[]{:S(2)}) collective-permute-start(f32[8,480]{1,0:T(8,128)S(1)} %get-tuple-element.33), channel_id=1, source_target_pairs={{0,1},{1,0},{2,3},{3,2},{4,5},{5,4},{6,7},{7,6},{8,9},{9,8},{10,11... | collective-permute-start | bytes 46088 | tf_op jit(solution)/shard_map/ppermute | solution.py:35
  61.3 1.4 %collective-permute-start.15 = (f32[8,480]{1,0:T(8,128)S(1)}, f32[8,480]{1,0:T(8,128)S(1)}, u32[]{:S(2)}, u32[]{:S(2)}) collective-permute-start(f32[8,480]{1,0:T(8,128)S(1)} %collective-permute-done.11), channel_id=1, source_target_pairs={{0,1},{1,0},{2,3},{3,2},{4,5},{5,4},{6,7},{7,6},{8,9},{9,8},{10,11... | collective-permute-start | bytes 46088 | tf_op jit(solution)/shard_map/ppermute | solution.py:35
  62.7 6.7 %collective-permute-start.17 = (f32[2,2,8,480]{3,2,1,0:T(8,128)S(1)}, f32[2,2,8,480]{3,2,1,0:T(8,128)S(1)}, u32[]{:S(2)}, u32[]{:S(2)}) collective-permute-start(f32[2,2,8,480]{3,2,1,0:T(8,128)S(1)} %pad_maximum_fusion.4.refs_3_), channel_id=1, source_target_pairs={{0,4},{2,6},{4,8},{5,1},{6,10},{7,3},{8,12},{9,5},{10,14},{11,7},{... | collective-permute-start | bytes 184328 | tf_op jit(solution)/shard_map/ppermute | solution.py:35
  69.5 4.5 %collective-permute-start.18 = (bf16[2,2,480,256]{3,2,1,0:T(8,128)(2,1)}, bf16[2,2,480,256]{3,2,1,0:T(8,128)(2,1)S(1)}, u32[]{:S(2)}, u32[]{:S(2)}) collective-permute-start(bf16[2,2,480,256]{3,2,1,0:T(8,128)(2,1)} %collective-permute-done.16.refs_1_), channel_id=1, source_target_pairs={{0,1},{1,0},{2,3},{3,2},{4,5},{5,4},{6,7},{7,6},{8,9},{9,8},{10,11... | collective-permute-start | bytes 2949128 | tf_op jit(solution)/shard_map/ppermute | solution.py:35
  71.5 2.2 %collective-permute-start.19 = (f32[2,2,8,480]{3,2,1,0:T(8,128)S(1)}, f32[2,2,8,480]{3,2,1,0:T(8,128)S(1)}, u32[]{:S(2)}, u32[]{:S(2)}) collective-permute-start(f32[2,2,8,480]{3,2,1,0:T(8,128)S(1)} %collective-permute-done.17.refs_4_), channel_id=1, source_target_pairs={{0,1},{1,0},{2,3},{3,2},{4,5},{5,4},{6,7},{7,6},{8,9},{9,8},{10,11... | collective-permute-start | bytes 184328 | tf_op jit(solution)/shard_map/ppermute | solution.py:35
  (1 other events, 1.3 us)

commit v4 on v3

--- a/solution.py
+++ b/solution.py
@@ -21,6 +21,7 @@
 RB = 16
 COST = pl.CostEstimate(flops=10**6, bytes_accessed=10**4, transcendentals=0)
 ANY = pl.BlockSpec(memory_space=pl.ANY)
+HBM = pl.BlockSpec(memory_space=pltpu.HBM)
 
 
 def send(value, step):
@@ -143,23 +144,22 @@
     )(sc, mine, got, xl, xr, z, w1, w2)
 
 
+def load(tiles, buf, sems, at):
+    pltpu.make_async_copy(tiles, buf.at[at], sems.at[at]).start()
+
+
 def load_rows(level, got, other, buf, sems, core):
-    first = 2 * core
-    pltpu.make_async_copy(level, buf.at[1], sems.at[1]).start()
-    pltpu.make_async_copy(got, buf.at[first], sems.at[first]).start()
-    pltpu.make_async_copy(other, buf.at[2 - first], sems.at[2 - first]).start()
-
-
-def load_far(got, other, buf, sems, core):
-    n_cs = len(got)
-    for j in range(n_cs):
-        first, last = jnp.where(core == 0, j, n_cs + j), jnp.where(core == 0, n_cs + j, j)
-        pltpu.make_async_copy(got[j], buf.at[first], sems.at[first]).start()
-        pltpu.make_async_copy(other[j], buf.at[last], sems.at[last]).start()
-
-
-def wait_for(tile, buf, sems, slot):
-    pltpu.make_async_copy(tile, buf.at[slot], sems.at[slot]).wait()
+    load(level, buf, sems, 1)
+    load(got, buf, sems, 2 * core)
+    load(other, buf, sems, 2 - 2 * core)
+
+
+def wait_for(tiles, buf, sems, at):
+    pltpu.make_async_copy(tiles, buf.at[at], sems.at[at]).wait()
+
+
+def half_tile(buf, a, j, i):
+    return buf[a, pl.ds(pl.multiple_of((2 * j + i) * HC, HC), HC)]
 
 
 def slot_steps(slot, n_cs, n_c, col):
@@ -190,10 +190,10 @@
     return lane, lane % PADW < TILE, lane < HC - 384
 
 
-def add_tile(c2, slot, dr, dc, core, q, buf, s_scr, state):
+def add_tile(c2, a, j, dr, dc, core, q, buf, s_scr, state):
     for i in range(2):
         s_scr[:, i * 512 : i * 512 + HC] = lax.dot_general(
-            q[...], buf[slot, i], (((1,), (1,)), ((), ())), preferred_element_type=jnp.float32
+            q[...], half_tile(buf, a, j, i), (((1,), (1,)), ((), ())), preferred_element_type=jnp.float32
         )
     base = [(30 * dr + 15 * half_of(dr, i, core)).astype(jnp.float32) for i in range(2)]
     col_base = (30 * dc).astype(jnp.float32)
@@ -231,43 +231,47 @@
         state[3, rows] = state[3, rows] * factor + col_base * both
 
 
-def near_kernel(n_c, n_cs, c2, sc, cand, count, q, *refs):
-    level, (state, buf, sems, s_scr) = refs[:n_cs], refs[n_cs:]
+def near_kernel(n_c, n_cs, c2, sc, cand, count, q, level, state, buf, sems, s_scr):
     core, col = sc[0], sc[2]
-    for j in range(n_cs):
-        pltpu.make_async_copy(level[j], buf.at[j], sems.at[j]).start()
+    load(level, buf, sems, 0)
     state[0] = jnp.full(state.shape[1:], -jnp.inf, jnp.float32)
     for k in range(1, 4):
         state[k] = jnp.zeros(state.shape[1:], jnp.float32)
 
     def step(j, carry):
         dr, dc, _, hit = listed(n_cs + j, n_cs, n_c, col, cand, count)
-        wait_for(level[0], buf, sems, j)
+
+        @pl.when(j == 0)
+        def _():
+            wait_for(level, buf, sems, 0)
 
         @pl.when(hit == 1)
         def _():
-            add_tile(c2, j, dr, dc, core, q, buf, s_scr, state)
+            add_tile(c2, 0, j, dr, dc, core, q, buf, s_scr, state)
 
         return carry
 
     lax.fori_loop(0, n_cs, step, 0)
 
 
-def far_kernel(n_c, n_cs, c2, sc, cand, count, q, ctg, begun, *refs):
-    got, other = refs[:n_cs], refs[n_cs : 2 * n_cs]
-    flow, stats, packed_out, buf, sems, s_scr, state = refs[2 * n_cs :]
+def far_kernel(n_c, n_cs, c2, sc, cand, count, q, ctg, begun, got, other, *refs):
+    flow, stats, packed_out, buf, sems, s_scr, state = refs
     core, col = sc[0], sc[2]
-    load_far(got, other, buf, sems, core)
+    load(got, buf, sems, core)
+    load(other, buf, sems, 1 - core)
     state[...] = begun[...]
 
-    def step(j, carry):
-        slot = jnp.where(j < n_cs, j, n_cs + j)
-        dr, dc, _, hit = listed(slot, n_cs, n_c, col, cand, count)
-        wait_for(got[0], buf, sems, j)
+    def step(i, carry):
+        a, j = i // n_cs, i % n_cs
+        dr, dc, _, hit = listed(2 * a * n_cs + j, n_cs, n_c, col, cand, count)
+
+        @pl.when(j == 0)
+        def _():
+            wait_for(got, buf, sems, a)
 
         @pl.when(hit == 1)
         def _():
-            add_tile(c2, j, dr, dc, core, q, buf, s_scr, state)
+            add_tile(c2, a, j, dr, dc, core, q, buf, s_scr, state)
 
         return carry
 
@@ -318,13 +322,13 @@
         q4[k] = jnp.broadcast_to(packed[:, k : k + 1], (HC, 128))
 
 
-def grad_tile(c2, slot, dr, dc, core, q, buf, s_scr, d_scr, acc, q4):
+def grad_tile(c2, a, j, dr, dc, core, q, buf, s_scr, d_scr, acc, q4):
     lane, lane_ok, in_row = lanes(RB)
     lane_row = (lane // PADW).astype(jnp.float32)
     lane_col = (lane % PADW + 30 * dc).astype(jnp.float32)
     for i in range(2):
         s_scr[:, 0:HC] = lax.dot_general(
-            q[...], buf[slot, i], (((1,), (1,)), ((), ())), preferred_element_type=jnp.float32
+            q[...], half_tile(buf, a, j, i), (((1,), (1,)), ((), ())), preferred_element_type=jnp.float32
         )
         base = lane_row + (30 * dr + 15 * half_of(dr, i, core)).astype(jnp.float32)
         for g in range(HC // RB):
@@ -337,133 +341,83 @@
                 d_scr[rows, v * 128 : v * 128 + 128] = d.astype(jnp.bfloat16)
                 if v < 3:
                     pull = pull + 4.0 * gr
-        acc[...] += jnp.dot(d_scr[:, 0:HC], buf[slot, i], preferred_element_type=jnp.float32)
-
-
-def grad_near_kernel(n_c, n_cs, c2, sc, cand, count, q, packed, *refs):
-    level, (acc, buf, sems, s_scr, d_scr, q4) = refs[:n_cs], refs[n_cs:]
+        acc[...] += jnp.dot(d_scr[:, 0:HC], half_tile(buf, a, j, i), preferred_element_type=jnp.float32)
+
+
+def grad_kernel(n_c, n_cs, c2, sc, cand, count, q, packed, level, got, other, *refs):
+    out, buf, sems, s_scr, d_scr, q4, acc = refs
     core, col = sc[0], sc[2]
-    for j in range(n_cs):
-        pltpu.make_async_copy(level[j], buf.at[j], sems.at[j]).start()
+    load_rows(level, got, other, buf, sems, core)
     acc[...] = jnp.zeros(acc.shape, jnp.float32)
     spread(packed, q4)
 
-    def step(j, carry):
-        dr, dc, _, hit = listed(n_cs + j, n_cs, n_c, col, cand, count)
-        wait_for(level[0], buf, sems, j)
+    def step(slot, carry):
+        a, j = slot // n_cs, slot % n_cs
+        dr, dc, _, hit = listed(slot, n_cs, n_c, col, cand, count)
+
+        @pl.when(j == 0)
+        def _():
+            wait_for(level, buf, sems, a)
 
         @pl.when(hit == 1)
         def _():
-            grad_tile(c2, j, dr, dc, core, q, buf, s_scr, d_scr, acc, q4)
+            grad_tile(c2, a, j, dr, dc, core, q, buf, s_scr, d_scr, acc, q4)
 
         return carry
 
-    lax.fori_loop(0, n_cs, step, 0)
-
-
-def grad_far_kernel(n_c, n_cs, c2, sc, cand, count, q, packed, begun, *refs):
-    got, other = refs[:n_cs], refs[n_cs : 2 * n_cs]
-    out, buf, sems, s_scr, d_scr, q4, acc = refs[2 * n_cs :]
-    core, col = sc[0], sc[2]
-    load_far(got, other, buf, sems, core)
-    acc[...] = begun[...]
-    spread(packed, q4)
-
-    def step(j, carry):
-        slot = jnp.where(j < n_cs, j, n_cs + j)
-        dr, dc, _, hit = listed(slot, n_cs, n_c, col, cand, count)
-        wait_for(got[0], buf, sems, j)
-
-        @pl.when(hit == 1)
-        def _():
-            grad_tile(c2, j, dr, dc, core, q, buf, s_scr, d_scr, acc, q4)
-
-        return carry
-
-    lax.fori_loop(0, 2 * n_cs, step, 0)
+    lax.fori_loop(0, 3 * n_cs, step, 0)
     out[...] = acc[...].reshape(HALF, PADW, acc.shape[1])[:, :TILE]
 
 
-def query_near(n_c, sc, cand, count, q, level):
-    n_cs, ch = len(level), q.shape[1]
+def tiles_call(kernel, n_c, ch, rows, n_cs, out_shape, scratch, vmem_ins, ins, tiles):
     return pl.pallas_call(
-        functools.partial(near_kernel, n_c, n_cs, math.log2(math.e) / math.sqrt(ch)),
-        out_shape=jax.ShapeDtypeStruct((4, HC, 128), jnp.float32),
-        in_specs=[SMEM, SMEM, SMEM, VMEM] + [ANY] * n_cs,
-        out_specs=VMEM,
+        functools.partial(kernel, n_c, n_cs, math.log2(math.e) / math.sqrt(ch)),
+        out_shape=out_shape,
+        in_specs=[SMEM] * 3 + [VMEM] * vmem_ins + [HBM] * len(tiles),
+        out_specs=jax.tree.map(lambda _: VMEM, out_shape),
         scratch_shapes=[
-            pltpu.VMEM((n_cs, 2, HC, ch), jnp.bfloat16),
-            pltpu.SemaphoreType.DMA((n_cs,)),
-            pltpu.VMEM((HC, 1024), jnp.float32),
-        ],
+            pltpu.VMEM((rows, n_cs * 2 * HC, ch), jnp.bfloat16),
+            pltpu.SemaphoreType.DMA((rows,)),
+        ]
+        + scratch,
         compiler_params=pltpu.CompilerParams(vmem_limit_bytes=12 * 2**20),
         cost_estimate=COST,
-        name="query_near",
-    )(sc, cand, count, q, *level)
+        name=kernel.__name__,
+    )(*ins, *tiles)
+
+
+def query_near(n_c, sc, cand, count, q, level):
+    ch, n_cs = q.shape[1], level.shape[0] // (2 * HC)
+    out_shape = jax.ShapeDtypeStruct((4, HC, 128), jnp.float32)
+    scratch = [pltpu.VMEM((HC, 1024), jnp.float32)]
+    return tiles_call(
+        near_kernel, n_c, ch, 1, n_cs, out_shape, scratch, 1, (sc, cand, count, q), (level,)
+    )
 
 
 def query_far(n_c, sc, cand, count, q, ctg, begun, got, other):
-    n_cs, ch = len(got), q.shape[1]
-    return pl.pallas_call(
-        functools.partial(far_kernel, n_c, n_cs, math.log2(math.e) / math.sqrt(ch)),
-        out_shape=(
-            jax.ShapeDtypeStruct((2, HC), jnp.float32),
-            jax.ShapeDtypeStruct((8, HC), jnp.float32),
-            jax.ShapeDtypeStruct((HC, 128), jnp.float32),
-        ),
-        in_specs=[SMEM, SMEM, SMEM, VMEM, VMEM, VMEM] + [ANY] * (2 * n_cs),
-        out_specs=(VMEM, VMEM, VMEM),
-        scratch_shapes=[
-            pltpu.VMEM((2 * n_cs, 2, HC, ch), jnp.bfloat16),
-            pltpu.SemaphoreType.DMA((2 * n_cs,)),
-            pltpu.VMEM((HC, 1024), jnp.float32),
-            pltpu.VMEM((4, HC, 128), jnp.float32),
-        ],
-        compiler_params=pltpu.CompilerParams(vmem_limit_bytes=12 * 2**20),
-        cost_estimate=COST,
-        name="query_far",
-    )(sc, cand, count, q, ctg, begun, *got, *other)
-
-
-def grad_near(n_c, sc, cand, count, q, packed, level):
-    n_cs, ch = len(level), q.shape[1]
-    return pl.pallas_call(
-        functools.partial(grad_near_kernel, n_c, n_cs, math.log2(math.e) / math.sqrt(ch)),
-        out_shape=jax.ShapeDtypeStruct((HC, ch), jnp.float32),
-        in_specs=[SMEM, SMEM, SMEM, VMEM, VMEM] + [ANY] * n_cs,
-        out_specs=VMEM,
-        scratch_shapes=[
-            pltpu.VMEM((n_cs, 2, HC, ch), jnp.bfloat16),
-            pltpu.SemaphoreType.DMA((n_cs,)),
-            pltpu.VMEM((HC, 512), jnp.float32),
-            pltpu.VMEM((HC, 512), jnp.bfloat16),
-            pltpu.VMEM((4, HC, 128), jnp.float32),
-        ],
-        compiler_params=pltpu.CompilerParams(vmem_limit_bytes=12 * 2**20),
-        cost_estimate=COST,
-        name="grad_near",
-    )(sc, cand, count, q, packed, *level)
-
-
-def grad_far(n_c, sc, cand, count, q, packed, begun, got, other):
-    n_cs, ch = len(got), q.shape[1]
-    return pl.pallas_call(
-        functools.partial(grad_far_kernel, n_c, n_cs, math.log2(math.e) / math.sqrt(ch)),
-        out_shape=jax.ShapeDtypeStruct((HALF, TILE, ch), jnp.float32),
-        in_specs=[SMEM, SMEM, SMEM, VMEM, VMEM, VMEM] + [ANY] * (2 * n_cs),
-        out_specs=VMEM,
-        scratch_shapes=[
-            pltpu.VMEM((2 * n_cs, 2, HC, ch), jnp.bfloat16),
-            pltpu.SemaphoreType.DMA((2 * n_cs,)),
-            pltpu.VMEM((HC, 512), jnp.float32),
-            pltpu.VMEM((HC, 512), jnp.bfloat16),
-            pltpu.VMEM((4, HC, 128), jnp.float32),
-            pltpu.VMEM((HC, ch), jnp.float32),
-        ],
-        compiler_params=pltpu.CompilerParams(vmem_limit_bytes=12 * 2**20),
-        cost_estimate=COST,
-        name="grad_far",
-    )(sc, cand, count, q, packed, begun, *got, *other)
+    ch, n_cs = q.shape[1], got.shape[0] // (2 * HC)
+    out_shape = (
+        jax.ShapeDtypeStruct((2, HC), jnp.float32),
+        jax.ShapeDtypeStruct((8, HC), jnp.float32),
+        jax.ShapeDtypeStruct((HC, 128), jnp.float32),
+    )
+    scratch = [pltpu.VMEM((HC, 1024), jnp.float32), pltpu.VMEM((4, HC, 128), jnp.float32)]
+    ins = (sc, cand, count, q, ctg, begun)
+    return tiles_call(far_kernel, n_c, ch, 2, n_cs, out_shape, scratch, 3, ins, (got, other))
+
+
+def query_grad(n_c, sc, cand, count, q, packed, level, got, other):
+    ch, n_cs = q.shape[1], level.shape[0] // (2 * HC)
+    out_shape = jax.ShapeDtypeStruct((HALF, TILE, ch), jnp.float32)
+    scratch = [
+        pltpu.VMEM((HC, 512), jnp.float32),
+        pltpu.VMEM((HC, 512), jnp.bfloat16),
+        pltpu.VMEM((4, HC, 128), jnp.float32),
+        pltpu.VMEM((HC, ch), jnp.float32),
+    ]
+    ins, tiles = (sc, cand, count, q, packed), (level, got, other)
+    return tiles_call(grad_kernel, n_c, ch, 3, n_cs, out_shape, scratch, 2, ins, tiles)
 
 
 def target_kernel(n_c, n_cs, c2, sc, tgt, *refs):
@@ -486,7 +440,7 @@
         code = 8 - (3 * (dr + 1) + dc + 1)
         where_at = lax.broadcasted_iota(jnp.int32, (8, HC), 1)
         which = lax.broadcasted_iota(jnp.int32, (8, HC), 0)
-        flag = jnp.sum(jnp.where((where_at == code) & (which == 4), st[a, j, 0], 0.0))
+        flag = jnp.sum(jnp.where((where_at == code) & (which == 4), st[a, pl.ds(pl.multiple_of(16 * j, 16), 8)], 0.0))
 
         @pl.when(flag > 0.5)
         def _():
@@ -495,9 +449,10 @@
             ).astype(jnp.float32)
             for i in range(2):
                 s_scr[...] = lax.dot_general(
-                    tgt[...], buf[a, j, i], (((1,), (1,)), ((), ())), preferred_element_type=jnp.float32
+                    tgt[...], half_tile(buf, a, j, i), (((1,), (1,)), ((), ())), preferred_element_type=jnp.float32
                 )
-                lev, gr, gc, sh = (st[a, j, i, k : k + 1, :] for k in range(4))
+                four = st[a, pl.ds(pl.multiple_of((2 * j + i) * 8, 8), 8)]
+                lev, gr, gc, sh = (four[k : k + 1] for k in range(4))
                 v_scr[...] = gc * col_t - sh
                 for g in range(HALF):
                     rows = slice(g * PADW, (g + 1) * PADW)
@@ -505,7 +460,7 @@
                     p = jnp.exp2(s_scr[rows] * c2 - lev)
                     d = p * (v_scr[...] + gr * row_t)
                     d_scr[rows] = d.astype(jnp.bfloat16)
-                acc[...] += jnp.dot(d_scr[...], buf[a, j, i], preferred_element_type=jnp.float32)
+                acc[...] += jnp.dot(d_scr[...], half_tile(buf, a, j, i), preferred_element_type=jnp.float32)
 
         return carry
 
@@ -514,16 +469,16 @@
 
 
 def target_side(n_c, sc, tgt, feats, stats):
-    n_cs, ch = feats[0].shape[0], tgt.shape[1]
+    n_cs, ch = feats[0].shape[0] // (2 * HC), tgt.shape[1]
     return pl.pallas_call(
         functools.partial(target_kernel, n_c, n_cs, math.log2(math.e) / math.sqrt(ch)),
         out_shape=jax.ShapeDtypeStruct((HALF, TILE, ch), jnp.float32),
-        in_specs=[SMEM, VMEM] + [ANY] * 6,
+        in_specs=[SMEM, VMEM] + [HBM] * 6,
         out_specs=VMEM,
         scratch_shapes=[
-            pltpu.VMEM((3, n_cs, 2, HC, ch), jnp.bfloat16),
+            pltpu.VMEM((3, n_cs * 2 * HC, ch), jnp.bfloat16),
             pltpu.SemaphoreType.DMA((3,)),
-            pltpu.VMEM((3, n_cs, 2, 8, HC), jnp.float32),
+            pltpu.VMEM((3, n_cs * 2 * 8, HC), jnp.float32),
             pltpu.SemaphoreType.DMA((3,)),
             pltpu.VMEM((HC, HC), jnp.float32),
             pltpu.VMEM((HC, HC), jnp.bfloat16),
@@ -564,28 +519,30 @@
     z = send(jnp.stack(lines), lambda r, k, c: (r - 1 + 2 * c, k, 1 - c))
     second = encode(1, n_r, n_c, sc, mine, other_frame, xl, xr, z, w1, w2)
     side = sideways(second)
-    own_tile = jnp.stack([second, partner(second)])
-    own_got = updown(own_tile)
-    first = encode(0, n_r, n_c, sc, after(mine, own_tile), other_frame, xl, xr, z, w1, w2)
-    q_side = sideways(first)
-    side = after(tuple(side), (first, own_got))
-    level = [own_tile] + [jnp.stack([x, partner(x)]) for x in side]
-    got = [own_got] + [updown(t) for t in level[1:]]
+    parts = [second, partner(second)]
+    first = encode(0, n_r, n_c, sc, mine, other_frame, xl, xr, z, w1, w2)
+    side = after(tuple(side), first)
+    for x in side:
+        parts += [x, partner(x)]
+    level = jnp.concatenate(parts)
+    got = updown(level)
+    q_side = sideways(after(first, side))
+    q_parts = [first, partner(after(first, side))]
     begun = query_near(n_c, sc, cand, count, first, level)
-    got = list(after(tuple(got), begun))
-    other = [partner(t) for t in got]
+    for x in after(tuple(q_side), begun):
+        q_parts += [x, partner(x)]
+    q_level = jnp.concatenate(q_parts)
+    q_got = updown(q_level)
+    got = after(got, q_level)
+    other = partner(got)
     flow, stats, packed = query_far(n_c, sc, cand, count, first, ctg, begun, got, other)
-    q_own = jnp.stack([first, partner(after(first, begun))])
-    q_side = after(tuple(q_side), packed)
-    q_level = jnp.stack([q_own] + [jnp.stack([x, partner(x)]) for x in q_side])
-    q_got = updown(q_level)
     st_side = sideways(stats)
-    st_own = jnp.stack([stats, partner(stats)])
-    part = grad_near(n_c, sc, cand, count, first, after(packed, (st_own, q_level)), level)
-    st_side = after(tuple(st_side), part)
-    st_level = jnp.stack([st_own] + [jnp.stack([x, partner(x)]) for x in st_side])
+    st_parts = [stats, partner(stats)]
+    for x in st_side:
+        st_parts += [x, partner(x)]
+    st_level = jnp.concatenate(st_parts)
     st_got = updown(st_level)
-    grad_first = grad_far(n_c, sc, cand, count, first, after(packed, st_level), part, got, other)
+    grad_first = query_grad(n_c, sc, cand, count, first, after(packed, st_level), level, got, other)
     q_got, st_got = after((q_got, st_got), grad_first)
     q_other, st_other = partner(q_got), partner(st_got)
     grad_second = target_side(

time: 83.7 us -> 79.4 us (0.949)
  starting transfers between devices: 23.4 us -> 17.7 us
  waiting for transfers between devices: 18.6 us -> 21.3 us
  other arithmetic: 4.27 us -> 3.18 us
    ppermute x20 -> x18, starting transfers between devices: 23.4 us -> 17.7 us  [send(): return lax.ppermute(value, AXES, pairs)]
    ppermute x20 -> x18, waiting for transfers between devices: 18.6 us -> 21.3 us  [send(): return lax.ppermute(value, AXES, pairs)]
    another operation x8 -> x0, other arithmetic: 2.19 us -> none  [the longest x3 2.08 us: shards(): q_level = jnp.stack([q_own] + [jnp.stack([x, partner(x)]) for x in q_side])]
    concatenate x0 -> x2, other arithmetic: none -> 1.1 us  [the longest x1 1.03 us: shards(): q_level = jnp.concatenate(q_parts)]
    pallas_call x4 -> x3, Pallas kernels: 16 us -> 16.8 us  [tiles_call(): pl.pallas_call(functools.partial(kernel, n_c, n_cs, math.log2(math.e) / m...]
    unnamed x12 -> x15, local copies, waits for them, and re-layouts: 3.17 us -> 3.17 us
  transfers between devices with their start and end apart: 20 -> 18, of which waited for: 14 -> 11; matrix products, arithmetic and copies ran while one was open for 4% -> 5% of each run, Pallas kernels for 24% -> 26%
where the time goes in v4:
time: 79.4 us; the launch traced here: 78 us
  Pallas kernels  30.9 us (39%)
  waiting for transfers between devices  21.3 us (27%)
  starting transfers between devices  17.7 us (22%)
  local copies, waits for them, and re-layouts  3.35 us (4%)
  other arithmetic  3.18 us (4%)
  between operations  1.55 us (2%)
    ppermute x18, waiting for transfers between devices, send(): return lax.ppermute(value, AXES, pairs)  21.3 us
    ppermute x18, starting transfers between devices, send(): return lax.ppermute(value, AXES, pairs)  17.7 us
    pallas_call x3, Pallas kernels, tiles_call(): pl.pallas_call(functools.partial(kernel, n_c, n_cs, math.log2(math.e) / m...  16.8 us
    pallas_call x1, Pallas kernels, target_side(): pl.pallas_call(functools.partial(target_kernel, n_c, n_cs, math.log2(math...  7.35 us
    pallas_call x2, Pallas kernels, encode(): pl.pallas_call(functools.partial(encode_kernel, frame, n_r, n_c), out_sha...  6.25 us
    unnamed x15, local copies, waits for them, and re-layouts  3.17 us
  transfers between devices with their start and end apart: 18, of which 11 were waited for; matrix products, arithmetic and copies ran while one was open for 5% of the time, Pallas kernels for 26%

profile of v4, /device:TPU:12, one launch (start us, length us, event | category | flops | bytes accessed | tf_op | source)
XLA Modules:
  0.0 78.0 jit_solution(7644016998031960263)
XLA Ops:
  2.9 1.6 %collective-permute-start.1 = (bf16[2,30,2,256]{3,2,1,0:T(2,128)(2,1)S(1)}, bf16[2,30,2,256]{3,2,1,0:T(2,128)(2,1)S(1)}, u32[]{:S(2)}, u32[]{:S(2)}) collective-permute-start(bf16[2,30,2,256]{3,2,1,0:T(2,128)(2,1)S(1)} %pad_maximum_fusion.3), channel_id=1, source_target_pairs={{0,2},{1,3},{2,0},{3,1},{4,6},{5,7},{6,4},{7,5},{8,10},{9,11},{10,... | collective-permute-start | bytes 184328 | tf_op jit(solution)/shard_map/ppermute | solution.py:36
  4.5 1.3 %copy-done.1 = bf16[9,256,256]{2,1,0:T(8,128)(2,1)S(1)} copy-done((bf16[9,256,256]{2,1,0:T(8,128)(2,1)S(1)}, bf16[9,256,256]{2,1,0:T(8,128)(2,1)}, u32[]{:S(2)}) %copy-start.1) | copy-done | bytes 1179672
  5.8 1.3 %copy-done.2 = bf16[9,256,256]{2,1,0:T(8,128)(2,1)S(1)} copy-done((bf16[9,256,256]{2,1,0:T(8,128)(2,1)S(1)}, bf16[9,256,256]{2,1,0:T(8,128)(2,1)}, u32[]{:S(2)}) %copy-start.2) | copy-done | bytes 1179672
  7.6 1.9 %collective-permute-start.2 = (bf16[2,2,34,256]{3,2,1,0:T(8,128)(2,1)S(1)}, bf16[2,2,34,256]{3,2,1,0:T(8,128)(2,1)S(1)}, u32[]{:S(2)}, u32[]{:S(2)}) collective-permute-start(bf16[2,2,34,256]{3,2,1,0:T(8,128)(2,1)S(1)} %pad_maximum_fusion.2), channel_id=1, source_target_pairs={{1,4},{3,6},{4,1},{5,8},{6,3},{7,10},{8,5},{9,12},{10,7},{11,14},{... | collective-permute-start | bytes 208904 | tf_op jit(solution)/shard_map/ppermute | solution.py:36
  9.7 3.7 %collective-permute-done.2.z = bf16[2,2,34,256]{3,2,1,0:T(8,128)(2,1)S(1)} collective-permute-done((bf16[2,2,34,256]{3,2,1,0:T(8,128)(2,1)S(1)}, bf16[2,2,34,256]{3,2,1,0:T(8,128)(2,1)S(1)}, u32[]{:S(2)}, u32[]{:S(2)}) %collective-permute-start.2) | collective-permute-done | bytes 69664 | tf_op jit(solution)/shard_map/ppermute | solution.py:36
  13.4 3.1 %encode_frame1.1.tgt = bf16[480,256]{1,0:T(8,128)(2,1)S(1)} custom-call(s32[3]{0:T(128)S(1)} %pad_add_fusion.sc, bf16[30,30,256]{2,1,0:T(8,128)(2,1)S(1)} %bitcast.36, bf16[30,30,256]{2,1,0:T(8,128)(2,1)S(1)} %collective-permute-done.got, bf16[2,30,2,256]{3,2,1,0:T(2,128)(2,1)S(1)} %collective-permute-done.1.xl.xr, ...), custom_call_target="tpu_custom_call" | custom-call | flops 1000000 | bytes 10000 | tf_op jit(solution)/shard_map/encode_frame1/pallas_call | solution.py:130
  16.5 1.2 %collective-permute-start.4 = (bf16[480,256]{1,0:T(8,128)(2,1)S(1)}, bf16[480,256]{1,0:T(8,128)(2,1)S(1)}, u32[]{:S(2)}, u32[]{:S(2)}) collective-permute-start(bf16[480,256]{1,0:T(8,128)(2,1)S(1)} %encode_frame1.1.tgt), channel_id=1, source_target_pairs={{0,2},{1,3},{2,0},{3,1},{4,6},{5,7},{6,4},{7,5},{8,10},{9,11},{10,... | collective-permute-start | bytes 737288 | tf_op jit(solution)/shard_map/ppermute | solution.py:36
  17.7 3.1 %encode_frame0.1.q = bf16[480,256]{1,0:T(8,128)(2,1)S(1)} custom-call(s32[3]{0:T(128)S(1)} %pad_add_fusion.sc, bf16[30,30,256]{2,1,0:T(8,128)(2,1)S(1)} %bitcast.37, bf16[30,30,256]{2,1,0:T(8,128)(2,1)S(1)} %collective-permute-done.got, bf16[2,30,2,256]{3,2,1,0:T(2,128)(2,1)S(1)} %collective-permute-done.1.xl.xr, ...), custom_call_target="tpu_custom_call" | custom-call | flops 1000000 | bytes 10000 | tf_op jit(solution)/shard_map/encode_frame0/pallas_call | solution.py:130
  20.9 3.7 %collective-permute-done.4 = bf16[480,256]{1,0:T(8,128)(2,1)S(1)} collective-permute-done((bf16[480,256]{1,0:T(8,128)(2,1)S(1)}, bf16[480,256]{1,0:T(8,128)(2,1)S(1)}, u32[]{:S(2)}, u32[]{:S(2)}) %collective-permute-start.4) | collective-permute-done | bytes 245792 | tf_op jit(solution)/shard_map/ppermute | solution.py:36
  24.6 1.5 %collective-permute-done.5 = bf16[480,256]{1,0:T(8,128)(2,1)S(1)} collective-permute-done((bf16[480,256]{1,0:T(8,128)(2,1)S(1)}, bf16[480,256]{1,0:T(8,128)(2,1)S(1)}, u32[]{:S(2)}, u32[]{:S(2)}) %collective-permute-start.5) | collective-permute-done | bytes 245792 | tf_op jit(solution)/shard_map/ppermute | solution.py:36
  26.1 3.5 %collective-permute-start.6 = (bf16[1920,256]{1,0:T(8,128)(2,1)S(1)}, bf16[1920,256]{1,0:T(8,128)(2,1)S(1)}, u32[]{:S(2)}, u32[]{:S(2)}) collective-permute-start(bf16[1920,256]{1,0:T(8,128)(2,1)S(1)} %pad_maximum_fusion.level), channel_id=1, source_target_pairs={{0,4},{2,6},{4,8},{5,1},{6,10},{7,3},{8,12},{9,5},{10,14},{11,7},{... | collective-permute-start | bytes 2949128 | tf_op jit(solution)/shard_map/ppermute | solution.py:36
  29.6 1.2 %collective-permute-start.8 = (bf16[480,256]{1,0:T(8,128)(2,1)S(1)}, bf16[480,256]{1,0:T(8,128)(2,1)S(1)}, u32[]{:S(2)}, u32[]{:S(2)}) collective-permute-start(bf16[480,256]{1,0:T(8,128)(2,1)S(1)} %encode_frame0.1.q), channel_id=1, source_target_pairs={{0,2},{1,3},{2,0},{3,1},{4,6},{5,7},{6,4},{7,5},{8,10},{9,11},{10,... | collective-permute-start | bytes 737288 | tf_op jit(solution)/shard_map/ppermute | solution.py:36
  31.6 2.8 %near_kernel.1.begun = f32[4,480,128]{2,1,0:T(8,128)S(1)} custom-call(s32[3]{0:T(128)S(1)} %pad_add_fusion.sc, s32[9]{0:T(128)S(1)} %bitcast.38, s32[1]{0:T(128)} %bitcast.27.count, bf16[480,256]{1,0:T(8,128)(2,1)S(1)} %encode_frame0.1.q, bf16[1920,256]{1,0:T(8,128)(2,1)S(1)} %pad_maximum_fusion.level), custom_call_target="tpu_custom_call" | custom-call | flops 1000000 | bytes 10000 | tf_op jit(solution)/shard_map/near_kernel/pallas_call | solution.py:373
  34.4 1.7 %collective-permute-done.8 = bf16[480,256]{1,0:T(8,128)(2,1)S(1)} collective-permute-done((bf16[480,256]{1,0:T(8,128)(2,1)S(1)}, bf16[480,256]{1,0:T(8,128)(2,1)S(1)}, u32[]{:S(2)}, u32[]{:S(2)}) %collective-permute-start.8) | collective-permute-done | bytes 245792 | tf_op jit(solution)/shard_map/ppermute | solution.py:36
  36.1 1.5 %collective-permute-done.9 = bf16[480,256]{1,0:T(8,128)(2,1)S(1)} collective-permute-done((bf16[480,256]{1,0:T(8,128)(2,1)S(1)}, bf16[480,256]{1,0:T(8,128)(2,1)S(1)}, u32[]{:S(2)}, u32[]{:S(2)}) %collective-permute-start.9) | collective-permute-done | bytes 245792 | tf_op jit(solution)/shard_map/ppermute | solution.py:36
  38.7 3.5 %collective-permute-done.6.got = bf16[1920,256]{1,0:T(8,128)(2,1)S(1)} collective-permute-done((bf16[1920,256]{1,0:T(8,128)(2,1)S(1)}, bf16[1920,256]{1,0:T(8,128)(2,1)S(1)}, u32[]{:S(2)}, u32[]{:S(2)}) %collective-permute-start.6) | collective-permute-done | bytes 983072 | tf_op jit(solution)/shard_map/ppermute | solution.py:36
  42.1 3.5 %collective-permute-start.14 = (bf16[1920,256]{1,0:T(8,128)(2,1)}, bf16[1920,256]{1,0:T(8,128)(2,1)}, u32[]{:S(2)}, u32[]{:S(2)}) collective-permute-start(bf16[1920,256]{1,0:T(8,128)(2,1)} %pad_maximum_fusion.1.refs_0_), channel_id=1, source_target_pairs={{0,4},{2,6},{4,8},{5,1},{6,10},{7,3},{8,12},{9,5},{10,14},{11,7},{... | collective-permute-start | bytes 2949128 | tf_op jit(solution)/shard_map/ppermute | solution.py:36
  45.8 5.5 %far_kernel.1 = (f32[2,480]{1,0:T(2,128)S(1)}, f32[8,480]{1,0:T(8,128)S(1)}, f32[480,128]{1,0:T(8,128)S(1)}) custom-call(s32[3]{0:T(128)S(1)} %pad_add_fusion.sc, s32[9]{0:T(128)S(1)} %bitcast.39, s32[1]{0:T(128)} %bitcast.28.count, bf16[480,256]{1,0:T(8,128)(2,1)S(1)} %encode_frame0.1.q, f32[8,480]{1,0:T(8,128)S(1)} %reshape.60.ctg, ...), custom_call_target="tpu_custom_call" | custom-call | flops 1000000 | bytes 10000 | tf_op jit(solution)/shard_map/far_kernel/pallas_call | solution.py:373
  52.8 2.6 %collective-permute-done.12 = f32[8,480]{1,0:T(8,128)S(1)} collective-permute-done((f32[8,480]{1,0:T(8,128)S(1)}, f32[8,480]{1,0:T(8,128)S(1)}, u32[]{:S(2)}, u32[]{:S(2)}) %collective-permute-start.12) | collective-permute-done | bytes 15392 | tf_op jit(solution)/shard_map/ppermute | solution.py:36
  55.5 1.2 %collective-permute-done.13 = f32[8,480]{1,0:T(8,128)S(1)} collective-permute-done((f32[8,480]{1,0:T(8,128)S(1)}, f32[8,480]{1,0:T(8,128)S(1)}, u32[]{:S(2)}, u32[]{:S(2)}) %collective-permute-start.13) | collective-permute-done | bytes 15392 | tf_op jit(solution)/shard_map/ppermute | solution.py:36
  56.6 2.6 %collective-permute-start.15 = (f32[32,480]{1,0:T(8,128)S(1)}, f32[32,480]{1,0:T(8,128)S(1)}, u32[]{:S(2)}, u32[]{:S(2)}) collective-permute-start(f32[32,480]{1,0:T(8,128)S(1)} %constant_dynamic-update-slice_fusion.refs_3_), channel_id=1, source_target_pairs={{0,4},{2,6},{4,8},{5,1},{6,10},{7,3},{8,12},{9,5},{10,14},{11,7},{... | collective-permute-start | bytes 184328 | tf_op jit(solution)/shard_map/ppermute | solution.py:36
  59.2 8.4 %grad_kernel.1 = f32[15,30,256]{2,1,0:T(8,128)} custom-call(s32[3]{0:T(128)S(1)} %pad_add_fusion.sc, s32[9]{0:T(128)S(1)} %bitcast.40, s32[1]{0:T(128)} %bitcast.29.count, bf16[480,256]{1,0:T(8,128)(2,1)S(1)} %encode_frame0.1.q, f32[480,128]{1,0:T(8,128)S(1)} %get-tuple-element.30.packed, bf16[1920,256]{1,0:T(8,128)(2,1)S(1)} %pad_maximum_fusion.level, ...), custom_call_target="tpu_custom_call" | custom-call | flops 1000000 | bytes 10000 | tf_op jit(solution)/shard_map/grad_kernel/pallas_call | solution.py:373
  69.0 1.5 %collective-permute-done.17.refs_5_ = f32[32,480]{1,0:T(8,128)S(1)} collective-permute-done((f32[32,480]{1,0:T(8,128)S(1)}, f32[32,480]{1,0:T(8,128)S(1)}, u32[]{:S(2)}, u32[]{:S(2)}) %collective-permute-start.17) | collective-permute-done | bytes 61472 | tf_op jit(solution)/shard_map/ppermute | solution.py:36
  70.7 7.3 %target_side.1 = f32[15,30,256]{2,1,0:T(8,128)} custom-call(s32[3]{0:T(128)S(1)} %pad_add_fusion.sc, bf16[480,256]{1,0:T(8,128)(2,1)S(1)} %encode_frame1.1.tgt, bf16[1920,256]{1,0:T(8,128)(2,1)} %pad_maximum_fusion.1.refs_0_, bf16[1920,256]{1,0:T(8,128)(2,1)} %collective-permute-done.14.refs_1_, bf16[1920,256]{1,0:T(8,128)(2,1)S(1)} %collective-permute-done.16.refs_2_, ...), custom_call_target="tpu_custom_call" | custom-call | flops 1000000 | bytes 10000 | tf_op jit(solution)/shard_map/target_side/pallas_call | solution.py:473
  (50 shorter events, 7.3 us)
Async XLA Ops:
  0.6 2.1 %collective-permute-start = (bf16[30,30,256]{2,1,0:T(8,128)(2,1)}, bf16[30,30,256]{2,1,0:T(8,128)(2,1)S(1)}, u32[]{:S(2)}, u32[]{:S(2)}) collective-permute-start(bf16[30,30,256]{2,1,0:T(8,128)(2,1)} %bitcast.34), channel_id=1, source_target_pairs={{0,1},{1,0},{2,3},{3,2},{4,5},{5,4},{6,7},{7,6},{8,9},{9,8},{10,11... | collective-permute-start | bytes 1382408 | tf_op jit(solution)/shard_map/ppermute | solution.py:36
  2.9 4.6 %collective-permute-start.1 = (bf16[2,30,2,256]{3,2,1,0:T(2,128)(2,1)S(1)}, bf16[2,30,2,256]{3,2,1,0:T(2,128)(2,1)S(1)}, u32[]{:S(2)}, u32[]{:S(2)}) collective-permute-start(bf16[2,30,2,256]{3,2,1,0:T(2,128)(2,1)S(1)} %pad_maximum_fusion.3), channel_id=1, source_target_pairs={{0,2},{1,3},{2,0},{3,1},{4,6},{5,7},{6,4},{7,5},{8,10},{9,11},{10,... | collective-permute-start | bytes 184328 | tf_op jit(solution)/shard_map/ppermute | solution.py:36
  4.5 1.3 %copy-start.1 = (bf16[9,256,256]{2,1,0:T(8,128)(2,1)S(1)}, bf16[9,256,256]{2,1,0:T(8,128)(2,1)}, u32[]{:S(2)}) copy-start(bf16[9,256,256]{2,1,0:T(8,128)(2,1)} %a) | copy-start | bytes 3538948
  5.8 1.3 %copy-start.2 = (bf16[9,256,256]{2,1,0:T(8,128)(2,1)S(1)}, bf16[9,256,256]{2,1,0:T(8,128)(2,1)}, u32[]{:S(2)}) copy-start(bf16[9,256,256]{2,1,0:T(8,128)(2,1)} %b.1) | copy-start | bytes 3538948
  7.0 6.4 %copy-start = (bf16[1,30,30,256]{3,2,1,0:T(8,128)(2,1)S(1)}, bf16[1,30,30,256]{3,2,1,0:T(8,128)(2,1)}, u32[]{:S(2)}) copy-start(bf16[1,30,30,256]{3,2,1,0:T(8,128)(2,1)} %param.6) | copy-start | bytes 1382404
  7.6 5.8 %collective-permute-start.2 = (bf16[2,2,34,256]{3,2,1,0:T(8,128)(2,1)S(1)}, bf16[2,2,34,256]{3,2,1,0:T(8,128)(2,1)S(1)}, u32[]{:S(2)}, u32[]{:S(2)}) collective-permute-start(bf16[2,2,34,256]{3,2,1,0:T(8,128)(2,1)S(1)} %pad_maximum_fusion.2), channel_id=1, source_target_pairs={{1,4},{3,6},{4,1},{5,8},{6,3},{7,10},{8,5},{9,12},{10,7},{11,14},{... | collective-permute-start | bytes 208904 | tf_op jit(solution)/shard_map/ppermute | solution.py:36
  16.5 8.0 %collective-permute-start.4 = (bf16[480,256]{1,0:T(8,128)(2,1)S(1)}, bf16[480,256]{1,0:T(8,128)(2,1)S(1)}, u32[]{:S(2)}, u32[]{:S(2)}) collective-permute-start(bf16[480,256]{1,0:T(8,128)(2,1)S(1)} %encode_frame1.1.tgt), channel_id=1, source_target_pairs={{0,2},{1,3},{2,0},{3,1},{4,6},{5,7},{6,4},{7,5},{8,10},{9,11},{10,... | collective-permute-start | bytes 737288 | tf_op jit(solution)/shard_map/ppermute | solution.py:36
  17.7 6.8 %collective-permute-start.3 = (bf16[480,256]{1,0:T(8,128)(2,1)S(1)}, bf16[480,256]{1,0:T(8,128)(2,1)S(1)}, u32[]{:S(2)}, u32[]{:S(2)}) collective-permute-start(bf16[480,256]{1,0:T(8,128)(2,1)S(1)} %encode_frame1.1.tgt), channel_id=1, source_target_pairs={{0,1},{1,0},{2,3},{3,2},{4,5},{5,4},{6,7},{7,6},{8,9},{9,8},{10,11... | collective-permute-start | bytes 737288 | tf_op jit(solution)/shard_map/ppermute | solution.py:36
  20.9 10.7 %copy-start.3 = (s32[1,1,9]{2,1,0:T(1,128)S(1)}, s32[1,1,9]{2,1,0:T(1,128)}, u32[]{:S(2)}) copy-start(s32[1,1,9]{2,1,0:T(1,128)} %param.9) | copy-start | bytes 112
  24.6 1.5 %collective-permute-start.5 = (bf16[480,256]{1,0:T(8,128)(2,1)S(1)}, bf16[480,256]{1,0:T(8,128)(2,1)S(1)}, u32[]{:S(2)}, u32[]{:S(2)}) collective-permute-start(bf16[480,256]{1,0:T(8,128)(2,1)S(1)} %collective-permute-done.4), channel_id=1, source_target_pairs={{0,1},{1,0},{2,3},{3,2},{4,5},{5,4},{6,7},{7,6},{8,9},{9,8},{10,11... | collective-permute-start | bytes 737288 | tf_op jit(solution)/shard_map/ppermute | solution.py:36
  26.1 16.0 %collective-permute-start.6 = (bf16[1920,256]{1,0:T(8,128)(2,1)S(1)}, bf16[1920,256]{1,0:T(8,128)(2,1)S(1)}, u32[]{:S(2)}, u32[]{:S(2)}) collective-permute-start(bf16[1920,256]{1,0:T(8,128)(2,1)S(1)} %pad_maximum_fusion.level), channel_id=1, source_target_pairs={{0,4},{2,6},{4,8},{5,1},{6,10},{7,3},{8,12},{9,5},{10,14},{11,7},{... | collective-permute-start | bytes 2949128 | tf_op jit(solution)/shard_map/ppermute | solution.py:36
  29.6 6.5 %collective-permute-start.8 = (bf16[480,256]{1,0:T(8,128)(2,1)S(1)}, bf16[480,256]{1,0:T(8,128)(2,1)S(1)}, u32[]{:S(2)}, u32[]{:S(2)}) collective-permute-start(bf16[480,256]{1,0:T(8,128)(2,1)S(1)} %encode_frame0.1.q), channel_id=1, source_target_pairs={{0,2},{1,3},{2,0},{3,1},{4,6},{5,7},{6,4},{7,5},{8,10},{9,11},{10,... | collective-permute-start | bytes 737288 | tf_op jit(solution)/shard_map/ppermute | solution.py:36
  31.5 4.6 %collective-permute-start.7 = (bf16[480,256]{1,0:T(8,128)(2,1)S(1)}, bf16[480,256]{1,0:T(8,128)(2,1)S(1)}, u32[]{:S(2)}, u32[]{:S(2)}) collective-permute-start(bf16[480,256]{1,0:T(8,128)(2,1)S(1)} %encode_frame0.1.q), channel_id=1, source_target_pairs={{0,1},{1,0},{2,3},{3,2},{4,5},{5,4},{6,7},{7,6},{8,9},{9,8},{10,11... | collective-permute-start | bytes 737288 | tf_op jit(solution)/shard_map/ppermute | solution.py:36
  34.4 11.2 %copy-start.4 = (f32[2,15,30]{2,0,1:T(2,128)S(1)}, f32[2,15,30]{2,0,1:T(2,128)}, u32[]{:S(2)}) copy-start(f32[2,15,30]{2,0,1:T(2,128)} %param.11) | copy-start | bytes 10804
  36.1 1.5 %collective-permute-start.9 = (bf16[480,256]{1,0:T(8,128)(2,1)S(1)}, bf16[480,256]{1,0:T(8,128)(2,1)S(1)}, u32[]{:S(2)}, u32[]{:S(2)}) collective-permute-start(bf16[480,256]{1,0:T(8,128)(2,1)S(1)} %collective-permute-done.8), channel_id=1, source_target_pairs={{0,1},{1,0},{2,3},{3,2},{4,5},{5,4},{6,7},{7,6},{8,9},{9,8},{10,11... | collective-permute-start | bytes 737288 | tf_op jit(solution)/shard_map/ppermute | solution.py:36
  42.1 3.6 %collective-permute-start.10 = (bf16[1920,256]{1,0:T(8,128)(2,1)S(1)}, bf16[1920,256]{1,0:T(8,128)(2,1)}, u32[]{:S(2)}, u32[]{:S(2)}) collective-permute-start(bf16[1920,256]{1,0:T(8,128)(2,1)S(1)} %collective-permute-done.6.got), channel_id=1, source_target_pairs={{0,1},{1,0},{2,3},{3,2},{4,5},{5,4},{6,7},{7,6},{8,9},{9,8},{10,11... | collective-permute-start | bytes 2949128 | tf_op jit(solution)/shard_map/ppermute | solution.py:36
  42.1 25.5 %collective-permute-start.14 = (bf16[1920,256]{1,0:T(8,128)(2,1)}, bf16[1920,256]{1,0:T(8,128)(2,1)}, u32[]{:S(2)}, u32[]{:S(2)}) collective-permute-start(bf16[1920,256]{1,0:T(8,128)(2,1)} %pad_maximum_fusion.1.refs_0_), channel_id=1, source_target_pairs={{0,4},{2,6},{4,8},{5,1},{6,10},{7,3},{8,12},{9,5},{10,14},{11,7},{... | collective-permute-start | bytes 2949128 | tf_op jit(solution)/shard_map/ppermute | solution.py:36
  51.3 4.1 %collective-permute-start.11 = (f32[8,480]{1,0:T(8,128)S(1)}, f32[8,480]{1,0:T(8,128)S(1)}, u32[]{:S(2)}, u32[]{:S(2)}) collective-permute-start(f32[8,480]{1,0:T(8,128)S(1)} %get-tuple-element.29), channel_id=1, source_target_pairs={{0,1},{1,0},{2,3},{3,2},{4,5},{5,4},{6,7},{7,6},{8,9},{9,8},{10,11... | collective-permute-start | bytes 46088 | tf_op jit(solution)/shard_map/ppermute | solution.py:36
  51.7 3.7 %collective-permute-start.12 = (f32[8,480]{1,0:T(8,128)S(1)}, f32[8,480]{1,0:T(8,128)S(1)}, u32[]{:S(2)}, u32[]{:S(2)}) collective-permute-start(f32[8,480]{1,0:T(8,128)S(1)} %get-tuple-element.29), channel_id=1, source_target_pairs={{0,2},{1,3},{2,0},{3,1},{4,6},{5,7},{6,4},{7,5},{8,10},{9,11},{10,... | collective-permute-start | bytes 46088 | tf_op jit(solution)/shard_map/ppermute | solution.py:36
  55.4 1.2 %collective-permute-start.13 = (f32[8,480]{1,0:T(8,128)S(1)}, f32[8,480]{1,0:T(8,128)S(1)}, u32[]{:S(2)}, u32[]{:S(2)}) collective-permute-start(f32[8,480]{1,0:T(8,128)S(1)} %collective-permute-done.12), channel_id=1, source_target_pairs={{0,1},{1,0},{2,3},{3,2},{4,5},{5,4},{6,7},{7,6},{8,9},{9,8},{10,11... | collective-permute-start | bytes 46088 | tf_op jit(solution)/shard_map/ppermute | solution.py:36
  56.6 11.1 %collective-permute-start.15 = (f32[32,480]{1,0:T(8,128)S(1)}, f32[32,480]{1,0:T(8,128)S(1)}, u32[]{:S(2)}, u32[]{:S(2)}) collective-permute-start(f32[32,480]{1,0:T(8,128)S(1)} %constant_dynamic-update-slice_fusion.refs_3_), channel_id=1, source_target_pairs={{0,4},{2,6},{4,8},{5,1},{6,10},{7,3},{8,12},{9,5},{10,14},{11,7},{... | collective-permute-start | bytes 184328 | tf_op jit(solution)/shard_map/ppermute | solution.py:36
  67.7 3.0 %collective-permute-start.16 = (bf16[1920,256]{1,0:T(8,128)(2,1)}, bf16[1920,256]{1,0:T(8,128)(2,1)S(1)}, u32[]{:S(2)}, u32[]{:S(2)}) collective-permute-start(bf16[1920,256]{1,0:T(8,128)(2,1)} %collective-permute-done.14.refs_1_), channel_id=1, source_target_pairs={{0,1},{1,0},{2,3},{3,2},{4,5},{5,4},{6,7},{7,6},{8,9},{9,8},{10,11... | collective-permute-start | bytes 2949128 | tf_op jit(solution)/shard_map/ppermute | solution.py:36
  68.2 2.3 %collective-permute-start.17 = (f32[32,480]{1,0:T(8,128)S(1)}, f32[32,480]{1,0:T(8,128)S(1)}, u32[]{:S(2)}, u32[]{:S(2)}) collective-permute-start(f32[32,480]{1,0:T(8,128)S(1)} %collective-permute-done.15.refs_4_), channel_id=1, source_target_pairs={{0,1},{1,0},{2,3},{3,2},{4,5},{5,4},{6,7},{7,6},{8,9},{9,8},{10,11... | collective-permute-start | bytes 184328 | tf_op jit(solution)/shard_map/ppermute | solution.py:36

commit v5 on v4

--- a/solution.py
+++ b/solution.py
@@ -145,7 +145,11 @@
 
 
 def load(tiles, buf, sems, at):
-    pltpu.make_async_copy(tiles, buf.at[at], sems.at[at]).start()
+    row = 0
+    for tile in tiles:
+        rows = tile.shape[0]
+        pltpu.make_async_copy(tile, buf.at[at, pl.ds(row, rows)], sems.at[at]).start()
+        row += rows
 
 
 def load_rows(level, got, other, buf, sems, core):
@@ -154,8 +158,8 @@
     load(other, buf, sems, 2 - 2 * core)
 
 
-def wait_for(tiles, buf, sems, at):
-    pltpu.make_async_copy(tiles, buf.at[at], sems.at[at]).wait()
+def wait_for(buf, sems, at):
+    pltpu.make_async_copy(buf.at[at], buf.at[at], sems.at[at]).wait()
 
 
 def half_tile(buf, a, j, i):
@@ -231,7 +235,8 @@
         state[3, rows] = state[3, rows] * factor + col_base * both
 
 
-def near_kernel(n_c, n_cs, c2, sc, cand, count, q, level, state, buf, sems, s_scr):
+def near_kernel(n_c, n_cs, c2, sc, cand, count, q, *refs):
+    level, (state, buf, sems, s_scr) = refs[:n_cs], refs[n_cs:]
     core, col = sc[0], sc[2]
     load(level, buf, sems, 0)
     state[0] = jnp.full(state.shape[1:], -jnp.inf, jnp.float32)
@@ -243,7 +248,7 @@
 
         @pl.when(j == 0)
         def _():
-            wait_for(level, buf, sems, 0)
+            wait_for(buf, sems, 0)
 
         @pl.when(hit == 1)
         def _():
@@ -254,8 +259,9 @@
     lax.fori_loop(0, n_cs, step, 0)
 
 
-def far_kernel(n_c, n_cs, c2, sc, cand, count, q, ctg, begun, got, other, *refs):
-    flow, stats, packed_out, buf, sems, s_scr, state = refs
+def far_kernel(n_c, n_cs, c2, sc, cand, count, q, ctg, begun, *refs):
+    got, other = refs[:n_cs], refs[n_cs : 2 * n_cs]
+    flow, stats, packed_out, buf, sems, s_scr, state = refs[2 * n_cs :]
     core, col = sc[0], sc[2]
     load(got, buf, sems, core)
     load(other, buf, sems, 1 - core)
@@ -267,7 +273,7 @@
 
         @pl.when(j == 0)
         def _():
-            wait_for(got, buf, sems, a)
+            wait_for(buf, sems, a)
 
         @pl.when(hit == 1)
         def _():
@@ -344,8 +350,9 @@
         acc[...] += jnp.dot(d_scr[:, 0:HC], half_tile(buf, a, j, i), preferred_element_type=jnp.float32)
 
 
-def grad_kernel(n_c, n_cs, c2, sc, cand, count, q, packed, level, got, other, *refs):
-    out, buf, sems, s_scr, d_scr, q4, acc = refs
+def grad_kernel(n_c, n_cs, c2, sc, cand, count, q, packed, *refs):
+    level, got, other = refs[:n_cs], refs[n_cs : 2 * n_cs], refs[2 * n_cs : 3 * n_cs]
+    out, buf, sems, s_scr, d_scr, q4, acc = refs[3 * n_cs :]
     core, col = sc[0], sc[2]
     load_rows(level, got, other, buf, sems, core)
     acc[...] = jnp.zeros(acc.shape, jnp.float32)
@@ -357,7 +364,7 @@
 
         @pl.when(j == 0)
         def _():
-            wait_for(level, buf, sems, a)
+            wait_for(buf, sems, a)
 
         @pl.when(hit == 1)
         def _():
@@ -387,16 +394,16 @@
 
 
 def query_near(n_c, sc, cand, count, q, level):
-    ch, n_cs = q.shape[1], level.shape[0] // (2 * HC)
+    ch, n_cs = q.shape[1], len(level)
     out_shape = jax.ShapeDtypeStruct((4, HC, 128), jnp.float32)
     scratch = [pltpu.VMEM((HC, 1024), jnp.float32)]
     return tiles_call(
-        near_kernel, n_c, ch, 1, n_cs, out_shape, scratch, 1, (sc, cand, count, q), (level,)
+        near_kernel, n_c, ch, 1, n_cs, out_shape, scratch, 1, (sc, cand, count, q), level
     )
 
 
 def query_far(n_c, sc, cand, count, q, ctg, begun, got, other):
-    ch, n_cs = q.shape[1], got.shape[0] // (2 * HC)
+    ch, n_cs = q.shape[1], len(got)
     out_shape = (
         jax.ShapeDtypeStruct((2, HC), jnp.float32),
         jax.ShapeDtypeStruct((8, HC), jnp.float32),
@@ -404,11 +411,11 @@
     )
     scratch = [pltpu.VMEM((HC, 1024), jnp.float32), pltpu.VMEM((4, HC, 128), jnp.float32)]
     ins = (sc, cand, count, q, ctg, begun)
-    return tiles_call(far_kernel, n_c, ch, 2, n_cs, out_shape, scratch, 3, ins, (got, other))
+    return tiles_call(far_kernel, n_c, ch, 2, n_cs, out_shape, scratch, 3, ins, (*got, *other))
 
 
 def query_grad(n_c, sc, cand, count, q, packed, level, got, other):
-    ch, n_cs = q.shape[1], level.shape[0] // (2 * HC)
+    ch, n_cs = q.shape[1], len(level)
     out_shape = jax.ShapeDtypeStruct((HALF, TILE, ch), jnp.float32)
     scratch = [
         pltpu.VMEM((HC, 512), jnp.float32),
@@ -416,7 +423,7 @@
         pltpu.VMEM((4, HC, 128), jnp.float32),
         pltpu.VMEM((HC, ch), jnp.float32),
     ]
-    ins, tiles = (sc, cand, count, q, packed), (level, got, other)
+    ins, tiles = (sc, cand, count, q, packed), (*level, *got, *other)
     return tiles_call(grad_kernel, n_c, ch, 3, n_cs, out_shape, scratch, 2, ins, tiles)
 
 
@@ -424,8 +431,8 @@
     feats, stats = refs[:3], refs[3:6]
     out, buf, sems, st, st_sems, s_scr, d_scr, v_scr, acc = refs[6:]
     core, col = sc[0], sc[2]
-    load_rows(*stats, st, st_sems, core)
-    load_rows(*feats, buf, sems, core)
+    load_rows(*([x] for x in stats), st, st_sems, core)
+    load_rows(*([x] for x in feats), buf, sems, core)
     acc[...] = jnp.zeros(acc.shape, jnp.float32)
 
     def step(slot, carry):
@@ -434,8 +441,8 @@
 
         @pl.when(j == 0)
         def _():
-            wait_for(feats[0], buf, sems, a)
-            wait_for(stats[0], st, st_sems, a)
+            wait_for(buf, sems, a)
+            wait_for(st, st_sems, a)
 
         code = 8 - (3 * (dr + 1) + dc + 1)
         where_at = lax.broadcasted_iota(jnp.int32, (8, HC), 1)
@@ -519,22 +526,25 @@
     z = send(jnp.stack(lines), lambda r, k, c: (r - 1 + 2 * c, k, 1 - c))
     second = encode(1, n_r, n_c, sc, mine, other_frame, xl, xr, z, w1, w2)
     side = sideways(second)
-    parts = [second, partner(second)]
+    own = jnp.concatenate([second, partner(second)])
     first = encode(0, n_r, n_c, sc, mine, other_frame, xl, xr, z, w1, w2)
+    own_got = updown(after(own, first))
     side = after(tuple(side), first)
-    for x in side:
-        parts += [x, partner(x)]
-    level = jnp.concatenate(parts)
-    got = updown(level)
+    level = [own] + [jnp.concatenate([x, partner(x)]) for x in side]
+    side_got = [updown(t) for t in level[1:]]
     q_side = sideways(after(first, side))
     q_parts = [first, partner(after(first, side))]
-    begun = query_near(n_c, sc, cand, count, first, level)
-    for x in after(tuple(q_side), begun):
+    begun = query_near(n_c, sc, cand, count, after(first, own_got), level)
+    side_got = after(tuple(side_got), begun)
+    for x in after(tuple(q_side), side_got):
         q_parts += [x, partner(x)]
     q_level = jnp.concatenate(q_parts)
     q_got = updown(q_level)
-    got = after(got, q_level)
-    other = partner(got)
+    own_got = after(own_got, begun)
+    own_other = partner(own_got)
+    got = [own_got, *side_got]
+    other = [own_other] + [partner(t) for t in side_got]
+    begun = after(begun, q_level)
     flow, stats, packed = query_far(n_c, sc, cand, count, first, ctg, begun, got, other)
     st_side = sideways(stats)
     st_parts = [stats, partner(stats)]
@@ -542,9 +552,11 @@
         st_parts += [x, partner(x)]
     st_level = jnp.concatenate(st_parts)
     st_got = updown(st_level)
-    grad_first = query_grad(n_c, sc, cand, count, first, after(packed, st_level), level, got, other)
-    q_got, st_got = after((q_got, st_got), grad_first)
-    q_other, st_other = partner(q_got), partner(st_got)
+    q_got = after(q_got, st_level)
+    q_other = partner(q_got)
+    grad_first = query_grad(n_c, sc, cand, count, first, after(packed, (st_level, q_got)), level, got, other)
+    st_got = after(st_got, grad_first)
+    st_other = partner(st_got)
     grad_second = target_side(
         n_c, sc, second, (q_level, q_got, q_other), (st_level, st_got, st_other)
     )

time: 79.4 us -> 81.9 us (1.031)
  the two profiles are of different devices: /device:TPU:12 before, /device:TPU:10 now
where the time goes in v5:
time: 81.9 us; the launch traced here: 81.5 us
  Pallas kernels  32.9 us (40%)
  waiting for transfers between devices  22.3 us (27%)
  starting transfers between devices  17.7 us (22%)
  local copies, waits for them, and re-layouts  4.85 us (6%)
  other arithmetic  2.18 us (3%)
  between operations  1.55 us (2%)
    ppermute x20, waiting for transfers between devices, send(): return lax.ppermute(value, AXES, pairs)  22.3 us
    ppermute x20, starting transfers between devices, send(): return lax.ppermute(value, AXES, pairs)  17.7 us
    pallas_call x3, Pallas kernels, tiles_call(): pl.pallas_call(functools.partial(kernel, n_c, n_cs, math.log2(math.e) / m...  17 us
    pallas_call x1, Pallas kernels, target_side(): pl.pallas_call(functools.partial(target_kernel, n_c, n_cs, math.log2(math...  9.12 us
    pallas_call x2, Pallas kernels, encode(): pl.pallas_call(functools.partial(encode_kernel, frame, n_r, n_c), out_sha...  6.27 us
    unnamed x16, local copies, waits for them, and re-layouts  3.19 us
  transfers between devices with their start and end apart: 20, of which 12 were waited for; matrix products, arithmetic and copies ran while one was open for 5% of the time, Pallas kernels for 25%

profile of v5, /device:TPU:10, one launch (start us, length us, event | category | flops | bytes accessed | tf_op | source)
XLA Modules:
  0.0 81.5 jit_solution(9676965109657642230)
XLA Ops:
  1.5 1.0 %fusion = bf16[1,30,2,256]{3,2,1,0:T(2,128)(2,1)S(1)} fusion(pred[]{:T(512)S(6)} %eq.4, bf16[30,30,256]{2,1,0:T(8,128)(2,1)} %bitcast.35), kind=kLoop, calls=%fused_computation.10 | loop fusion | flops 15360 | bytes 92161 | tf_op jit(solution)/shard_map/stack | solution.py:512
  3.5 1.3 %copy-done.1 = bf16[9,256,256]{2,1,0:T(8,128)(2,1)S(1)} copy-done((bf16[9,256,256]{2,1,0:T(8,128)(2,1)S(1)}, bf16[9,256,256]{2,1,0:T(8,128)(2,1)}, u32[]{:S(2)}) %copy-start.1) | copy-done | bytes 1179672
  4.8 1.3 %copy-done.2 = bf16[9,256,256]{2,1,0:T(8,128)(2,1)S(1)} copy-done((bf16[9,256,256]{2,1,0:T(8,128)(2,1)S(1)}, bf16[9,256,256]{2,1,0:T(8,128)(2,1)}, u32[]{:S(2)}) %copy-start.2) | copy-done | bytes 1179672
  7.3 1.9 %collective-permute-start.2 = (bf16[2,2,34,256]{3,2,1,0:T(8,128)(2,1)S(1)}, bf16[2,2,34,256]{3,2,1,0:T(8,128)(2,1)S(1)}, u32[]{:S(2)}, u32[]{:S(2)}) collective-permute-start(bf16[2,2,34,256]{3,2,1,0:T(8,128)(2,1)S(1)} %pad_maximum_fusion.2), channel_id=1, source_target_pairs={{1,4},{3,6},{4,1},{5,8},{6,3},{7,10},{8,5},{9,12},{10,7},{11,14},{... | collective-permute-start | bytes 208904 | tf_op jit(solution)/shard_map/ppermute | solution.py:36
  9.3 3.8 %collective-permute-done.2.z = bf16[2,2,34,256]{3,2,1,0:T(8,128)(2,1)S(1)} collective-permute-done((bf16[2,2,34,256]{3,2,1,0:T(8,128)(2,1)S(1)}, bf16[2,2,34,256]{3,2,1,0:T(8,128)(2,1)S(1)}, u32[]{:S(2)}, u32[]{:S(2)}) %collective-permute-start.2) | collective-permute-done | bytes 69664 | tf_op jit(solution)/shard_map/ppermute | solution.py:36
  13.1 3.1 %encode_frame1.1.tgt = bf16[480,256]{1,0:T(8,128)(2,1)S(1)} custom-call(s32[3]{0:T(128)S(1)} %pad_add_fusion.sc, bf16[30,30,256]{2,1,0:T(8,128)(2,1)S(1)} %bitcast.36, bf16[30,30,256]{2,1,0:T(8,128)(2,1)S(1)} %collective-permute-done.got, bf16[2,30,2,256]{3,2,1,0:T(2,128)(2,1)S(1)} %collective-permute-done.1.xl.xr, ...), custom_call_target="tpu_custom_call" | custom-call | flops 1000000 | bytes 10000 | tf_op jit(solution)/shard_map/encode_frame1/pallas_call | solution.py:130
  16.2 0.9 %collective-permute-start.5 = (bf16[480,256]{1,0:T(8,128)(2,1)S(1)}, bf16[480,256]{1,0:T(8,128)(2,1)S(1)}, u32[]{:S(2)}, u32[]{:S(2)}) collective-permute-start(bf16[480,256]{1,0:T(8,128)(2,1)S(1)} %encode_frame1.1.tgt), channel_id=1, source_target_pairs={{0,2},{1,3},{2,0},{3,1},{4,6},{5,7},{6,4},{7,5},{8,10},{9,11},{10,... | collective-permute-start | bytes 737288 | tf_op jit(solution)/shard_map/ppermute | solution.py:36
  17.1 3.1 %encode_frame0.1.q = bf16[480,256]{1,0:T(8,128)(2,1)S(1)} custom-call(s32[3]{0:T(128)S(1)} %pad_add_fusion.sc, bf16[30,30,256]{2,1,0:T(8,128)(2,1)S(1)} %bitcast.37, bf16[30,30,256]{2,1,0:T(8,128)(2,1)S(1)} %collective-permute-done.got, bf16[2,30,2,256]{3,2,1,0:T(2,128)(2,1)S(1)} %collective-permute-done.1.xl.xr, ...), custom_call_target="tpu_custom_call" | custom-call | flops 1000000 | bytes 10000 | tf_op jit(solution)/shard_map/encode_frame0/pallas_call | solution.py:130
  20.3 3.9 %collective-permute-done.5 = bf16[480,256]{1,0:T(8,128)(2,1)S(1)} collective-permute-done((bf16[480,256]{1,0:T(8,128)(2,1)S(1)}, bf16[480,256]{1,0:T(8,128)(2,1)S(1)}, u32[]{:S(2)}, u32[]{:S(2)}) %collective-permute-start.5) | collective-permute-done | bytes 245792 | tf_op jit(solution)/shard_map/ppermute | solution.py:36
  24.3 3.5 %collective-permute-start.4 = (bf16[960,256]{1,0:T(8,128)(2,1)S(1)}, bf16[960,256]{1,0:T(8,128)(2,1)}, u32[]{:S(2)}, u32[]{:S(2)}) collective-permute-start(bf16[960,256]{1,0:T(8,128)(2,1)S(1)} %pad_maximum_fusion.1.refs_0_), channel_id=1, source_target_pairs={{0,4},{2,6},{4,8},{5,1},{6,10},{7,3},{8,12},{9,5},{10,14},{11,7},{... | collective-permute-start | bytes 1474568 | tf_op jit(solution)/shard_map/ppermute | solution.py:36
  27.8 1.9 %collective-permute-start.9 = (bf16[960,256]{1,0:T(8,128)(2,1)S(1)}, bf16[960,256]{1,0:T(8,128)(2,1)}, u32[]{:S(2)}, u32[]{:S(2)}) collective-permute-start(bf16[960,256]{1,0:T(8,128)(2,1)S(1)} %constant_dynamic-update-slice_fusion.refs_1_), channel_id=1, source_target_pairs={{0,4},{2,6},{4,8},{5,1},{6,10},{7,3},{8,12},{9,5},{10,14},{11,7},{... | collective-permute-start | bytes 1474568 | tf_op jit(solution)/shard_map/ppermute | solution.py:36
  29.8 0.9 %collective-permute-start.8 = (bf16[480,256]{1,0:T(8,128)(2,1)S(1)}, bf16[480,256]{1,0:T(8,128)(2,1)S(1)}, u32[]{:S(2)}, u32[]{:S(2)}) collective-permute-start(bf16[480,256]{1,0:T(8,128)(2,1)S(1)} %encode_frame0.1.q), channel_id=1, source_target_pairs={{0,2},{1,3},{2,0},{3,1},{4,6},{5,7},{6,4},{7,5},{8,10},{9,11},{10,... | collective-permute-start | bytes 737288 | tf_op jit(solution)/shard_map/ppermute | solution.py:36
  31.4 3.7 %collective-permute-done.4.refs_0_.refs_2_ = bf16[960,256]{1,0:T(8,128)(2,1)} collective-permute-done((bf16[960,256]{1,0:T(8,128)(2,1)S(1)}, bf16[960,256]{1,0:T(8,128)(2,1)}, u32[]{:S(2)}, u32[]{:S(2)}) %collective-permute-start.4) | collective-permute-done | bytes 491552 | tf_op jit(solution)/shard_map/ppermute | solution.py:36
  35.1 3.2 %near_kernel.1.begun = f32[4,480,128]{2,1,0:T(8,128)S(1)} custom-call(s32[3]{0:T(128)S(1)} %pad_add_fusion.sc, s32[9]{0:T(128)S(1)} %bitcast.38, s32[1]{0:T(128)} %bitcast.27.count, bf16[480,256]{1,0:T(8,128)(2,1)S(1)} %encode_frame0.1.q, bf16[960,256]{1,0:T(8,128)(2,1)S(1)} %pad_maximum_fusion.1.refs_0_, ...), custom_call_target="tpu_custom_call" | custom-call | flops 1000000 | bytes 10000 | tf_op jit(solution)/shard_map/near_kernel/pallas_call | solution.py:380
  38.3 2.1 %collective-permute-done.9.refs_1_.refs_3_ = bf16[960,256]{1,0:T(8,128)(2,1)} collective-permute-done((bf16[960,256]{1,0:T(8,128)(2,1)S(1)}, bf16[960,256]{1,0:T(8,128)(2,1)}, u32[]{:S(2)}, u32[]{:S(2)}) %collective-permute-start.9) | collective-permute-done | bytes 491552 | tf_op jit(solution)/shard_map/ppermute | solution.py:36
  40.4 1.5 %collective-permute-done.10 = bf16[480,256]{1,0:T(8,128)(2,1)S(1)} collective-permute-done((bf16[480,256]{1,0:T(8,128)(2,1)S(1)}, bf16[480,256]{1,0:T(8,128)(2,1)S(1)}, u32[]{:S(2)}, u32[]{:S(2)}) %collective-permute-start.10) | collective-permute-done | bytes 245792 | tf_op jit(solution)/shard_map/ppermute | solution.py:36
  42.0 3.5 %collective-permute-start.16 = (bf16[1920,256]{1,0:T(8,128)(2,1)S(1)}, bf16[1920,256]{1,0:T(8,128)(2,1)}, u32[]{:S(2)}, u32[]{:S(2)}) collective-permute-start(bf16[1920,256]{1,0:T(8,128)(2,1)S(1)} %pad_maximum_fusion.refs_0_), channel_id=1, source_target_pairs={{0,4},{2,6},{4,8},{5,1},{6,10},{7,3},{8,12},{9,5},{10,14},{11,7},{... | collective-permute-start | bytes 2949128 | tf_op jit(solution)/shard_map/ppermute | solution.py:36
  46.7 0.9 %reshape.60.ctg = f32[8,480]{1,0:T(8,128)S(1)} reshape(f32[8,15,32]{2,1,0:T(8,128)} %pad.4.clone) | data formatting | bytes 30720 | tf_op jit(solution)/shard_map/reshape | solution.py:508
  48.4 5.4 %far_kernel.1 = (f32[2,480]{1,0:T(2,128)S(1)}, f32[8,480]{1,0:T(8,128)S(1)}, f32[480,128]{1,0:T(8,128)S(1)}) custom-call(s32[3]{0:T(128)S(1)} %pad_add_fusion.sc, s32[9]{0:T(128)S(1)} %bitcast.39, s32[1]{0:T(128)} %bitcast.28.count, bf16[480,256]{1,0:T(8,128)(2,1)S(1)} %encode_frame0.1.q, f32[8,480]{1,0:T(8,128)S(1)} %reshape.60.ctg, ...), custom_call_target="tpu_custom_call" | custom-call | flops 1000000 | bytes 10000 | tf_op jit(solution)/shard_map/far_kernel/pallas_call | solution.py:380
  54.3 3.7 %collective-permute-done.14 = f32[8,480]{1,0:T(8,128)S(1)} collective-permute-done((f32[8,480]{1,0:T(8,128)S(1)}, f32[8,480]{1,0:T(8,128)S(1)}, u32[]{:S(2)}, u32[]{:S(2)}) %collective-permute-start.14) | collective-permute-done | bytes 15392 | tf_op jit(solution)/shard_map/ppermute | solution.py:36
  58.1 1.2 %collective-permute-done.15 = f32[8,480]{1,0:T(8,128)S(1)} collective-permute-done((f32[8,480]{1,0:T(8,128)S(1)}, f32[8,480]{1,0:T(8,128)S(1)}, u32[]{:S(2)}, u32[]{:S(2)}) %collective-permute-start.15) | collective-permute-done | bytes 15392 | tf_op jit(solution)/shard_map/ppermute | solution.py:36
  59.4 3.0 %collective-permute-start.18 = (f32[32,480]{1,0:T(8,128)S(1)}, f32[32,480]{1,0:T(8,128)}, u32[]{:S(2)}, u32[]{:S(2)}) collective-permute-start(f32[32,480]{1,0:T(8,128)S(1)} %constant_dynamic-update-slice_fusion.2.refs_3_), channel_id=1, source_target_pairs={{0,4},{2,6},{4,8},{5,1},{6,10},{7,3},{8,12},{9,5},{10,14},{11,7},{... | collective-permute-start | bytes 184328 | tf_op jit(solution)/shard_map/ppermute | solution.py:36
  62.4 8.4 %grad_kernel.1 = f32[15,30,256]{2,1,0:T(8,128)} custom-call(s32[3]{0:T(128)S(1)} %pad_add_fusion.sc, s32[9]{0:T(128)S(1)} %bitcast.40, s32[1]{0:T(128)} %bitcast.29.count, bf16[480,256]{1,0:T(8,128)(2,1)S(1)} %encode_frame0.1.q, f32[480,128]{1,0:T(8,128)S(1)} %get-tuple-element.39.packed, bf16[960,256]{1,0:T(8,128)(2,1)S(1)} %pad_maximum_fusion.1.refs_0_, ...), custom_call_target="tpu_custom_call" | custom-call | flops 1000000 | bytes 10000 | tf_op jit(solution)/shard_map/grad_kernel/pallas_call | solution.py:380
  72.4 9.1 %target_side.1 = f32[15,30,256]{2,1,0:T(8,128)} custom-call(s32[3]{0:T(128)S(1)} %pad_add_fusion.sc, bf16[480,256]{1,0:T(8,128)(2,1)S(1)} %encode_frame1.1.tgt, bf16[1920,256]{1,0:T(8,128)(2,1)S(1)} %pad_maximum_fusion.refs_0_, bf16[1920,256]{1,0:T(8,128)(2,1)} %collective-permute-done.16.refs_1_, bf16[1920,256]{1,0:T(8,128)(2,1)S(1)} %collective-permute-done.17.refs_2_, ...), custom_call_target="tpu_custom_call" | custom-call | flops 1000000 | bytes 10000 | tf_op jit(solution)/shard_map/target_side/pallas_call | solution.py:480
  (56 shorter events, 7.6 us)
Async XLA Ops:
  0.6 2.1 %collective-permute-start = (bf16[30,30,256]{2,1,0:T(8,128)(2,1)}, bf16[30,30,256]{2,1,0:T(8,128)(2,1)S(1)}, u32[]{:S(2)}, u32[]{:S(2)}) collective-permute-start(bf16[30,30,256]{2,1,0:T(8,128)(2,1)} %bitcast.34), channel_id=1, source_target_pairs={{0,1},{1,0},{2,3},{3,2},{4,5},{5,4},{6,7},{7,6},{8,9},{9,8},{10,11... | collective-permute-start | bytes 1382408 | tf_op jit(solution)/shard_map/ppermute | solution.py:36
  2.9 4.3 %collective-permute-start.1 = (bf16[2,30,2,256]{3,2,1,0:T(2,128)(2,1)S(1)}, bf16[2,30,2,256]{3,2,1,0:T(2,128)(2,1)S(1)}, u32[]{:S(2)}, u32[]{:S(2)}) collective-permute-start(bf16[2,30,2,256]{3,2,1,0:T(2,128)(2,1)S(1)} %pad_maximum_fusion.3), channel_id=1, source_target_pairs={{0,2},{1,3},{2,0},{3,1},{4,6},{5,7},{6,4},{7,5},{8,10},{9,11},{10,... | collective-permute-start | bytes 184328 | tf_op jit(solution)/shard_map/ppermute | solution.py:36
  3.5 1.3 %copy-start.1 = (bf16[9,256,256]{2,1,0:T(8,128)(2,1)S(1)}, bf16[9,256,256]{2,1,0:T(8,128)(2,1)}, u32[]{:S(2)}) copy-start(bf16[9,256,256]{2,1,0:T(8,128)(2,1)} %a) | copy-start | bytes 3538948
  6.1 7.0 %copy-start = (bf16[1,30,30,256]{3,2,1,0:T(8,128)(2,1)S(1)}, bf16[1,30,30,256]{3,2,1,0:T(8,128)(2,1)}, u32[]{:S(2)}) copy-start(bf16[1,30,30,256]{3,2,1,0:T(8,128)(2,1)} %param.6) | copy-start | bytes 1382404
  7.3 5.8 %collective-permute-start.2 = (bf16[2,2,34,256]{3,2,1,0:T(8,128)(2,1)S(1)}, bf16[2,2,34,256]{3,2,1,0:T(8,128)(2,1)S(1)}, u32[]{:S(2)}, u32[]{:S(2)}) collective-permute-start(bf16[2,2,34,256]{3,2,1,0:T(8,128)(2,1)S(1)} %pad_maximum_fusion.2), channel_id=1, source_target_pairs={{1,4},{3,6},{4,1},{5,8},{6,3},{7,10},{8,5},{9,12},{10,7},{11,14},{... | collective-permute-start | bytes 208904 | tf_op jit(solution)/shard_map/ppermute | solution.py:36
  16.2 8.0 %collective-permute-start.5 = (bf16[480,256]{1,0:T(8,128)(2,1)S(1)}, bf16[480,256]{1,0:T(8,128)(2,1)S(1)}, u32[]{:S(2)}, u32[]{:S(2)}) collective-permute-start(bf16[480,256]{1,0:T(8,128)(2,1)S(1)} %encode_frame1.1.tgt), channel_id=1, source_target_pairs={{0,2},{1,3},{2,0},{3,1},{4,6},{5,7},{6,4},{7,5},{8,10},{9,11},{10,... | collective-permute-start | bytes 737288 | tf_op jit(solution)/shard_map/ppermute | solution.py:36
  17.1 7.1 %collective-permute-start.3 = (bf16[480,256]{1,0:T(8,128)(2,1)S(1)}, bf16[480,256]{1,0:T(8,128)(2,1)S(1)}, u32[]{:S(2)}, u32[]{:S(2)}) collective-permute-start(bf16[480,256]{1,0:T(8,128)(2,1)S(1)} %encode_frame1.1.tgt), channel_id=1, source_target_pairs={{0,1},{1,0},{2,3},{3,2},{4,5},{5,4},{6,7},{7,6},{8,9},{9,8},{10,11... | collective-permute-start | bytes 737288 | tf_op jit(solution)/shard_map/ppermute | solution.py:36
  20.3 14.8 %copy-start.3 = (s32[1,1,9]{2,1,0:T(1,128)S(1)}, s32[1,1,9]{2,1,0:T(1,128)}, u32[]{:S(2)}) copy-start(s32[1,1,9]{2,1,0:T(1,128)} %param.9) | copy-start | bytes 112
  24.2 3.6 %collective-permute-start.6 = (bf16[480,256]{1,0:T(8,128)(2,1)S(1)}, bf16[480,256]{1,0:T(8,128)(2,1)S(1)}, u32[]{:S(2)}, u32[]{:S(2)}) collective-permute-start(bf16[480,256]{1,0:T(8,128)(2,1)S(1)} %collective-permute-done.5), channel_id=1, source_target_pairs={{0,1},{1,0},{2,3},{3,2},{4,5},{5,4},{6,7},{7,6},{8,9},{9,8},{10,11... | collective-permute-start | bytes 737288 | tf_op jit(solution)/shard_map/ppermute | solution.py:36
  24.3 10.8 %collective-permute-start.4 = (bf16[960,256]{1,0:T(8,128)(2,1)S(1)}, bf16[960,256]{1,0:T(8,128)(2,1)}, u32[]{:S(2)}, u32[]{:S(2)}) collective-permute-start(bf16[960,256]{1,0:T(8,128)(2,1)S(1)} %pad_maximum_fusion.1.refs_0_), channel_id=1, source_target_pairs={{0,4},{2,6},{4,8},{5,1},{6,10},{7,3},{8,12},{9,5},{10,14},{11,7},{... | collective-permute-start | bytes 1474568 | tf_op jit(solution)/shard_map/ppermute | solution.py:36
  27.8 12.5 %collective-permute-start.9 = (bf16[960,256]{1,0:T(8,128)(2,1)S(1)}, bf16[960,256]{1,0:T(8,128)(2,1)}, u32[]{:S(2)}, u32[]{:S(2)}) collective-permute-start(bf16[960,256]{1,0:T(8,128)(2,1)S(1)} %constant_dynamic-update-slice_fusion.refs_1_), channel_id=1, source_target_pairs={{0,4},{2,6},{4,8},{5,1},{6,10},{7,3},{8,12},{9,5},{10,14},{11,7},{... | collective-permute-start | bytes 1474568 | tf_op jit(solution)/shard_map/ppermute | solution.py:36
  29.8 10.6 %collective-permute-start.8 = (bf16[480,256]{1,0:T(8,128)(2,1)S(1)}, bf16[480,256]{1,0:T(8,128)(2,1)S(1)}, u32[]{:S(2)}, u32[]{:S(2)}) collective-permute-start(bf16[480,256]{1,0:T(8,128)(2,1)S(1)} %encode_frame0.1.q), channel_id=1, source_target_pairs={{0,2},{1,3},{2,0},{3,1},{4,6},{5,7},{6,4},{7,5},{8,10},{9,11},{10,... | collective-permute-start | bytes 737288 | tf_op jit(solution)/shard_map/ppermute | solution.py:36
  31.4 9.0 %collective-permute-start.7 = (bf16[480,256]{1,0:T(8,128)(2,1)S(1)}, bf16[480,256]{1,0:T(8,128)(2,1)S(1)}, u32[]{:S(2)}, u32[]{:S(2)}) collective-permute-start(bf16[480,256]{1,0:T(8,128)(2,1)S(1)} %encode_frame0.1.q), channel_id=1, source_target_pairs={{0,1},{1,0},{2,3},{3,2},{4,5},{5,4},{6,7},{7,6},{8,9},{9,8},{10,11... | collective-permute-start | bytes 737288 | tf_op jit(solution)/shard_map/ppermute | solution.py:36
  38.3 7.7 %copy-start.4 = (f32[2,15,30]{2,0,1:T(2,128)S(1)}, f32[2,15,30]{2,0,1:T(2,128)}, u32[]{:S(2)}) copy-start(f32[2,15,30]{2,0,1:T(2,128)} %param.11) | copy-start | bytes 10804
  40.4 1.5 %collective-permute-start.10 = (bf16[480,256]{1,0:T(8,128)(2,1)S(1)}, bf16[480,256]{1,0:T(8,128)(2,1)S(1)}, u32[]{:S(2)}, u32[]{:S(2)}) collective-permute-start(bf16[480,256]{1,0:T(8,128)(2,1)S(1)} %collective-permute-done.8), channel_id=1, source_target_pairs={{0,1},{1,0},{2,3},{3,2},{4,5},{5,4},{6,7},{7,6},{8,9},{9,8},{10,11... | collective-permute-start | bytes 737288 | tf_op jit(solution)/shard_map/ppermute | solution.py:36
  42.0 17.3 %collective-permute-start.16 = (bf16[1920,256]{1,0:T(8,128)(2,1)S(1)}, bf16[1920,256]{1,0:T(8,128)(2,1)}, u32[]{:S(2)}, u32[]{:S(2)}) collective-permute-start(bf16[1920,256]{1,0:T(8,128)(2,1)S(1)} %pad_maximum_fusion.refs_0_), channel_id=1, source_target_pairs={{0,4},{2,6},{4,8},{5,1},{6,10},{7,3},{8,12},{9,5},{10,14},{11,7},{... | collective-permute-start | bytes 2949128 | tf_op jit(solution)/shard_map/ppermute | solution.py:36
  45.5 2.3 %collective-permute-start.11 = (bf16[960,256]{1,0:T(8,128)(2,1)}, bf16[960,256]{1,0:T(8,128)(2,1)}, u32[]{:S(2)}, u32[]{:S(2)}) collective-permute-start(bf16[960,256]{1,0:T(8,128)(2,1)} %collective-permute-done.4.refs_0_.refs_2_), channel_id=1, source_target_pairs={{0,1},{1,0},{2,3},{3,2},{4,5},{5,4},{6,7},{7,6},{8,9},{9,8},{10,11... | collective-permute-start | bytes 1474568 | tf_op jit(solution)/shard_map/ppermute | solution.py:36
  45.5 2.9 %collective-permute-start.12 = (bf16[960,256]{1,0:T(8,128)(2,1)}, bf16[960,256]{1,0:T(8,128)(2,1)}, u32[]{:S(2)}, u32[]{:S(2)}) collective-permute-start(bf16[960,256]{1,0:T(8,128)(2,1)} %collective-permute-done.9.refs_1_.refs_3_), channel_id=1, source_target_pairs={{0,1},{1,0},{2,3},{3,2},{4,5},{5,4},{6,7},{7,6},{8,9},{9,8},{10,11... | collective-permute-start | bytes 1474568 | tf_op jit(solution)/shard_map/ppermute | solution.py:36
  53.8 4.2 %collective-permute-start.13 = (f32[8,480]{1,0:T(8,128)S(1)}, f32[8,480]{1,0:T(8,128)S(1)}, u32[]{:S(2)}, u32[]{:S(2)}) collective-permute-start(f32[8,480]{1,0:T(8,128)S(1)} %get-tuple-element.37), channel_id=1, source_target_pairs={{0,1},{1,0},{2,3},{3,2},{4,5},{5,4},{6,7},{7,6},{8,9},{9,8},{10,11... | collective-permute-start | bytes 46088 | tf_op jit(solution)/shard_map/ppermute | solution.py:36
  54.3 3.7 %collective-permute-start.14 = (f32[8,480]{1,0:T(8,128)S(1)}, f32[8,480]{1,0:T(8,128)S(1)}, u32[]{:S(2)}, u32[]{:S(2)}) collective-permute-start(f32[8,480]{1,0:T(8,128)S(1)} %get-tuple-element.37), channel_id=1, source_target_pairs={{0,2},{1,3},{2,0},{3,1},{4,6},{5,7},{6,4},{7,5},{8,10},{9,11},{10,... | collective-permute-start | bytes 46088 | tf_op jit(solution)/shard_map/ppermute | solution.py:36
  58.1 1.2 %collective-permute-start.15 = (f32[8,480]{1,0:T(8,128)S(1)}, f32[8,480]{1,0:T(8,128)S(1)}, u32[]{:S(2)}, u32[]{:S(2)}) collective-permute-start(f32[8,480]{1,0:T(8,128)S(1)} %collective-permute-done.14), channel_id=1, source_target_pairs={{0,1},{1,0},{2,3},{3,2},{4,5},{5,4},{6,7},{7,6},{8,9},{9,8},{10,11... | collective-permute-start | bytes 46088 | tf_op jit(solution)/shard_map/ppermute | solution.py:36
  59.3 13.1 %collective-permute-start.17 = (bf16[1920,256]{1,0:T(8,128)(2,1)}, bf16[1920,256]{1,0:T(8,128)(2,1)S(1)}, u32[]{:S(2)}, u32[]{:S(2)}) collective-permute-start(bf16[1920,256]{1,0:T(8,128)(2,1)} %collective-permute-done.16.refs_1_), channel_id=1, source_target_pairs={{0,1},{1,0},{2,3},{3,2},{4,5},{5,4},{6,7},{7,6},{8,9},{9,8},{10,11... | collective-permute-start | bytes 2949128 | tf_op jit(solution)/shard_map/ppermute | solution.py:36
  59.4 11.4 %collective-permute-start.18 = (f32[32,480]{1,0:T(8,128)S(1)}, f32[32,480]{1,0:T(8,128)}, u32[]{:S(2)}, u32[]{:S(2)}) collective-permute-start(f32[32,480]{1,0:T(8,128)S(1)} %constant_dynamic-update-slice_fusion.2.refs_3_), channel_id=1, source_target_pairs={{0,4},{2,6},{4,8},{5,1},{6,10},{7,3},{8,12},{9,5},{10,14},{11,7},{... | collective-permute-start | bytes 184328 | tf_op jit(solution)/shard_map/ppermute | solution.py:36
  70.9 1.5 %collective-permute-start.19 = (f32[32,480]{1,0:T(8,128)}, f32[32,480]{1,0:T(8,128)S(1)}, u32[]{:S(2)}, u32[]{:S(2)}) collective-permute-start(f32[32,480]{1,0:T(8,128)} %collective-permute-done.18.refs_4_), channel_id=1, source_target_pairs={{0,1},{1,0},{2,3},{3,2},{4,5},{5,4},{6,7},{7,6},{8,9},{9,8},{10,11... | collective-permute-start | bytes 184328 | tf_op jit(solution)/shard_map/ppermute | solution.py:36
  (1 other events, 1.3 us)

commit v6 on v4

--- a/solution.py
+++ b/solution.py
@@ -138,7 +138,7 @@
             pltpu.VMEM((HID * PADW + 8, ch), jnp.float32),
             pltpu.VMEM((HID * PADW, 3 * ch), jnp.bfloat16),
         ],
-        compiler_params=pltpu.CompilerParams(vmem_limit_bytes=12 * 2**20),
+        compiler_params=pltpu.CompilerParams(vmem_limit_bytes=14 * 2**20),
         cost_estimate=COST,
         name=f"encode_frame{frame}",
     )(sc, mine, got, xl, xr, z, w1, w2)
@@ -190,17 +190,23 @@
     return lane, lane % PADW < TILE, lane < HC - 384
 
 
-def add_tile(c2, a, j, dr, dc, core, q, buf, s_scr, state):
-    for i in range(2):
-        s_scr[:, i * 512 : i * 512 + HC] = lax.dot_general(
+def add_tile(c2, a, j, dr, dc, core, q, buf, state):
+    whole = [
+        lax.dot_general(
             q[...], half_tile(buf, a, j, i), (((1,), (1,)), ((), ())), preferred_element_type=jnp.float32
         )
+        for i in range(2)
+    ]
     base = [(30 * dr + 15 * half_of(dr, i, core)).astype(jnp.float32) for i in range(2)]
     col_base = (30 * dc).astype(jnp.float32)
     lane, lane_ok, in_row = lanes(RB)
+    zero = jnp.zeros((RB, 512 - HC), jnp.float32)
     for g in range(HC // RB):
         rows = slice(g * RB, (g + 1) * RB)
-        s = [s_scr[rows, v * 128 : v * 128 + 128] for v in range(8)]
+        s = []
+        for part in whole:
+            s += [part[rows, v * 128 : v * 128 + 128] for v in range(3)]
+            s.append(jnp.concatenate([part[rows, 384:], zero], axis=1))
         top = jnp.maximum(
             jnp.maximum(jnp.maximum(s[0], s[1]), s[2]),
             jnp.maximum(jnp.maximum(s[4], s[5]), s[6]),
@@ -231,7 +237,7 @@
         state[3, rows] = state[3, rows] * factor + col_base * both
 
 
-def near_kernel(n_c, n_cs, c2, sc, cand, count, q, level, state, buf, sems, s_scr):
+def near_kernel(n_c, n_cs, c2, sc, cand, count, q, level, state, buf, sems):
     core, col = sc[0], sc[2]
     load(level, buf, sems, 0)
     state[0] = jnp.full(state.shape[1:], -jnp.inf, jnp.float32)
@@ -247,7 +253,7 @@
 
         @pl.when(hit == 1)
         def _():
-            add_tile(c2, 0, j, dr, dc, core, q, buf, s_scr, state)
+            add_tile(c2, 0, j, dr, dc, core, q, buf, state)
 
         return carry
 
@@ -255,7 +261,7 @@
 
 
 def far_kernel(n_c, n_cs, c2, sc, cand, count, q, ctg, begun, got, other, *refs):
-    flow, stats, packed_out, buf, sems, s_scr, state = refs
+    flow, stats, packed_out, buf, sems, state = refs
     core, col = sc[0], sc[2]
     load(got, buf, sems, core)
     load(other, buf, sems, 1 - core)
@@ -271,7 +277,7 @@
 
         @pl.when(hit == 1)
         def _():
-            add_tile(c2, a, j, dr, dc, core, q, buf, s_scr, state)
+            add_tile(c2, a, j, dr, dc, core, q, buf, state)
 
         return carry
 
@@ -322,50 +328,75 @@
         q4[k] = jnp.broadcast_to(packed[:, k : k + 1], (HC, 128))
 
 
-def grad_tile(c2, a, j, dr, dc, core, q, buf, s_scr, d_scr, acc, q4):
-    lane, lane_ok, in_row = lanes(RB)
+def grad_tile(c2, a, j, dr, dc, core, q, buf, acc, q4):
+    lane, lane_ok, _ = lanes(RB)
     lane_row = (lane // PADW).astype(jnp.float32)
     lane_col = (lane % PADW + 30 * dc).astype(jnp.float32)
     for i in range(2):
-        s_scr[:, 0:HC] = lax.dot_general(
-            q[...], half_tile(buf, a, j, i), (((1,), (1,)), ((), ())), preferred_element_type=jnp.float32
+        tile = half_tile(buf, a, j, i)
+        base = lane_row + (30 * dr + 15 * half_of(dr, i, core)).astype(jnp.float32)
+        s = lax.dot_general(
+            q[...], tile, (((1,), (1,)), ((), ())), preferred_element_type=jnp.float32
         )
-        base = lane_row + (30 * dr + 15 * half_of(dr, i, core)).astype(jnp.float32)
+        ds = []
         for g in range(HC // RB):
             rows = slice(g * RB, (g + 1) * RB)
             lev, gr, gc, sh = (q4[k, rows] for k in range(4))
             pull = gr * base + (gc * lane_col - sh)
+            parts = []
             for v in range(4):
-                p = jnp.exp2(s_scr[rows, v * 128 : v * 128 + 128] * c2 - lev)
-                d = jnp.where(lane_ok & in_row if v == 3 else lane_ok, p * pull, 0.0)
-                d_scr[rows, v * 128 : v * 128 + 128] = d.astype(jnp.bfloat16)
+                width = min(128, HC - v * 128)
+                p = jnp.exp2(s[rows, v * 128 : v * 128 + width] * c2 - lev[:, :width])
+                d = jnp.where(lane_ok[:, :width], p * pull[:, :width], 0.0)
+                parts.append(d.astype(jnp.bfloat16))
                 if v < 3:
                     pull = pull + 4.0 * gr
-        acc[...] += jnp.dot(d_scr[:, 0:HC], half_tile(buf, a, j, i), preferred_element_type=jnp.float32)
-
-
-def grad_kernel(n_c, n_cs, c2, sc, cand, count, q, packed, level, got, other, *refs):
-    out, buf, sems, s_scr, d_scr, q4, acc = refs
+            ds.append(jnp.concatenate(parts, axis=1))
+        acc[...] += jnp.dot(jnp.concatenate(ds), tile, preferred_element_type=jnp.float32)
+
+
+def grad_near_kernel(n_c, n_cs, c2, sc, cand, count, q, packed, level, acc, buf, sems, q4):
     core, col = sc[0], sc[2]
-    load_rows(level, got, other, buf, sems, core)
+    load(level, buf, sems, 0)
     acc[...] = jnp.zeros(acc.shape, jnp.float32)
     spread(packed, q4)
-
-    def step(slot, carry):
-        a, j = slot // n_cs, slot % n_cs
-        dr, dc, _, hit = listed(slot, n_cs, n_c, col, cand, count)
+    wait_for(level, buf, sems, 0)
+
+    def step(j, carry):
+        dr, dc, _, hit = listed(n_cs + j, n_cs, n_c, col, cand, count)
+
+        @pl.when(hit == 1)
+        def _():
+            grad_tile(c2, 0, j, dr, dc, core, q, buf, acc, q4)
+
+        return carry
+
+    lax.fori_loop(0, n_cs, step, 0)
+
+
+def grad_far_kernel(n_c, n_cs, c2, sc, cand, count, q, packed, begun, got, other, *refs):
+    out, buf, sems, q4, acc = refs
+    core, col = sc[0], sc[2]
+    load(got, buf, sems, core)
+    load(other, buf, sems, 1 - core)
+    acc[...] = begun[...]
+    spread(packed, q4)
+
+    def step(i, carry):
+        a, j = i // n_cs, i % n_cs
+        dr, dc, _, hit = listed(2 * a * n_cs + j, n_cs, n_c, col, cand, count)
 
         @pl.when(j == 0)
         def _():
-            wait_for(level, buf, sems, a)
+            wait_for(got, buf, sems, a)
 
         @pl.when(hit == 1)
         def _():
-            grad_tile(c2, a, j, dr, dc, core, q, buf, s_scr, d_scr, acc, q4)
+            grad_tile(c2, a, j, dr, dc, core, q, buf, acc, q4)
 
         return carry
 
-    lax.fori_loop(0, 3 * n_cs, step, 0)
+    lax.fori_loop(0, 2 * n_cs, step, 0)
     out[...] = acc[...].reshape(HALF, PADW, acc.shape[1])[:, :TILE]
 
 
@@ -380,7 +411,7 @@
             pltpu.SemaphoreType.DMA((rows,)),
         ]
         + scratch,
-        compiler_params=pltpu.CompilerParams(vmem_limit_bytes=12 * 2**20),
+        compiler_params=pltpu.CompilerParams(vmem_limit_bytes=14 * 2**20),
         cost_estimate=COST,
         name=kernel.__name__,
     )(*ins, *tiles)
@@ -389,9 +420,8 @@
 def query_near(n_c, sc, cand, count, q, level):
     ch, n_cs = q.shape[1], level.shape[0] // (2 * HC)
     out_shape = jax.ShapeDtypeStruct((4, HC, 128), jnp.float32)
-    scratch = [pltpu.VMEM((HC, 1024), jnp.float32)]
     return tiles_call(
-        near_kernel, n_c, ch, 1, n_cs, out_shape, scratch, 1, (sc, cand, count, q), (level,)
+        near_kernel, n_c, ch, 1, n_cs, out_shape, [], 1, (sc, cand, count, q), (level,)
     )
 
 
@@ -402,27 +432,30 @@
         jax.ShapeDtypeStruct((8, HC), jnp.float32),
         jax.ShapeDtypeStruct((HC, 128), jnp.float32),
     )
-    scratch = [pltpu.VMEM((HC, 1024), jnp.float32), pltpu.VMEM((4, HC, 128), jnp.float32)]
+    scratch = [pltpu.VMEM((4, HC, 128), jnp.float32)]
     ins = (sc, cand, count, q, ctg, begun)
     return tiles_call(far_kernel, n_c, ch, 2, n_cs, out_shape, scratch, 3, ins, (got, other))
 
 
-def query_grad(n_c, sc, cand, count, q, packed, level, got, other):
+def grad_near(n_c, sc, cand, count, q, packed, level):
     ch, n_cs = q.shape[1], level.shape[0] // (2 * HC)
+    out_shape = jax.ShapeDtypeStruct((HC, ch), jnp.float32)
+    scratch = [pltpu.VMEM((4, HC, 128), jnp.float32)]
+    ins = (sc, cand, count, q, packed)
+    return tiles_call(grad_near_kernel, n_c, ch, 1, n_cs, out_shape, scratch, 2, ins, (level,))
+
+
+def grad_far(n_c, sc, cand, count, q, packed, begun, got, other):
+    ch, n_cs = q.shape[1], got.shape[0] // (2 * HC)
     out_shape = jax.ShapeDtypeStruct((HALF, TILE, ch), jnp.float32)
-    scratch = [
-        pltpu.VMEM((HC, 512), jnp.float32),
-        pltpu.VMEM((HC, 512), jnp.bfloat16),
-        pltpu.VMEM((4, HC, 128), jnp.float32),
-        pltpu.VMEM((HC, ch), jnp.float32),
-    ]
-    ins, tiles = (sc, cand, count, q, packed), (level, got, other)
-    return tiles_call(grad_kernel, n_c, ch, 3, n_cs, out_shape, scratch, 2, ins, tiles)
+    scratch = [pltpu.VMEM((4, HC, 128), jnp.float32), pltpu.VMEM((HC, ch), jnp.float32)]
+    ins = (sc, cand, count, q, packed, begun)
+    return tiles_call(grad_far_kernel, n_c, ch, 2, n_cs, out_shape, scratch, 3, ins, (got, other))
 
 
 def target_kernel(n_c, n_cs, c2, sc, tgt, *refs):
     feats, stats = refs[:3], refs[3:6]
-    out, buf, sems, st, st_sems, s_scr, d_scr, v_scr, acc = refs[6:]
+    out, buf, sems, st, st_sems, v_scr, acc = refs[6:]
     core, col = sc[0], sc[2]
     load_rows(*stats, st, st_sems, core)
     load_rows(*feats, buf, sems, core)
@@ -448,19 +481,19 @@
                 lax.broadcasted_iota(jnp.int32, (PADW, HC), 0) - 30 * dc
             ).astype(jnp.float32)
             for i in range(2):
-                s_scr[...] = lax.dot_general(
-                    tgt[...], half_tile(buf, a, j, i), (((1,), (1,)), ((), ())), preferred_element_type=jnp.float32
-                )
+                tile = half_tile(buf, a, j, i)
                 four = st[a, pl.ds(pl.multiple_of((2 * j + i) * 8, 8), 8)]
                 lev, gr, gc, sh = (four[k : k + 1] for k in range(4))
                 v_scr[...] = gc * col_t - sh
+                s = lax.dot_general(
+                    tgt[...], tile, (((1,), (1,)), ((), ())), preferred_element_type=jnp.float32
+                )
+                ds = []
                 for g in range(HALF):
-                    rows = slice(g * PADW, (g + 1) * PADW)
                     row_t = (g + HALF * core - 30 * dr).astype(jnp.float32)
-                    p = jnp.exp2(s_scr[rows] * c2 - lev)
-                    d = p * (v_scr[...] + gr * row_t)
-                    d_scr[rows] = d.astype(jnp.bfloat16)
-                acc[...] += jnp.dot(d_scr[...], half_tile(buf, a, j, i), preferred_element_type=jnp.float32)
+                    p = jnp.exp2(s[g * PADW : (g + 1) * PADW] * c2 - lev)
+                    ds.append((p * (v_scr[...] + gr * row_t)).astype(jnp.bfloat16))
+                acc[...] += jnp.dot(jnp.concatenate(ds), tile, preferred_element_type=jnp.float32)
 
         return carry
 
@@ -480,12 +513,10 @@
             pltpu.SemaphoreType.DMA((3,)),
             pltpu.VMEM((3, n_cs * 2 * 8, HC), jnp.float32),
             pltpu.SemaphoreType.DMA((3,)),
-            pltpu.VMEM((HC, HC), jnp.float32),
-            pltpu.VMEM((HC, HC), jnp.bfloat16),
             pltpu.VMEM((PADW, HC), jnp.float32),
             pltpu.VMEM((HC, ch), jnp.float32),
         ],
-        compiler_params=pltpu.CompilerParams(vmem_limit_bytes=12 * 2**20),
+        compiler_params=pltpu.CompilerParams(vmem_limit_bytes=14 * 2**20),
         cost_estimate=COST,
         name="target_side",
     )(sc, tgt, *feats, *stats)
@@ -538,13 +569,17 @@
     flow, stats, packed = query_far(n_c, sc, cand, count, first, ctg, begun, got, other)
     st_side = sideways(stats)
     st_parts = [stats, partner(stats)]
-    for x in st_side:
+    part = grad_near(n_c, sc, cand, count, first, after(packed, st_parts[1]), level)
+    for x in after(tuple(st_side), part):
         st_parts += [x, partner(x)]
     st_level = jnp.concatenate(st_parts)
     st_got = updown(st_level)
-    grad_first = query_grad(n_c, sc, cand, count, first, after(packed, st_level), level, got, other)
-    q_got, st_got = after((q_got, st_got), grad_first)
-    q_other, st_other = partner(q_got), partner(st_got)
+    q_got = after(q_got, st_level)
+    q_other = partner(q_got)
+    packed = after(packed, (st_level, q_got))
+    grad_first = grad_far(n_c, sc, cand, count, first, packed, part, got, other)
+    st_got = after(st_got, grad_first)
+    st_other = partner(st_got)
     grad_second = target_side(
         n_c, sc, second, (q_level, q_got, q_other), (st_level, st_got, st_other)
     )

time: 79.4 us -> 75.4 us (0.950)
  the two profiles are of different devices: /device:TPU:12 before, /device:TPU:0 now
where the time goes in v6:
time: 75.4 us; the launch traced here: 74.5 us
  starting transfers between devices  31.4 us (42%)
  Pallas kernels  26.8 us (36%)
  waiting for transfers between devices  9.18 us (12%)
  local copies, waits for them, and re-layouts  3.35 us (4%)
  other arithmetic  2.22 us (3%)
  between operations  1.53 us (2%)
    ppermute x18, starting transfers between devices, send(): return lax.ppermute(value, AXES, pairs)  31.4 us
    pallas_call x4, Pallas kernels, tiles_call(): pl.pallas_call(functools.partial(kernel, n_c, n_cs, math.log2(math.e) / m...  14.6 us
    ppermute x18, waiting for transfers between devices, send(): return lax.ppermute(value, AXES, pairs)  9.18 us
    pallas_call x2, Pallas kernels, encode(): pl.pallas_call(functools.partial(encode_kernel, frame, n_r, n_c), out_sha...  6.25 us
    pallas_call x1, Pallas kernels, target_side(): pl.pallas_call(functools.partial(target_kernel, n_c, n_cs, math.log2(math...  5.45 us
    unnamed x15, local copies, waits for them, and re-layouts  3.17 us
  transfers between devices with their start and end apart: 18, of which 7 were waited for; matrix products, arithmetic and copies ran while one was open for 4% of the time, Pallas kernels for 24%

profile of v6, /device:TPU:0, one launch (start us, length us, event | category | flops | bytes accessed | tf_op | source)
XLA Modules:
  0.0 74.5 jit_solution(10622552603189248026)
XLA Ops:
  1.9 1.0 %fusion = bf16[1,30,2,256]{3,2,1,0:T(2,128)(2,1)S(1)} fusion(pred[]{:T(512)S(6)} %eq.4, bf16[30,30,256]{2,1,0:T(8,128)(2,1)} %bitcast.36), kind=kLoop, calls=%fused_computation.10 | loop fusion | flops 15360 | bytes 92161 | tf_op jit(solution)/shard_map/stack | solution.py:536
  3.1 2.8 %collective-permute-start.1 = (bf16[2,30,2,256]{3,2,1,0:T(2,128)(2,1)S(1)}, bf16[2,30,2,256]{3,2,1,0:T(2,128)(2,1)S(1)}, u32[]{:S(2)}, u32[]{:S(2)}) collective-permute-start(bf16[2,30,2,256]{3,2,1,0:T(2,128)(2,1)S(1)} %pad_maximum_fusion.3), channel_id=1, source_target_pairs={{0,2},{1,3},{2,0},{3,1},{4,6},{5,7},{6,4},{7,5},{8,10},{9,11},{10,... | collective-permute-start | bytes 184328 | tf_op jit(solution)/shard_map/ppermute | solution.py:36
  5.9 1.3 %copy-done.1 = bf16[9,256,256]{2,1,0:T(8,128)(2,1)S(1)} copy-done((bf16[9,256,256]{2,1,0:T(8,128)(2,1)S(1)}, bf16[9,256,256]{2,1,0:T(8,128)(2,1)}, u32[]{:S(2)}) %copy-start.1) | copy-done | bytes 1179672
  7.2 1.3 %copy-done.2 = bf16[9,256,256]{2,1,0:T(8,128)(2,1)S(1)} copy-done((bf16[9,256,256]{2,1,0:T(8,128)(2,1)S(1)}, bf16[9,256,256]{2,1,0:T(8,128)(2,1)}, u32[]{:S(2)}) %copy-start.2) | copy-done | bytes 1179672
  9.8 3.1 %encode_frame1.1.tgt = bf16[480,256]{1,0:T(8,128)(2,1)S(1)} custom-call(s32[3]{0:T(128)S(1)} %pad_add_fusion.sc, bf16[30,30,256]{2,1,0:T(8,128)(2,1)S(1)} %bitcast.37, bf16[30,30,256]{2,1,0:T(8,128)(2,1)S(1)} %collective-permute-done.got, bf16[2,30,2,256]{3,2,1,0:T(2,128)(2,1)S(1)} %collective-permute-done.1.xl.xr, ...), custom_call_target="tpu_custom_call" | custom-call | flops 1000000 | bytes 10000 | tf_op jit(solution)/shard_map/encode_frame1/pallas_call | solution.py:130
  13.0 1.2 %collective-permute-start.4 = (bf16[480,256]{1,0:T(8,128)(2,1)S(1)}, bf16[480,256]{1,0:T(8,128)(2,1)S(1)}, u32[]{:S(2)}, u32[]{:S(2)}) collective-permute-start(bf16[480,256]{1,0:T(8,128)(2,1)S(1)} %encode_frame1.1.tgt), channel_id=1, source_target_pairs={{0,2},{1,3},{2,0},{3,1},{4,6},{5,7},{6,4},{7,5},{8,10},{9,11},{10,... | collective-permute-start | bytes 737288 | tf_op jit(solution)/shard_map/ppermute | solution.py:36
  14.2 4.7 %collective-permute-start.3 = (bf16[480,256]{1,0:T(8,128)(2,1)S(1)}, bf16[480,256]{1,0:T(8,128)(2,1)S(1)}, u32[]{:S(2)}, u32[]{:S(2)}) collective-permute-start(bf16[480,256]{1,0:T(8,128)(2,1)S(1)} %encode_frame1.1.tgt), channel_id=1, source_target_pairs={{0,1},{1,0},{2,3},{3,2},{4,5},{5,4},{6,7},{7,6},{8,9},{9,8},{10,11... | collective-permute-start | bytes 737288 | tf_op jit(solution)/shard_map/ppermute | solution.py:36
  18.9 3.1 %encode_frame0.1.q = bf16[480,256]{1,0:T(8,128)(2,1)S(1)} custom-call(s32[3]{0:T(128)S(1)} %pad_add_fusion.sc, bf16[30,30,256]{2,1,0:T(8,128)(2,1)S(1)} %bitcast.38, bf16[30,30,256]{2,1,0:T(8,128)(2,1)S(1)} %collective-permute-done.got, bf16[2,30,2,256]{3,2,1,0:T(2,128)(2,1)S(1)} %collective-permute-done.1.xl.xr, ...), custom_call_target="tpu_custom_call" | custom-call | flops 1000000 | bytes 10000 | tf_op jit(solution)/shard_map/encode_frame0/pallas_call | solution.py:130
  22.0 1.0 %collective-permute-start.5 = (bf16[480,256]{1,0:T(8,128)(2,1)S(1)}, bf16[480,256]{1,0:T(8,128)(2,1)S(1)}, u32[]{:S(2)}, u32[]{:S(2)}) collective-permute-start(bf16[480,256]{1,0:T(8,128)(2,1)S(1)} %collective-permute-done.4), channel_id=1, source_target_pairs={{0,1},{1,0},{2,3},{3,2},{4,5},{5,4},{6,7},{7,6},{8,9},{9,8},{10,11... | collective-permute-start | bytes 737288 | tf_op jit(solution)/shard_map/ppermute | solution.py:36
  23.1 1.1 %collective-permute-done.5 = bf16[480,256]{1,0:T(8,128)(2,1)S(1)} collective-permute-done((bf16[480,256]{1,0:T(8,128)(2,1)S(1)}, bf16[480,256]{1,0:T(8,128)(2,1)S(1)}, u32[]{:S(2)}, u32[]{:S(2)}) %collective-permute-start.5) | collective-permute-done | bytes 245792 | tf_op jit(solution)/shard_map/ppermute | solution.py:36
  24.3 7.8 %collective-permute-start.6 = (bf16[1920,256]{1,0:T(8,128)(2,1)S(1)}, bf16[1920,256]{1,0:T(8,128)(2,1)}, u32[]{:S(2)}, u32[]{:S(2)}) collective-permute-start(bf16[1920,256]{1,0:T(8,128)(2,1)S(1)} %pad_maximum_fusion.level), channel_id=1, source_target_pairs={{0,4},{2,6},{4,8},{5,1},{6,10},{7,3},{8,12},{9,5},{10,14},{11,7},{... | collective-permute-start | bytes 2949128 | tf_op jit(solution)/shard_map/ppermute | solution.py:36
  32.1 1.1 %collective-permute-start.8 = (bf16[480,256]{1,0:T(8,128)(2,1)S(1)}, bf16[480,256]{1,0:T(8,128)(2,1)S(1)}, u32[]{:S(2)}, u32[]{:S(2)}) collective-permute-start(bf16[480,256]{1,0:T(8,128)(2,1)S(1)} %encode_frame0.1.q), channel_id=1, source_target_pairs={{0,2},{1,3},{2,0},{3,1},{4,6},{5,7},{6,4},{7,5},{8,10},{9,11},{10,... | collective-permute-start | bytes 737288 | tf_op jit(solution)/shard_map/ppermute | solution.py:36
  33.9 2.8 %near_kernel.1.begun = f32[4,480,128]{2,1,0:T(8,128)S(1)} custom-call(s32[3]{0:T(128)S(1)} %pad_add_fusion.sc, s32[9]{0:T(128)S(1)} %bitcast.39, s32[1]{0:T(128)} %bitcast.27.count, bf16[480,256]{1,0:T(8,128)(2,1)S(1)} %encode_frame0.1.q, bf16[1920,256]{1,0:T(8,128)(2,1)S(1)} %pad_maximum_fusion.level), custom_call_target="tpu_custom_call" | custom-call | flops 1000000 | bytes 10000 | tf_op jit(solution)/shard_map/near_kernel/pallas_call | solution.py:404
  36.7 1.5 %collective-permute-done.8 = bf16[480,256]{1,0:T(8,128)(2,1)S(1)} collective-permute-done((bf16[480,256]{1,0:T(8,128)(2,1)S(1)}, bf16[480,256]{1,0:T(8,128)(2,1)S(1)}, u32[]{:S(2)}, u32[]{:S(2)}) %collective-permute-start.8) | collective-permute-done | bytes 245792 | tf_op jit(solution)/shard_map/ppermute | solution.py:36
  38.3 1.5 %collective-permute-done.9 = bf16[480,256]{1,0:T(8,128)(2,1)S(1)} collective-permute-done((bf16[480,256]{1,0:T(8,128)(2,1)S(1)}, bf16[480,256]{1,0:T(8,128)(2,1)S(1)}, u32[]{:S(2)}, u32[]{:S(2)}) %collective-permute-start.9) | collective-permute-done | bytes 245792 | tf_op jit(solution)/shard_map/ppermute | solution.py:36
  39.8 2.9 %collective-permute-done.6.got = bf16[1920,256]{1,0:T(8,128)(2,1)} collective-permute-done((bf16[1920,256]{1,0:T(8,128)(2,1)S(1)}, bf16[1920,256]{1,0:T(8,128)(2,1)}, u32[]{:S(2)}, u32[]{:S(2)}) %collective-permute-start.6) | collective-permute-done | bytes 983072 | tf_op jit(solution)/shard_map/ppermute | solution.py:36
  42.7 5.4 %collective-permute-start.14 = (bf16[1920,256]{1,0:T(8,128)(2,1)S(1)}, bf16[1920,256]{1,0:T(8,128)(2,1)}, u32[]{:S(2)}, u32[]{:S(2)}) collective-permute-start(bf16[1920,256]{1,0:T(8,128)(2,1)S(1)} %pad_maximum_fusion.1.refs_0_), channel_id=1, source_target_pairs={{0,4},{2,6},{4,8},{5,1},{6,10},{7,3},{8,12},{9,5},{10,14},{11,7},{... | collective-permute-start | bytes 2949128 | tf_op jit(solution)/shard_map/ppermute | solution.py:36
  48.2 4.7 %far_kernel.1 = (f32[2,480]{1,0:T(2,128)S(1)}, f32[8,480]{1,0:T(8,128)S(1)}, f32[480,128]{1,0:T(8,128)S(1)}) custom-call(s32[3]{0:T(128)S(1)} %pad_add_fusion.sc, s32[9]{0:T(128)S(1)} %bitcast.40, s32[1]{0:T(128)} %bitcast.28.count, bf16[480,256]{1,0:T(8,128)(2,1)S(1)} %encode_frame0.1.q, f32[8,480]{1,0:T(8,128)S(1)} %reshape.60.ctg, ...), custom_call_target="tpu_custom_call" | custom-call | flops 1000000 | bytes 10000 | tf_op jit(solution)/shard_map/far_kernel/pallas_call | solution.py:404
  53.0 1.2 %collective-permute-start.12 = (f32[8,480]{1,0:T(8,128)S(1)}, f32[8,480]{1,0:T(8,128)S(1)}, u32[]{:S(2)}, u32[]{:S(2)}) collective-permute-start(f32[8,480]{1,0:T(8,128)S(1)} %get-tuple-element.31), channel_id=1, source_target_pairs={{0,2},{1,3},{2,0},{3,1},{4,6},{5,7},{6,4},{7,5},{8,10},{9,11},{10,... | collective-permute-start | bytes 46088 | tf_op jit(solution)/shard_map/ppermute | solution.py:36
  54.2 2.7 %grad_near_kernel.1.begun = f32[480,256]{1,0:T(8,128)S(1)} custom-call(s32[3]{0:T(128)S(1)} %pad_add_fusion.sc, s32[9]{0:T(128)S(1)} %bitcast.41, s32[1]{0:T(128)} %bitcast.29.count, bf16[480,256]{1,0:T(8,128)(2,1)S(1)} %encode_frame0.1.q, f32[480,128]{1,0:T(8,128)S(1)} %get-tuple-element.35.packed, bf16[1920,256]{1,0:T(8,128)(2,1)S(1)} %pad_maximum_fusion.level), custom_call_target="tpu_custom_call" | custom-call | flops 1000000 | bytes 10000 | tf_op jit(solution)/shard_map/grad_near_kernel/pallas_call | solution.py:404
  57.2 1.0 %collective-permute-done.13 = f32[8,480]{1,0:T(8,128)S(1)} collective-permute-done((f32[8,480]{1,0:T(8,128)S(1)}, f32[8,480]{1,0:T(8,128)S(1)}, u32[]{:S(2)}, u32[]{:S(2)}) %collective-permute-start.13) | collective-permute-done | bytes 15392 | tf_op jit(solution)/shard_map/ppermute | solution.py:36
  59.0 4.3 %collective-permute-start.16 = (f32[32,480]{1,0:T(8,128)S(1)}, f32[32,480]{1,0:T(8,128)S(1)}, u32[]{:S(2)}, u32[]{:S(2)}) collective-permute-start(f32[32,480]{1,0:T(8,128)S(1)} %constant_dynamic-update-slice_fusion.refs_3_), channel_id=1, source_target_pairs={{0,4},{2,6},{4,8},{5,1},{6,10},{7,3},{8,12},{9,5},{10,14},{11,7},{... | collective-permute-start | bytes 184328 | tf_op jit(solution)/shard_map/ppermute | solution.py:36
  63.3 4.4 %grad_far_kernel.1 = f32[15,30,256]{2,1,0:T(8,128)} custom-call(s32[3]{0:T(128)S(1)} %pad_add_fusion.sc, s32[9]{0:T(128)S(1)} %bitcast.42, s32[1]{0:T(128)} %bitcast.30.count, bf16[480,256]{1,0:T(8,128)(2,1)S(1)} %encode_frame0.1.q, f32[480,128]{1,0:T(8,128)S(1)} %get-tuple-element.35.packed, f32[480,256]{1,0:T(8,128)S(1)} %grad_near_kernel.1.begun, ...), custom_call_target="tpu_custom_call" | custom-call | flops 1000000 | bytes 10000 | tf_op jit(solution)/shard_map/grad_far_kernel/pallas_call | solution.py:404
  69.0 5.4 %target_side.1 = f32[15,30,256]{2,1,0:T(8,128)} custom-call(s32[3]{0:T(128)S(1)} %pad_add_fusion.sc, bf16[480,256]{1,0:T(8,128)(2,1)S(1)} %encode_frame1.1.tgt, bf16[1920,256]{1,0:T(8,128)(2,1)S(1)} %pad_maximum_fusion.1.refs_0_, bf16[1920,256]{1,0:T(8,128)(2,1)} %collective-permute-done.14.refs_1_, bf16[1920,256]{1,0:T(8,128)(2,1)S(1)} %collective-permute-done.15.refs_2_, ...), custom_call_target="tpu_custom_call" | custom-call | flops 1000000 | bytes 10000 | tf_op jit(solution)/shard_map/target_side/pallas_call | solution.py:506
  (51 shorter events, 5.5 us)
Async XLA Ops:
  0.6 2.3 %collective-permute-start = (bf16[30,30,256]{2,1,0:T(8,128)(2,1)}, bf16[30,30,256]{2,1,0:T(8,128)(2,1)S(1)}, u32[]{:S(2)}, u32[]{:S(2)}) collective-permute-start(bf16[30,30,256]{2,1,0:T(8,128)(2,1)} %bitcast.35), channel_id=1, source_target_pairs={{0,1},{1,0},{2,3},{3,2},{4,5},{5,4},{6,7},{7,6},{8,9},{9,8},{10,11... | collective-permute-start | bytes 1382408 | tf_op jit(solution)/shard_map/ppermute | solution.py:36
  3.1 5.9 %collective-permute-start.1 = (bf16[2,30,2,256]{3,2,1,0:T(2,128)(2,1)S(1)}, bf16[2,30,2,256]{3,2,1,0:T(2,128)(2,1)S(1)}, u32[]{:S(2)}, u32[]{:S(2)}) collective-permute-start(bf16[2,30,2,256]{3,2,1,0:T(2,128)(2,1)S(1)} %pad_maximum_fusion.3), channel_id=1, source_target_pairs={{0,2},{1,3},{2,0},{3,1},{4,6},{5,7},{6,4},{7,5},{8,10},{9,11},{10,... | collective-permute-start | bytes 184328 | tf_op jit(solution)/shard_map/ppermute | solution.py:36
  5.9 1.3 %copy-start.1 = (bf16[9,256,256]{2,1,0:T(8,128)(2,1)S(1)}, bf16[9,256,256]{2,1,0:T(8,128)(2,1)}, u32[]{:S(2)}) copy-start(bf16[9,256,256]{2,1,0:T(8,128)(2,1)} %a) | copy-start | bytes 3538948
  7.2 1.3 %copy-start.2 = (bf16[9,256,256]{2,1,0:T(8,128)(2,1)S(1)}, bf16[9,256,256]{2,1,0:T(8,128)(2,1)}, u32[]{:S(2)}) copy-start(bf16[9,256,256]{2,1,0:T(8,128)(2,1)} %b.1) | copy-start | bytes 3538948
  8.5 1.4 %copy-start = (bf16[1,30,30,256]{3,2,1,0:T(8,128)(2,1)S(1)}, bf16[1,30,30,256]{3,2,1,0:T(8,128)(2,1)}, u32[]{:S(2)}) copy-start(bf16[1,30,30,256]{3,2,1,0:T(8,128)(2,1)} %param.6) | copy-start | bytes 1382404
  9.1 0.8 %collective-permute-start.2 = (bf16[2,2,34,256]{3,2,1,0:T(8,128)(2,1)S(1)}, bf16[2,2,34,256]{3,2,1,0:T(8,128)(2,1)S(1)}, u32[]{:S(2)}, u32[]{:S(2)}) collective-permute-start(bf16[2,2,34,256]{3,2,1,0:T(8,128)(2,1)S(1)} %pad_maximum_fusion.2), channel_id=1, source_target_pairs={{1,4},{3,6},{4,1},{5,8},{6,3},{7,10},{8,5},{9,12},{10,7},{11,14},{... | collective-permute-start | bytes 208904 | tf_op jit(solution)/shard_map/ppermute | solution.py:36
  13.0 9.0 %collective-permute-start.4 = (bf16[480,256]{1,0:T(8,128)(2,1)S(1)}, bf16[480,256]{1,0:T(8,128)(2,1)S(1)}, u32[]{:S(2)}, u32[]{:S(2)}) collective-permute-start(bf16[480,256]{1,0:T(8,128)(2,1)S(1)} %encode_frame1.1.tgt), channel_id=1, source_target_pairs={{0,2},{1,3},{2,0},{3,1},{4,6},{5,7},{6,4},{7,5},{8,10},{9,11},{10,... | collective-permute-start | bytes 737288 | tf_op jit(solution)/shard_map/ppermute | solution.py:36
  14.2 8.9 %collective-permute-start.3 = (bf16[480,256]{1,0:T(8,128)(2,1)S(1)}, bf16[480,256]{1,0:T(8,128)(2,1)S(1)}, u32[]{:S(2)}, u32[]{:S(2)}) collective-permute-start(bf16[480,256]{1,0:T(8,128)(2,1)S(1)} %encode_frame1.1.tgt), channel_id=1, source_target_pairs={{0,1},{1,0},{2,3},{3,2},{4,5},{5,4},{6,7},{7,6},{8,9},{9,8},{10,11... | collective-permute-start | bytes 737288 | tf_op jit(solution)/shard_map/ppermute | solution.py:36
  22.0 11.9 %copy-start.3 = (s32[1,1,9]{2,1,0:T(1,128)S(1)}, s32[1,1,9]{2,1,0:T(1,128)}, u32[]{:S(2)}) copy-start(s32[1,1,9]{2,1,0:T(1,128)} %param.9) | copy-start | bytes 112
  22.0 2.2 %collective-permute-start.5 = (bf16[480,256]{1,0:T(8,128)(2,1)S(1)}, bf16[480,256]{1,0:T(8,128)(2,1)S(1)}, u32[]{:S(2)}, u32[]{:S(2)}) collective-permute-start(bf16[480,256]{1,0:T(8,128)(2,1)S(1)} %collective-permute-done.4), channel_id=1, source_target_pairs={{0,1},{1,0},{2,3},{3,2},{4,5},{5,4},{6,7},{7,6},{8,9},{9,8},{10,11... | collective-permute-start | bytes 737288 | tf_op jit(solution)/shard_map/ppermute | solution.py:36
  24.3 18.4 %collective-permute-start.6 = (bf16[1920,256]{1,0:T(8,128)(2,1)S(1)}, bf16[1920,256]{1,0:T(8,128)(2,1)}, u32[]{:S(2)}, u32[]{:S(2)}) collective-permute-start(bf16[1920,256]{1,0:T(8,128)(2,1)S(1)} %pad_maximum_fusion.level), channel_id=1, source_target_pairs={{0,4},{2,6},{4,8},{5,1},{6,10},{7,3},{8,12},{9,5},{10,14},{11,7},{... | collective-permute-start | bytes 2949128 | tf_op jit(solution)/shard_map/ppermute | solution.py:36
  32.1 6.2 %collective-permute-start.8 = (bf16[480,256]{1,0:T(8,128)(2,1)S(1)}, bf16[480,256]{1,0:T(8,128)(2,1)S(1)}, u32[]{:S(2)}, u32[]{:S(2)}) collective-permute-start(bf16[480,256]{1,0:T(8,128)(2,1)S(1)} %encode_frame0.1.q), channel_id=1, source_target_pairs={{0,2},{1,3},{2,0},{3,1},{4,6},{5,7},{6,4},{7,5},{8,10},{9,11},{10,... | collective-permute-start | bytes 737288 | tf_op jit(solution)/shard_map/ppermute | solution.py:36
  33.9 4.4 %collective-permute-start.7 = (bf16[480,256]{1,0:T(8,128)(2,1)S(1)}, bf16[480,256]{1,0:T(8,128)(2,1)S(1)}, u32[]{:S(2)}, u32[]{:S(2)}) collective-permute-start(bf16[480,256]{1,0:T(8,128)(2,1)S(1)} %encode_frame0.1.q), channel_id=1, source_target_pairs={{0,1},{1,0},{2,3},{3,2},{4,5},{5,4},{6,7},{7,6},{8,9},{9,8},{10,11... | collective-permute-start | bytes 737288 | tf_op jit(solution)/shard_map/ppermute | solution.py:36
  36.7 11.4 %copy-start.4 = (f32[2,15,30]{2,0,1:T(2,128)S(1)}, f32[2,15,30]{2,0,1:T(2,128)}, u32[]{:S(2)}) copy-start(f32[2,15,30]{2,0,1:T(2,128)} %param.11) | copy-start | bytes 10804
  38.3 1.5 %collective-permute-start.9 = (bf16[480,256]{1,0:T(8,128)(2,1)S(1)}, bf16[480,256]{1,0:T(8,128)(2,1)S(1)}, u32[]{:S(2)}, u32[]{:S(2)}) collective-permute-start(bf16[480,256]{1,0:T(8,128)(2,1)S(1)} %collective-permute-done.8), channel_id=1, source_target_pairs={{0,1},{1,0},{2,3},{3,2},{4,5},{5,4},{6,7},{7,6},{8,9},{9,8},{10,11... | collective-permute-start | bytes 737288 | tf_op jit(solution)/shard_map/ppermute | solution.py:36
  42.7 5.5 %collective-permute-start.10 = (bf16[1920,256]{1,0:T(8,128)(2,1)}, bf16[1920,256]{1,0:T(8,128)(2,1)}, u32[]{:S(2)}, u32[]{:S(2)}) collective-permute-start(bf16[1920,256]{1,0:T(8,128)(2,1)} %collective-permute-done.6.got), channel_id=1, source_target_pairs={{0,1},{1,0},{2,3},{3,2},{4,5},{5,4},{6,7},{7,6},{8,9},{9,8},{10,11... | collective-permute-start | bytes 2949128 | tf_op jit(solution)/shard_map/ppermute | solution.py:36
  42.7 16.1 %collective-permute-start.14 = (bf16[1920,256]{1,0:T(8,128)(2,1)S(1)}, bf16[1920,256]{1,0:T(8,128)(2,1)}, u32[]{:S(2)}, u32[]{:S(2)}) collective-permute-start(bf16[1920,256]{1,0:T(8,128)(2,1)S(1)} %pad_maximum_fusion.1.refs_0_), channel_id=1, source_target_pairs={{0,4},{2,6},{4,8},{5,1},{6,10},{7,3},{8,12},{9,5},{10,14},{11,7},{... | collective-permute-start | bytes 2949128 | tf_op jit(solution)/shard_map/ppermute | solution.py:36
  52.9 1.3 %collective-permute-start.11 = (f32[8,480]{1,0:T(8,128)S(1)}, f32[8,480]{1,0:T(8,128)S(1)}, u32[]{:S(2)}, u32[]{:S(2)}) collective-permute-start(f32[8,480]{1,0:T(8,128)S(1)} %get-tuple-element.31), channel_id=1, source_target_pairs={{0,1},{1,0},{2,3},{3,2},{4,5},{5,4},{6,7},{7,6},{8,9},{9,8},{10,11... | collective-permute-start | bytes 46088 | tf_op jit(solution)/shard_map/ppermute | solution.py:36
  53.0 3.9 %collective-permute-start.12 = (f32[8,480]{1,0:T(8,128)S(1)}, f32[8,480]{1,0:T(8,128)S(1)}, u32[]{:S(2)}, u32[]{:S(2)}) collective-permute-start(f32[8,480]{1,0:T(8,128)S(1)} %get-tuple-element.31), channel_id=1, source_target_pairs={{0,2},{1,3},{2,0},{3,1},{4,6},{5,7},{6,4},{7,5},{8,10},{9,11},{10,... | collective-permute-start | bytes 46088 | tf_op jit(solution)/shard_map/ppermute | solution.py:36
  56.9 1.2 %collective-permute-start.13 = (f32[8,480]{1,0:T(8,128)S(1)}, f32[8,480]{1,0:T(8,128)S(1)}, u32[]{:S(2)}, u32[]{:S(2)}) collective-permute-start(f32[8,480]{1,0:T(8,128)S(1)} %collective-permute-done.12), channel_id=1, source_target_pairs={{0,1},{1,0},{2,3},{3,2},{4,5},{5,4},{6,7},{7,6},{8,9},{9,8},{10,11... | collective-permute-start | bytes 46088 | tf_op jit(solution)/shard_map/ppermute | solution.py:36
  58.8 10.3 %collective-permute-start.15 = (bf16[1920,256]{1,0:T(8,128)(2,1)}, bf16[1920,256]{1,0:T(8,128)(2,1)S(1)}, u32[]{:S(2)}, u32[]{:S(2)}) collective-permute-start(bf16[1920,256]{1,0:T(8,128)(2,1)} %collective-permute-done.14.refs_1_), channel_id=1, source_target_pairs={{0,1},{1,0},{2,3},{3,2},{4,5},{5,4},{6,7},{7,6},{8,9},{9,8},{10,11... | collective-permute-start | bytes 2949128 | tf_op jit(solution)/shard_map/ppermute | solution.py:36
  59.0 8.7 %collective-permute-start.16 = (f32[32,480]{1,0:T(8,128)S(1)}, f32[32,480]{1,0:T(8,128)S(1)}, u32[]{:S(2)}, u32[]{:S(2)}) collective-permute-start(f32[32,480]{1,0:T(8,128)S(1)} %constant_dynamic-update-slice_fusion.refs_3_), channel_id=1, source_target_pairs={{0,4},{2,6},{4,8},{5,1},{6,10},{7,3},{8,12},{9,5},{10,14},{11,7},{... | collective-permute-start | bytes 184328 | tf_op jit(solution)/shard_map/ppermute | solution.py:36
  67.7 1.3 %collective-permute-start.17 = (f32[32,480]{1,0:T(8,128)S(1)}, f32[32,480]{1,0:T(8,128)S(1)}, u32[]{:S(2)}, u32[]{:S(2)}) collective-permute-start(f32[32,480]{1,0:T(8,128)S(1)} %collective-permute-done.16.refs_4_), channel_id=1, source_target_pairs={{0,1},{1,0},{2,3},{3,2},{4,5},{5,4},{6,7},{7,6},{8,9},{9,8},{10,11... | collective-permute-start | bytes 184328 | tf_op jit(solution)/shard_map/ppermute | solution.py:36

commit v7 on v6

--- a/solution.py
+++ b/solution.py
@@ -282,45 +282,38 @@
         return carry
 
     lax.fori_loop(0, 2 * n_cs, step, 0)
-    wide, ok, _ = lanes(HC)
-    norm = state[1]
-    n_sum = jnp.sum(jnp.where(ok, norm, 0.0), axis=1, keepdims=True)
-    r_sum = jnp.sum(
-        jnp.where(ok, state[2] + (wide // PADW).astype(jnp.float32) * norm, 0.0),
-        axis=1,
-        keepdims=True,
-    )
-    c_sum = jnp.sum(
-        jnp.where(ok, state[3] + (wide % PADW).astype(jnp.float32) * norm, 0.0),
-        axis=1,
-        keepdims=True,
-    )
-    cell = lax.broadcasted_iota(jnp.int32, (HC, 128), 0)
+    where_at = lax.broadcasted_iota(jnp.int32, (128, HC), 0)
+    ok = where_at % PADW < TILE
+    norm = jnp.transpose(state[1])
+    rows = jnp.transpose(state[2]) + (where_at // PADW).astype(jnp.float32) * norm
+    cols = jnp.transpose(state[3]) + (where_at % PADW).astype(jnp.float32) * norm
+    n_sum, r_sum, c_sum = (
+        jnp.sum(jnp.where(ok, x, 0.0), axis=0, keepdims=True) for x in (norm, rows, cols)
+    )
+    cell = lax.broadcasted_iota(jnp.int32, (1, HC), 1)
     q_row = (cell // PADW + HALF * core).astype(jnp.float32)
     q_col = (cell % PADW).astype(jnp.float32)
     mean_r = r_sum / n_sum
     mean_c = c_sum / n_sum
-    pulls = jnp.transpose(
-        jnp.concatenate([ctg[...], jnp.zeros((120, HC), jnp.float32)], axis=0)
-    )
     scale = 1.0 / (TILE * math.sqrt(q.shape[1]))
-    cr = pulls[:, 0:1] * scale
-    cc = pulls[:, 1:2] * scale
+    cr = ctg[0:1] * scale
+    cc = ctg[1:2] * scale
     shift = cr * mean_r + cc * mean_c
-    level2 = jnp.where(q_col < TILE, state[0] + jnp.log2(n_sum), 1e30)
-    flags = jnp.zeros((HC, 128), jnp.float32)
+    best = jnp.transpose(state[0])[0:1]
+    level2 = jnp.where(q_col < TILE, best + jnp.log2(n_sum), 1e30)
+    flags = jnp.zeros((1, HC), jnp.float32)
     for slot in range(3 * n_cs):
         _, _, code, hit = listed(slot, n_cs, n_c, col, cand, count)
         flags = jnp.where((cell == code) & (hit == 1), 1.0, flags)
-    packed = flags
-    for k, value in enumerate(
-        (level2, cr, cc, shift, flags, (mean_r - q_row) / TILE, (mean_c - q_col) / TILE)
-    ):
-        packed = jnp.where(wide == k, value, packed)
-    packed_out[...] = packed
-    turned = jnp.transpose(packed)
-    stats[...] = turned[0:8]
-    flow[...] = turned[5:7]
+    flow_r, flow_c = (mean_r - q_row) / TILE, (mean_c - q_col) / TILE
+    eight = jnp.concatenate(
+        [level2, cr, cc, shift, flags, flow_r, flow_c, jnp.zeros((1, HC), jnp.float32)], axis=0
+    )
+    stats[...] = eight
+    flow[...] = eight[5:7]
+    packed_out[...] = jnp.transpose(
+        jnp.concatenate([eight, jnp.zeros((120, HC), jnp.float32)], axis=0)
+    )
 
 
 def spread(packed, q4):

time: 75.4 us -> 76 us (level)
  the two profiles are of different devices: /device:TPU:0 before, /device:TPU:12 now
where the time goes in v7:
time: 76 us; the launch traced here: 75.7 us
  Pallas kernels  28.1 us (37%)
  waiting for transfers between devices  23.7 us (31%)
  starting transfers between devices  16.7 us (22%)
  local copies, waits for them, and re-layouts  3.35 us (4%)
  other arithmetic  2.22 us (3%)
  between operations  1.58 us (2%)
    ppermute x18, waiting for transfers between devices, send(): return lax.ppermute(value, AXES, pairs)  23.7 us
    ppermute x18, starting transfers between devices, send(): return lax.ppermute(value, AXES, pairs)  16.7 us
    pallas_call x4, Pallas kernels, tiles_call(): pl.pallas_call(functools.partial(kernel, n_c, n_cs, math.log2(math.e) / m...  13.8 us
    pallas_call x1, Pallas kernels, target_side(): pl.pallas_call(functools.partial(target_kernel, n_c, n_cs, math.log2(math...  7.63 us
    pallas_call x2, Pallas kernels, encode(): pl.pallas_call(functools.partial(encode_kernel, frame, n_r, n_c), out_sha...  6.25 us
    unnamed x15, local copies, waits for them, and re-layouts  3.17 us
  transfers between devices with their start and end apart: 18, of which 12 were waited for; matrix products, arithmetic and copies ran while one was open for 4% of the time, Pallas kernels for 23%

profile of v7, /device:TPU:12, one launch (start us, length us, event | category | flops | bytes accessed | tf_op | source)
XLA Modules:
  0.0 75.7 jit_solution(12267032102053207783)
XLA Ops:
  2.9 1.6 %collective-permute-start.1 = (bf16[2,30,2,256]{3,2,1,0:T(2,128)(2,1)S(1)}, bf16[2,30,2,256]{3,2,1,0:T(2,128)(2,1)S(1)}, u32[]{:S(2)}, u32[]{:S(2)}) collective-permute-start(bf16[2,30,2,256]{3,2,1,0:T(2,128)(2,1)S(1)} %pad_maximum_fusion.3), channel_id=1, source_target_pairs={{0,2},{1,3},{2,0},{3,1},{4,6},{5,7},{6,4},{7,5},{8,10},{9,11},{10,... | collective-permute-start | bytes 184328 | tf_op jit(solution)/shard_map/ppermute | solution.py:36
  4.5 1.3 %copy-done.1 = bf16[9,256,256]{2,1,0:T(8,128)(2,1)S(1)} copy-done((bf16[9,256,256]{2,1,0:T(8,128)(2,1)S(1)}, bf16[9,256,256]{2,1,0:T(8,128)(2,1)}, u32[]{:S(2)}) %copy-start.1) | copy-done | bytes 1179672
  5.8 1.3 %copy-done.2 = bf16[9,256,256]{2,1,0:T(8,128)(2,1)S(1)} copy-done((bf16[9,256,256]{2,1,0:T(8,128)(2,1)S(1)}, bf16[9,256,256]{2,1,0:T(8,128)(2,1)}, u32[]{:S(2)}) %copy-start.2) | copy-done | bytes 1179672
  7.6 1.9 %collective-permute-start.2 = (bf16[2,2,34,256]{3,2,1,0:T(8,128)(2,1)S(1)}, bf16[2,2,34,256]{3,2,1,0:T(8,128)(2,1)S(1)}, u32[]{:S(2)}, u32[]{:S(2)}) collective-permute-start(bf16[2,2,34,256]{3,2,1,0:T(8,128)(2,1)S(1)} %pad_maximum_fusion.2), channel_id=1, source_target_pairs={{1,4},{3,6},{4,1},{5,8},{6,3},{7,10},{8,5},{9,12},{10,7},{11,14},{... | collective-permute-start | bytes 208904 | tf_op jit(solution)/shard_map/ppermute | solution.py:36
  9.7 3.7 %collective-permute-done.2.z = bf16[2,2,34,256]{3,2,1,0:T(8,128)(2,1)S(1)} collective-permute-done((bf16[2,2,34,256]{3,2,1,0:T(8,128)(2,1)S(1)}, bf16[2,2,34,256]{3,2,1,0:T(8,128)(2,1)S(1)}, u32[]{:S(2)}, u32[]{:S(2)}) %collective-permute-start.2) | collective-permute-done | bytes 69664 | tf_op jit(solution)/shard_map/ppermute | solution.py:36
  13.4 3.1 %encode_frame1.1.tgt = bf16[480,256]{1,0:T(8,128)(2,1)S(1)} custom-call(s32[3]{0:T(128)S(1)} %pad_add_fusion.sc, bf16[30,30,256]{2,1,0:T(8,128)(2,1)S(1)} %bitcast.37, bf16[30,30,256]{2,1,0:T(8,128)(2,1)S(1)} %collective-permute-done.got, bf16[2,30,2,256]{3,2,1,0:T(2,128)(2,1)S(1)} %collective-permute-done.1.xl.xr, ...), custom_call_target="tpu_custom_call" | custom-call | flops 1000000 | bytes 10000 | tf_op jit(solution)/shard_map/encode_frame1/pallas_call | solution.py:130
  16.5 1.2 %collective-permute-start.4 = (bf16[480,256]{1,0:T(8,128)(2,1)S(1)}, bf16[480,256]{1,0:T(8,128)(2,1)S(1)}, u32[]{:S(2)}, u32[]{:S(2)}) collective-permute-start(bf16[480,256]{1,0:T(8,128)(2,1)S(1)} %encode_frame1.1.tgt), channel_id=1, source_target_pairs={{0,2},{1,3},{2,0},{3,1},{4,6},{5,7},{6,4},{7,5},{8,10},{9,11},{10,... | collective-permute-start | bytes 737288 | tf_op jit(solution)/shard_map/ppermute | solution.py:36
  17.7 3.1 %encode_frame0.1.q = bf16[480,256]{1,0:T(8,128)(2,1)S(1)} custom-call(s32[3]{0:T(128)S(1)} %pad_add_fusion.sc, bf16[30,30,256]{2,1,0:T(8,128)(2,1)S(1)} %bitcast.38, bf16[30,30,256]{2,1,0:T(8,128)(2,1)S(1)} %collective-permute-done.got, bf16[2,30,2,256]{3,2,1,0:T(2,128)(2,1)S(1)} %collective-permute-done.1.xl.xr, ...), custom_call_target="tpu_custom_call" | custom-call | flops 1000000 | bytes 10000 | tf_op jit(solution)/shard_map/encode_frame0/pallas_call | solution.py:130
  20.9 3.7 %collective-permute-done.4 = bf16[480,256]{1,0:T(8,128)(2,1)S(1)} collective-permute-done((bf16[480,256]{1,0:T(8,128)(2,1)S(1)}, bf16[480,256]{1,0:T(8,128)(2,1)S(1)}, u32[]{:S(2)}, u32[]{:S(2)}) %collective-permute-start.4) | collective-permute-done | bytes 245792 | tf_op jit(solution)/shard_map/ppermute | solution.py:36
  24.6 1.5 %collective-permute-done.5 = bf16[480,256]{1,0:T(8,128)(2,1)S(1)} collective-permute-done((bf16[480,256]{1,0:T(8,128)(2,1)S(1)}, bf16[480,256]{1,0:T(8,128)(2,1)S(1)}, u32[]{:S(2)}, u32[]{:S(2)}) %collective-permute-start.5) | collective-permute-done | bytes 245792 | tf_op jit(solution)/shard_map/ppermute | solution.py:36
  26.1 3.5 %collective-permute-start.6 = (bf16[1920,256]{1,0:T(8,128)(2,1)S(1)}, bf16[1920,256]{1,0:T(8,128)(2,1)}, u32[]{:S(2)}, u32[]{:S(2)}) collective-permute-start(bf16[1920,256]{1,0:T(8,128)(2,1)S(1)} %pad_maximum_fusion.level), channel_id=1, source_target_pairs={{0,4},{2,6},{4,8},{5,1},{6,10},{7,3},{8,12},{9,5},{10,14},{11,7},{... | collective-permute-start | bytes 2949128 | tf_op jit(solution)/shard_map/ppermute | solution.py:36
  29.6 1.2 %collective-permute-start.8 = (bf16[480,256]{1,0:T(8,128)(2,1)S(1)}, bf16[480,256]{1,0:T(8,128)(2,1)S(1)}, u32[]{:S(2)}, u32[]{:S(2)}) collective-permute-start(bf16[480,256]{1,0:T(8,128)(2,1)S(1)} %encode_frame0.1.q), channel_id=1, source_target_pairs={{0,2},{1,3},{2,0},{3,1},{4,6},{5,7},{6,4},{7,5},{8,10},{9,11},{10,... | collective-permute-start | bytes 737288 | tf_op jit(solution)/shard_map/ppermute | solution.py:36
  31.6 1.9 %near_kernel.1.begun = f32[4,480,128]{2,1,0:T(8,128)S(1)} custom-call(s32[3]{0:T(128)S(1)} %pad_add_fusion.sc, s32[9]{0:T(128)S(1)} %bitcast.39, s32[1]{0:T(128)} %bitcast.27.count, bf16[480,256]{1,0:T(8,128)(2,1)S(1)} %encode_frame0.1.q, bf16[1920,256]{1,0:T(8,128)(2,1)S(1)} %pad_maximum_fusion.level), custom_call_target="tpu_custom_call" | custom-call | flops 1000000 | bytes 10000 | tf_op jit(solution)/shard_map/near_kernel/pallas_call | solution.py:397
  33.5 2.6 %collective-permute-done.8 = bf16[480,256]{1,0:T(8,128)(2,1)S(1)} collective-permute-done((bf16[480,256]{1,0:T(8,128)(2,1)S(1)}, bf16[480,256]{1,0:T(8,128)(2,1)S(1)}, u32[]{:S(2)}, u32[]{:S(2)}) %collective-permute-start.8) | collective-permute-done | bytes 245792 | tf_op jit(solution)/shard_map/ppermute | solution.py:36
  36.1 1.5 %collective-permute-done.9 = bf16[480,256]{1,0:T(8,128)(2,1)S(1)} collective-permute-done((bf16[480,256]{1,0:T(8,128)(2,1)S(1)}, bf16[480,256]{1,0:T(8,128)(2,1)S(1)}, u32[]{:S(2)}, u32[]{:S(2)}) %collective-permute-start.9) | collective-permute-done | bytes 245792 | tf_op jit(solution)/shard_map/ppermute | solution.py:36
  37.7 4.5 %collective-permute-done.6.got = bf16[1920,256]{1,0:T(8,128)(2,1)} collective-permute-done((bf16[1920,256]{1,0:T(8,128)(2,1)S(1)}, bf16[1920,256]{1,0:T(8,128)(2,1)}, u32[]{:S(2)}, u32[]{:S(2)}) %collective-permute-start.6) | collective-permute-done | bytes 983072 | tf_op jit(solution)/shard_map/ppermute | solution.py:36
  42.2 3.5 %collective-permute-start.14 = (bf16[1920,256]{1,0:T(8,128)(2,1)S(1)}, bf16[1920,256]{1,0:T(8,128)(2,1)}, u32[]{:S(2)}, u32[]{:S(2)}) collective-permute-start(bf16[1920,256]{1,0:T(8,128)(2,1)S(1)} %pad_maximum_fusion.1.refs_0_), channel_id=1, source_target_pairs={{0,4},{2,6},{4,8},{5,1},{6,10},{7,3},{8,12},{9,5},{10,14},{11,7},{... | collective-permute-start | bytes 2949128 | tf_op jit(solution)/shard_map/ppermute | solution.py:36
  45.9 5.0 %far_kernel.1 = (f32[2,480]{1,0:T(2,128)S(1)}, f32[8,480]{1,0:T(8,128)S(1)}, f32[480,128]{1,0:T(8,128)S(1)}) custom-call(s32[3]{0:T(128)S(1)} %pad_add_fusion.sc, s32[9]{0:T(128)S(1)} %bitcast.40, s32[1]{0:T(128)} %bitcast.28.count, bf16[480,256]{1,0:T(8,128)(2,1)S(1)} %encode_frame0.1.q, f32[8,480]{1,0:T(8,128)S(1)} %reshape.60.ctg, ...), custom_call_target="tpu_custom_call" | custom-call | flops 1000000 | bytes 10000 | tf_op jit(solution)/shard_map/far_kernel/pallas_call | solution.py:397
  52.1 2.0 %grad_near_kernel.1.begun = f32[480,256]{1,0:T(8,128)S(1)} custom-call(s32[3]{0:T(128)S(1)} %pad_add_fusion.sc, s32[9]{0:T(128)S(1)} %bitcast.41, s32[1]{0:T(128)} %bitcast.29.count, bf16[480,256]{1,0:T(8,128)(2,1)S(1)} %encode_frame0.1.q, f32[480,128]{1,0:T(8,128)S(1)} %get-tuple-element.35.packed, bf16[1920,256]{1,0:T(8,128)(2,1)S(1)} %pad_maximum_fusion.level), custom_call_target="tpu_custom_call" | custom-call | flops 1000000 | bytes 10000 | tf_op jit(solution)/shard_map/grad_near_kernel/pallas_call | solution.py:397
  54.8 1.2 %collective-permute-done.13 = f32[8,480]{1,0:T(8,128)S(1)} collective-permute-done((f32[8,480]{1,0:T(8,128)S(1)}, f32[8,480]{1,0:T(8,128)S(1)}, u32[]{:S(2)}, u32[]{:S(2)}) %collective-permute-start.13) | collective-permute-done | bytes 15392 | tf_op jit(solution)/shard_map/ppermute | solution.py:36
  55.9 2.4 %collective-permute-done.14.refs_1_ = bf16[1920,256]{1,0:T(8,128)(2,1)} collective-permute-done((bf16[1920,256]{1,0:T(8,128)(2,1)S(1)}, bf16[1920,256]{1,0:T(8,128)(2,1)}, u32[]{:S(2)}, u32[]{:S(2)}) %collective-permute-start.14) | collective-permute-done | bytes 983072 | tf_op jit(solution)/shard_map/ppermute | solution.py:36
  58.3 3.5 %collective-permute-start.16 = (f32[32,480]{1,0:T(8,128)S(1)}, f32[32,480]{1,0:T(8,128)S(1)}, u32[]{:S(2)}, u32[]{:S(2)}) collective-permute-start(f32[32,480]{1,0:T(8,128)S(1)} %constant_dynamic-update-slice_fusion.refs_3_), channel_id=1, source_target_pairs={{0,4},{2,6},{4,8},{5,1},{6,10},{7,3},{8,12},{9,5},{10,14},{11,7},{... | collective-permute-start | bytes 184328 | tf_op jit(solution)/shard_map/ppermute | solution.py:36
  61.8 4.9 %grad_far_kernel.1 = f32[15,30,256]{2,1,0:T(8,128)} custom-call(s32[3]{0:T(128)S(1)} %pad_add_fusion.sc, s32[9]{0:T(128)S(1)} %bitcast.42, s32[1]{0:T(128)} %bitcast.30.count, bf16[480,256]{1,0:T(8,128)(2,1)S(1)} %encode_frame0.1.q, f32[480,128]{1,0:T(8,128)S(1)} %get-tuple-element.35.packed, f32[480,256]{1,0:T(8,128)S(1)} %grad_near_kernel.1.begun, ...), custom_call_target="tpu_custom_call" | custom-call | flops 1000000 | bytes 10000 | tf_op jit(solution)/shard_map/grad_far_kernel/pallas_call | solution.py:397
  68.1 7.6 %target_side.1 = f32[15,30,256]{2,1,0:T(8,128)} custom-call(s32[3]{0:T(128)S(1)} %pad_add_fusion.sc, bf16[480,256]{1,0:T(8,128)(2,1)S(1)} %encode_frame1.1.tgt, bf16[1920,256]{1,0:T(8,128)(2,1)S(1)} %pad_maximum_fusion.1.refs_0_, bf16[1920,256]{1,0:T(8,128)(2,1)} %collective-permute-done.14.refs_1_, bf16[1920,256]{1,0:T(8,128)(2,1)S(1)} %collective-permute-done.15.refs_2_, ...), custom_call_target="tpu_custom_call" | custom-call | flops 1000000 | bytes 10000 | tf_op jit(solution)/shard_map/target_side/pallas_call | solution.py:499
  (51 shorter events, 6.4 us)
Async XLA Ops:
  0.6 2.1 %collective-permute-start = (bf16[30,30,256]{2,1,0:T(8,128)(2,1)}, bf16[30,30,256]{2,1,0:T(8,128)(2,1)S(1)}, u32[]{:S(2)}, u32[]{:S(2)}) collective-permute-start(bf16[30,30,256]{2,1,0:T(8,128)(2,1)} %bitcast.35), channel_id=1, source_target_pairs={{0,1},{1,0},{2,3},{3,2},{4,5},{5,4},{6,7},{7,6},{8,9},{9,8},{10,11... | collective-permute-start | bytes 1382408 | tf_op jit(solution)/shard_map/ppermute | solution.py:36
  2.9 4.6 %collective-permute-start.1 = (bf16[2,30,2,256]{3,2,1,0:T(2,128)(2,1)S(1)}, bf16[2,30,2,256]{3,2,1,0:T(2,128)(2,1)S(1)}, u32[]{:S(2)}, u32[]{:S(2)}) collective-permute-start(bf16[2,30,2,256]{3,2,1,0:T(2,128)(2,1)S(1)} %pad_maximum_fusion.3), channel_id=1, source_target_pairs={{0,2},{1,3},{2,0},{3,1},{4,6},{5,7},{6,4},{7,5},{8,10},{9,11},{10,... | collective-permute-start | bytes 184328 | tf_op jit(solution)/shard_map/ppermute | solution.py:36
  4.5 1.3 %copy-start.1 = (bf16[9,256,256]{2,1,0:T(8,128)(2,1)S(1)}, bf16[9,256,256]{2,1,0:T(8,128)(2,1)}, u32[]{:S(2)}) copy-start(bf16[9,256,256]{2,1,0:T(8,128)(2,1)} %a) | copy-start | bytes 3538948
  5.8 1.3 %copy-start.2 = (bf16[9,256,256]{2,1,0:T(8,128)(2,1)S(1)}, bf16[9,256,256]{2,1,0:T(8,128)(2,1)}, u32[]{:S(2)}) copy-start(bf16[9,256,256]{2,1,0:T(8,128)(2,1)} %b.1) | copy-start | bytes 3538948
  7.0 6.4 %copy-start = (bf16[1,30,30,256]{3,2,1,0:T(8,128)(2,1)S(1)}, bf16[1,30,30,256]{3,2,1,0:T(8,128)(2,1)}, u32[]{:S(2)}) copy-start(bf16[1,30,30,256]{3,2,1,0:T(8,128)(2,1)} %param.6) | copy-start | bytes 1382404
  7.6 5.8 %collective-permute-start.2 = (bf16[2,2,34,256]{3,2,1,0:T(8,128)(2,1)S(1)}, bf16[2,2,34,256]{3,2,1,0:T(8,128)(2,1)S(1)}, u32[]{:S(2)}, u32[]{:S(2)}) collective-permute-start(bf16[2,2,34,256]{3,2,1,0:T(8,128)(2,1)S(1)} %pad_maximum_fusion.2), channel_id=1, source_target_pairs={{1,4},{3,6},{4,1},{5,8},{6,3},{7,10},{8,5},{9,12},{10,7},{11,14},{... | collective-permute-start | bytes 208904 | tf_op jit(solution)/shard_map/ppermute | solution.py:36
  16.5 8.0 %collective-permute-start.4 = (bf16[480,256]{1,0:T(8,128)(2,1)S(1)}, bf16[480,256]{1,0:T(8,128)(2,1)S(1)}, u32[]{:S(2)}, u32[]{:S(2)}) collective-permute-start(bf16[480,256]{1,0:T(8,128)(2,1)S(1)} %encode_frame1.1.tgt), channel_id=1, source_target_pairs={{0,2},{1,3},{2,0},{3,1},{4,6},{5,7},{6,4},{7,5},{8,10},{9,11},{10,... | collective-permute-start | bytes 737288 | tf_op jit(solution)/shard_map/ppermute | solution.py:36
  17.7 6.8 %collective-permute-start.3 = (bf16[480,256]{1,0:T(8,128)(2,1)S(1)}, bf16[480,256]{1,0:T(8,128)(2,1)S(1)}, u32[]{:S(2)}, u32[]{:S(2)}) collective-permute-start(bf16[480,256]{1,0:T(8,128)(2,1)S(1)} %encode_frame1.1.tgt), channel_id=1, source_target_pairs={{0,1},{1,0},{2,3},{3,2},{4,5},{5,4},{6,7},{7,6},{8,9},{9,8},{10,11... | collective-permute-start | bytes 737288 | tf_op jit(solution)/shard_map/ppermute | solution.py:36
  20.9 10.7 %copy-start.3 = (s32[1,1,9]{2,1,0:T(1,128)S(1)}, s32[1,1,9]{2,1,0:T(1,128)}, u32[]{:S(2)}) copy-start(s32[1,1,9]{2,1,0:T(1,128)} %param.9) | copy-start | bytes 112
  24.6 1.5 %collective-permute-start.5 = (bf16[480,256]{1,0:T(8,128)(2,1)S(1)}, bf16[480,256]{1,0:T(8,128)(2,1)S(1)}, u32[]{:S(2)}, u32[]{:S(2)}) collective-permute-start(bf16[480,256]{1,0:T(8,128)(2,1)S(1)} %collective-permute-done.4), channel_id=1, source_target_pairs={{0,1},{1,0},{2,3},{3,2},{4,5},{5,4},{6,7},{7,6},{8,9},{9,8},{10,11... | collective-permute-start | bytes 737288 | tf_op jit(solution)/shard_map/ppermute | solution.py:36
  26.1 16.1 %collective-permute-start.6 = (bf16[1920,256]{1,0:T(8,128)(2,1)S(1)}, bf16[1920,256]{1,0:T(8,128)(2,1)}, u32[]{:S(2)}, u32[]{:S(2)}) collective-permute-start(bf16[1920,256]{1,0:T(8,128)(2,1)S(1)} %pad_maximum_fusion.level), channel_id=1, source_target_pairs={{0,4},{2,6},{4,8},{5,1},{6,10},{7,3},{8,12},{9,5},{10,14},{11,7},{... | collective-permute-start | bytes 2949128 | tf_op jit(solution)/shard_map/ppermute | solution.py:36
  29.6 6.5 %collective-permute-start.8 = (bf16[480,256]{1,0:T(8,128)(2,1)S(1)}, bf16[480,256]{1,0:T(8,128)(2,1)S(1)}, u32[]{:S(2)}, u32[]{:S(2)}) collective-permute-start(bf16[480,256]{1,0:T(8,128)(2,1)S(1)} %encode_frame0.1.q), channel_id=1, source_target_pairs={{0,2},{1,3},{2,0},{3,1},{4,6},{5,7},{6,4},{7,5},{8,10},{9,11},{10,... | collective-permute-start | bytes 737288 | tf_op jit(solution)/shard_map/ppermute | solution.py:36
  31.5 4.6 %collective-permute-start.7 = (bf16[480,256]{1,0:T(8,128)(2,1)S(1)}, bf16[480,256]{1,0:T(8,128)(2,1)S(1)}, u32[]{:S(2)}, u32[]{:S(2)}) collective-permute-start(bf16[480,256]{1,0:T(8,128)(2,1)S(1)} %encode_frame0.1.q), channel_id=1, source_target_pairs={{0,1},{1,0},{2,3},{3,2},{4,5},{5,4},{6,7},{7,6},{8,9},{9,8},{10,11... | collective-permute-start | bytes 737288 | tf_op jit(solution)/shard_map/ppermute | solution.py:36
  33.5 12.3 %copy-start.4 = (f32[2,15,30]{2,0,1:T(2,128)S(1)}, f32[2,15,30]{2,0,1:T(2,128)}, u32[]{:S(2)}) copy-start(f32[2,15,30]{2,0,1:T(2,128)} %param.11) | copy-start | bytes 10804
  36.1 1.5 %collective-permute-start.9 = (bf16[480,256]{1,0:T(8,128)(2,1)S(1)}, bf16[480,256]{1,0:T(8,128)(2,1)S(1)}, u32[]{:S(2)}, u32[]{:S(2)}) collective-permute-start(bf16[480,256]{1,0:T(8,128)(2,1)S(1)} %collective-permute-done.8), channel_id=1, source_target_pairs={{0,1},{1,0},{2,3},{3,2},{4,5},{5,4},{6,7},{7,6},{8,9},{9,8},{10,11... | collective-permute-start | bytes 737288 | tf_op jit(solution)/shard_map/ppermute | solution.py:36
  42.2 3.6 %collective-permute-start.10 = (bf16[1920,256]{1,0:T(8,128)(2,1)}, bf16[1920,256]{1,0:T(8,128)(2,1)}, u32[]{:S(2)}, u32[]{:S(2)}) collective-permute-start(bf16[1920,256]{1,0:T(8,128)(2,1)} %collective-permute-done.6.got), channel_id=1, source_target_pairs={{0,1},{1,0},{2,3},{3,2},{4,5},{5,4},{6,7},{7,6},{8,9},{9,8},{10,11... | collective-permute-start | bytes 2949128 | tf_op jit(solution)/shard_map/ppermute | solution.py:36
  42.2 16.1 %collective-permute-start.14 = (bf16[1920,256]{1,0:T(8,128)(2,1)S(1)}, bf16[1920,256]{1,0:T(8,128)(2,1)}, u32[]{:S(2)}, u32[]{:S(2)}) collective-permute-start(bf16[1920,256]{1,0:T(8,128)(2,1)S(1)} %pad_maximum_fusion.1.refs_0_), channel_id=1, source_target_pairs={{0,4},{2,6},{4,8},{5,1},{6,10},{7,3},{8,12},{9,5},{10,14},{11,7},{... | collective-permute-start | bytes 2949128 | tf_op jit(solution)/shard_map/ppermute | solution.py:36
  50.9 1.2 %collective-permute-start.11 = (f32[8,480]{1,0:T(8,128)S(1)}, f32[8,480]{1,0:T(8,128)S(1)}, u32[]{:S(2)}, u32[]{:S(2)}) collective-permute-start(f32[8,480]{1,0:T(8,128)S(1)} %get-tuple-element.31), channel_id=1, source_target_pairs={{0,1},{1,0},{2,3},{3,2},{4,5},{5,4},{6,7},{7,6},{8,9},{9,8},{10,11... | collective-permute-start | bytes 46088 | tf_op jit(solution)/shard_map/ppermute | solution.py:36
  50.9 3.8 %collective-permute-start.12 = (f32[8,480]{1,0:T(8,128)S(1)}, f32[8,480]{1,0:T(8,128)S(1)}, u32[]{:S(2)}, u32[]{:S(2)}) collective-permute-start(f32[8,480]{1,0:T(8,128)S(1)} %get-tuple-element.31), channel_id=1, source_target_pairs={{0,2},{1,3},{2,0},{3,1},{4,6},{5,7},{6,4},{7,5},{8,10},{9,11},{10,... | collective-permute-start | bytes 46088 | tf_op jit(solution)/shard_map/ppermute | solution.py:36
  54.7 1.2 %collective-permute-start.13 = (f32[8,480]{1,0:T(8,128)S(1)}, f32[8,480]{1,0:T(8,128)S(1)}, u32[]{:S(2)}, u32[]{:S(2)}) collective-permute-start(f32[8,480]{1,0:T(8,128)S(1)} %collective-permute-done.12), channel_id=1, source_target_pairs={{0,1},{1,0},{2,3},{3,2},{4,5},{5,4},{6,7},{7,6},{8,9},{9,8},{10,11... | collective-permute-start | bytes 46088 | tf_op jit(solution)/shard_map/ppermute | solution.py:36
  58.3 9.8 %collective-permute-start.15 = (bf16[1920,256]{1,0:T(8,128)(2,1)}, bf16[1920,256]{1,0:T(8,128)(2,1)S(1)}, u32[]{:S(2)}, u32[]{:S(2)}) collective-permute-start(bf16[1920,256]{1,0:T(8,128)(2,1)} %collective-permute-done.14.refs_1_), channel_id=1, source_target_pairs={{0,1},{1,0},{2,3},{3,2},{4,5},{5,4},{6,7},{7,6},{8,9},{9,8},{10,11... | collective-permute-start | bytes 2949128 | tf_op jit(solution)/shard_map/ppermute | solution.py:36
  58.3 8.4 %collective-permute-start.16 = (f32[32,480]{1,0:T(8,128)S(1)}, f32[32,480]{1,0:T(8,128)S(1)}, u32[]{:S(2)}, u32[]{:S(2)}) collective-permute-start(f32[32,480]{1,0:T(8,128)S(1)} %constant_dynamic-update-slice_fusion.refs_3_), channel_id=1, source_target_pairs={{0,4},{2,6},{4,8},{5,1},{6,10},{7,3},{8,12},{9,5},{10,14},{11,7},{... | collective-permute-start | bytes 184328 | tf_op jit(solution)/shard_map/ppermute | solution.py:36
  66.8 1.3 %collective-permute-start.17 = (f32[32,480]{1,0:T(8,128)S(1)}, f32[32,480]{1,0:T(8,128)S(1)}, u32[]{:S(2)}, u32[]{:S(2)}) collective-permute-start(f32[32,480]{1,0:T(8,128)S(1)} %collective-permute-done.16.refs_4_), channel_id=1, source_target_pairs={{0,1},{1,0},{2,3},{3,2},{4,5},{5,4},{6,7},{7,6},{8,9},{9,8},{10,11... | collective-permute-start | bytes 184328 | tf_op jit(solution)/shard_map/ppermute | solution.py:36

commit v8 on v7

--- a/solution.py
+++ b/solution.py
@@ -21,7 +21,7 @@
 RB = 16
 COST = pl.CostEstimate(flops=10**6, bytes_accessed=10**4, transcendentals=0)
 ANY = pl.BlockSpec(memory_space=pl.ANY)
-HBM = pl.BlockSpec(memory_space=pltpu.HBM)
+LIMIT = 12 * 2**20
 
 
 def send(value, step):
@@ -138,28 +138,14 @@
             pltpu.VMEM((HID * PADW + 8, ch), jnp.float32),
             pltpu.VMEM((HID * PADW, 3 * ch), jnp.bfloat16),
         ],
-        compiler_params=pltpu.CompilerParams(vmem_limit_bytes=14 * 2**20),
+        compiler_params=pltpu.CompilerParams(vmem_limit_bytes=LIMIT),
         cost_estimate=COST,
         name=f"encode_frame{frame}",
     )(sc, mine, got, xl, xr, z, w1, w2)
 
 
-def load(tiles, buf, sems, at):
-    pltpu.make_async_copy(tiles, buf.at[at], sems.at[at]).start()
-
-
-def load_rows(level, got, other, buf, sems, core):
-    load(level, buf, sems, 1)
-    load(got, buf, sems, 2 * core)
-    load(other, buf, sems, 2 - 2 * core)
-
-
-def wait_for(tiles, buf, sems, at):
-    pltpu.make_async_copy(tiles, buf.at[at], sems.at[at]).wait()
-
-
-def half_tile(buf, a, j, i):
-    return buf[a, pl.ds(pl.multiple_of((2 * j + i) * HC, HC), HC)]
+def half_tile(tiles, j, i):
+    return tiles[pl.ds(pl.multiple_of((2 * j + i) * HC, HC), HC)]
 
 
 def slot_steps(slot, n_cs, n_c, col):
@@ -190,10 +176,10 @@
     return lane, lane % PADW < TILE, lane < HC - 384
 
 
-def add_tile(c2, a, j, dr, dc, core, q, buf, state):
+def add_tile(c2, j, dr, dc, core, q, tiles, state):
     whole = [
         lax.dot_general(
-            q[...], half_tile(buf, a, j, i), (((1,), (1,)), ((), ())), preferred_element_type=jnp.float32
+            q[...], half_tile(tiles, j, i), (((1,), (1,)), ((), ())), preferred_element_type=jnp.float32
         )
         for i in range(2)
     ]
@@ -237,9 +223,8 @@
         state[3, rows] = state[3, rows] * factor + col_base * both
 
 
-def near_kernel(n_c, n_cs, c2, sc, cand, count, q, level, state, buf, sems):
+def near_kernel(n_c, n_cs, c2, sc, cand, count, q, level, state):
     core, col = sc[0], sc[2]
-    load(level, buf, sems, 0)
     state[0] = jnp.full(state.shape[1:], -jnp.inf, jnp.float32)
     for k in range(1, 4):
         state[k] = jnp.zeros(state.shape[1:], jnp.float32)
@@ -247,13 +232,9 @@
     def step(j, carry):
         dr, dc, _, hit = listed(n_cs + j, n_cs, n_c, col, cand, count)
 
-        @pl.when(j == 0)
-        def _():
-            wait_for(level, buf, sems, 0)
-
         @pl.when(hit == 1)
         def _():
-            add_tile(c2, 0, j, dr, dc, core, q, buf, state)
+            add_tile(c2, j, dr, dc, core, q, level, state)
 
         return carry
 
@@ -261,27 +242,22 @@
 
 
 def far_kernel(n_c, n_cs, c2, sc, cand, count, q, ctg, begun, got, other, *refs):
-    flow, stats, packed_out, buf, sems, state = refs
+    flow, stats, packed_out, state = refs
     core, col = sc[0], sc[2]
-    load(got, buf, sems, core)
-    load(other, buf, sems, 1 - core)
     state[...] = begun[...]
 
-    def step(i, carry):
-        a, j = i // n_cs, i % n_cs
-        dr, dc, _, hit = listed(2 * a * n_cs + j, n_cs, n_c, col, cand, count)
-
-        @pl.when(j == 0)
-        def _():
-            wait_for(got, buf, sems, a)
-
-        @pl.when(hit == 1)
-        def _():
-            add_tile(c2, a, j, dr, dc, core, q, buf, state)
-
-        return carry
-
-    lax.fori_loop(0, 2 * n_cs, step, 0)
+    for a, tiles in ((core, got), (1 - core, other)):
+
+        def step(j, carry):
+            dr, dc, _, hit = listed(2 * a * n_cs + j, n_cs, n_c, col, cand, count)
+
+            @pl.when(hit == 1)
+            def _():
+                add_tile(c2, j, dr, dc, core, q, tiles, state)
+
+            return carry
+
+        lax.fori_loop(0, n_cs, step, 0)
     where_at = lax.broadcasted_iota(jnp.int32, (128, HC), 0)
     ok = where_at % PADW < TILE
     norm = jnp.transpose(state[1])
@@ -321,12 +297,12 @@
         q4[k] = jnp.broadcast_to(packed[:, k : k + 1], (HC, 128))
 
 
-def grad_tile(c2, a, j, dr, dc, core, q, buf, acc, q4):
+def grad_tile(c2, j, dr, dc, core, q, tiles, acc, q4):
     lane, lane_ok, _ = lanes(RB)
     lane_row = (lane // PADW).astype(jnp.float32)
     lane_col = (lane % PADW + 30 * dc).astype(jnp.float32)
     for i in range(2):
-        tile = half_tile(buf, a, j, i)
+        tile = half_tile(tiles, j, i)
         base = lane_row + (30 * dr + 15 * half_of(dr, i, core)).astype(jnp.float32)
         s = lax.dot_general(
             q[...], tile, (((1,), (1,)), ((), ())), preferred_element_type=jnp.float32
@@ -348,19 +324,17 @@
         acc[...] += jnp.dot(jnp.concatenate(ds), tile, preferred_element_type=jnp.float32)
 
 
-def grad_near_kernel(n_c, n_cs, c2, sc, cand, count, q, packed, level, acc, buf, sems, q4):
+def grad_near_kernel(n_c, n_cs, c2, sc, cand, count, q, packed, level, acc, q4):
     core, col = sc[0], sc[2]
-    load(level, buf, sems, 0)
     acc[...] = jnp.zeros(acc.shape, jnp.float32)
     spread(packed, q4)
-    wait_for(level, buf, sems, 0)
 
     def step(j, carry):
         dr, dc, _, hit = listed(n_cs + j, n_cs, n_c, col, cand, count)
 
         @pl.when(hit == 1)
         def _():
-            grad_tile(c2, 0, j, dr, dc, core, q, buf, acc, q4)
+            grad_tile(c2, j, dr, dc, core, q, level, acc, q4)
 
         return carry
 
@@ -368,43 +342,34 @@
 
 
 def grad_far_kernel(n_c, n_cs, c2, sc, cand, count, q, packed, begun, got, other, *refs):
-    out, buf, sems, q4, acc = refs
+    out, q4, acc = refs
     core, col = sc[0], sc[2]
-    load(got, buf, sems, core)
-    load(other, buf, sems, 1 - core)
     acc[...] = begun[...]
     spread(packed, q4)
 
-    def step(i, carry):
-        a, j = i // n_cs, i % n_cs
-        dr, dc, _, hit = listed(2 * a * n_cs + j, n_cs, n_c, col, cand, count)
-
-        @pl.when(j == 0)
-        def _():
-            wait_for(got, buf, sems, a)
-
-        @pl.when(hit == 1)
-        def _():
-            grad_tile(c2, a, j, dr, dc, core, q, buf, acc, q4)
-
-        return carry
-
-    lax.fori_loop(0, 2 * n_cs, step, 0)
+    for a, tiles in ((core, got), (1 - core, other)):
+
+        def step(j, carry):
+            dr, dc, _, hit = listed(2 * a * n_cs + j, n_cs, n_c, col, cand, count)
+
+            @pl.when(hit == 1)
+            def _():
+                grad_tile(c2, j, dr, dc, core, q, tiles, acc, q4)
+
+            return carry
+
+        lax.fori_loop(0, n_cs, step, 0)
     out[...] = acc[...].reshape(HALF, PADW, acc.shape[1])[:, :TILE]
 
 
-def tiles_call(kernel, n_c, ch, rows, n_cs, out_shape, scratch, vmem_ins, ins, tiles):
+def tiles_call(kernel, n_c, ch, n_cs, out_shape, scratch, ins, tiles):
     return pl.pallas_call(
         functools.partial(kernel, n_c, n_cs, math.log2(math.e) / math.sqrt(ch)),
         out_shape=out_shape,
-        in_specs=[SMEM] * 3 + [VMEM] * vmem_ins + [HBM] * len(tiles),
+        in_specs=[SMEM] * 3 + [VMEM] * (len(ins) - 3 + len(tiles)),
         out_specs=jax.tree.map(lambda _: VMEM, out_shape),
-        scratch_shapes=[
-            pltpu.VMEM((rows, n_cs * 2 * HC, ch), jnp.bfloat16),
-            pltpu.SemaphoreType.DMA((rows,)),
-        ]
-        + scratch,
-        compiler_params=pltpu.CompilerParams(vmem_limit_bytes=14 * 2**20),
+        scratch_shapes=scratch,
+        compiler_params=pltpu.CompilerParams(vmem_limit_bytes=LIMIT),
         cost_estimate=COST,
         name=kernel.__name__,
     )(*ins, *tiles)
@@ -413,8 +378,7 @@
 def query_near(n_c, sc, cand, count, q, level):
     ch, n_cs = q.shape[1], level.shape[0] // (2 * HC)
     out_shape = jax.ShapeDtypeStruct((4, HC, 128), jnp.float32)
-    return tiles_call(
-        near_kernel, n_c, ch, 1, n_cs, out_shape, [], 1, (sc, cand, count, q), (level,)
+    return tiles_call(near_kernel, n_c, ch, n_cs, out_shape, [], (sc, cand, count, q), (level,)
     )
 
 
@@ -427,7 +391,7 @@
     )
     scratch = [pltpu.VMEM((4, HC, 128), jnp.float32)]
     ins = (sc, cand, count, q, ctg, begun)
-    return tiles_call(far_kernel, n_c, ch, 2, n_cs, out_shape, scratch, 3, ins, (got, other))
+    return tiles_call(far_kernel, n_c, ch, n_cs, out_shape, scratch, ins, (got, other))
 
 
 def grad_near(n_c, sc, cand, count, q, packed, level):
@@ -435,7 +399,7 @@
     out_shape = jax.ShapeDtypeStruct((HC, ch), jnp.float32)
     scratch = [pltpu.VMEM((4, HC, 128), jnp.float32)]
     ins = (sc, cand, count, q, packed)
-    return tiles_call(grad_near_kernel, n_c, ch, 1, n_cs, out_shape, scratch, 2, ins, (level,))
+    return tiles_call(grad_near_kernel, n_c, ch, n_cs, out_shape, scratch, ins, (level,))
 
 
 def grad_far(n_c, sc, cand, count, q, packed, begun, got, other):
@@ -443,54 +407,45 @@
     out_shape = jax.ShapeDtypeStruct((HALF, TILE, ch), jnp.float32)
     scratch = [pltpu.VMEM((4, HC, 128), jnp.float32), pltpu.VMEM((HC, ch), jnp.float32)]
     ins = (sc, cand, count, q, packed, begun)
-    return tiles_call(grad_far_kernel, n_c, ch, 2, n_cs, out_shape, scratch, 3, ins, (got, other))
+    return tiles_call(grad_far_kernel, n_c, ch, n_cs, out_shape, scratch, ins, (got, other))
 
 
 def target_kernel(n_c, n_cs, c2, sc, tgt, *refs):
-    feats, stats = refs[:3], refs[3:6]
-    out, buf, sems, st, st_sems, v_scr, acc = refs[6:]
+    feats, stats, (out, v_scr, acc) = refs[:3], refs[3:6], refs[6:]
     core, col = sc[0], sc[2]
-    load_rows(*stats, st, st_sems, core)
-    load_rows(*feats, buf, sems, core)
     acc[...] = jnp.zeros(acc.shape, jnp.float32)
-
-    def step(slot, carry):
-        dr, dc = slot_steps(slot, n_cs, n_c, col)
-        a, j = slot // n_cs, slot % n_cs
-
-        @pl.when(j == 0)
-        def _():
-            wait_for(feats[0], buf, sems, a)
-            wait_for(stats[0], st, st_sems, a)
-
-        code = 8 - (3 * (dr + 1) + dc + 1)
-        where_at = lax.broadcasted_iota(jnp.int32, (8, HC), 1)
-        which = lax.broadcasted_iota(jnp.int32, (8, HC), 0)
-        flag = jnp.sum(jnp.where((where_at == code) & (which == 4), st[a, pl.ds(pl.multiple_of(16 * j, 16), 8)], 0.0))
-
-        @pl.when(flag > 0.5)
-        def _():
-            col_t = (
-                lax.broadcasted_iota(jnp.int32, (PADW, HC), 0) - 30 * dc
-            ).astype(jnp.float32)
-            for i in range(2):
-                tile = half_tile(buf, a, j, i)
-                four = st[a, pl.ds(pl.multiple_of((2 * j + i) * 8, 8), 8)]
-                lev, gr, gc, sh = (four[k : k + 1] for k in range(4))
-                v_scr[...] = gc * col_t - sh
-                s = lax.dot_general(
-                    tgt[...], tile, (((1,), (1,)), ((), ())), preferred_element_type=jnp.float32
-                )
-                ds = []
-                for g in range(HALF):
-                    row_t = (g + HALF * core - 30 * dr).astype(jnp.float32)
-                    p = jnp.exp2(s[g * PADW : (g + 1) * PADW] * c2 - lev)
-                    ds.append((p * (v_scr[...] + gr * row_t)).astype(jnp.bfloat16))
-                acc[...] += jnp.dot(jnp.concatenate(ds), tile, preferred_element_type=jnp.float32)
-
-        return carry
-
-    lax.fori_loop(0, 3 * n_cs, step, 0)
+    for a, tiles, st in zip((1, 2 * core, 2 - 2 * core), feats, stats):
+
+        def step(j, carry):
+            dr, dc = slot_steps(a * n_cs + j, n_cs, n_c, col)
+            code = 8 - (3 * (dr + 1) + dc + 1)
+            where_at = lax.broadcasted_iota(jnp.int32, (8, HC), 1)
+            which = lax.broadcasted_iota(jnp.int32, (8, HC), 0)
+            flag = jnp.sum(jnp.where((where_at == code) & (which == 4), st[pl.ds(pl.multiple_of(16 * j, 16), 8)], 0.0))
+
+            @pl.when(flag > 0.5)
+            def _():
+                col_t = (
+                    lax.broadcasted_iota(jnp.int32, (PADW, HC), 0) - 30 * dc
+                ).astype(jnp.float32)
+                for i in range(2):
+                    tile = half_tile(tiles, j, i)
+                    four = st[pl.ds(pl.multiple_of((2 * j + i) * 8, 8), 8)]
+                    lev, gr, gc, sh = (four[k : k + 1] for k in range(4))
+                    v_scr[...] = gc * col_t - sh
+                    s = lax.dot_general(
+                        tgt[...], tile, (((1,), (1,)), ((), ())), preferred_element_type=jnp.float32
+                    )
+                    ds = []
+                    for g in range(HALF):
+                        row_t = (g + HALF * core - 30 * dr).astype(jnp.float32)
+                        p = jnp.exp2(s[g * PADW : (g + 1) * PADW] * c2 - lev)
+                        ds.append((p * (v_scr[...] + gr * row_t)).astype(jnp.bfloat16))
+                    acc[...] += jnp.dot(jnp.concatenate(ds), tile, preferred_element_type=jnp.float32)
+
+            return carry
+
+        lax.fori_loop(0, n_cs, step, 0)
     out[...] = acc[...].reshape(HALF, PADW, acc.shape[1])[:, :TILE]
 
 
@@ -499,17 +454,13 @@
     return pl.pallas_call(
         functools.partial(target_kernel, n_c, n_cs, math.log2(math.e) / math.sqrt(ch)),
         out_shape=jax.ShapeDtypeStruct((HALF, TILE, ch), jnp.float32),
-        in_specs=[SMEM, VMEM] + [HBM] * 6,
+        in_specs=[SMEM] + [VMEM] * 7,
         out_specs=VMEM,
         scratch_shapes=[
-            pltpu.VMEM((3, n_cs * 2 * HC, ch), jnp.bfloat16),
-            pltpu.SemaphoreType.DMA((3,)),
-            pltpu.VMEM((3, n_cs * 2 * 8, HC), jnp.float32),
-            pltpu.SemaphoreType.DMA((3,)),
             pltpu.VMEM((PADW, HC), jnp.float32),
             pltpu.VMEM((HC, ch), jnp.float32),
         ],
-        compiler_params=pltpu.CompilerParams(vmem_limit_bytes=14 * 2**20),
+        compiler_params=pltpu.CompilerParams(vmem_limit_bytes=LIMIT),
         cost_estimate=COST,
         name="target_side",
     )(sc, tgt, *feats, *stats)

time: 76 us -> 75.4 us (level); the launches traced: 75.7 us -> 74 us
  waiting for transfers between devices: 23.7 us -> 22.1 us
    pallas_call x1, Pallas kernels: 7.63 us -> 5.04 us  [target_side(): pl.pallas_call(functools.partial(target_kernel, n_c, n_cs, math.log2(math...]
    pallas_call x4, Pallas kernels: 13.8 us -> 16.2 us  [tiles_call(): pl.pallas_call(functools.partial(kernel, n_c, n_cs, math.log2(math.e) / m...]
    ppermute x18, waiting for transfers between devices: 23.7 us -> 22.1 us  [send(): return lax.ppermute(value, AXES, pairs)]
  transfers between devices with their start and end apart: 18 -> 18, of which waited for: 12 -> 12; matrix products, arithmetic and copies ran while one was open for 4% -> 4% of each run, Pallas kernels for 23% -> 27%
where the time goes in v8:
time: 75.4 us; the launch traced here: 74 us
  Pallas kernels  28 us (37%)
  waiting for transfers between devices  22.1 us (29%)
  starting transfers between devices  16.8 us (22%)
  local copies, waits for them, and re-layouts  3.35 us (4%)
  other arithmetic  2.22 us (3%)
  between operations  1.55 us (2%)
    ppermute x18, waiting for transfers between devices, send(): return lax.ppermute(value, AXES, pairs)  22.1 us
    ppermute x18, starting transfers between devices, send(): return lax.ppermute(value, AXES, pairs)  16.8 us
    pallas_call x4, Pallas kernels, tiles_call(): pl.pallas_call(functools.partial(kernel, n_c, n_cs, math.log2(math.e) / m...  16.2 us
    pallas_call x2, Pallas kernels, encode(): pl.pallas_call(functools.partial(encode_kernel, frame, n_r, n_c), out_sha...  6.25 us
    pallas_call x1, Pallas kernels, target_side(): pl.pallas_call(functools.partial(target_kernel, n_c, n_cs, math.log2(math...  5.04 us
    unnamed x15, local copies, waits for them, and re-layouts  3.17 us
  transfers between devices with their start and end apart: 18, of which 12 were waited for; matrix products, arithmetic and copies ran while one was open for 4% of the time, Pallas kernels for 27%

profile of v8, /device:TPU:12, one launch (start us, length us, event | category | flops | bytes accessed | tf_op | source)
XLA Modules:
  0.0 74.0 jit_solution(14860417660761312403)
XLA Ops:
  2.9 1.6 %collective-permute-start.1 = (bf16[2,30,2,256]{3,2,1,0:T(2,128)(2,1)S(1)}, bf16[2,30,2,256]{3,2,1,0:T(2,128)(2,1)S(1)}, u32[]{:S(2)}, u32[]{:S(2)}) collective-permute-start(bf16[2,30,2,256]{3,2,1,0:T(2,128)(2,1)S(1)} %pad_maximum_fusion.3), channel_id=1, source_target_pairs={{0,2},{1,3},{2,0},{3,1},{4,6},{5,7},{6,4},{7,5},{8,10},{9,11},{10,... | collective-permute-start | bytes 184328 | tf_op jit(solution)/shard_map/ppermute | solution.py:36
  4.5 1.3 %copy-done.1 = bf16[9,256,256]{2,1,0:T(8,128)(2,1)S(1)} copy-done((bf16[9,256,256]{2,1,0:T(8,128)(2,1)S(1)}, bf16[9,256,256]{2,1,0:T(8,128)(2,1)}, u32[]{:S(2)}) %copy-start.1) | copy-done | bytes 1179672
  5.8 1.3 %copy-done.2 = bf16[9,256,256]{2,1,0:T(8,128)(2,1)S(1)} copy-done((bf16[9,256,256]{2,1,0:T(8,128)(2,1)S(1)}, bf16[9,256,256]{2,1,0:T(8,128)(2,1)}, u32[]{:S(2)}) %copy-start.2) | copy-done | bytes 1179672
  7.6 1.9 %collective-permute-start.2 = (bf16[2,2,34,256]{3,2,1,0:T(8,128)(2,1)S(1)}, bf16[2,2,34,256]{3,2,1,0:T(8,128)(2,1)S(1)}, u32[]{:S(2)}, u32[]{:S(2)}) collective-permute-start(bf16[2,2,34,256]{3,2,1,0:T(8,128)(2,1)S(1)} %pad_maximum_fusion.2), channel_id=1, source_target_pairs={{1,4},{3,6},{4,1},{5,8},{6,3},{7,10},{8,5},{9,12},{10,7},{11,14},{... | collective-permute-start | bytes 208904 | tf_op jit(solution)/shard_map/ppermute | solution.py:36
  9.7 3.7 %collective-permute-done.2.z = bf16[2,2,34,256]{3,2,1,0:T(8,128)(2,1)S(1)} collective-permute-done((bf16[2,2,34,256]{3,2,1,0:T(8,128)(2,1)S(1)}, bf16[2,2,34,256]{3,2,1,0:T(8,128)(2,1)S(1)}, u32[]{:S(2)}, u32[]{:S(2)}) %collective-permute-start.2) | collective-permute-done | bytes 69664 | tf_op jit(solution)/shard_map/ppermute | solution.py:36
  13.4 3.1 %encode_frame1.1.tgt = bf16[480,256]{1,0:T(8,128)(2,1)S(1)} custom-call(s32[3]{0:T(128)S(1)} %pad_add_fusion.sc, bf16[30,30,256]{2,1,0:T(8,128)(2,1)S(1)} %bitcast.37, bf16[30,30,256]{2,1,0:T(8,128)(2,1)S(1)} %collective-permute-done.got, bf16[2,30,2,256]{3,2,1,0:T(2,128)(2,1)S(1)} %collective-permute-done.1.xl.xr, ...), custom_call_target="tpu_custom_call" | custom-call | flops 1000000 | bytes 10000 | tf_op jit(solution)/shard_map/encode_frame1/pallas_call | solution.py:130
  16.5 1.2 %collective-permute-start.4 = (bf16[480,256]{1,0:T(8,128)(2,1)S(1)}, bf16[480,256]{1,0:T(8,128)(2,1)S(1)}, u32[]{:S(2)}, u32[]{:S(2)}) collective-permute-start(bf16[480,256]{1,0:T(8,128)(2,1)S(1)} %encode_frame1.1.tgt), channel_id=1, source_target_pairs={{0,2},{1,3},{2,0},{3,1},{4,6},{5,7},{6,4},{7,5},{8,10},{9,11},{10,... | collective-permute-start | bytes 737288 | tf_op jit(solution)/shard_map/ppermute | solution.py:36
  17.8 3.1 %encode_frame0.1.q = bf16[480,256]{1,0:T(8,128)(2,1)S(1)} custom-call(s32[3]{0:T(128)S(1)} %pad_add_fusion.sc, bf16[30,30,256]{2,1,0:T(8,128)(2,1)S(1)} %bitcast.38, bf16[30,30,256]{2,1,0:T(8,128)(2,1)S(1)} %collective-permute-done.got, bf16[2,30,2,256]{3,2,1,0:T(2,128)(2,1)S(1)} %collective-permute-done.1.xl.xr, ...), custom_call_target="tpu_custom_call" | custom-call | flops 1000000 | bytes 10000 | tf_op jit(solution)/shard_map/encode_frame0/pallas_call | solution.py:130
  20.9 3.7 %collective-permute-done.4 = bf16[480,256]{1,0:T(8,128)(2,1)S(1)} collective-permute-done((bf16[480,256]{1,0:T(8,128)(2,1)S(1)}, bf16[480,256]{1,0:T(8,128)(2,1)S(1)}, u32[]{:S(2)}, u32[]{:S(2)}) %collective-permute-start.4) | collective-permute-done | bytes 245792 | tf_op jit(solution)/shard_map/ppermute | solution.py:36
  24.6 1.5 %collective-permute-done.5 = bf16[480,256]{1,0:T(8,128)(2,1)S(1)} collective-permute-done((bf16[480,256]{1,0:T(8,128)(2,1)S(1)}, bf16[480,256]{1,0:T(8,128)(2,1)S(1)}, u32[]{:S(2)}, u32[]{:S(2)}) %collective-permute-start.5) | collective-permute-done | bytes 245792 | tf_op jit(solution)/shard_map/ppermute | solution.py:36
  26.1 3.5 %collective-permute-start.6 = (bf16[1920,256]{1,0:T(8,128)(2,1)S(1)}, bf16[1920,256]{1,0:T(8,128)(2,1)}, u32[]{:S(2)}, u32[]{:S(2)}) collective-permute-start(bf16[1920,256]{1,0:T(8,128)(2,1)S(1)} %pad_maximum_fusion.level), channel_id=1, source_target_pairs={{0,4},{2,6},{4,8},{5,1},{6,10},{7,3},{8,12},{9,5},{10,14},{11,7},{... | collective-permute-start | bytes 2949128 | tf_op jit(solution)/shard_map/ppermute | solution.py:36
  29.6 1.2 %collective-permute-start.8 = (bf16[480,256]{1,0:T(8,128)(2,1)S(1)}, bf16[480,256]{1,0:T(8,128)(2,1)S(1)}, u32[]{:S(2)}, u32[]{:S(2)}) collective-permute-start(bf16[480,256]{1,0:T(8,128)(2,1)S(1)} %encode_frame0.1.q), channel_id=1, source_target_pairs={{0,2},{1,3},{2,0},{3,1},{4,6},{5,7},{6,4},{7,5},{8,10},{9,11},{10,... | collective-permute-start | bytes 737288 | tf_op jit(solution)/shard_map/ppermute | solution.py:36
  31.6 2.4 %near_kernel.1.begun = f32[4,480,128]{2,1,0:T(8,128)S(1)} custom-call(s32[3]{0:T(128)S(1)} %pad_add_fusion.sc, s32[9]{0:T(128)S(1)} %bitcast.39, s32[1]{0:T(128)} %bitcast.27.count, bf16[480,256]{1,0:T(8,128)(2,1)S(1)} %encode_frame0.1.q, bf16[1920,256]{1,0:T(8,128)(2,1)S(1)} %pad_maximum_fusion.level), custom_call_target="tpu_custom_call" | custom-call | flops 1000000 | bytes 10000 | tf_op jit(solution)/shard_map/near_kernel/pallas_call | solution.py:366
  34.1 2.1 %collective-permute-done.8 = bf16[480,256]{1,0:T(8,128)(2,1)S(1)} collective-permute-done((bf16[480,256]{1,0:T(8,128)(2,1)S(1)}, bf16[480,256]{1,0:T(8,128)(2,1)S(1)}, u32[]{:S(2)}, u32[]{:S(2)}) %collective-permute-start.8) | collective-permute-done | bytes 245792 | tf_op jit(solution)/shard_map/ppermute | solution.py:36
  36.1 1.5 %collective-permute-done.9 = bf16[480,256]{1,0:T(8,128)(2,1)S(1)} collective-permute-done((bf16[480,256]{1,0:T(8,128)(2,1)S(1)}, bf16[480,256]{1,0:T(8,128)(2,1)S(1)}, u32[]{:S(2)}, u32[]{:S(2)}) %collective-permute-start.9) | collective-permute-done | bytes 245792 | tf_op jit(solution)/shard_map/ppermute | solution.py:36
  37.7 4.5 %collective-permute-done.6.got = bf16[1920,256]{1,0:T(8,128)(2,1)} collective-permute-done((bf16[1920,256]{1,0:T(8,128)(2,1)S(1)}, bf16[1920,256]{1,0:T(8,128)(2,1)}, u32[]{:S(2)}, u32[]{:S(2)}) %collective-permute-start.6) | collective-permute-done | bytes 983072 | tf_op jit(solution)/shard_map/ppermute | solution.py:36
  42.2 3.5 %collective-permute-start.14 = (bf16[1920,256]{1,0:T(8,128)(2,1)S(1)}, bf16[1920,256]{1,0:T(8,128)(2,1)}, u32[]{:S(2)}, u32[]{:S(2)}) collective-permute-start(bf16[1920,256]{1,0:T(8,128)(2,1)S(1)} %pad_maximum_fusion.1.refs_0_), channel_id=1, source_target_pairs={{0,4},{2,6},{4,8},{5,1},{6,10},{7,3},{8,12},{9,5},{10,14},{11,7},{... | collective-permute-start | bytes 2949128 | tf_op jit(solution)/shard_map/ppermute | solution.py:36
  45.9 5.7 %far_kernel.1 = (f32[2,480]{1,0:T(2,128)S(1)}, f32[8,480]{1,0:T(8,128)S(1)}, f32[480,128]{1,0:T(8,128)S(1)}) custom-call(s32[3]{0:T(128)S(1)} %pad_add_fusion.sc, s32[9]{0:T(128)S(1)} %bitcast.40, s32[1]{0:T(128)} %bitcast.28.count, bf16[480,256]{1,0:T(8,128)(2,1)S(1)} %encode_frame0.1.q, f32[8,480]{1,0:T(8,128)S(1)} %reshape.60.ctg, ...), custom_call_target="tpu_custom_call" | custom-call | flops 1000000 | bytes 10000 | tf_op jit(solution)/shard_map/far_kernel/pallas_call | solution.py:366
  52.8 2.4 %grad_near_kernel.1.begun = f32[480,256]{1,0:T(8,128)S(1)} custom-call(s32[3]{0:T(128)S(1)} %pad_add_fusion.sc, s32[9]{0:T(128)S(1)} %bitcast.41, s32[1]{0:T(128)} %bitcast.29.count, bf16[480,256]{1,0:T(8,128)(2,1)S(1)} %encode_frame0.1.q, f32[480,128]{1,0:T(8,128)S(1)} %get-tuple-element.35.packed, bf16[1920,256]{1,0:T(8,128)(2,1)S(1)} %pad_maximum_fusion.level), custom_call_target="tpu_custom_call" | custom-call | flops 1000000 | bytes 10000 | tf_op jit(solution)/shard_map/grad_near_kernel/pallas_call | solution.py:366
  55.4 1.2 %collective-permute-done.13 = f32[8,480]{1,0:T(8,128)S(1)} collective-permute-done((f32[8,480]{1,0:T(8,128)S(1)}, f32[8,480]{1,0:T(8,128)S(1)}, u32[]{:S(2)}, u32[]{:S(2)}) %collective-permute-start.13) | collective-permute-done | bytes 15392 | tf_op jit(solution)/shard_map/ppermute | solution.py:36
  56.6 1.7 %collective-permute-done.14.refs_1_ = bf16[1920,256]{1,0:T(8,128)(2,1)} collective-permute-done((bf16[1920,256]{1,0:T(8,128)(2,1)S(1)}, bf16[1920,256]{1,0:T(8,128)(2,1)}, u32[]{:S(2)}, u32[]{:S(2)}) %collective-permute-start.14) | collective-permute-done | bytes 983072 | tf_op jit(solution)/shard_map/ppermute | solution.py:36
  58.3 3.7 %collective-permute-start.16 = (f32[32,480]{1,0:T(8,128)S(1)}, f32[32,480]{1,0:T(8,128)S(1)}, u32[]{:S(2)}, u32[]{:S(2)}) collective-permute-start(f32[32,480]{1,0:T(8,128)S(1)} %constant_dynamic-update-slice_fusion.refs_3_), channel_id=1, source_target_pairs={{0,4},{2,6},{4,8},{5,1},{6,10},{7,3},{8,12},{9,5},{10,14},{11,7},{... | collective-permute-start | bytes 184328 | tf_op jit(solution)/shard_map/ppermute | solution.py:36
  62.0 5.7 %grad_far_kernel.1 = f32[15,30,256]{2,1,0:T(8,128)} custom-call(s32[3]{0:T(128)S(1)} %pad_add_fusion.sc, s32[9]{0:T(128)S(1)} %bitcast.42, s32[1]{0:T(128)} %bitcast.30.count, bf16[480,256]{1,0:T(8,128)(2,1)S(1)} %encode_frame0.1.q, f32[480,128]{1,0:T(8,128)S(1)} %get-tuple-element.35.packed, f32[480,256]{1,0:T(8,128)S(1)} %grad_near_kernel.1.begun, ...), custom_call_target="tpu_custom_call" | custom-call | flops 1000000 | bytes 10000 | tf_op jit(solution)/shard_map/grad_far_kernel/pallas_call | solution.py:366
  69.0 5.0 %target_side.1 = f32[15,30,256]{2,1,0:T(8,128)} custom-call(s32[3]{0:T(128)S(1)} %pad_add_fusion.sc, bf16[480,256]{1,0:T(8,128)(2,1)S(1)} %encode_frame1.1.tgt, bf16[1920,256]{1,0:T(8,128)(2,1)S(1)} %pad_maximum_fusion.1.refs_0_, bf16[1920,256]{1,0:T(8,128)(2,1)} %collective-permute-done.14.refs_1_, bf16[1920,256]{1,0:T(8,128)(2,1)S(1)} %collective-permute-done.15.refs_2_, ...), custom_call_target="tpu_custom_call" | custom-call | flops 1000000 | bytes 10000 | tf_op jit(solution)/shard_map/target_side/pallas_call | solution.py:454
  (51 shorter events, 6.0 us)
Async XLA Ops:
  0.6 2.1 %collective-permute-start = (bf16[30,30,256]{2,1,0:T(8,128)(2,1)}, bf16[30,30,256]{2,1,0:T(8,128)(2,1)S(1)}, u32[]{:S(2)}, u32[]{:S(2)}) collective-permute-start(bf16[30,30,256]{2,1,0:T(8,128)(2,1)} %bitcast.35), channel_id=1, source_target_pairs={{0,1},{1,0},{2,3},{3,2},{4,5},{5,4},{6,7},{7,6},{8,9},{9,8},{10,11... | collective-permute-start | bytes 1382408 | tf_op jit(solution)/shard_map/ppermute | solution.py:36
  2.9 4.6 %collective-permute-start.1 = (bf16[2,30,2,256]{3,2,1,0:T(2,128)(2,1)S(1)}, bf16[2,30,2,256]{3,2,1,0:T(2,128)(2,1)S(1)}, u32[]{:S(2)}, u32[]{:S(2)}) collective-permute-start(bf16[2,30,2,256]{3,2,1,0:T(2,128)(2,1)S(1)} %pad_maximum_fusion.3), channel_id=1, source_target_pairs={{0,2},{1,3},{2,0},{3,1},{4,6},{5,7},{6,4},{7,5},{8,10},{9,11},{10,... | collective-permute-start | bytes 184328 | tf_op jit(solution)/shard_map/ppermute | solution.py:36
  4.5 1.3 %copy-start.1 = (bf16[9,256,256]{2,1,0:T(8,128)(2,1)S(1)}, bf16[9,256,256]{2,1,0:T(8,128)(2,1)}, u32[]{:S(2)}) copy-start(bf16[9,256,256]{2,1,0:T(8,128)(2,1)} %a) | copy-start | bytes 3538948
  5.8 1.3 %copy-start.2 = (bf16[9,256,256]{2,1,0:T(8,128)(2,1)S(1)}, bf16[9,256,256]{2,1,0:T(8,128)(2,1)}, u32[]{:S(2)}) copy-start(bf16[9,256,256]{2,1,0:T(8,128)(2,1)} %b.1) | copy-start | bytes 3538948
  7.0 6.4 %copy-start = (bf16[1,30,30,256]{3,2,1,0:T(8,128)(2,1)S(1)}, bf16[1,30,30,256]{3,2,1,0:T(8,128)(2,1)}, u32[]{:S(2)}) copy-start(bf16[1,30,30,256]{3,2,1,0:T(8,128)(2,1)} %param.6) | copy-start | bytes 1382404
  7.6 5.8 %collective-permute-start.2 = (bf16[2,2,34,256]{3,2,1,0:T(8,128)(2,1)S(1)}, bf16[2,2,34,256]{3,2,1,0:T(8,128)(2,1)S(1)}, u32[]{:S(2)}, u32[]{:S(2)}) collective-permute-start(bf16[2,2,34,256]{3,2,1,0:T(8,128)(2,1)S(1)} %pad_maximum_fusion.2), channel_id=1, source_target_pairs={{1,4},{3,6},{4,1},{5,8},{6,3},{7,10},{8,5},{9,12},{10,7},{11,14},{... | collective-permute-start | bytes 208904 | tf_op jit(solution)/shard_map/ppermute | solution.py:36
  16.5 8.0 %collective-permute-start.4 = (bf16[480,256]{1,0:T(8,128)(2,1)S(1)}, bf16[480,256]{1,0:T(8,128)(2,1)S(1)}, u32[]{:S(2)}, u32[]{:S(2)}) collective-permute-start(bf16[480,256]{1,0:T(8,128)(2,1)S(1)} %encode_frame1.1.tgt), channel_id=1, source_target_pairs={{0,2},{1,3},{2,0},{3,1},{4,6},{5,7},{6,4},{7,5},{8,10},{9,11},{10,... | collective-permute-start | bytes 737288 | tf_op jit(solution)/shard_map/ppermute | solution.py:36
  17.7 6.8 %collective-permute-start.3 = (bf16[480,256]{1,0:T(8,128)(2,1)S(1)}, bf16[480,256]{1,0:T(8,128)(2,1)S(1)}, u32[]{:S(2)}, u32[]{:S(2)}) collective-permute-start(bf16[480,256]{1,0:T(8,128)(2,1)S(1)} %encode_frame1.1.tgt), channel_id=1, source_target_pairs={{0,1},{1,0},{2,3},{3,2},{4,5},{5,4},{6,7},{7,6},{8,9},{9,8},{10,11... | collective-permute-start | bytes 737288 | tf_op jit(solution)/shard_map/ppermute | solution.py:36
  20.9 10.7 %copy-start.3 = (s32[1,1,9]{2,1,0:T(1,128)S(1)}, s32[1,1,9]{2,1,0:T(1,128)}, u32[]{:S(2)}) copy-start(s32[1,1,9]{2,1,0:T(1,128)} %param.9) | copy-start | bytes 112
  24.6 1.5 %collective-permute-start.5 = (bf16[480,256]{1,0:T(8,128)(2,1)S(1)}, bf16[480,256]{1,0:T(8,128)(2,1)S(1)}, u32[]{:S(2)}, u32[]{:S(2)}) collective-permute-start(bf16[480,256]{1,0:T(8,128)(2,1)S(1)} %collective-permute-done.4), channel_id=1, source_target_pairs={{0,1},{1,0},{2,3},{3,2},{4,5},{5,4},{6,7},{7,6},{8,9},{9,8},{10,11... | collective-permute-start | bytes 737288 | tf_op jit(solution)/shard_map/ppermute | solution.py:36
  26.1 16.1 %collective-permute-start.6 = (bf16[1920,256]{1,0:T(8,128)(2,1)S(1)}, bf16[1920,256]{1,0:T(8,128)(2,1)}, u32[]{:S(2)}, u32[]{:S(2)}) collective-permute-start(bf16[1920,256]{1,0:T(8,128)(2,1)S(1)} %pad_maximum_fusion.level), channel_id=1, source_target_pairs={{0,4},{2,6},{4,8},{5,1},{6,10},{7,3},{8,12},{9,5},{10,14},{11,7},{... | collective-permute-start | bytes 2949128 | tf_op jit(solution)/shard_map/ppermute | solution.py:36
  29.6 6.5 %collective-permute-start.8 = (bf16[480,256]{1,0:T(8,128)(2,1)S(1)}, bf16[480,256]{1,0:T(8,128)(2,1)S(1)}, u32[]{:S(2)}, u32[]{:S(2)}) collective-permute-start(bf16[480,256]{1,0:T(8,128)(2,1)S(1)} %encode_frame0.1.q), channel_id=1, source_target_pairs={{0,2},{1,3},{2,0},{3,1},{4,6},{5,7},{6,4},{7,5},{8,10},{9,11},{10,... | collective-permute-start | bytes 737288 | tf_op jit(solution)/shard_map/ppermute | solution.py:36
  31.5 4.6 %collective-permute-start.7 = (bf16[480,256]{1,0:T(8,128)(2,1)S(1)}, bf16[480,256]{1,0:T(8,128)(2,1)S(1)}, u32[]{:S(2)}, u32[]{:S(2)}) collective-permute-start(bf16[480,256]{1,0:T(8,128)(2,1)S(1)} %encode_frame0.1.q), channel_id=1, source_target_pairs={{0,1},{1,0},{2,3},{3,2},{4,5},{5,4},{6,7},{7,6},{8,9},{9,8},{10,11... | collective-permute-start | bytes 737288 | tf_op jit(solution)/shard_map/ppermute | solution.py:36
  34.1 11.7 %copy-start.4 = (f32[2,15,30]{2,0,1:T(2,128)S(1)}, f32[2,15,30]{2,0,1:T(2,128)}, u32[]{:S(2)}) copy-start(f32[2,15,30]{2,0,1:T(2,128)} %param.11) | copy-start | bytes 10804
  36.1 1.5 %collective-permute-start.9 = (bf16[480,256]{1,0:T(8,128)(2,1)S(1)}, bf16[480,256]{1,0:T(8,128)(2,1)S(1)}, u32[]{:S(2)}, u32[]{:S(2)}) collective-permute-start(bf16[480,256]{1,0:T(8,128)(2,1)S(1)} %collective-permute-done.8), channel_id=1, source_target_pairs={{0,1},{1,0},{2,3},{3,2},{4,5},{5,4},{6,7},{7,6},{8,9},{9,8},{10,11... | collective-permute-start | bytes 737288 | tf_op jit(solution)/shard_map/ppermute | solution.py:36
  42.2 3.6 %collective-permute-start.10 = (bf16[1920,256]{1,0:T(8,128)(2,1)}, bf16[1920,256]{1,0:T(8,128)(2,1)}, u32[]{:S(2)}, u32[]{:S(2)}) collective-permute-start(bf16[1920,256]{1,0:T(8,128)(2,1)} %collective-permute-done.6.got), channel_id=1, source_target_pairs={{0,1},{1,0},{2,3},{3,2},{4,5},{5,4},{6,7},{7,6},{8,9},{9,8},{10,11... | collective-permute-start | bytes 2949128 | tf_op jit(solution)/shard_map/ppermute | solution.py:36
  42.2 16.1 %collective-permute-start.14 = (bf16[1920,256]{1,0:T(8,128)(2,1)S(1)}, bf16[1920,256]{1,0:T(8,128)(2,1)}, u32[]{:S(2)}, u32[]{:S(2)}) collective-permute-start(bf16[1920,256]{1,0:T(8,128)(2,1)S(1)} %pad_maximum_fusion.1.refs_0_), channel_id=1, source_target_pairs={{0,4},{2,6},{4,8},{5,1},{6,10},{7,3},{8,12},{9,5},{10,14},{11,7},{... | collective-permute-start | bytes 2949128 | tf_op jit(solution)/shard_map/ppermute | solution.py:36
  51.5 1.2 %collective-permute-start.11 = (f32[8,480]{1,0:T(8,128)S(1)}, f32[8,480]{1,0:T(8,128)S(1)}, u32[]{:S(2)}, u32[]{:S(2)}) collective-permute-start(f32[8,480]{1,0:T(8,128)S(1)} %get-tuple-element.31), channel_id=1, source_target_pairs={{0,1},{1,0},{2,3},{3,2},{4,5},{5,4},{6,7},{7,6},{8,9},{9,8},{10,11... | collective-permute-start | bytes 46088 | tf_op jit(solution)/shard_map/ppermute | solution.py:36
  51.6 3.8 %collective-permute-start.12 = (f32[8,480]{1,0:T(8,128)S(1)}, f32[8,480]{1,0:T(8,128)S(1)}, u32[]{:S(2)}, u32[]{:S(2)}) collective-permute-start(f32[8,480]{1,0:T(8,128)S(1)} %get-tuple-element.31), channel_id=1, source_target_pairs={{0,2},{1,3},{2,0},{3,1},{4,6},{5,7},{6,4},{7,5},{8,10},{9,11},{10,... | collective-permute-start | bytes 46088 | tf_op jit(solution)/shard_map/ppermute | solution.py:36
  55.4 1.2 %collective-permute-start.13 = (f32[8,480]{1,0:T(8,128)S(1)}, f32[8,480]{1,0:T(8,128)S(1)}, u32[]{:S(2)}, u32[]{:S(2)}) collective-permute-start(f32[8,480]{1,0:T(8,128)S(1)} %collective-permute-done.12), channel_id=1, source_target_pairs={{0,1},{1,0},{2,3},{3,2},{4,5},{5,4},{6,7},{7,6},{8,9},{9,8},{10,11... | collective-permute-start | bytes 46088 | tf_op jit(solution)/shard_map/ppermute | solution.py:36
  58.3 10.7 %collective-permute-start.15 = (bf16[1920,256]{1,0:T(8,128)(2,1)}, bf16[1920,256]{1,0:T(8,128)(2,1)S(1)}, u32[]{:S(2)}, u32[]{:S(2)}) collective-permute-start(bf16[1920,256]{1,0:T(8,128)(2,1)} %collective-permute-done.14.refs_1_), channel_id=1, source_target_pairs={{0,1},{1,0},{2,3},{3,2},{4,5},{5,4},{6,7},{7,6},{8,9},{9,8},{10,11... | collective-permute-start | bytes 2949128 | tf_op jit(solution)/shard_map/ppermute | solution.py:36
  58.3 9.4 %collective-permute-start.16 = (f32[32,480]{1,0:T(8,128)S(1)}, f32[32,480]{1,0:T(8,128)S(1)}, u32[]{:S(2)}, u32[]{:S(2)}) collective-permute-start(f32[32,480]{1,0:T(8,128)S(1)} %constant_dynamic-update-slice_fusion.refs_3_), channel_id=1, source_target_pairs={{0,4},{2,6},{4,8},{5,1},{6,10},{7,3},{8,12},{9,5},{10,14},{11,7},{... | collective-permute-start | bytes 184328 | tf_op jit(solution)/shard_map/ppermute | solution.py:36
  67.7 1.3 %collective-permute-start.17 = (f32[32,480]{1,0:T(8,128)S(1)}, f32[32,480]{1,0:T(8,128)S(1)}, u32[]{:S(2)}, u32[]{:S(2)}) collective-permute-start(f32[32,480]{1,0:T(8,128)S(1)} %collective-permute-done.16.refs_4_), channel_id=1, source_target_pairs={{0,1},{1,0},{2,3},{3,2},{4,5},{5,4},{6,7},{7,6},{8,9},{9,8},{10,11... | collective-permute-start | bytes 184328 | tf_op jit(solution)/shard_map/ppermute | solution.py:36
